TPU v7x, 32 devices: a whole 2x2x4 slice. The times are simulated.
32 devices in a mesh: dp: 2 (over y), ctx: 16 (over z, x, core).
Axes of the slice: x: 2, y: 2, z: 4, core: 2. Of those that a mesh axis runs over, the one named last changes fastest.
Arguments:
- tokens: bfloat16 [8192, 1024], P(('dp', 'ctx')), may hold values from -6 to 6
- lengths: int32 [2, 3], P('dp'), may hold values from 1 to 3840, as said below
- cotangent: bfloat16 [8192, 1024], P(('dp', 'ctx')), may hold values from -6 to 6
- mixgain: bfloat16 [1024], replicated, may hold values from 0.5 to 1.5
- mixentry: bfloat16 [1024, 3072], replicated, may hold values from -0.1875 to 0.1875
- mixtaps: bfloat16 [3, 1024], replicated, may hold values from -3.5 to 3.5
- mixexit: bfloat16 [1024, 1024], replicated, may hold values from -0.1875 to 0.1875
- lowgain: bfloat16 [1024], replicated, may hold values from 0.5 to 1.5
- lowgate: bfloat16 [1024, 4608], replicated, may hold values from -0.1875 to 0.1875
- lowlift: bfloat16 [1024, 4608], replicated, may hold values from -0.1875 to 0.1875
- lowdrop: bfloat16 [4608, 1024], replicated, may hold values from -0.09375 to 0.09375
- attgain: bfloat16 [1024], replicated, may hold values from 0.5 to 1.5
- attquery: bfloat16 [1024, 1024], replicated, may hold values from -0.1875 to 0.1875
- attkeys: bfloat16 [1024, 512], replicated, may hold values from -0.1875 to 0.1875
- attvalues: bfloat16 [1024, 512], replicated, may hold values from -0.1875 to 0.1875
- querygain: bfloat16 [64], replicated, may hold values from 1.1953125 to 2
- keysgain: bfloat16 [64], replicated, may hold values from 1.1953125 to 2
- attexit: bfloat16 [1024, 1024], replicated, may hold values from -0.75 to 0.75
- topgain: bfloat16 [1024], replicated, may hold values from 0.5 to 1.5
- topgate: bfloat16 [1024, 4608], replicated, may hold values from -0.1875 to 0.1875
- toplift: bfloat16 [1024, 4608], replicated, may hold values from -0.1875 to 0.1875
- topdrop: bfloat16 [4608, 1024], replicated, may hold values from -0.09375 to 0.09375
Outputs:
- output: float32 [8192, 1024], P(('dp', 'ctx'))
- tokens_grad: float32 [8192, 1024], P(('dp', 'ctx'))
- mixgain_grad: float32 [1024], replicated
- mixentry_grad: float32 [1024, 3072], P('ctx')
- mixtaps_grad: float32 [3, 1024], replicated
- mixexit_grad: float32 [1024, 1024], P('ctx')
- lowgain_grad: float32 [1024], replicated
- lowgate_grad: float32 [1024, 4608], P('ctx')
- lowlift_grad: float32 [1024, 4608], P('ctx')
- lowdrop_grad: float32 [4608, 1024], P('ctx')
- attgain_grad: float32 [1024], replicated
- attquery_grad: float32 [1024, 1024], P('ctx')
- attkeys_grad: float32 [1024, 512], P('ctx')
- attvalues_grad: float32 [1024, 512], P('ctx')
- querygain_grad: float32 [64], replicated
- keysgain_grad: float32 [64], replicated
- attexit_grad: float32 [1024, 1024], P('ctx')
- topgain_grad: float32 [1024], replicated
- topgate_grad: float32 [1024, 4608], P('ctx')
- toplift_grad: float32 [1024, 4608], P('ctx')
- topdrop_grad: float32 [4608, 1024], P('ctx')
Inputs may be any that keep to these rules, and one draw needn't show every extreme that they name: `lengths`: each group holds three documents in order: the first shorter than 256 tokens, the second of 3840 tokens, the third of 256 minus the first's length.
All inputs are finite; a program needn't handle non-finite values.
Results may differ from a plain program's by a relative error of at most 0.04.
Values may be sent and summed in bfloat16 or wider, within the bound.
A program may use at most 384 MiB of HBM per device.

v0:
```python
import math

import jax
import jax.numpy as jnp
from jax import lax
from jax.sharding import PartitionSpec as P

EPS = 1e-05
THETA = 1000000.0
NEGATIVE = -1e30


def passed_along(value, axis, steps):
    count = lax.axis_size(axis)
    first, last = (max(0, -steps), min(count, count - steps))
    return lax.ppermute(value, axis, [(source, source + steps) for source in range(first, last)])


def passed_along_2(block, axis, distance):
    devices = range(lax.axis_size(axis))
    route = [((i - distance) % len(devices), i) for i in devices]
    return lax.ppermute(block, axis, route)


def root_mean_square_scale(hidden, gain):
    return hidden * lax.rsqrt(jnp.mean(hidden * hidden, axis=-1, keepdims=True) + EPS) * gain


def rotary_embed(value_rows, position_index):
    half = value_rows.shape[-1] // 2
    freq = THETA ** (-jnp.arange(half, dtype=jnp.float32) * 2.0 / value_rows.shape[-1])
    angle = position_index.astype(jnp.float32)[:, None] * freq[None, :]
    cosine = jnp.cos(angle)[:, None, :]
    sine = jnp.sin(angle)[:, None, :]
    front = value_rows[..., :half]
    behind = value_rows[..., half:]
    return jnp.concatenate(
        [front * cosine - behind * sine, behind * cosine + front * sine], axis=-1
    )


def head_prep(raw, gain, position_index, heads):
    shaped = raw.reshape(raw.shape[0], heads, -1)
    return rotary_embed(root_mean_square_scale(shaped, gain), position_index)


def segment_of(where, first, second):
    return (where >= first).astype(jnp.int32) + (where >= second).astype(jnp.int32)


def block_width(count):
    best = 1
    for candidate in range(1, min(count, 1024) + 1):
        if count % candidate == 0:
            best = candidate
    return best


def sweep(carry, count, visit):
    width = block_width(count)
    return lax.fori_loop(
        0, count // width, lambda index, inner: visit(inner, index * width, width), carry
    )


def inner_dot(left, right):
    return lax.dot_general(
        left, right, (((0,), (0,)), ((), ())), preferred_element_type=jnp.float32
    )


def outer_dot(left, right):
    return lax.dot_general(
        left, right, (((1,), (1,)), ((), ())), preferred_element_type=jnp.float32
    )


def scores_of(query_part, key_part, query_where, key_where, query_seg, key_seg, scale):
    raw = (
        jnp.einsum("tkgd,pkd->kgtp", query_part, key_part, preferred_element_type=jnp.float32)
        * scale
    )
    allowed = (query_seg[:, None] == key_seg[None, :]) & (
        query_where[:, None] >= key_where[None, :]
    )
    return (raw, allowed)


def grad_block(
    query_part,
    grad_part,
    logsum_part,
    delta_part,
    key_part,
    value_part,
    query_where,
    key_where,
    query_seg,
    key_seg,
    scale,
):
    raw, allowed = scores_of(
        query_part, key_part, query_where, key_where, query_seg, key_seg, scale
    )
    prob = jnp.where(allowed, jnp.exp(raw - logsum_part[..., None]), 0.0)
    prob_grad = jnp.einsum(
        "tkgd,pkd->kgtp", grad_part, value_part, preferred_element_type=jnp.float32
    )
    score_grad = (prob * (prob_grad - delta_part[..., None])).astype(jnp.bfloat16)
    query_grad = (
        jnp.einsum("kgtp,pkd->tkgd", score_grad, key_part, preferred_element_type=jnp.float32)
        * scale
    )
    key_grad = (
        jnp.einsum("kgtp,tkgd->pkd", score_grad, query_part, preferred_element_type=jnp.float32)
        * scale
    )
    value_grad = jnp.einsum(
        "kgtp,tkgd->pkd", prob.astype(jnp.bfloat16), grad_part, preferred_element_type=jnp.float32
    )
    return (query_grad, key_grad, value_grad)


def conv_local(extended, taps, fits_one, fits_two):
    rows = extended.shape[0] - 2
    return (
        taps[2] * extended[2:]
        + taps[1] * extended[1 : rows + 1] * fits_one
        + taps[0] * extended[:rows] * fits_two
    )


def feed_forward(hidden, gain, gate_weight, lift_weight, drop_weight):
    fnormed = root_mean_square_scale(hidden, gain).astype(jnp.bfloat16)
    gate_act = jnp.dot(fnormed, gate_weight, preferred_element_type=jnp.float32)
    lift_act = jnp.dot(fnormed, lift_weight, preferred_element_type=jnp.float32)
    inner = (jax.nn.silu(gate_act) * lift_act).astype(jnp.bfloat16)
    result = hidden + jnp.dot(inner, drop_weight, preferred_element_type=jnp.float32)
    return (result, (fnormed, gate_act, lift_act, inner))


def feed_back(grad, hidden, gain, kept, gate_weight, lift_weight, drop_weight):
    fnormed, gate_act, lift_act, inner = kept
    grad_low = grad.astype(jnp.bfloat16)
    drop_grad = inner_dot(inner, grad_low)
    inner_grad = outer_dot(grad_low, drop_weight)
    _, pull_gate = jax.vjp(
        lambda gate_in, lift_in: jax.nn.silu(gate_in) * lift_in, gate_act, lift_act
    )
    gate_grad, lift_grad = pull_gate(inner_grad)
    gate_low = gate_grad.astype(jnp.bfloat16)
    lift_low = lift_grad.astype(jnp.bfloat16)
    gate_wgrad = inner_dot(fnormed, gate_low)
    lift_wgrad = inner_dot(fnormed, lift_low)
    normed_grad = outer_dot(gate_low, gate_weight) + outer_dot(lift_low, lift_weight)
    _, pull_norm = jax.vjp(root_mean_square_scale, hidden, gain)
    hidden_grad, gain_grad = pull_norm(normed_grad)
    return (grad + hidden_grad, (gain_grad, gate_wgrad, lift_wgrad, drop_grad))


def per_device(
    tokens,
    lengths,
    cotangent,
    mixgain,
    mixentry,
    mixtaps,
    mixexit,
    lowgain,
    lowgate,
    lowlift,
    lowdrop,
    attgain,
    attquery,
    attkeys,
    attvalues,
    querygain,
    keysgain,
    attexit,
    topgain,
    topgate,
    toplift,
    topdrop,
):
    rows = tokens.shape[0]
    width_model = tokens.shape[1]
    head_size = querygain.shape[0]
    query_heads = attquery.shape[1] // head_size
    kv_heads = attkeys.shape[1] // head_size
    shared_gradient = query_heads // kv_heads
    scale = 1.0 / math.sqrt(head_size)
    place = lax.axis_index("ctx")
    first = lengths[0, 0]
    second = first + lengths[0, 1]
    mine = place * rows + jnp.arange(rows, dtype=jnp.int32)
    my_seg = segment_of(mine, first, second)
    begin = jnp.where(my_seg == 0, 0, jnp.where(my_seg == 1, first, second))
    position_index = mine - begin
    last_row = place * rows + rows - 1
    mixgain_f = mixgain.astype(jnp.float32)
    taps_f = mixtaps.astype(jnp.float32)
    lowgain_f = lowgain.astype(jnp.float32)
    attgain_f = attgain.astype(jnp.float32)
    querygain_f = querygain.astype(jnp.float32)
    keysgain_f = keysgain.astype(jnp.float32)
    topgain_f = topgain.astype(jnp.float32)
    hidden = tokens.astype(jnp.float32)
    normed_one = root_mean_square_scale(hidden, mixgain_f).astype(jnp.bfloat16)
    mixed = jnp.dot(normed_one, mixentry, preferred_element_type=jnp.float32)
    part_b = mixed[:, :width_model]
    part_c = mixed[:, width_model : 2 * width_model]
    part_x = mixed[:, 2 * width_model :]
    product = (part_b * part_x).astype(jnp.bfloat16)
    borrowed = passed_along(product[rows - 2 :], "ctx", 1)
    extended = jnp.concatenate([borrowed, product], axis=0).astype(jnp.float32)
    fits_one = ((mine >= 1) & (segment_of(mine - 1, first, second) == my_seg)).astype(jnp.float32)[
        :, None
    ]
    fits_two = ((mine >= 2) & (segment_of(mine - 2, first, second) == my_seg)).astype(jnp.float32)[
        :, None
    ]
    conved = conv_local(extended, taps_f, fits_one, fits_two)
    gated = (part_c * conved).astype(jnp.bfloat16)
    hidden_one = hidden + jnp.dot(gated, mixexit, preferred_element_type=jnp.float32)
    hidden_two, kept_low = feed_forward(hidden_one, lowgain_f, lowgate, lowlift, lowdrop)
    normed_two = root_mean_square_scale(hidden_two, attgain_f).astype(jnp.bfloat16)
    query_unrotated = jnp.dot(normed_two, attquery, preferred_element_type=jnp.float32)
    key_unrotated = jnp.dot(normed_two, attkeys, preferred_element_type=jnp.float32)
    value_projected = jnp.dot(normed_two, attvalues, preferred_element_type=jnp.float32)
    query_low = head_prep(query_unrotated, querygain_f, position_index, query_heads).astype(
        jnp.bfloat16
    )
    key_low = head_prep(key_unrotated, keysgain_f, position_index, kv_heads).astype(jnp.bfloat16)
    value_low = value_projected.astype(jnp.bfloat16).reshape(rows, kv_heads, head_size)
    query_grouped = query_low.reshape(rows, kv_heads, shared_gradient, head_size)

    def stat_visit(carry, keys_in, start, offset, width):
        top, total = carry
        key_part = lax.dynamic_slice_in_dim(keys_in, offset, width, 0)
        key_where = start + offset + jnp.arange(width, dtype=jnp.int32)
        raw, allowed = scores_of(
            query_grouped,
            key_part,
            mine,
            key_where,
            my_seg,
            segment_of(key_where, first, second),
            scale,
        )
        new_top = jnp.maximum(top, jnp.max(jnp.where(allowed, raw, NEGATIVE), axis=-1))
        weights = jnp.where(allowed, jnp.exp(raw - new_top[..., None]), 0.0)
        total = total * jnp.exp(top - new_top) + jnp.sum(weights, axis=-1)
        return (new_top, total)

    stat_state = (
        jnp.full((kv_heads, shared_gradient, rows), NEGATIVE, jnp.float32),
        jnp.zeros((kv_heads, shared_gradient, rows), jnp.float32),
    )
    piece = lax.all_gather(key_low, "ctx", axis=0, tiled=True)
    start = jnp.int32(0)
    count = piece.shape[0]

    def stat_running(inner):
        return sweep(
            inner, count, lambda acc, offset, width: stat_visit(acc, piece, start, offset, width)
        )

    top, total = lax.cond(start > last_row, lambda inner: inner, stat_running, stat_state)
    logsum = top + jnp.log(total)

    def forward_visit(accum, keys_in, values_in, start, offset, width):
        key_part = lax.dynamic_slice_in_dim(keys_in, offset, width, 0)
        value_part = lax.dynamic_slice_in_dim(values_in, offset, width, 0)
        key_where = start + offset + jnp.arange(width, dtype=jnp.int32)
        raw, allowed = scores_of(
            query_grouped,
            key_part,
            mine,
            key_where,
            my_seg,
            segment_of(key_where, first, second),
            scale,
        )
        prob_low = jnp.where(allowed, jnp.exp(raw - logsum[..., None]), 0.0).astype(jnp.bfloat16)
        return accum + jnp.einsum(
            "kgtp,pkd->kgtd", prob_low, value_part, preferred_element_type=jnp.float32
        )

    forward_start = jnp.int32(0)
    keys_in = lax.all_gather(key_low, "ctx", axis=0, tiled=True)
    values_in = lax.all_gather(value_low, "ctx", axis=0, tiled=True)
    forward_count = keys_in.shape[0]

    def forward_running(inner):
        return sweep(
            inner,
            forward_count,
            lambda acc, offset, width: forward_visit(
                acc, keys_in, values_in, forward_start, offset, width
            ),
        )

    accum = lax.cond(
        forward_start > last_row,
        lambda inner: inner,
        forward_running,
        jnp.zeros((kv_heads, shared_gradient, rows, head_size), jnp.float32),
    )
    attended = accum.transpose(2, 0, 1, 3).reshape(rows, -1)
    attended_low = attended.astype(jnp.bfloat16)
    hidden_three = hidden_two + jnp.dot(attended_low, attexit, preferred_element_type=jnp.float32)
    output, kept_top = feed_forward(hidden_three, topgain_f, topgate, toplift, topdrop)
    grad = cotangent.astype(jnp.float32)
    grad, top_grads = feed_back(grad, hidden_three, topgain_f, kept_top, topgate, toplift, topdrop)
    grad_low = grad.astype(jnp.bfloat16)
    attexit_grad = inner_dot(attended_low, grad_low)
    out_grads = (
        outer_dot(grad_low, attexit)
        .astype(jnp.bfloat16)
        .reshape(rows, kv_heads, shared_gradient, head_size)
    )
    delta = jnp.einsum(
        "tkgd,tkgd->kgt",
        out_grads.astype(jnp.float32),
        attended.reshape(rows, kv_heads, shared_gradient, head_size),
    )
    cycle_size = lax.axis_size("ctx")

    def cycle_visit(state, keys_in, values_in, start, offset, width):
        query_acc, key_acc, value_acc = state
        key_part = lax.dynamic_slice_in_dim(keys_in, offset, width, 0)
        value_part = lax.dynamic_slice_in_dim(values_in, offset, width, 0)
        key_where = start + offset + jnp.arange(width, dtype=jnp.int32)
        query_grad, key_grad, value_grad = grad_block(
            query_grouped,
            out_grads,
            logsum,
            delta,
            key_part,
            value_part,
            mine,
            key_where,
            my_seg,
            segment_of(key_where, first, second),
            scale,
        )
        key_acc = lax.dynamic_update_slice_in_dim(
            key_acc, lax.dynamic_slice_in_dim(key_acc, offset, width, 0) + key_grad, offset, 0
        )
        value_acc = lax.dynamic_update_slice_in_dim(
            value_acc, lax.dynamic_slice_in_dim(value_acc, offset, width, 0) + value_grad, offset, 0
        )
        return (query_acc + query_grad, key_acc, value_acc)

    def cycle_step(step, carry):
        keys_cur, values_cur, key_acc, value_acc, query_acc = carry
        anchor = (place - step + cycle_size) % cycle_size
        start = anchor * rows

        def cycle_running(state):
            return sweep(
                state,
                rows,
                lambda acc, offset, width: cycle_visit(
                    acc, keys_cur, values_cur, start, offset, width
                ),
            )

        query_acc, key_acc, value_acc = lax.cond(
            start > last_row, lambda state: state, cycle_running, (query_acc, key_acc, value_acc)
        )
        keys_cur, values_cur = passed_along((keys_cur, values_cur), "ctx", 1)
        key_acc, value_acc = (
            passed_along_2(key_acc.astype(jnp.bfloat16), "ctx", 1).astype(key_acc.dtype),
            passed_along_2(value_acc.astype(jnp.bfloat16), "ctx", 1).astype(value_acc.dtype),
        )
        return (keys_cur, values_cur, key_acc, value_acc, query_acc)

    cycle_state = (
        key_low,
        value_low,
        jnp.zeros((rows, kv_heads, head_size), jnp.float32),
        jnp.zeros((rows, kv_heads, head_size), jnp.float32),
        jnp.zeros((rows, kv_heads, shared_gradient, head_size), jnp.float32),
    )
    _, _, key_grads, value_grads, query_acc = lax.fori_loop(0, cycle_size, cycle_step, cycle_state)
    _, pull_query = jax.vjp(
        lambda raw, gain: head_prep(raw, gain, position_index, query_heads),
        query_unrotated,
        querygain_f,
    )
    query_raw_grad, querygain_grad = pull_query(query_acc.reshape(rows, query_heads, head_size))
    _, pull_key = jax.vjp(
        lambda raw, gain: head_prep(raw, gain, position_index, kv_heads), key_unrotated, keysgain_f
    )
    key_raw_grad, keysgain_grad = pull_key(key_grads)
    query_raw_low = query_raw_grad.astype(jnp.bfloat16)
    key_raw_low = key_raw_grad.astype(jnp.bfloat16)
    value_raw_low = value_grads.reshape(rows, -1).astype(jnp.bfloat16)
    attquery_grad = inner_dot(normed_two, query_raw_low)
    attkeys_grad = inner_dot(normed_two, key_raw_low)
    attvalues_grad = inner_dot(normed_two, value_raw_low)
    normed_two_grad = (
        outer_dot(query_raw_low, attquery)
        + outer_dot(key_raw_low, attkeys)
        + outer_dot(value_raw_low, attvalues)
    )
    _, pull_att = jax.vjp(root_mean_square_scale, hidden_two, attgain_f)
    hidden_two_grad, attgain_grad = pull_att(normed_two_grad)
    grad = grad + hidden_two_grad
    grad, low_grads = feed_back(grad, hidden_one, lowgain_f, kept_low, lowgate, lowlift, lowdrop)
    grad_low = grad.astype(jnp.bfloat16)
    mixexit_grad = inner_dot(gated, grad_low)
    gated_grad = outer_dot(grad_low, mixexit)
    part_c_grad = gated_grad * conved
    conved_grad = gated_grad * part_c
    _, pull_conv = jax.vjp(
        lambda ext, taps: conv_local(ext, taps, fits_one, fits_two), extended, taps_f
    )
    extended_grad, mixtaps_grad = pull_conv(conved_grad)
    returned_rim = passed_along(extended_grad[:2], "ctx", -1)
    product_grad = extended_grad[2:].at[rows - 2 :].add(returned_rim)
    mixed_grad = jnp.concatenate(
        [product_grad * part_x, part_c_grad, product_grad * part_b], axis=1
    ).astype(jnp.bfloat16)
    mixentry_grad = inner_dot(normed_one, mixed_grad)
    normed_one_grad = outer_dot(mixed_grad, mixentry)
    _, pull_mix = jax.vjp(root_mean_square_scale, hidden, mixgain_f)
    hidden_grad, mixgain_grad = pull_mix(normed_one_grad)
    tokens_grad = grad + hidden_grad
    lowgain_grad, lowgate_grad, lowlift_grad, lowdrop_grad = low_grads
    topgain_grad, topgate_grad, toplift_grad, topdrop_grad = top_grads
    shares = (
        lax.psum_scatter(mixentry_grad, "ctx", scatter_dimension=0, tiled=True),
        lax.psum_scatter(mixexit_grad, "ctx", scatter_dimension=0, tiled=True),
        lax.psum_scatter(lowgate_grad, "ctx", scatter_dimension=0, tiled=True),
        lax.psum_scatter(lowlift_grad, "ctx", scatter_dimension=0, tiled=True),
        lax.psum_scatter(lowdrop_grad, "ctx", scatter_dimension=0, tiled=True),
        lax.psum_scatter(attquery_grad, "ctx", scatter_dimension=0, tiled=True),
        lax.psum_scatter(attkeys_grad, "ctx", scatter_dimension=0, tiled=True),
        lax.psum_scatter(attvalues_grad, "ctx", scatter_dimension=0, tiled=True),
        lax.psum_scatter(attexit_grad, "ctx", scatter_dimension=0, tiled=True),
        lax.psum_scatter(topgate_grad, "ctx", scatter_dimension=0, tiled=True),
        lax.psum_scatter(toplift_grad, "ctx", scatter_dimension=0, tiled=True),
        lax.psum_scatter(topdrop_grad, "ctx", scatter_dimension=0, tiled=True),
    )
    smalls = lax.psum(
        (
            mixgain_grad,
            mixtaps_grad,
            lowgain_grad,
            attgain_grad,
            querygain_grad,
            keysgain_grad,
            topgain_grad,
        ),
        "ctx",
    )
    summed = (
        lax.psum(shares[0].astype(jnp.bfloat16), "dp").astype(jnp.float32),
        lax.psum(shares[1].astype(jnp.bfloat16), "dp").astype(jnp.float32),
        lax.psum(shares[2].astype(jnp.bfloat16), "dp").astype(jnp.float32),
        lax.psum(shares[3].astype(jnp.bfloat16), "dp").astype(jnp.float32),
        lax.psum(shares[4].astype(jnp.bfloat16), "dp").astype(jnp.float32),
        lax.psum(shares[5].astype(jnp.bfloat16), "dp").astype(jnp.float32),
        lax.psum(shares[6].astype(jnp.bfloat16), "dp").astype(jnp.float32),
        lax.psum(shares[7].astype(jnp.bfloat16), "dp").astype(jnp.float32),
        lax.psum(shares[8].astype(jnp.bfloat16), "dp").astype(jnp.float32),
        lax.psum(shares[9].astype(jnp.bfloat16), "dp").astype(jnp.float32),
        lax.psum(shares[10].astype(jnp.bfloat16), "dp").astype(jnp.float32),
        lax.psum(shares[11].astype(jnp.bfloat16), "dp").astype(jnp.float32),
        lax.psum(smalls[0].astype(jnp.bfloat16), "dp").astype(jnp.float32),
        lax.psum(smalls[1].astype(jnp.bfloat16), "dp").astype(jnp.float32),
        lax.psum(smalls[2].astype(jnp.bfloat16), "dp").astype(jnp.float32),
        lax.psum(smalls[3].astype(jnp.bfloat16), "dp").astype(jnp.float32),
        lax.psum(smalls[4].astype(jnp.bfloat16), "dp").astype(jnp.float32),
        lax.psum(smalls[5].astype(jnp.bfloat16), "dp").astype(jnp.float32),
        lax.psum(smalls[6].astype(jnp.bfloat16), "dp").astype(jnp.float32),
    )
    return (
        output,
        tokens_grad,
        summed[12],
        summed[0],
        summed[13],
        summed[1],
        summed[14],
        summed[2],
        summed[3],
        summed[4],
        summed[15],
        summed[5],
        summed[6],
        summed[7],
        summed[16],
        summed[17],
        summed[8],
        summed[18],
        summed[9],
        summed[10],
        summed[11],
    )


def solution(mesh):
    placed = (
        P(("dp", "ctx"), None),
        P("dp", None),
        P(("dp", "ctx"), None),
        P(),
        P(),
        P(),
        P(),
        P(),
        P(),
        P(),
        P(),
        P(),
        P(),
        P(),
        P(),
        P(),
        P(),
        P(),
        P(),
        P(),
        P(),
        P(),
    )
    return jax.shard_map(
        per_device,
        mesh=mesh,
        in_specs=placed,
        out_specs=(
            P(("dp", "ctx"), None),
            P(("dp", "ctx"), None),
            P(),
            P("ctx", None),
            P(),
            P("ctx", None),
            P(),
            P("ctx", None),
            P("ctx", None),
            P("ctx", None),
            P(),
            P("ctx", None),
            P("ctx", None),
            P("ctx", None),
            P(),
            P(),
            P("ctx", None),
            P(),
            P("ctx", None),
            P("ctx", None),
            P("ctx", None),
        ),
        check_vma=False,
    )
```

profile of v0, /device:TPU:0, one launch (start us, length us, event | category | flops | bytes accessed | tf_op | source)
XLA Modules:
  0.0 2538.2 jit_solution(15885875035768633562)
XLA Ops:
  51.4 50.4 %all-gather.3.cloned.1.call-done = bf16[4096,8,64]{0,2,1:T(8,128)(2,1)} async-done(((bf16[256,8,64]{0,2,1:T(8,128)(2,1)}), bf16[4096,8,64]{0,2,1:T(8,128)(2,1)}) %all-gather.3.cloned.1.call-update) | async-done | bytes 4194320 | tf_op jit(solution)/shard_map/all_gather | solution.py:290
  101.8 76.2 %conditional.3 = (f32[8,2,256]{2,1,0:T(2,128)S(1)}, f32[8,2,256]{2,1,0:T(2,128)S(1)}) conditional(s32[]{:T(128)} %convert_element_type.450, (s32[256]{0:T(256)S(1)}, s32[]{:T(128)}, s32[]{:T(128)}, s32[256]{0:T(256)S(1)}, bf16[4096,8,64]{0,2,1:T(8,128)(2,1)}, /*index=5*/bf16[256,8,2,64]{0,3,2,1:T(8,128)(2,1)S(1)}) %tuple.88, () %tuple.89), branch_computations={%region_5.10_spmd, %region_10.11_spmd} | conditional | flops 567044096 | bytes 36145484 | solution.py:268
  101.8 76.2 %while.63 = (s32[]{:T(128)}, f32[8,2,256]{2,1,0:T(2,128)S(1)}, f32[8,2,256]{2,1,0:T(2,128)S(1)}, s32[256]{0:T(256)S(1)}, s32[]{:T(128)}, /*index=5*/s32[]{:T(128...) while((s32[]{:T(128)}, f32[8,2,256]{2,1,0:T(2,128)S(1)}, ...), condition=%wide.region_9.9_spmd.clone, body=%wide.region_6.8_spmd.clone.sunk | while | flops 567044096 | bytes 36145356 | solution.py:61
  103.0 8.8 fusion.207
  111.8 9.2 fusion.209
  122.1 8.5 fusion.207
  130.6 9.4 fusion.209
  141.1 8.6 fusion.207
  149.7 9.5 fusion.209
  160.3 8.5 fusion.207
  168.8 9.2 fusion.209
  178.1 64.9 %conditional.4 = (f32[8,2,256,64]{2,3,1,0:T(8,128)}) conditional(s32[]{:T(128)} %convert_element_type.450, (s32[256]{0:T(256)S(1)}, s32[]{:T(128)}, s32[]{:T(128)}, s32[256]{0:T(256)S(1)}, bf16[4096,8,64]{0,2,1:T(8,128)(2,1)}, /*index=5*/bf16[256,8,2,64]{0,3,2,1:T(8,128)(2,1)S(1)}, f32[8,2,256]{2,1,0:T(2,128)S(1)}, ...), branch_computations={%region_11.14_spmd, %region_14.15_spmd} | conditional | flops 1091835904 | bytes 12093785 | solution.py:303
  180.1 62.8 %while.62 = (s32[]{:T(128)}, f32[8,2,256,64]{2,3,1,0:T(8,128)}, s32[256]{0:T(256)S(1)}, s32[]{:T(128)}, s32[]{:T(128)}, /*index=5*/s32[256]{0:T(256)S(1)}, bf16[...) while((s32[]{:T(128)}, f32[8,2,256,64]{2,3,1,0:T(8,128)}, ...), condition=%wide.region_13.13_spmd.clone, body=%wide.region_12.12_spmd.clone.sunk | while | flops 1091835904 | bytes 11045081 | solution.py:61
  186.8 8.7 fusion.205
  202.2 9.0 fusion.205
  217.9 9.0 fusion.205
  233.6 9.0 fusion.205
  247.4 8.3 fusion.111
  263.8 14.3 multiply_convert_fusion.1
  294.6 407.5 %while.64 = (s32[]{:T(128)}, bf16[256,8,64]{0,2,1:T(8,128)(2,1)S(1)}, bf16[256,8,64]{0,2,1:T(8,128)(2,1)S(1)}, f32[256,8,64]{0,2,1:T(8,128)}, f32[256,8,64]{0,2,...) while((s32[]{:T(128)}, ...), condition=%wide.region_20.21_spmd.clone.clone.clone, body=%wide.region_17.20_spmd.clone.clone.clone.sunk | while | flops 683478272 | bytes 48231224 | solution.py:386
  351.0 9.8 collective-permute-start.3
  379.4 9.0 collective-permute-start
  408.2 12.4 collective-permute-start.1
  475.9 8.8 collective-permute-start.3
  505.2 8.2 collective-permute-start
  533.8 11.7 collective-permute-start.1
  628.6 8.2 collective-permute-start
  657.2 11.6 collective-permute-start.1
  720.3 11.3 multiply_convert_fusion
  772.5 9.6 fusion.116
  782.2 9.9 fusion.117
  793.3 9.7 fusion.84
  804.0 9.6 fusion.121
  813.7 9.5 fusion.122
  824.4 9.7 fusion.123
  838.3 73.5 %reduce-scatter.15.cloned.1.call-done = f32[64,1024]{1,0:T(8,128)} async-done(((f32[1024,1024]{1,0:T(8,128)}), f32[64,1024]{1,0:T(8,128)}) %reduce-scatter.15.cloned.1.call-update) | async-done | bytes 262160 | tf_op jit(solution)/shard_map/reduce_scatter | solution.py:435
  913.5 74.1 %reduce-scatter.23.cloned.1.call-done = f32[64,1024]{1,0:T(8,128)} async-done(((f32[1024,1024]{1,0:T(8,128)}), f32[64,1024]{1,0:T(8,128)}) %reduce-scatter.23.cloned.1.call-update) | async-done | bytes 262160 | tf_op jit(solution)/shard_map/reduce_scatter | solution.py:439
  989.2 73.8 %reduce-scatter.29.cloned.1.call-done = f32[64,1024]{1,0:T(8,128)} async-done(((f32[1024,1024]{1,0:T(8,128)}), f32[64,1024]{1,0:T(8,128)}) %reduce-scatter.29.cloned.1.call-update) | async-done | bytes 262160 | tf_op jit(solution)/shard_map/reduce_scatter | solution.py:442
  1064.6 136.7 %reduce-scatter.13.cloned.1.call-done = f32[64,3072]{1,0:T(8,128)} async-done(((f32[1024,3072]{1,0:T(8,128)}), f32[64,3072]{1,0:T(8,128)}) %reduce-scatter.13.cloned.1.call-update) | async-done | bytes 786448 | tf_op jit(solution)/shard_map/reduce_scatter | solution.py:434
  1203.3 196.8 %reduce-scatter.17.cloned.1.call-done = f32[64,4608]{1,0:T(8,128)} async-done(((f32[1024,4608]{1,0:T(8,128)}), f32[64,4608]{1,0:T(8,128)}) %reduce-scatter.17.cloned.1.call-update) | async-done | bytes 1179664 | tf_op jit(solution)/shard_map/reduce_scatter | solution.py:436
  1402.3 196.4 %reduce-scatter.19.cloned.1.call-done = f32[64,4608]{1,0:T(8,128)} async-done(((f32[1024,4608]{1,0:T(8,128)}), f32[64,4608]{1,0:T(8,128)}) %reduce-scatter.19.cloned.1.call-update) | async-done | bytes 1179664 | tf_op jit(solution)/shard_map/reduce_scatter | solution.py:437
  1600.9 196.6 %reduce-scatter.21.cloned.1.call-done = f32[288,1024]{1,0:T(8,128)} async-done(((f32[4608,1024]{1,0:T(8,128)}), f32[288,1024]{1,0:T(8,128)}) %reduce-scatter.21.cloned.1.call-update) | async-done | bytes 1179664 | tf_op jit(solution)/shard_map/reduce_scatter | solution.py:438
  1799.7 196.3 %reduce-scatter.31.cloned.1.call-done = f32[64,4608]{1,0:T(8,128)} async-done(((f32[1024,4608]{1,0:T(8,128)}), f32[64,4608]{1,0:T(8,128)}) %reduce-scatter.31.cloned.1.call-update) | async-done | bytes 1179664 | tf_op jit(solution)/shard_map/reduce_scatter | solution.py:443
  1998.1 196.4 %reduce-scatter.33.cloned.1.call-done = f32[64,4608]{1,0:T(8,128)} async-done(((f32[1024,4608]{1,0:T(8,128)}), f32[64,4608]{1,0:T(8,128)}) %reduce-scatter.33.cloned.1.call-update) | async-done | bytes 1179664 | tf_op jit(solution)/shard_map/reduce_scatter | solution.py:444
  2196.6 196.3 %reduce-scatter.35.cloned.1.call-done = f32[288,1024]{1,0:T(8,128)} async-done(((f32[4608,1024]{1,0:T(8,128)}), f32[288,1024]{1,0:T(8,128)}) %reduce-scatter.35.cloned.1.call-update) | async-done | bytes 1179664 | tf_op jit(solution)/shard_map/reduce_scatter | solution.py:445
  2409.4 60.0 %all-reduce.10 = (bf16[1024]{0:T(1024)(128)(2,1)S(1)}, bf16[3,1024]{1,0:T(4,128)(2,1)S(1)}, bf16[1024]{0:T(1024)(128)(2,1)S(1)}, bf16[1024]{0:T(1024)(128)(2,1)S...) all-reduce(f32[1024]{0:T(1024)S(1)} %get-tuple-element.1146, ...), channel_id=1, replica_groups=mesh['dp'=2,'ctx'=16] {'ctx'}, use_global_device_ids=true, to_apply=%region_27.28 | all-reduce | flops 7296 | bytes 43776 | tf_op jit(solution)/shard_map/psum | solution.py:447
  2469.4 8.8 all-reduce.11
  2484.8 31.0 %all-reduce.15.cloned.1.call-done = (bf16[64,3072]{1,0:T(8,128)(2,1)}, bf16[64,1024]{1,0:T(8,128)(2,1)}, bf16[64,4608]{1,0:T(8,128)(2,1)}, bf16[64,4608]{1,0:T(8...) async-done(((bf16[64,3072]{1,0:T(8,128)(2,1)}, ...) | async-done | bytes 4456464 | tf_op jit(solution)/shard_map/psum | solution.py:460
  (750 shorter events, 560.2 us)
Async XLA Ops:
  7.2 94.6 %all-gather.3.cloned.1.call-start = ((), (), s32[]{:S(2)}) async-start(), calls=%async_computation.12 | async-start | bytes 4456448 | tf_op jit(solution)/shard_map/all_gather | solution.py:290
  45.8 132.2 %all-gather.5.cloned.1.call-start = ((), (), s32[]{:S(2)}) async-start(), calls=%async_computation.13 | async-start | bytes 4456448 | tf_op jit(solution)/shard_map/all_gather | solution.py:291
  48.4 786.0 %reduce-scatter.25.cloned.1.call-start = ((), (), s32[]{:S(2)}) async-start(), calls=%async_computation.20 | async-start | bytes 2228224 | tf_op jit(solution)/shard_map/reduce_scatter | solution.py:440
  322.8 16.9 collective-permute-start.2
  347.6 19.1 collective-permute-start.2
  351.0 17.5 collective-permute-start.3
  374.5 19.1 collective-permute-start.2
  377.1 18.4 collective-permute-start.3
  379.4 17.8 collective-permute-start
  401.4 19.1 collective-permute-start.2
  403.9 18.5 collective-permute-start.3
  406.3 17.9 collective-permute-start
  408.2 15.9 collective-permute-start.1
  447.9 17.7 collective-permute-start.2
  473.4 19.1 collective-permute-start.2
  475.9 18.5 collective-permute-start.3
  500.3 18.2 collective-permute-start.2
  502.8 17.6 collective-permute-start.3
  505.2 17.0 collective-permute-start
  526.4 19.1 collective-permute-start.2
  528.9 18.4 collective-permute-start.3
  531.2 17.8 collective-permute-start
  573.9 17.2 collective-permute-start.2
  599.9 17.2 collective-permute-start.2
  601.7 18.2 collective-permute-start.3
  625.9 17.7 collective-permute-start.2
  627.7 18.7 collective-permute-start.3
  628.6 19.6 collective-permute-start
  652.4 18.1 collective-permute-start.2
  654.2 19.2 collective-permute-start.3
  654.6 20.5 collective-permute-start
  657.2 17.9 collective-permute-start.1
  679.4 18.1 collective-permute-start.2
  681.2 19.2 collective-permute-start.3
  681.6 20.5 collective-permute-start
  684.2 17.9 collective-permute-start.1
  708.0 128.8 %reduce-scatter.27.cloned.1.call-start = ((), (), s32[]{:S(2)}) async-start(), calls=%async_computation.21 | async-start | bytes 2228224 | tf_op jit(solution)/shard_map/reduce_scatter | solution.py:441
  720.0 191.9 %reduce-scatter.15.cloned.1.call-start = ((), (), s32[]{:S(2)}) async-start(), calls=%async_computation.15 | async-start | bytes 4456448 | tf_op jit(solution)/shard_map/reduce_scatter | solution.py:435
  748.4 239.2 %reduce-scatter.23.cloned.1.call-start = ((), (), s32[]{:S(2)}) async-start(), calls=%async_computation.19 | async-start | bytes 4456448 | tf_op jit(solution)/shard_map/reduce_scatter | solution.py:439
  751.2 311.9 %reduce-scatter.29.cloned.1.call-start = ((), (), s32[]{:S(2)}) async-start(), calls=%async_computation.22 | async-start | bytes 4456448 | tf_op jit(solution)/shard_map/reduce_scatter | solution.py:442
  756.2 445.2 %reduce-scatter.13.cloned.1.call-start = ((), (), s32[]{:S(2)}) async-start(), calls=%async_computation.14 | async-start | bytes 13369344 | tf_op jit(solution)/shard_map/reduce_scatter | solution.py:434
  771.5 628.6 %reduce-scatter.17.cloned.1.call-start = ((), (), s32[]{:S(2)}) async-start(), calls=%async_computation.16 | async-start | bytes 20054016 | tf_op jit(solution)/shard_map/reduce_scatter | solution.py:436
  782.1 816.6 %reduce-scatter.19.cloned.1.call-start = ((), (), s32[]{:S(2)}) async-start(), calls=%async_computation.17 | async-start | bytes 20054016 | tf_op jit(solution)/shard_map/reduce_scatter | solution.py:437
  792.1 1005.4 %reduce-scatter.21.cloned.1.call-start = ((), (), s32[]{:S(2)}) async-start(), calls=%async_computation.18 | async-start | bytes 20054016 | tf_op jit(solution)/shard_map/reduce_scatter | solution.py:438
  803.0 1192.9 %reduce-scatter.31.cloned.1.call-start = ((), (), s32[]{:S(2)}) async-start(), calls=%async_computation.23 | async-start | bytes 20054016 | tf_op jit(solution)/shard_map/reduce_scatter | solution.py:443
  813.7 1380.8 %reduce-scatter.33.cloned.1.call-start = ((), (), s32[]{:S(2)}) async-start(), calls=%async_computation.24 | async-start | bytes 20054016 | tf_op jit(solution)/shard_map/reduce_scatter | solution.py:444
  823.3 1569.6 %reduce-scatter.35.cloned.1.call-start = ((), (), s32[]{:S(2)}) async-start(), calls=%async_computation.25 | async-start | bytes 20054016 | tf_op jit(solution)/shard_map/reduce_scatter | solution.py:445
  834.0 1681.7 %all-reduce.15.cloned.1.call-start = ((), (), s32[]{:S(2)}) async-start(), calls=%async_computation.26 | async-start | bytes 8912896 | tf_op jit(solution)/shard_map/psum | solution.py:460
  (162 other events, 3762.1 us)
Sparse Core Ops, SparseCore 0:
  46.0 55.7 all-gather.2
  104.5 51.3 all-gather.4
  708.1 64.0 reduce-scatter.24
  776.2 60.5 reduce-scatter.26
  840.5 71.3 reduce-scatter.14
  916.1 71.4 reduce-scatter.22
  991.4 71.5 reduce-scatter.28
  1067.6 133.7 reduce-scatter.12
  1206.1 194.0 reduce-scatter.16
  1404.7 194.0 reduce-scatter.18
  1603.4 194.0 reduce-scatter.20
  1802.0 193.8 reduce-scatter.30
  2000.6 193.8 reduce-scatter.32
  2199.0 193.8 reduce-scatter.34
  2398.6 117.0 all-reduce.14
where the time goes:
time: 2550 us; the launch traced here: 2540 us
  waiting for transfers between devices  1640 us (64%)
  matrix products  263 us (10%)
  other arithmetic  256 us (10%)
  starting transfers between devices  231 us (9%)
  blocking collectives  68.7 us (3%)
  local copies, waits for them, and re-layouts  56.9 us (2%)
    reduce_scatter x1, waiting for transfers between devices, per_device(): lax.psum_scatter(lowgate_grad, 'ctx', scatter_dimension=0, tiled=True)  197 us
    reduce_scatter x1, waiting for transfers between devices, per_device(): lax.psum_scatter(lowdrop_grad, 'ctx', scatter_dimension=0, tiled=True)  197 us
    reduce_scatter x1, waiting for transfers between devices, per_device(): lax.psum_scatter(toplift_grad, 'ctx', scatter_dimension=0, tiled=True)  196 us
    reduce_scatter x1, waiting for transfers between devices, per_device(): lax.psum_scatter(lowlift_grad, 'ctx', scatter_dimension=0, tiled=True)  196 us
    reduce_scatter x1, waiting for transfers between devices, per_device(): lax.psum_scatter(topdrop_grad, 'ctx', scatter_dimension=0, tiled=True)  196 us
    reduce_scatter x1, waiting for transfers between devices, per_device(): lax.psum_scatter(topgate_grad, 'ctx', scatter_dimension=0, tiled=True)  196 us
    ppermute x34, starting transfers between devices, passed_along(): lax.ppermute(value, axis, [(source, source + steps) for source in range(f...  156 us
    reduce_scatter x1, waiting for transfers between devices, per_device(): lax.psum_scatter(mixentry_grad, 'ctx', scatter_dimension=0, tiled=True)  137 us
  transfers between devices with their start and end apart: 81, of which 27 were waited for; matrix products, arithmetic and copies ran while one was open for 13% of the time, Pallas kernels for 0%

commit v1 on v0

--- a/solution.py
+++ b/solution.py
@@ -1,8 +1,11 @@
+import functools
 import math
 
 import jax
 import jax.numpy as jnp
 from jax import lax
+from jax.experimental import pallas as pl
+from jax.experimental.pallas import tpu as pltpu
 from jax.sharding import PartitionSpec as P
 
 EPS = 1e-05
@@ -502,57 +505,790 @@
     )
 
 
+LANES = 128
+BF = jnp.bfloat16
+F32 = jnp.float32
+ONES_NT = (((1,), (1,)), ((), ()))
+ONES_TN = (((0,), (0,)), ((), ()))
+VMEM_LIMIT = 60 * 1024 * 1024
+
+
+def vmem_specs(count):
+    return [pl.BlockSpec(memory_space=pltpu.VMEM)] * count
+
+
+def lane_of(shape):
+    return lax.broadcasted_iota(jnp.int32, shape, len(shape) - 1)
+
+
+def same_head(head):
+    row = lax.broadcasted_iota(jnp.int32, (LANES, LANES), 0) // head
+    column = lax.broadcasted_iota(jnp.int32, (LANES, LANES), 1) // head
+    return jnp.where(row == column, 1.0 / head, 0.0).astype(F32)
+
+
+def head_mean(value, blocks):
+    return jnp.dot(value, blocks, precision=lax.Precision.HIGHEST, preferred_element_type=F32)
+
+
+def other_half(value, head):
+    lane = lane_of(value.shape)
+    ahead = pltpu.roll(value, LANES - head // 2, 1)
+    behind = pltpu.roll(value, head // 2, 1)
+    return jnp.where(lane % head < head // 2, ahead, behind)
+
+
+def swap_heads(value, head):
+    return pltpu.roll(value, head, 1)
+
+
+def three_parts(value):
+    high = value.astype(BF)
+    rest = value - high.astype(F32)
+    middle = rest.astype(BF)
+    low = (rest - middle.astype(F32)).astype(BF)
+    return high.astype(F32), middle.astype(F32), low.astype(F32)
+
+
+def project_kernel(head, hid_ref, gain_ref, wq_ref, wk_ref, wv_ref, cos_ref, sin_ref, qg_ref, kg_ref,
+                   msg_ref, normed_ref, qraw_ref, kraw_ref):
+    hid = hid_ref[...]
+    scale = lax.rsqrt(jnp.mean(hid * hid, axis=-1, keepdims=True) + EPS)
+    normed = (hid * scale * gain_ref[...]).astype(BF)
+    normed_ref[...] = normed
+    blocks = same_head(head)
+    cosine, sine = cos_ref[...], sin_ref[...]
+    half_rows = msg_ref.shape[1]
+    lane = lane_of(cosine.shape)
+
+    def prepared(raw, gain):
+        unit = raw * lax.rsqrt(head_mean(raw * raw, blocks) + EPS) * gain
+        return unit * cosine + other_half(unit, head) * sine
+
+    def put(dest, start, tile):
+        low = tile.astype(BF)
+        for part in range(2):
+            msg_ref[2 * dest + part, :, start:start + LANES] = low[part * half_rows:(part + 1) * half_rows]
+
+    qraw = jnp.dot(normed, wq_ref[...], preferred_element_type=F32)
+    qraw_ref[...] = qraw
+    for tile in range(qraw.shape[1] // LANES):
+        put(tile, 0, prepared(qraw[:, tile * LANES:(tile + 1) * LANES], qg_ref[...]))
+    kraw = jnp.dot(normed, wk_ref[...], preferred_element_type=F32)
+    kraw_ref[...] = kraw
+    vraw = jnp.dot(normed, wv_ref[...], preferred_element_type=F32)
+    for tile in range(kraw.shape[1] // LANES):
+        keys = prepared(kraw[:, tile * LANES:(tile + 1) * LANES], kg_ref[...])
+        values = vraw[:, tile * LANES:(tile + 1) * LANES]
+        put(2 * tile, LANES, jnp.where(lane < head, keys, swap_heads(values, head)))
+        put(2 * tile + 1, LANES, jnp.where(lane < head, swap_heads(keys, head), values))
+
+
+def project_back_kernel(head, back_ref, hid_ref, gain_ref, wq_ref, wk_ref, wv_ref, cos_ref, sin_ref, qg_ref,
+                        kg_ref, qraw_ref, kraw_ref, grad_ref,
+                        raw_ref, two_ref, again_ref, qgain_ref, kgain_ref):
+    blocks = same_head(head)
+    cosine, sine = cos_ref[...], sin_ref[...]
+    half_rows = back_ref.shape[1]
+    lane = lane_of(cosine.shape)
+
+    def fetch(dest, start):
+        return jnp.concatenate(
+            [back_ref[2 * dest + part, :, start:start + LANES] for part in range(2)], axis=0).astype(F32)
+
+    def through(grad, raw, gain):
+        scale = lax.rsqrt(head_mean(raw * raw, blocks) + EPS)
+        unit = raw * scale
+        turned = grad * cosine - other_half(grad, head) * sine
+        gain_part = jnp.sum(turned * unit, axis=0, keepdims=True)
+        inward = turned * gain
+        return scale * (inward - unit * head_mean(inward * unit, blocks)), gain_part
+
+    width_q = wq_ref.shape[1]
+    width_k = wk_ref.shape[1]
+    gain_total = jnp.zeros((1, LANES), F32)
+    for tile in range(width_q // LANES):
+        got, part = through(fetch(tile, 0), qraw_ref[:, tile * LANES:(tile + 1) * LANES], qg_ref[...])
+        gain_total = gain_total + part
+        raw_ref[:, tile * LANES:(tile + 1) * LANES] = got.astype(BF)
+    qgain_ref[...] = gain_total
+    gain_total = jnp.zeros((1, LANES), F32)
+    for tile in range(width_k // LANES):
+        even, odd = fetch(2 * tile, LANES), fetch(2 * tile + 1, LANES)
+        keys = jnp.where(lane < head, even, swap_heads(odd, head))
+        values = jnp.where(lane < head, swap_heads(even, head), odd)
+        got, part = through(keys, kraw_ref[:, tile * LANES:(tile + 1) * LANES], kg_ref[...])
+        gain_total = gain_total + part
+        raw_ref[:, width_q + tile * LANES:width_q + (tile + 1) * LANES] = got.astype(BF)
+        raw_ref[:, width_q + width_k + tile * LANES:width_q + width_k + (tile + 1) * LANES] = values.astype(BF)
+    kgain_ref[...] = gain_total
+    normed_grad = lax.dot_general(raw_ref[:, :width_q], wq_ref[...], ONES_NT, preferred_element_type=F32)
+    normed_grad += lax.dot_general(raw_ref[:, width_q:width_q + width_k], wk_ref[...], ONES_NT,
+                                   preferred_element_type=F32)
+    normed_grad += lax.dot_general(raw_ref[:, width_q + width_k:], wv_ref[...], ONES_NT,
+                                   preferred_element_type=F32)
+    hid = hid_ref[...]
+    scale = lax.rsqrt(jnp.mean(hid * hid, axis=-1, keepdims=True) + EPS)
+    unit = hid * scale
+    again_ref[...] = jnp.sum(normed_grad * unit, axis=0, keepdims=True)
+    inward = normed_grad * gain_ref[...]
+    two_ref[...] = grad_ref[...] + scale * (inward - unit * jnp.mean(inward * unit, axis=-1, keepdims=True))
+
+
+def allowed_block(row_axis, key_axis, shape, first, second, part, base, start, rows, half_rows):
+    row = lax.broadcasted_iota(jnp.int32, shape, row_axis)
+    token = (base + row // (2 * half_rows)) * rows + part * half_rows + row % half_rows
+    key = start + lax.broadcasted_iota(jnp.int32, shape, key_axis)
+    begin = jnp.where(token >= second, second, jnp.where(token >= first, first, 0))
+    return (key >= begin) & (key <= token)
+
+
+def need_mask(first, second, part, base, start, rows, half_rows, keys, sources):
+    lowest = base * rows + part * half_rows
+    highest = (base + sources - 1) * rows + (part + 1) * half_rows - 1
+    begin = jnp.where(highest >= second, second, jnp.where(highest >= first, first, 0))
+    return (start + keys - 1 > lowest) | (start < begin)
+
+
+def attend_kernel(head, rows, keys, sources, info_ref, q_ref, kv_ref, out_ref, aug_ref, ones_ref, acc_ref):
+    first, second, part = info_ref[0], info_ref[1], info_ref[2]
+    half_rows = q_ref.shape[1]
+    wide = sources * 2 * half_rows
+    factor = math.log2(math.e) / math.sqrt(head)
+    ones_ref[...] = jnp.where(lane_of(kv_ref.shape) < head, jnp.ones_like(kv_ref), kv_ref[...])
+    lane = lane_of((half_rows, LANES))
+
+    def block(index, _):
+        base = index * sources
+        stack = []
+        for source in range(sources):
+            tile = q_ref[base + source][:, :LANES].astype(F32)
+            stack.append(jnp.where(lane < head, tile, 0.0))
+            stack.append(jnp.where(lane < head, swap_heads(tile, head), 0.0))
+        queries = jnp.concatenate(stack, axis=0).astype(BF)
+        acc_ref[...] = jnp.zeros_like(acc_ref)
+        last = (base + sources - 1) * rows + (part + 1) * half_rows
+        count = (last + keys - 1) // keys
+
+        def visit(step, _):
+            start = pl.multiple_of(step * keys, keys)
+            raw = lax.dot_general(queries, kv_ref[pl.ds(start, keys)], ONES_NT, preferred_element_type=F32)
+            raised = jnp.exp2(raw * factor)
+            masked = need_mask(first, second, part, base, start, rows, half_rows, keys, sources)
+
+            @pl.when(masked)
+            def _():
+                ok = allowed_block(0, 1, (wide, keys), first, second, part, base, start, rows, half_rows)
+                acc_ref[...] += jnp.dot(jnp.where(ok, raised, 0.0).astype(BF), ones_ref[pl.ds(start, keys)],
+                                        preferred_element_type=F32)
+
+            @pl.when(jnp.logical_not(masked))
+            def _():
+                acc_ref[...] += jnp.dot(raised.astype(BF), ones_ref[pl.ds(start, keys)],
+                                        preferred_element_type=F32)
+
+        lax.fori_loop(0, count, visit, None)
+        for source in range(sources):
+            tile = q_ref[base + source][:, :LANES].astype(F32)
+            outs = []
+            for which in range(2):
+                place = (2 * source + which) * half_rows
+                acc = acc_ref[place:place + half_rows]
+                turned = swap_heads(acc, head)
+                outs.append(turned / acc if which == 0 else acc / turned)
+                high, middle, low = three_parts(-math.sqrt(head) * jnp.log(turned))
+                query = tile if which == 0 else swap_heads(tile, head)
+                extra = jnp.where(lane == head, high, jnp.where(lane == head + 1, middle,
+                                                                jnp.where(lane == head + 2, low, 0.0)))
+                aug_ref[base + source, which] = jnp.where(lane < head, query, extra).astype(BF)
+            out_ref[base + source] = jnp.where(lane < head, outs[0], outs[1])
+
+    lax.fori_loop(0, q_ref.shape[0] // sources, block, None)
+
+
+def attend_back_kernel(head, rows, keys, sources, info_ref, aug_ref, out_ref, grad_ref, kv_ref,
+                       dq_ref, dkv_ref, kone_ref, vone_ref, dk_ref, dv_ref, acc_ref):
+    first, second, part = info_ref[0], info_ref[1], info_ref[2]
+    half_rows = grad_ref.shape[1]
+    wide = sources * 2 * half_rows
+    factor = math.log2(math.e) / math.sqrt(head)
+    whole = lane_of(kv_ref.shape)
+    vone_ref[...] = jnp.where(whole < head, jnp.ones_like(kv_ref), kv_ref[...])
+    kone_ref[...] = jnp.where(whole < head, kv_ref[...], jnp.ones_like(kv_ref))
+    dk_ref[...] = jnp.zeros_like(dk_ref)
+    dv_ref[...] = jnp.zeros_like(dv_ref)
+    lane = lane_of((half_rows, LANES))
+
+    def block(index, _):
+        base = index * sources
+        stack_q, stack_d = [], []
+        for source in range(sources):
+            grad = grad_ref[base + source].astype(F32)
+            spread = grad * out_ref[base + source]
+            for which in range(2):
+                stack_q.append(aug_ref[base + source, which])
+                mine = (lane < head) if which == 0 else (lane >= head)
+                delta = jnp.sum(jnp.where(mine, spread, 0.0), axis=1, keepdims=True)
+                high, middle, low = three_parts(-delta)
+                extra = jnp.where(lane == 0, high, jnp.where(lane == 1, middle, jnp.where(lane == 2, low, 0.0)))
+                moved = swap_heads(grad, head) if which == 0 else grad
+                stack_d.append(jnp.where(lane < head, extra, moved).astype(BF))
+        queries = jnp.concatenate(stack_q, axis=0)
+        grads = jnp.concatenate(stack_d, axis=0)
+        acc_ref[...] = jnp.zeros_like(acc_ref)
+        last = (base + sources - 1) * rows + (part + 1) * half_rows
+        count = (last + keys - 1) // keys
+
+        def visit(step, _):
+            start = pl.multiple_of(step * keys, keys)
+            here = pl.ds(start, keys)
+
+            def finish(prob):
+                along = lax.dot_general(vone_ref[here], grads, ONES_NT, preferred_element_type=F32)
+                score = (prob * along).astype(BF)
+                dv_ref[here] += jnp.dot(prob.astype(BF), grads, preferred_element_type=F32)
+                dk_ref[here] += jnp.dot(score, queries, preferred_element_type=F32)
+                acc_ref[...] += lax.dot_general(score, kone_ref[here], ONES_TN, preferred_element_type=F32)
+
+            raw = lax.dot_general(kone_ref[here], queries, ONES_NT, preferred_element_type=F32)
+            masked = need_mask(first, second, part, base, start, rows, half_rows, keys, sources)
+
+            @pl.when(masked)
+            def _():
+                ok = allowed_block(1, 0, (keys, wide), first, second, part, base, start, rows, half_rows)
+                finish(jnp.where(ok, jnp.exp2(jnp.where(ok, raw, 0.0) * factor), 0.0))
+
+            @pl.when(jnp.logical_not(masked))
+            def _():
+                finish(jnp.exp2(raw * factor))
+
+        lax.fori_loop(0, count, visit, None)
+        for source in range(sources):
+            place = 2 * source * half_rows
+            one = acc_ref[place:place + half_rows]
+            two = acc_ref[place + half_rows:place + 2 * half_rows]
+            both = jnp.where(lane < head, one, swap_heads(two, head)) * (1.0 / math.sqrt(head))
+            dq_ref[base + source] = both.astype(BF)
+
+    lax.fori_loop(0, grad_ref.shape[0] // sources, block, None)
+    dkv_ref[...] = jnp.where(whole < head, dk_ref[...] * (1.0 / math.sqrt(head)), dv_ref[...]).astype(BF)
+
+
+SUB = 64
+STRIP = 256
+RING = 8
+LAG = 2
+
+
+def sum_kernel(jobs, lines, *refs):
+    count = len(jobs)
+    lefts, rights, out_ref = refs[:count], refs[count:2 * count], refs[2 * count]
+    (lbuf, rbuf, xp, xr, yp, yr, zp, us, ur, ds_, dr, fs, fr, stage,
+     lsem, rsem, xs, xv, ys, yv, uss, urv, dss, drv, fss, frv, osem) = refs[2 * count + 1:]
+    steps = sum(job[2] for job in jobs)
+    last = steps - 1 + LAG
+    half = STRIP // 2
+    quarter = SUB // 2
+    tall = SUB + quarter
+    me = lax.axis_index("ctx")
+    y = lax.axis_index("dp")
+    z = me // 4
+    x = (me // 2) % 2
+    c = me % 2
+    across_x = {"ctx": me + 2 - 4 * x}
+    across_y = {"dp": 1 - y}
+    above = {"ctx": jnp.minimum(me + 4, 4 * lines - 4 + me % 4)}
+    below = {"ctx": jnp.maximum(me - 4, me % 4)}
+    top = lines - 1
+
+    for buf in (xp, ur, dr, zp):
+        buf[...] = jnp.zeros_like(buf)
+
+    barrier = pltpu.get_barrier_semaphore()
+    pl.semaphore_signal(barrier, inc=1, device_id=across_x, device_id_type=MESH)
+    pl.semaphore_signal(barrier, inc=1, device_id=across_y, device_id_type=MESH)
+
+    @pl.when(z < top)
+    def _():
+        pl.semaphore_signal(barrier, inc=1, device_id=above, device_id_type=MESH)
+
+    @pl.when(z > 0)
+    def _():
+        pl.semaphore_signal(barrier, inc=1, device_id=below, device_id_type=MESH)
+
+    pl.semaphore_wait(barrier, 2 + (z < top).astype(jnp.int32) + (z > 0).astype(jnp.int32))
+
+    def remote(src, dst, send, recv, where):
+        return pltpu.make_async_remote_copy(src_ref=src, dst_ref=dst, send_sem=send, recv_sem=recv,
+                                            device_id=where, device_id_type=MESH)
+
+    def x_copy(j):
+        s = j % RING
+        return remote(xp.at[s, 1 - x], xr.at[s], xs.at[s], xv.at[s], across_x)
+
+    def y_copy(j):
+        s = j % RING
+        return remote(yp.at[s, 1 - y], yr.at[s], ys.at[s], yv.at[s], across_y)
+
+    def up_copy(j):
+        s = j % RING
+        return remote(us.at[s], ur.at[s], uss.at[s], urv.at[s], above)
+
+    def down_copy(j):
+        s = j % RING
+        return remote(ds_.at[s], dr.at[s], dss.at[s], drv.at[s], below)
+
+    def f_copy(j):
+        s = j % RING
+        return remote(fs.at[s], fr.at[s], fss.at[s], frv.at[s], across_y)
+
+    def l_wait(j):
+        s = j % 2
+        pltpu.make_async_copy(lefts[0].at[:, pl.ds(0, SUB), :], lbuf.at[s], lsem.at[s]).wait()
+        pltpu.make_async_copy(rights[0].at[:, pl.ds(0, STRIP)], rbuf.at[s], rsem.at[s]).wait()
+
+    def load(j):
+        s = j % 2
+        begin = 0
+        for number, (subs, strips, total) in enumerate(jobs):
+            @pl.when((j >= begin) & (j < begin + total))
+            def _(number=number, subs=subs, begin=begin):
+                k = j - begin
+                row = pl.multiple_of((k % subs) * SUB, SUB)
+                column = pl.multiple_of((k // subs) * STRIP, STRIP)
+                pltpu.make_async_copy(lefts[number].at[:, pl.ds(row, SUB), :], lbuf.at[s], lsem.at[s]).start()
+                pltpu.make_async_copy(rights[number].at[:, pl.ds(column, STRIP)], rbuf.at[s], rsem.at[s]).start()
+            begin += total
+
+    def out_copy(j):
+        s = j % 2
+        return pltpu.make_async_copy(stage.at[s], out_ref.at[j], osem.at[s])
+
+    load(0)
+
+    def step(t, _):
+        slot = t % RING
+
+        @pl.when(t < steps)
+        def _():
+            l_wait(t)
+
+            @pl.when(t + 1 < steps)
+            def _():
+                load(t + 1)
+
+            left = lbuf[t % 2].reshape(2 * lines * SUB, lbuf.shape[-1])
+            got = jnp.dot(left, rbuf[t % 2], preferred_element_type=F32).astype(BF)
+            for line in range(lines):
+                for side in range(2):
+                    row = (2 * line + side) * SUB
+                    xp[slot, side, line, :SUB] = got[row:row + SUB, :half]
+                    for part in range(2):
+                        yp[slot, part, side, line] = got[row + part * quarter:row + (part + 1) * quarter, half:]
+
+        @pl.when((t >= LAG) & (t <= last))
+        def _():
+            y_copy(t - LAG).wait()
+            s = (t - LAG) % RING
+            xp[slot, :, :, SUB:] = yp[s, y] + yr[s]
+
+        @pl.when(t < steps)
+        def _():
+            y_copy(t).start()
+
+        @pl.when(t <= last)
+        def _():
+            x_copy(t).start()
+
+        @pl.when((t >= LAG) & (t - LAG <= last))
+        def _():
+            x_copy(t - LAG).wait()
+            s = (t - LAG) % RING
+            zp[(t - LAG) % (2 * RING)] = xp[s, x] + xr[s]
+
+        ju = t - LAG * (1 + z)
+
+        @pl.when((ju >= 0) & (ju <= last))
+        def _():
+            s = ju % RING
+            held = ju % (2 * RING)
+
+            @pl.when(z > 0)
+            def _():
+                up_copy(ju).wait_recv()
+                zp[held, z] = zp[held, z] + ur[s, 0]
+
+            @pl.when(z < top)
+            def _():
+                @pl.when(ju >= RING)
+                def _():
+                    up_copy(ju).wait_send()
+
+                for m in range(top):
+                    own = zp[held, jnp.minimum(z + 1 + m, top)]
+                    if m + 1 < top:
+                        own = own + ur[s, m + 1]
+                    us[s, m] = own
+                up_copy(ju).start()
+
+        jd = t - LAG * (1 + top - z)
+
+        @pl.when((jd >= 0) & (jd <= last))
+        def _():
+            s = jd % RING
+            held = jd % (2 * RING)
+
+            @pl.when(z < top)
+            def _():
+                down_copy(jd).wait_recv()
+                zp[held, z] = zp[held, z] + dr[s, 0]
+
+            @pl.when(z > 0)
+            def _():
+                @pl.when(jd >= RING)
+                def _():
+                    down_copy(jd).wait_send()
+
+                for m in range(top):
+                    own = zp[held, jnp.maximum(z - 1 - m, 0)]
+                    if m + 1 < top:
+                        own = own + dr[s, m + 1]
+                    ds_[s, m] = own
+                down_copy(jd).start()
+
+        jf = t - LAG * (1 + top)
+
+        @pl.when((jf >= 0) & (jf <= last))
+        def _():
+            fs[jf % RING] = zp[jf % (2 * RING), z]
+            f_copy(jf).start()
+
+        jo = jf - LAG
+
+        @pl.when((jo >= 0) & (jo <= last))
+        def _():
+            f_copy(jo).wait()
+            s = jo % RING
+            o = jo % 2
+
+            @pl.when(jo >= 2)
+            def _():
+                out_copy(jo).wait()
+
+            stage[o, :SUB] = fs[s, :SUB] + fr[s, :SUB]
+            mine, other = fs[s, SUB:].astype(F32), fr[s, SUB:].astype(F32)
+            stage[o, SUB:tall] = jnp.where(y == 0, mine, other).astype(BF)
+            stage[o, tall:] = jnp.where(y == 0, other, mine).astype(BF)
+            out_copy(jo).start()
+
+    lax.fori_loop(0, last + LAG * (top + 2) + 1, step, None)
+    for j in (last - 1, last):
+        out_copy(j).wait()
+    for back in range(RING):
+        j = last - back
+
+        @pl.when(z < top)
+        def _(j=j):
+            up_copy(j).wait_send()
+
+        @pl.when(z > 0)
+        def _(j=j):
+            down_copy(j).wait_send()
+
+
+def sum_over_chips(pairs, lines, collective_id):
+    jobs = []
+    lefts, rights = [], []
+    for left, right in pairs:
+        rows = left.shape[0] // (2 * lines)
+        subs, strips = rows // SUB, right.shape[1] // STRIP
+        jobs.append((subs, strips, subs * strips))
+        lefts.append(left.reshape(2 * lines, rows, left.shape[1]))
+        rights.append(right)
+    steps = sum(job[2] for job in jobs)
+    tokens = pairs[0][0].shape[1]
+    half, quarter = STRIP // 2, SUB // 2
+    tall = SUB + quarter
+    top = lines - 1
+    dma = pltpu.SemaphoreType.DMA
+    scratch = [
+        pltpu.VMEM((2, 2 * lines, SUB, tokens), BF),
+        pltpu.VMEM((2, tokens, STRIP), BF),
+        pltpu.VMEM((RING, 2, lines, tall, half), BF),
+        pltpu.VMEM((RING, lines, tall, half), BF),
+        pltpu.VMEM((RING, 2, 2, lines, quarter, half), BF),
+        pltpu.VMEM((RING, 2, lines, quarter, half), BF),
+        pltpu.VMEM((2 * RING, lines, tall, half), BF),
+        pltpu.VMEM((RING, top, tall, half), BF),
+        pltpu.VMEM((RING, top, tall, half), BF),
+        pltpu.VMEM((RING, top, tall, half), BF),
+        pltpu.VMEM((RING, top, tall, half), BF),
+        pltpu.VMEM((RING, tall, half), BF),
+        pltpu.VMEM((RING, tall, half), BF),
+        pltpu.VMEM((2, 2 * SUB, half), BF),
+        dma((2,)), dma((2,)),
+        dma((RING,)), dma((RING,)), dma((RING,)), dma((RING,)),
+        dma((RING,)), dma((RING,)), dma((RING,)), dma((RING,)),
+        dma((RING,)), dma((RING,)),
+        dma((2,)),
+    ]
+    flops = 2 * steps * 2 * lines * SUB * STRIP * tokens
+    out = pl.pallas_call(
+        functools.partial(sum_kernel, jobs, lines),
+        out_shape=jax.ShapeDtypeStruct((steps + LAG, 2 * SUB, half), BF),
+        in_specs=[pl.BlockSpec(memory_space=pl.ANY)] * (2 * len(pairs)),
+        out_specs=pl.BlockSpec(memory_space=pl.ANY),
+        scratch_shapes=scratch,
+        compiler_params=pltpu.CompilerParams(collective_id=collective_id, has_side_effects=True,
+                                             vmem_limit_bytes=VMEM_LIMIT),
+        cost_estimate=pl.CostEstimate(flops=flops, bytes_accessed=steps * 800_000, transcendentals=0),
+        name="sum_over_chips",
+    )(*lefts, *rights)
+    results = []
+    begin = 0
+    for (subs, strips, total) in jobs:
+        one = out[begin:begin + total, :SUB].reshape(strips, subs * SUB, half)
+        two = out[begin + LAG:begin + total + LAG, SUB:].reshape(strips, subs * SUB, half)
+        both = jnp.concatenate([one, two], axis=2)
+        results.append(both.transpose(1, 0, 2).reshape(subs * SUB, strips * STRIP))
+        begin += total
+    return results
+
+
+MESH = pl.DeviceIdType.MESH
+
+
+def call_plain(kernel, outs, args, smem=0, scratch=(), flops=0, moved=0, name=None):
+    specs = [pl.BlockSpec(memory_space=pltpu.SMEM)] * smem + vmem_specs(len(args) - smem)
+    many = isinstance(outs, (tuple, list))
+    return pl.pallas_call(
+        kernel,
+        out_shape=tuple(outs) if many else outs,
+        in_specs=specs,
+        out_specs=tuple(vmem_specs(len(outs))) if many else vmem_specs(1)[0],
+        scratch_shapes=list(scratch),
+        compiler_params=pltpu.CompilerParams(vmem_limit_bytes=VMEM_LIMIT),
+        cost_estimate=pl.CostEstimate(flops=flops, bytes_accessed=moved, transcendentals=0),
+        name=name,
+    )(*args)
+
+
+def shape_of(shape, kind):
+    return jax.ShapeDtypeStruct(shape, kind)
+
+
+def sibling(value):
+    count = lax.axis_size("ctx")
+    return lax.ppermute(value, "ctx", [(i, i ^ 1) for i in range(count)])
+
+
+def halves(value, core):
+    width = value.shape[1] // 2
+    mine = lax.dynamic_slice_in_dim(value, core * width, width, 1)
+    send = lax.dynamic_slice_in_dim(value, (1 - core) * width, width, 1)
+    return mine, send
+
+
+def left_side(value):
+    return jnp.concatenate([value, sibling(value)], axis=0).T
+
+
+def right_side(values, core):
+    mine, send = zip(*[halves(value, core) for value in values])
+    mine, send = (jnp.concatenate(part, axis=1) for part in (mine, send))
+    return jnp.concatenate([mine, sibling(send)], axis=0)
+
+
+def silu_parts(gate_act, lift_act, inner_grad):
+    sigma = jax.nn.sigmoid(gate_act)
+    gate_grad = inner_grad * lift_act * sigma * (1 + gate_act * (1 - sigma))
+    return gate_grad.astype(BF), (inner_grad * gate_act * sigma).astype(BF)
+
+
+def norm_back(grad, hidden, gain):
+    scale = lax.rsqrt(jnp.mean(hidden * hidden, axis=-1, keepdims=True) + EPS)
+    unit = hidden * scale
+    inward = grad * gain
+    gain_grad = jnp.sum(grad * unit, axis=0)
+    return scale * (inward - unit * jnp.mean(inward * unit, axis=-1, keepdims=True)), gain_grad
+
+
+def feed_fwd(hidden, gain, gate_weight, lift_weight, drop_weight):
+    fnormed = root_mean_square_scale(hidden, gain).astype(BF)
+    gate_act = jnp.dot(fnormed, gate_weight, preferred_element_type=F32)
+    lift_act = jnp.dot(fnormed, lift_weight, preferred_element_type=F32)
+    inner = (jax.nn.silu(gate_act) * lift_act).astype(BF)
+    result = hidden + jnp.dot(inner, drop_weight, preferred_element_type=F32)
+    return result, (fnormed, gate_act.astype(BF), lift_act.astype(BF), inner)
+
+
+def feed_bwd(grad, hidden, gain, kept, gate_weight, lift_weight, drop_weight):
+    fnormed, gate_act, lift_act, inner = kept
+    grad_low = grad.astype(BF)
+    inner_grad = outer_dot(grad_low, drop_weight)
+    gate_low, lift_low = silu_parts(gate_act.astype(F32), lift_act.astype(F32), inner_grad)
+    normed_grad = outer_dot(gate_low, gate_weight) + outer_dot(lift_low, lift_weight)
+    hidden_grad, gain_grad = norm_back(normed_grad, hidden, gain)
+    return grad + hidden_grad, gain_grad, grad_low, gate_low, lift_low
+
+
+def fast_device(tokens, lengths, cotangent, mixgain, mixentry, mixtaps, mixexit, lowgain, lowgate, lowlift,
+                lowdrop, attgain, attquery, attkeys, attvalues, querygain, keysgain, attexit, topgain, topgate,
+                toplift, topdrop):
+    rows, width = tokens.shape
+    head = querygain.shape[0]
+    devices = lax.axis_size("ctx")
+    lines = devices // 4
+    half_rows = rows // 2
+    group = devices * rows
+    place = lax.axis_index("ctx")
+    core = place % 2
+    first = lengths[0, 0]
+    second = first + lengths[0, 1]
+    mine = place * rows + jnp.arange(rows, dtype=jnp.int32)
+    my_seg = segment_of(mine, first, second)
+    begin = jnp.where(my_seg == 0, 0, jnp.where(my_seg == 1, first, second))
+    position = (mine - begin).astype(F32)
+    gains = [value.astype(F32) for value in (mixgain, lowgain, attgain, topgain)]
+    mixgain_f, lowgain_f, attgain_f, topgain_f = gains
+    taps_f = mixtaps.astype(F32)
+    twice = lambda gain: jnp.tile(gain.astype(F32), LANES // head)[None, :]
+    querygain_2, keysgain_2 = twice(querygain), twice(keysgain)
+    spot = jnp.arange(LANES, dtype=jnp.int32) % (head // 2)
+    angle = position[:, None] * (THETA ** (-spot.astype(F32) * 2.0 / head))[None, :]
+    cosine = jnp.cos(angle)
+    sine = jnp.sin(angle) * jnp.where(jnp.arange(LANES) % head < head // 2, -1.0, 1.0)[None, :]
+    info = jnp.stack([first, second, core, core]).astype(jnp.int32)
+
+    hidden = tokens.astype(F32)
+    normed_one = root_mean_square_scale(hidden, mixgain_f).astype(BF)
+    mixed = jnp.dot(normed_one, mixentry, preferred_element_type=F32)
+    part_b, part_c, part_x = (mixed[:, i * width:(i + 1) * width] for i in range(3))
+    product = (part_b * part_x).astype(BF)
+    borrowed = passed_along(product[rows - 2:], "ctx", 1)
+    extended = jnp.concatenate([borrowed, product], axis=0).astype(F32)
+    fits_one = ((mine >= 1) & (segment_of(mine - 1, first, second) == my_seg)).astype(F32)[:, None]
+    fits_two = ((mine >= 2) & (segment_of(mine - 2, first, second) == my_seg)).astype(F32)[:, None]
+    conved = conv_local(extended, taps_f, fits_one, fits_two)
+    gated = (part_c * conved).astype(BF)
+    hidden_one = hidden + jnp.dot(gated, mixexit, preferred_element_type=F32)
+    hidden_two, kept_low = feed_fwd(hidden_one, lowgain_f, lowgate, lowlift, lowdrop)
+
+    heads_q, heads_k = attquery.shape[1] // head, attkeys.shape[1] // head
+    msg, normed_two, query_raw, key_raw = call_plain(
+        functools.partial(project_kernel, head),
+        (shape_of((devices, half_rows, 2 * LANES), BF), shape_of((rows, width), BF),
+         shape_of((rows, attquery.shape[1]), F32), shape_of((rows, attkeys.shape[1]), F32)),
+        (hidden_two, attgain_f[None, :], attquery, attkeys, attvalues, cosine, sine, querygain_2, keysgain_2),
+        flops=2 * rows * width * 2 * width, moved=6 << 20, name="project")
+    held = lax.all_to_all(msg, "ctx", 0, 0)
+    held_kv = held[:, :, LANES:]
+    other_kv = sibling(held_kv)
+    pair = jnp.where(core == 0, jnp.stack([held_kv, other_kv], axis=1), jnp.stack([other_kv, held_kv], axis=1))
+    all_kv = pair.reshape(group, LANES)
+    keys, sources = 512, 2
+    wide = sources * rows
+    area = group * group // 2 // 2 * 2
+    attended_f, augmented = call_plain(
+        functools.partial(attend_kernel, head, rows, keys, sources),
+        (shape_of((devices, half_rows, LANES), F32), shape_of((devices, 2, half_rows, LANES), BF)),
+        (info, held, all_kv), smem=1,
+        scratch=[pltpu.VMEM((group, LANES), BF), pltpu.VMEM((wide, LANES), F32)],
+        flops=4 * area * LANES, moved=5 << 20, name="attend")
+    got = lax.all_to_all(attended_f.astype(BF), "ctx", 0, 0)
+    attended_low = got.reshape(devices // 2, rows, LANES).transpose(1, 0, 2).reshape(rows, width)
+    hidden_three = hidden_two + jnp.dot(attended_low, attexit, preferred_element_type=F32)
+    output, kept_top = feed_fwd(hidden_three, topgain_f, topgate, toplift, topdrop)
+
+    grad = cotangent.astype(F32)
+    grad, topgain_grad, gb_top, gate_top, lift_top = feed_bwd(
+        grad, hidden_three, topgain_f, kept_top, topgate, toplift, topdrop)
+    grad_low3 = grad.astype(BF)
+    dattn = outer_dot(grad_low3, attexit).astype(BF)
+    send = dattn.reshape(2, half_rows, devices // 2, LANES).transpose(2, 0, 1, 3).reshape(devices, half_rows, LANES)
+    held_grad = lax.all_to_all(send, "ctx", 0, 0)
+    dq, dkv = call_plain(
+        functools.partial(attend_back_kernel, head, rows, keys, sources),
+        (shape_of((devices, half_rows, LANES), BF), shape_of((group, LANES), BF)),
+        (info, augmented, attended_f, held_grad, all_kv), smem=1,
+        scratch=[pltpu.VMEM((group, LANES), BF), pltpu.VMEM((group, LANES), BF),
+                 pltpu.VMEM((group, LANES), F32), pltpu.VMEM((group, LANES), F32), pltpu.VMEM((wide, LANES), F32)],
+        flops=10 * area * LANES, moved=8 << 20, name="attend_back")
+    dkv = dkv.reshape(devices, 2, half_rows, LANES)
+    mine_kv = lax.dynamic_index_in_dim(dkv, core, 1, keepdims=False)
+    send_kv = lax.dynamic_index_in_dim(dkv, 1 - core, 1, keepdims=False)
+    dkv_sum = (mine_kv.astype(F32) + sibling(send_kv).astype(F32)).astype(BF)
+    back = lax.all_to_all(jnp.concatenate([dq, dkv_sum], axis=2), "ctx", 0, 0)
+    raw_low, grad_two, attgain_grad, querygain_grad, keysgain_grad = call_plain(
+        functools.partial(project_back_kernel, head),
+        (shape_of((rows, 2 * width), BF), shape_of((rows, width), F32), shape_of((1, width), F32),
+         shape_of((1, LANES), F32), shape_of((1, LANES), F32)),
+        (back, hidden_two, attgain_f[None, :], attquery, attkeys, attvalues, cosine, sine, querygain_2, keysgain_2,
+         query_raw, key_raw, grad),
+        flops=2 * rows * width * 2 * width, moved=8 << 20, name="project_back")
+    fold = lambda value: value.reshape(LANES // head, head).sum(axis=0)
+    querygain_grad, keysgain_grad = fold(querygain_grad), fold(keysgain_grad)
+    grad, lowgain_grad, gb_low, gate_low, lift_low = feed_bwd(
+        grad_two, hidden_one, lowgain_f, kept_low, lowgate, lowlift, lowdrop)
+    grad_low1 = grad.astype(BF)
+    gated_grad = outer_dot(grad_low1, mixexit)
+    part_c_grad = gated_grad * conved
+    conved_grad = gated_grad * part_c
+    _, pull_conv = jax.vjp(lambda ext, taps: conv_local(ext, taps, fits_one, fits_two), extended, taps_f)
+    extended_grad, mixtaps_grad = pull_conv(conved_grad)
+    returned_rim = passed_along(extended_grad[:2], "ctx", -1)
+    product_grad = extended_grad[2:].at[rows - 2:].add(returned_rim)
+    mixed_grad = jnp.concatenate(
+        [product_grad * part_x, part_c_grad, product_grad * part_b], axis=1).astype(BF)
+    hidden_grad, mixgain_grad = norm_back(outer_dot(mixed_grad, mixentry), hidden, mixgain_f)
+    tokens_grad = grad + hidden_grad
+
+    kq, kk = attquery.shape[1], attkeys.shape[1]
+    pairs = [
+        (left_side(kept_top[3]), right_side([gb_top], core)),
+        (left_side(kept_top[0]), right_side([gate_top, lift_top], core)),
+        (left_side(attended_low), right_side([grad_low3], core)),
+        (left_side(normed_two), right_side([raw_low[:, :kq], raw_low[:, kq:kq + kk], raw_low[:, kq + kk:]], core)),
+        (left_side(kept_low[3]), right_side([gb_low], core)),
+        (left_side(kept_low[0]), right_side([gate_low, lift_low], core)),
+        (left_side(gated), right_side([grad_low1], core)),
+        (left_side(normed_one), right_side([mixed_grad], core)),
+    ]
+    sums = sum_over_chips(pairs, lines, 1)
+
+    def finish(value, cuts):
+        size = value.shape[0] // 2
+        own = lax.dynamic_slice_in_dim(value, core * size, size, 0)
+        away = sibling(lax.dynamic_slice_in_dim(value, (1 - core) * size, size, 0))
+        results, start = [], 0
+        for cut in cuts:
+            a, b = own[:, start:start + cut], away[:, start:start + cut]
+            results.append(jnp.where(core == 0, jnp.concatenate([a, b], axis=1),
+                                     jnp.concatenate([b, a], axis=1)).astype(F32))
+            start += cut
+        return results
+
+    ff = lowgate.shape[1]
+    (topdrop_grad,) = finish(sums[0], [width // 2])
+    topgate_grad, toplift_grad = finish(sums[1], [ff // 2, ff // 2])
+    (attexit_grad,) = finish(sums[2], [width // 2])
+    attquery_grad, attkeys_grad, attvalues_grad = finish(sums[3], [kq // 2, kk // 2, kk // 2])
+    (lowdrop_grad,) = finish(sums[4], [width // 2])
+    lowgate_grad, lowlift_grad = finish(sums[5], [ff // 2, ff // 2])
+    (mixexit_grad,) = finish(sums[6], [width // 2])
+    (mixentry_grad,) = finish(sums[7], [mixentry.shape[1] // 2])
+    smalls = lax.psum((mixgain_grad, mixtaps_grad, lowgain_grad, attgain_grad[0], querygain_grad, keysgain_grad,
+                       topgain_grad), ("dp", "ctx"))
+    return (output, tokens_grad, smalls[0], mixentry_grad, smalls[1], mixexit_grad, smalls[2], lowgate_grad,
+            lowlift_grad, lowdrop_grad, smalls[3], attquery_grad, attkeys_grad, attvalues_grad, smalls[4],
+            smalls[5], attexit_grad, smalls[6], topgate_grad, toplift_grad, topdrop_grad)
+
+
 def solution(mesh):
-    placed = (
-        P(("dp", "ctx"), None),
-        P("dp", None),
-        P(("dp", "ctx"), None),
-        P(),
-        P(),
-        P(),
-        P(),
-        P(),
-        P(),
-        P(),
-        P(),
-        P(),
-        P(),
-        P(),
-        P(),
-        P(),
-        P(),
-        P(),
-        P(),
-        P(),
-        P(),
-        P(),
-    )
-    return jax.shard_map(
-        per_device,
-        mesh=mesh,
-        in_specs=placed,
-        out_specs=(
-            P(("dp", "ctx"), None),
-            P(("dp", "ctx"), None),
-            P(),
-            P("ctx", None),
-            P(),
-            P("ctx", None),
-            P(),
-            P("ctx", None),
-            P("ctx", None),
-            P("ctx", None),
-            P(),
-            P("ctx", None),
-            P("ctx", None),
-            P("ctx", None),
-            P(),
-            P(),
-            P("ctx", None),
-            P(),
-            P("ctx", None),
-            P("ctx", None),
-            P("ctx", None),
-        ),
-        check_vma=False,
-    )
+    placed = (P(("dp", "ctx"), None), P("dp", None), P(("dp", "ctx"), None)) + (P(),) * 19
+    split = {0: P(("dp", "ctx"), None), 1: P(("dp", "ctx"), None)}
+    whole = (2, 4, 6, 10, 14, 15, 17)
+    outs = tuple(split.get(i, P() if i in whole else P("ctx", None)) for i in range(21))
+    small = mesh.shape["ctx"] == 16 and mesh.shape["dp"] == 2
+    return jax.shard_map(fast_device if small else per_device, mesh=mesh, in_specs=placed, out_specs=outs,
+                         check_vma=False)

time: 2550 us -> 849 us (0.33)
  waiting for transfers between devices: 1640 us -> 1.57 us
  Pallas kernels: 0 us -> 404 us
  starting transfers between devices: 231 us -> 30.1 us
  matrix products: 263 us -> 110 us
  other arithmetic: 256 us -> 111 us
  local copies, waits for them, and re-layouts: 56.9 us -> 97.4 us
    reduce_scatter x12 -> x0, waiting for transfers between devices: 1540 us -> none  [the longest x1 197 us: per_device(): lax.psum_scatter(lowgate_grad, 'ctx', scatter_dimension=0, tiled=True)]
    pallas_call x0 -> x5, Pallas kernels: none -> 404 us  [the longest x1 313 us: sum_over_chips(): pl.pallas_call(functools.partial(sum_kernel, jobs, lines), out_shape=jax....]
    ppermute x34 -> x2, starting transfers between devices: 156 us -> 3.64 us  [passed_along(): lax.ppermute(value, axis, [(source, source + steps) for source in range(f...]
    dot_general x37 -> x9, matrix products: 203 us -> 50.9 us  [the longest x2 17.7 us: feed_fwd(): lift_act = jnp.dot(fnormed, lift_weight, preferred_element_type=F32)]
    convert_element_type x129 -> x28, other arithmetic: 160 us -> 31.2 us  [the longest x12 16.4 us: finish(): results.append(jnp.where(core == 0, jnp.concatenate([a, b], axis=1), jnp....]
    ppermute x32 -> x26, starting transfers between devices: 73.2 us -> 9.5 us  [sibling(): return lax.ppermute(value, 'ctx', [(i, i ^ 1) for i in range(count)])]
    all_gather x2 -> x0, waiting for transfers between devices: 50.4 us -> none  [the longest x1 50.4 us: per_device(): keys_in = lax.all_gather(key_low, 'ctx', axis=0, tiled=True)]
    reduce_sum x6 -> x2, other arithmetic: 40.8 us -> 2.41 us  [fast_device(): fold = lambda value: value.reshape(LANES // head, head).sum(axis=0)]
  transfers between devices with their start and end apart: 81 -> 31, of which waited for: 27 -> 2; matrix products, arithmetic and copies ran while one was open for 13% -> 24% of each run, Pallas kernels for 0% -> 9%
where the time goes in v1:
time: 849 us; the launch traced here: 832 us
  Pallas kernels  404 us (48%)
  other arithmetic  111 us (13%)
  matrix products  110 us (13%)
  local copies, waits for them, and re-layouts  97.4 us (11%)
  blocking collectives  74.4 us (9%)
  starting transfers between devices  30.1 us (4%)
    pallas_call x1, Pallas kernels, sum_over_chips(): pl.pallas_call(functools.partial(sum_kernel, jobs, lines), out_shape=jax....  313 us
    pallas_call x4, Pallas kernels, call_plain(): pl.pallas_call(kernel, out_shape=tuple(outs) if many else outs, in_specs=...  91.4 us
    dot_general x9, matrix products, outer_dot(): lax.dot_general(left, right, (((1,), (1,)), ((), ())), preferred_element_...  59.1 us
    psum x1, blocking collectives, fast_device(): lax.psum((mixgain_grad, mixtaps_grad, lowgain_grad, attgain_grad[0], quer...  42.1 us
    all_to_all x1, blocking collectives, fast_device(): held = lax.all_to_all(msg, 'ctx', 0, 0)  32.3 us
    concatenate x8, other arithmetic, right_side(): return jnp.concatenate([mine, sibling(send)], axis=0)  27.6 us
    unnamed x164, local copies, waits for them, and re-layouts  20.8 us
    transpose x7, other arithmetic, left_side(): return jnp.concatenate([value, sibling(value)], axis=0).T  19.7 us
  transfers between devices with their start and end apart: 31, of which 2 were waited for; matrix products, arithmetic and copies ran while one was open for 24% of the time, Pallas kernels for 9%

profile of v1, /device:TPU:0, one launch (start us, length us, event | category | flops | bytes accessed | tf_op | source)
XLA Modules:
  0.0 832.5 jit_solution(7079830327161859503)
XLA Ops:
  5.4 4.8 fusion.68
  12.8 2.4 collective-permute-start
  22.7 2.8 multiply_convert_fusion.7
  26.5 5.6 fusion.69
  32.2 9.7 %multiply_convert_fusion.1 = (bf16[256,4608]{1,0:T(8,128)(2,1)S(1)}, bf16[256,4608]{1,0:T(8,128)(2,1)}) fusion(f32[256,4608]{1,0:T(8,128)S(1)} %fusion.69, bf16[256,1024]{1,0:T(8,128)(2,1)S(1)} %multiply_convert_fusion.6, bf16[1024,4608]{1,0:T(8,128)(2,1)} %param.33), kind=kOutput, calls=%fused_computation.27 | convolution fusion | flops 2424176640 | bytes 19398656 | tf_op jit(solution)/shard_map/dot_general | solution.py:1119
  41.9 3.6 convolution_add_fusion.4.hid_ref
  45.4 6.4 project.1
  51.8 32.3 %all_to_all.20.q_ref = bf16[16,128,256]{2,1,0:T(8,128)(2,1)S(1)} all-to-all(bf16[16,128,256]{2,1,0:T(8,128)(2,1)} %get-tuple-element.46), channel_id=1, replica_groups=mesh['dp'=2,'ctx'=16] {'ctx'}, dimensions={0} | all-to-all | bytes 2097152 | tf_op jit(solution)/shard_map/all_to_all | solution.py:1184
  91.7 28.5 %attend.1 = (f32[16,128,128]{2,1,0:T(8,128)}, bf16[16,2,128,128]{3,2,1,0:T(8,128)(2,1)}) custom-call(s32[4]{0:T(128)} %pad_add_fusion.3.info_ref, bf16[16,128,256]{2,1,0:T(8,128)(2,1)} %copy-done.27, bf16[4096,128]{1,0:T(8,128)(2,1)} %bitcast.169), custom_call_target="tpu_custom_call" | custom-call | flops 4294967296 | bytes 5242880 | tf_op jit(solution)/shard_map/attend/pallas_call | solution.py:1064
  122.3 4.9 all-to-all-start.1
  133.1 2.2 maximum_bitcast_fusion.6
  135.3 2.3 copy.124
  139.8 2.3 copy.93
  144.3 2.3 copy.122
  148.9 2.3 copy.123
  155.7 8.3 fusion.70
  164.0 8.1 fusion.71
  172.1 17.4 %fusion.7 = (bf16[256,4608]{1,0:T(8,128)(2,1)S(1)}, bf16[256,4608]{1,0:T(8,128)(2,1)}, bf16[256,4608]{1,0:T(8,128)(2,1)}) fusion(f32[256,4608]{1,0:T(8,128)} %fusion.70, f32[256,4608]{1,0:T(8,128)} %fusion.71, bf16[256,1024]{1,0:T(8,128)(2,1)S(1)} %copy-done.34, bf16[4608,1024]{1,0:T(8,128)(2,1)} %param.45), kind=kOutput, calls=%fused_computation.13 | convolution fusion | flops 2443051008 | bytes 26476544 | tf_op jit(solution)/shard_map/dot_general | solution.py:76
  189.5 5.1 fusion.72
  194.6 6.5 multiply_reduce_fusion
  204.2 5.8 all-to-all-start.2
  210.0 4.8 maximum_bitcast_fusion.1
  214.8 6.7 copy.94
  222.5 3.4 constant_dynamic-slice_fusion.37
  228.2 47.4 %attend_back.1 = (bf16[16,128,128]{2,1,0:T(8,128)(2,1)}, bf16[4096,128]{1,0:T(8,128)(2,1)}) custom-call(s32[4]{0:T(128)} %pad_add_fusion.3.info_ref, bf16[16,2,128,128]{3,2,1,0:T(8,128)(2,1)} %get-tuple-element.48.aug_ref, f32[16,128,128]{2,1,0:T(8,128)} %get-tuple-element.47.out_ref, bf16[16,128,128]{2,1,0:T(8,128)(2,1)} %copy-done.49, ...), custom_call_target="tpu_custom_call" | custom-call | flops 10737418240 | bytes 8388608 | tf_op jit(solution)/shard_map/attend_back/pallas_call | solution.py:1064
  278.3 3.3 pad_maximum_fusion.2
  284.2 6.3 all-to-all-start.3
  290.5 8.0 convolution_add_fusion.3
  304.9 4.8 maximum_bitcast_fusion
  309.8 6.8 copy.92
  316.6 4.4 pad_maximum_fusion.refs_9_
  321.0 9.1 %project_back.1 = (bf16[256,2048]{1,0:T(8,128)(2,1)}, f32[256,1024]{1,0:T(8,128)}, f32[1,1024]{1,0:T(1,128)}, f32[1,128]{1,0:T(1,128)}, f32[1,128]{1,0:T(1,128)}) custom-call(bf16[16,128,256]{2,1,0:T(8,128)(2,1)} %all-to-all-done.3.back_ref, f32[256,1024]{1,0:T(8,128)} %convolution_add_fusion.4.hid_ref, f32[1,1024]{1,0:T(1,128)} %bitcast.193, ...), custom_call_target="tpu_custom_call" | custom-call | flops 1073741824 | bytes 8388608 | tf_op jit(solution)/shard_map/project_back/pallas_call | solution.py:1064
  331.4 12.1 %fusion.15 = (bf16[256,4608]{1,0:T(8,128)(2,1)S(1)}, bf16[256,4608]{1,0:T(8,128)(2,1)S(1)}) fusion(f32[256,4608]{1,0:T(8,128)} %copy-done.17, bf16[256,4608]{1,0:T(8,128)(2,1)} %get-tuple-element.211, bf16[256,1024]{1,0:T(8,128)(2,1)S(1)} %convert_element_type.271, bf16[4608,1024]{1,0:T(8,128)(2,1)} %param.34), kind=kOutput, calls=%fused_computation.21 | convolution fusion | flops 2434793472 | bytes 21757952 | tf_op jit(solution)/shard_map/dot_general | solution.py:76
  343.5 5.3 fusion.73
  348.8 6.5 multiply_reduce_fusion.1
  358.0 2.5 multiply_reduce_fusion.4
  388.6 4.8 fusion.30
  394.9 42.1 %all-reduce.6 = (f32[1024]{0:T(1024)}, f32[3,1024]{1,0:T(4,128)}, f32[1024]{0:T(1024)}, f32[1024]{0:T(1024)}, f32[64]{0:T(128)}, /*index=5*/f32[64]{0:T(128)}, f32[1024]{0:T(1024)}) all-reduce(f32[1024]{0:T(1024)S(1)} %get-tuple-element.108, f32[3,1024]{1,0:T(4,128)S(1)} %pad_add_fusion.1, ...), channel_id=1, replica_groups=mesh['dp'=2,'ctx'=16] {'dp','ctx'}, use_global_device_ids=true, to_apply=%region_7.8 | all-reduce | flops 7296 | bytes 58368 | tf_op jit(solution)/shard_map/psum | solution.py:1280
  440.6 2.3 pad_maximum_fusion.10.refs_11_
  442.9 2.4 pad_maximum_fusion.5.refs_15_
  445.3 11.4 %pad_maximum_fusion.1.refs_13_ = bf16[512,4608]{1,0:T(8,128)(2,1)} fusion(bf16[256,4608]{1,0:T(8,128)(2,1)} %collective-permute-done.17, bf16[256,2304]{1,0:T(8,128)(2,1)S(1)} %copy-done.15, bf16[256,2304]{1,0:T(8,128)(2,1)S(1)} %copy-done.14), kind=kLoop, calls=%fused_computation.25 | loop fusion | flops 14155776 | bytes 9437184 | tf_op jit(solution)/shard_map/concatenate | solution.py:1099
  456.6 313.0 %sum_over_chips.1 = bf16[138,128,128]{2,1,0:T(8,128)(2,1)} custom-call(bf16[8,576,512]{2,1,0:T(8,128)(2,1)} %bitcast.147, bf16[8,128,512]{2,1,0:T(8,128)(2,1)} %bitcast.167, bf16[8,128,512]{2,1,0:T(8,128)(2,1)} %bitcast.168, bf16[8,128,512]{2,1,0:T(8,128)(2,1)} %bitcast.164, bf16[8,576,512]{2,1,0:T(8,128)(2,1)} %bitcast.146, bf16[8,128,512]{2,1,0:T(8,128)(2,1)} %bitcast.165, ...), custom_call_target="tpu_custom_call" | custom-call | flops 18253611008 | bytes 108800000 | tf_op jit(solution)/shard_map/sum_over_chips/pallas_call | solution.py:1036
  805.6 2.2 fusion.35
  807.8 2.3 fusion.34
  813.4 2.9 copy.120
  818.4 2.9 copy.119
  824.5 2.9 copy.118
  829.5 2.8 copy.117
  (357 shorter events, 142.6 us)
Async XLA Ops:
  0.7 152.6 %copy-start = (bf16[1024,1024]{1,0:T(8,128)(2,1)S(1)}, bf16[1024,1024]{1,0:T(8,128)(2,1)}, u32[]{:S(2)}) copy-start(bf16[1024,1024]{1,0:T(8,128)(2,1)} %param.41) | copy-start | bytes 6291460
  11.8 8.5 %copy-start.69 = (bf16[64]{0:T(256)(128)(2,1)S(1)}, bf16[64]{0:T(256)(128)(2,1)}, u32[]{:S(2)}) copy-start(bf16[64]{0:T(256)(128)(2,1)} %param.39) | copy-start | bytes 388
  11.8 9.0 %copy-start.70 = (bf16[64]{0:T(256)(128)(2,1)S(1)}, bf16[64]{0:T(256)(128)(2,1)}, u32[]{:S(2)}) copy-start(bf16[64]{0:T(256)(128)(2,1)} %param.40) | copy-start | bytes 388
  12.8 8.7 %collective-permute-start = (bf16[2,1024]{1,0:T(2,128)(2,1)S(1)}, bf16[2,1024]{1,0:T(2,128)(2,1)S(1)}, u32[]{:S(2)}, u32[]{:S(2)}) collective-permute-start(bf16[2,1024]{1,0:T(2,128)(2,1)S(1)} %slice.223), channel_id=1, source_target_pairs={{0,1},{1,2},{2,3},{3,4},{4,5},{5,6},{6,7},{7,8},{8,9},{9,10},{10,1... | collective-permute-start | bytes 12296 | tf_op jit(solution)/shard_map/ppermute | solution.py:19
  26.3 15.5 %copy-start.4 = (f32[256,1024]{1,0:T(8,128)}, f32[256,1024]{1,0:T(8,128)S(1)}, u32[]{:S(2)}) copy-start(f32[256,1024]{1,0:T(8,128)S(1)} %get-tuple-element.209) | copy-start | bytes 3145732
  26.5 15.3 %slice-start.3 = ((s8[9437184]{0:T(1024)(128)(4,1)}), s8[4194304]{0:T(1024)(128)(4,1)S(1)}, s32[]{:S(2)}) async-start(s8[9437184]{0:T(1024)(128)(4,1)} %bitcast.198), calls=%async_computation.7 | async-start | bytes 8388608
  32.1 9.7 %copy-start.17 = (f32[256,4608]{1,0:T(8,128)}, f32[256,4608]{1,0:T(8,128)S(1)}, u32[]{:S(2)}) copy-start(f32[256,4608]{1,0:T(8,128)S(1)} %fusion.69) | copy-start | bytes 14155780
  32.1 9.7 %slice-start.4 = ((s8[9437184]{0:T(1024)(128)(4,1)}), s8[4194304]{0:T(1024)(128)(4,1)S(1)}, s32[]{:S(2)}) async-start(s8[9437184]{0:T(1024)(128)(4,1)} %bitcast.198), calls=%async_computation.8 | async-start | bytes 8388608
  32.2 9.7 %slice-start.5 = ((s8[9437184]{0:T(1024)(128)(4,1)}), s8[1048576]{0:T(1024)(128)(4,1)S(1)}, s32[]{:S(2)}) async-start(s8[9437184]{0:T(1024)(128)(4,1)} %bitcast.198), calls=%async_computation.9 | async-start | bytes 2097152
  86.3 2.6 collective-permute-start.1
  87.0 46.0 %collective-permute-start.11 = (bf16[256,1024]{1,0:T(8,128)(2,1)}, bf16[256,1024]{1,0:T(8,128)(2,1)}, u32[]{:S(2)}, u32[]{:S(2)}) collective-permute-start(bf16[256,1024]{1,0:T(8,128)(2,1)} %fusion.25), channel_id=1, source_target_pairs={{0,1},{1,0},{2,3},{3,2},{4,5},{5,4},{6,7},{7,6},{8,9},{9,8},{10,11... | collective-permute-start | bytes 1572872 | tf_op jit(solution)/shard_map/ppermute | solution.py:1082
  120.2 9.7 %copy-start.67 = (bf16[1024]{0:T(1024)(128)(2,1)S(1)}, bf16[1024]{0:T(1024)(128)(2,1)}, u32[]{:S(2)}) copy-start(bf16[1024]{0:T(1024)(128)(2,1)} %param.42) | copy-start | bytes 6148
  122.3 28.9 %all-to-all-start.1 = ((bf16[16,128,128]{2,1,0:T(8,128)(2,1)}), bf16[16,128,128]{2,1,0:T(8,128)(2,1)}, u32[]{:S(2)}, u32[]{:S(2)}) async-start(bf16[16,128,128]{2,1,0:T(8,128)(2,1)} %convert_element_type.254), calls=%async_computation.1 | async-start | bytes 1048576 | tf_op jit(solution)/shard_map/all_to_all | solution.py:1198
  129.0 1.9 collective-permute-start.12
  129.4 8.2 collective-permute-start.7
  129.5 12.6 %collective-permute-start.9 = (bf16[256,1024]{1,0:T(8,128)(2,1)}, bf16[256,1024]{1,0:T(8,128)(2,1)}, u32[]{:S(2)}, u32[]{:S(2)}) collective-permute-start(bf16[256,1024]{1,0:T(8,128)(2,1)} %copy-done.21), channel_id=1, source_target_pairs={{0,1},{1,0},{2,3},{3,2},{4,5},{5,4},{6,7},{7,6},{8,9},{9,8},{10,11... | collective-permute-start | bytes 1572872 | tf_op jit(solution)/shard_map/ppermute | solution.py:1082
  129.9 80.1 %collective-permute-start.8 = (bf16[256,4608]{1,0:T(8,128)(2,1)}, bf16[256,4608]{1,0:T(8,128)(2,1)}, u32[]{:S(2)}, u32[]{:S(2)}) collective-permute-start(bf16[256,4608]{1,0:T(8,128)(2,1)} %copy-done.28), channel_id=1, source_target_pairs={{0,1},{1,0},{2,3},{3,2},{4,5},{5,4},{6,7},{7,6},{8,9},{9,8},{10,11... | collective-permute-start | bytes 7077896 | tf_op jit(solution)/shard_map/ppermute | solution.py:1082
  130.9 15.8 %collective-permute-start.10 = (bf16[256,1024]{1,0:T(8,128)(2,1)}, bf16[256,1024]{1,0:T(8,128)(2,1)}, u32[]{:S(2)}, u32[]{:S(2)}) collective-permute-start(bf16[256,1024]{1,0:T(8,128)(2,1)} %copy-done.19), channel_id=1, source_target_pairs={{0,1},{1,0},{2,3},{3,2},{4,5},{5,4},{6,7},{7,6},{8,9},{9,8},{10,11... | collective-permute-start | bytes 1572872 | tf_op jit(solution)/shard_map/ppermute | solution.py:1082
  155.5 45.6 %copy-start.6 = (f32[256,1024]{1,0:T(8,128)}, f32[256,1024]{1,0:T(8,128)S(1)}, u32[]{:S(2)}) copy-start(f32[256,1024]{1,0:T(8,128)S(1)} %get-tuple-element.213) | copy-start | bytes 3145732
  155.7 8.3 copy-start.12
  164.0 25.5 %slice-start = ((s8[9437184]{0:T(1024)(128)(4,1)}), s8[4194304]{0:T(1024)(128)(4,1)S(1)}, s32[]{:S(2)}) async-start(s8[9437184]{0:T(1024)(128)(4,1)} %bitcast.144), calls=%async_computation.4 | async-start | bytes 8388608
  172.1 17.4 %slice-start.1 = ((s8[9437184]{0:T(1024)(128)(4,1)}), s8[4194304]{0:T(1024)(128)(4,1)S(1)}, s32[]{:S(2)}) async-start(s8[9437184]{0:T(1024)(128)(4,1)} %bitcast.144), calls=%async_computation.5 | async-start | bytes 8388608
  172.1 17.4 %slice-start.2 = ((s8[9437184]{0:T(1024)(128)(4,1)}), s8[1048576]{0:T(1024)(128)(4,1)S(1)}, s32[]{:S(2)}) async-start(s8[9437184]{0:T(1024)(128)(4,1)} %bitcast.144), calls=%async_computation.6 | async-start | bytes 2097152
  204.2 23.2 %all-to-all-start.2 = ((bf16[16,128,128]{2,1,0:T(8,128)(2,1)}), bf16[16,128,128]{2,1,0:T(8,128)(2,1)S(1)}, u32[]{:S(2)}, u32[]{:S(2)}) async-start(bf16[16,128,128]{2,1,0:T(8,128)(2,1)} %bitcast.16), calls=%async_computation.2 | async-start | bytes 1048576 | tf_op jit(solution)/shard_map/all_to_all | solution.py:1209
  221.5 78.8 %collective-permute-start.5 = (bf16[256,1024]{1,0:T(8,128)(2,1)S(1)}, bf16[256,1024]{1,0:T(8,128)(2,1)}, u32[]{:S(2)}, u32[]{:S(2)}) collective-permute-start(bf16[256,1024]{1,0:T(8,128)(2,1)S(1)} %copy-done.13), channel_id=1, source_target_pairs={{0,1},{1,0},{2,3},{3,2},{4,5},{5,4},{6,7},{7,6},{8,9},{9,8},{10,11... | collective-permute-start | bytes 1572872 | tf_op jit(solution)/shard_map/ppermute | solution.py:1082
  221.9 80.8 %collective-permute-start.6 = (bf16[256,1024]{0,1:T(8,128)(2,1)S(1)}, bf16[256,1024]{0,1:T(8,128)(2,1)}, u32[]{:S(2)}, u32[]{:S(2)}) collective-permute-start(bf16[256,1024]{0,1:T(8,128)(2,1)S(1)} %bitcast.149), channel_id=1, source_target_pairs={{0,1},{1,0},{2,3},{3,2},{4,5},{5,4},{6,7},{7,6},{8,9},{9,8},{10,11... | collective-permute-start | bytes 1572872 | tf_op jit(solution)/shard_map/ppermute | solution.py:1082
  222.1 82.9 %collective-permute-start.4 = (bf16[256,4608]{1,0:T(8,128)(2,1)}, bf16[256,4608]{1,0:T(8,128)(2,1)}, u32[]{:S(2)}, u32[]{:S(2)}) collective-permute-start(bf16[256,4608]{1,0:T(8,128)(2,1)} %get-tuple-element.128), channel_id=1, source_target_pairs={{0,1},{1,0},{2,3},{3,2},{4,5},{5,4},{6,7},{7,6},{8,9},{9,8},{10,11... | collective-permute-start | bytes 7077896 | tf_op jit(solution)/shard_map/ppermute | solution.py:1082
  276.7 5.8 collective-permute-start.2
  281.6 34.9 %collective-permute-start.13 = (bf16[256,4608]{1,0:T(8,128)(2,1)}, bf16[256,4608]{1,0:T(8,128)(2,1)}, u32[]{:S(2)}, u32[]{:S(2)}) collective-permute-start(bf16[256,4608]{1,0:T(8,128)(2,1)} %pad_maximum_fusion.2), channel_id=1, source_target_pairs={{0,1},{1,0},{2,3},{3,2},{4,5},{5,4},{6,7},{7,6},{8,9},{9,8},{10,11... | collective-permute-start | bytes 7077896 | tf_op jit(solution)/shard_map/ppermute | solution.py:1082
  282.4 16.1 %collective-permute-start.14 = (bf16[256,512]{1,0:T(8,128)(2,1)}, bf16[256,512]{1,0:T(8,128)(2,1)}, u32[]{:S(2)}, u32[]{:S(2)}) collective-permute-start(bf16[256,512]{1,0:T(8,128)(2,1)} %get-tuple-element.184), channel_id=1, source_target_pairs={{0,1},{1,0},{2,3},{3,2},{4,5},{5,4},{6,7},{7,6},{8,9},{9,8},{10,11... | collective-permute-start | bytes 786440 | tf_op jit(solution)/shard_map/ppermute | solution.py:1082
  284.2 36.8 %all-to-all-start.3 = ((bf16[16,128,256]{2,1,0:T(8,128)(2,1)}), bf16[16,128,256]{2,1,0:T(8,128)(2,1)}, u32[]{:S(2)}, u32[]{:S(2)}) async-start(bf16[16,128,256]{2,1,0:T(8,128)(2,1)} %pad_maximum_fusion.8), calls=%async_computation.3 | async-start | bytes 2097152 | tf_op jit(solution)/shard_map/all_to_all | solution.py:1221
  366.2 17.2 %collective-permute-start.3 = (f32[2,1024]{1,0:T(2,128)}, f32[2,1024]{1,0:T(2,128)}, u32[]{:S(2)}, u32[]{:S(2)}) collective-permute-start(f32[2,1024]{1,0:T(2,128)} %pad_add_fusion.2), channel_id=1, source_target_pairs={{1,0},{2,1},{3,2},{4,3},{5,4},{6,5},{7,6},{8,7},{9,8},{10,9},{11,1... | collective-permute-start | bytes 24584 | tf_op jit(solution)/shard_map/ppermute | solution.py:19
  370.2 75.1 %collective-permute-start.17 = (bf16[256,4608]{1,0:T(8,128)(2,1)}, bf16[256,4608]{1,0:T(8,128)(2,1)}, u32[]{:S(2)}, u32[]{:S(2)}) collective-permute-start(bf16[256,4608]{1,0:T(8,128)(2,1)} %pad_maximum_fusion.3), channel_id=1, source_target_pairs={{0,1},{1,0},{2,3},{3,2},{4,5},{5,4},{6,7},{7,6},{8,9},{9,8},{10,11... | collective-permute-start | bytes 7077896 | tf_op jit(solution)/shard_map/ppermute | solution.py:1082
  373.6 67.0 %collective-permute-start.15 = (bf16[256,1024]{1,0:T(8,128)(2,1)}, bf16[256,1024]{1,0:T(8,128)(2,1)}, u32[]{:S(2)}, u32[]{:S(2)}) collective-permute-start(bf16[256,1024]{1,0:T(8,128)(2,1)} %pad_maximum_fusion.13), channel_id=1, source_target_pairs={{0,1},{1,0},{2,3},{3,2},{4,5},{5,4},{6,7},{7,6},{8,9},{9,8},{10,11... | collective-permute-start | bytes 1572872 | tf_op jit(solution)/shard_map/ppermute | solution.py:1082
  373.6 63.4 %collective-permute-start.18 = (bf16[256,512]{1,0:T(8,128)(2,1)}, bf16[256,512]{1,0:T(8,128)(2,1)}, u32[]{:S(2)}, u32[]{:S(2)}) collective-permute-start(bf16[256,512]{1,0:T(8,128)(2,1)} %get-tuple-element.178), channel_id=1, source_target_pairs={{0,1},{1,0},{2,3},{3,2},{4,5},{5,4},{6,7},{7,6},{8,9},{9,8},{10,11... | collective-permute-start | bytes 786440 | tf_op jit(solution)/shard_map/ppermute | solution.py:1082
  374.1 64.7 %collective-permute-start.16 = (bf16[256,512]{1,0:T(8,128)(2,1)}, bf16[256,512]{1,0:T(8,128)(2,1)}, u32[]{:S(2)}, u32[]{:S(2)}) collective-permute-start(bf16[256,512]{1,0:T(8,128)(2,1)} %get-tuple-element.180), channel_id=1, source_target_pairs={{0,1},{1,0},{2,3},{3,2},{4,5},{5,4},{6,7},{7,6},{8,9},{9,8},{10,11... | collective-permute-start | bytes 786440 | tf_op jit(solution)/shard_map/ppermute | solution.py:1082
  388.1 54.7 %collective-permute-start.19 = (bf16[256,1536]{1,0:T(8,128)(2,1)}, bf16[256,1536]{1,0:T(8,128)(2,1)}, u32[]{:S(2)}, u32[]{:S(2)}) collective-permute-start(bf16[256,1536]{1,0:T(8,128)(2,1)} %get-tuple-element.156), channel_id=1, source_target_pairs={{0,1},{1,0},{2,3},{3,2},{4,5},{5,4},{6,7},{7,6},{8,9},{9,8},{10,11... | collective-permute-start | bytes 2359304 | tf_op jit(solution)/shard_map/ppermute | solution.py:1082
  393.5 43.5 %copy-start.43 = (bf16[256,512]{1,0:T(8,128)(2,1)S(1)}, bf16[256,512]{1,0:T(8,128)(2,1)}, u32[]{:S(2)}) copy-start(bf16[256,512]{1,0:T(8,128)(2,1)} %get-tuple-element.177) | copy-start | bytes 786436
  393.5 47.0 %copy-start.45 = (bf16[256,512]{1,0:T(8,128)(2,1)S(1)}, bf16[256,512]{1,0:T(8,128)(2,1)}, u32[]{:S(2)}) copy-start(bf16[256,512]{1,0:T(8,128)(2,1)} %get-tuple-element.181) | copy-start | bytes 786436
  393.6 47.0 %copy-start.50 = (bf16[256,256]{1,0:T(8,128)(2,1)S(1)}, bf16[256,256]{1,0:T(8,128)(2,1)}, u32[]{:S(2)}) copy-start(bf16[256,256]{1,0:T(8,128)(2,1)} %get-tuple-element.193) | copy-start | bytes 393220
  788.9 16.7 %collective-permute-start.27 = (bf16[288,512]{1,0:T(8,128)(2,1)}, bf16[288,512]{1,0:T(8,128)(2,1)}, u32[]{:S(2)}, u32[]{:S(2)}) collective-permute-start(bf16[288,512]{1,0:T(8,128)(2,1)} %get-tuple-element.170), channel_id=1, source_target_pairs={{0,1},{1,0},{2,3},{3,2},{4,5},{5,4},{6,7},{7,6},{8,9},{9,8},{10,11... | collective-permute-start | bytes 884744 | tf_op jit(solution)/shard_map/ppermute | solution.py:1082
  790.2 20.0 %collective-permute-start.26 = (bf16[64,4608]{1,0:T(8,128)(2,1)}, bf16[64,4608]{1,0:T(8,128)(2,1)}, u32[]{:S(2)}, u32[]{:S(2)}) collective-permute-start(bf16[64,4608]{1,0:T(8,128)(2,1)} %copy.112), channel_id=1, source_target_pairs={{0,1},{1,0},{2,3},{3,2},{4,5},{5,4},{6,7},{7,6},{8,9},{9,8},{10,11... | collective-permute-start | bytes 1769480 | tf_op jit(solution)/shard_map/ppermute | solution.py:1082
  792.2 4.6 collective-permute-start.25
  792.2 7.5 collective-permute-start.24
  794.7 13.1 %collective-permute-start.23 = (bf16[288,512]{1,0:T(8,128)(2,1)}, bf16[288,512]{1,0:T(8,128)(2,1)}, u32[]{:S(2)}, u32[]{:S(2)}) collective-permute-start(bf16[288,512]{1,0:T(8,128)(2,1)} %get-tuple-element.174), channel_id=1, source_target_pairs={{0,1},{1,0},{2,3},{3,2},{4,5},{5,4},{6,7},{7,6},{8,9},{9,8},{10,11... | collective-permute-start | bytes 884744 | tf_op jit(solution)/shard_map/ppermute | solution.py:1082
  796.8 2.2 collective-permute-start.21
  799.0 22.3 %collective-permute-start.22 = (bf16[64,4608]{1,0:T(8,128)(2,1)S(1)}, bf16[64,4608]{1,0:T(8,128)(2,1)}, u32[]{:S(2)}, u32[]{:S(2)}) collective-permute-start(bf16[64,4608]{1,0:T(8,128)(2,1)S(1)} %copy-done.48), channel_id=1, source_target_pairs={{0,1},{1,0},{2,3},{3,2},{4,5},{5,4},{6,7},{7,6},{8,9},{9,8},{10,11... | collective-permute-start | bytes 1769480 | tf_op jit(solution)/shard_map/ppermute | solution.py:1082
  799.8 4.2 collective-permute-start.20
  (60 other events, 201.7 us)

commit v2 on v1

--- a/solution.py
+++ b/solution.py
@@ -551,11 +551,12 @@
 
 
 def project_kernel(head, hid_ref, gain_ref, wq_ref, wk_ref, wv_ref, cos_ref, sin_ref, qg_ref, kg_ref,
-                   msg_ref, normed_ref, qraw_ref, kraw_ref):
+                   msg_ref, normt_ref, qraw_ref, kraw_ref):
     hid = hid_ref[...]
     scale = lax.rsqrt(jnp.mean(hid * hid, axis=-1, keepdims=True) + EPS)
-    normed = (hid * scale * gain_ref[...]).astype(BF)
-    normed_ref[...] = normed
+    normed = hid * scale * gain_ref[...]
+    normt_ref[...] = turned(normed)
+    normed = normed.astype(BF)
     blocks = same_head(head)
     cosine, sine = cos_ref[...], sin_ref[...]
     half_rows = msg_ref.shape[1]
@@ -586,7 +587,7 @@
 
 def project_back_kernel(head, back_ref, hid_ref, gain_ref, wq_ref, wk_ref, wv_ref, cos_ref, sin_ref, qg_ref,
                         kg_ref, qraw_ref, kraw_ref, grad_ref,
-                        raw_ref, two_ref, again_ref, qgain_ref, kgain_ref):
+                        rawq_ref, rawk_ref, rawv_ref, two_ref, again_ref, qgain_ref, kgain_ref):
     blocks = same_head(head)
     cosine, sine = cos_ref[...], sin_ref[...]
     half_rows = back_ref.shape[1]
@@ -610,7 +611,7 @@
     for tile in range(width_q // LANES):
         got, part = through(fetch(tile, 0), qraw_ref[:, tile * LANES:(tile + 1) * LANES], qg_ref[...])
         gain_total = gain_total + part
-        raw_ref[:, tile * LANES:(tile + 1) * LANES] = got.astype(BF)
+        rawq_ref[:, tile * LANES:(tile + 1) * LANES] = got.astype(BF)
     qgain_ref[...] = gain_total
     gain_total = jnp.zeros((1, LANES), F32)
     for tile in range(width_k // LANES):
@@ -619,14 +620,11 @@
         values = jnp.where(lane < head, swap_heads(even, head), odd)
         got, part = through(keys, kraw_ref[:, tile * LANES:(tile + 1) * LANES], kg_ref[...])
         gain_total = gain_total + part
-        raw_ref[:, width_q + tile * LANES:width_q + (tile + 1) * LANES] = got.astype(BF)
-        raw_ref[:, width_q + width_k + tile * LANES:width_q + width_k + (tile + 1) * LANES] = values.astype(BF)
+        rawk_ref[:, tile * LANES:(tile + 1) * LANES] = got.astype(BF)
+        rawv_ref[:, tile * LANES:(tile + 1) * LANES] = values.astype(BF)
     kgain_ref[...] = gain_total
-    normed_grad = lax.dot_general(raw_ref[:, :width_q], wq_ref[...], ONES_NT, preferred_element_type=F32)
-    normed_grad += lax.dot_general(raw_ref[:, width_q:width_q + width_k], wk_ref[...], ONES_NT,
-                                   preferred_element_type=F32)
-    normed_grad += lax.dot_general(raw_ref[:, width_q + width_k:], wv_ref[...], ONES_NT,
-                                   preferred_element_type=F32)
+    normed_grad = nt_dot(rawq_ref[...], wq_ref[...]) + nt_dot(rawk_ref[...], wk_ref[...])
+    normed_grad += nt_dot(rawv_ref[...], wv_ref[...])
     hid = hid_ref[...]
     scale = lax.rsqrt(jnp.mean(hid * hid, axis=-1, keepdims=True) + EPS)
     unit = hid * scale
@@ -774,39 +772,253 @@
     dkv_ref[...] = jnp.where(whole < head, dk_ref[...] * (1.0 / math.sqrt(head)), dv_ref[...]).astype(BF)
 
 
-SUB = 64
+MESH = pl.DeviceIdType.MESH
+
+
+def turned(value):
+    return value.astype(F32).T.astype(BF)
+
+
+def norm_scale(hidden):
+    return lax.rsqrt(jnp.mean(hidden * hidden, axis=-1, keepdims=True) + EPS)
+
+
+def norm_pull(normed_grad, hidden, gain):
+    scale = norm_scale(hidden)
+    unit = hidden * scale
+    inward = normed_grad * gain
+    back = scale * (inward - unit * jnp.mean(inward * unit, axis=-1, keepdims=True))
+    return back, jnp.sum(normed_grad * unit, axis=0, keepdims=True)
+
+
+def nt_dot(left, right):
+    return lax.dot_general(left, right, ONES_NT, preferred_element_type=F32)
+
+
+def nn_dot(left, right):
+    return jnp.dot(left, right, preferred_element_type=F32)
+
+
+def activation_pull(gate_act, lift_act, sigma, inner_grad):
+    gate_grad = inner_grad * lift_act * sigma * (1 + gate_act * (1 - sigma))
+    return gate_grad.astype(BF), (inner_grad * gate_act * sigma).astype(BF)
+
+
+def low_kernel(hid_ref, gain_ref, gate_ref, lift_ref, drop_ref,
+               out_ref, normt_ref, gact_ref, lact_ref, innert_ref, norm_ref):
+    step = pl.program_id(0)
+
+    @pl.when(step == 0)
+    def _():
+        hid = hid_ref[...]
+        normed = hid * norm_scale(hid) * gain_ref[...]
+        norm_ref[...] = normed.astype(BF)
+        normt_ref[...] = turned(normed)
+        out_ref[...] = hid
+
+    normed = norm_ref[...]
+    gate_act = nn_dot(normed, gate_ref[...])
+    lift_act = nn_dot(normed, lift_ref[...])
+    inner = gate_act * jax.nn.sigmoid(gate_act) * lift_act
+    gact_ref[...] = gate_act.astype(BF)
+    lact_ref[...] = lift_act.astype(BF)
+    innert_ref[...] = turned(inner)
+    out_ref[...] += nn_dot(inner.astype(BF), drop_ref[...])
+
+
+def low_back_kernel(grad_ref, hid_ref, gain_ref, gact_ref, lact_ref, gate_ref, lift_ref, drop_ref,
+                    out_ref, again_ref, low_ref, outlow_ref, glow_ref, llow_ref, acc_ref):
+    step = pl.program_id(0)
+
+    @pl.when(step == 0)
+    def _():
+        low_ref[...] = grad_ref[...].astype(BF)
+        acc_ref[...] = jnp.zeros_like(acc_ref)
+
+    gate_act, lift_act = gact_ref[...].astype(F32), lact_ref[...].astype(F32)
+    inner_grad = nt_dot(low_ref[...], drop_ref[...])
+    gate_low, lift_low = activation_pull(gate_act, lift_act, jax.nn.sigmoid(gate_act), inner_grad)
+    glow_ref[...] = gate_low
+    llow_ref[...] = lift_low
+    acc_ref[...] += nt_dot(gate_low, gate_ref[...]) + nt_dot(lift_low, lift_ref[...])
+
+    @pl.when(step == pl.num_programs(0) - 1)
+    def _():
+        back, gain_part = norm_pull(acc_ref[...], hid_ref[...], gain_ref[...])
+        again_ref[...] = gain_part
+        out = grad_ref[...] + back
+        out_ref[...] = out
+        outlow_ref[...] = out.astype(BF)
+
+
+def top_kernel(got_ref, two_ref, exit_ref, cot_ref, gain_ref, gate_ref, lift_ref, drop_ref,
+               out_ref, grad_ref, gradlow_ref, send_ref, attt_ref, again_ref, normt_ref, innert_ref, glow_ref,
+               llow_ref, hid_ref, norm_ref, acc_ref):
+    step = pl.program_id(0)
+    half_rows = got_ref.shape[1]
+
+    @pl.when(step == 0)
+    def _():
+        tiles = []
+        for tile in range(got_ref.shape[0] // 2):
+            tiles.append(jnp.concatenate([got_ref[2 * tile], got_ref[2 * tile + 1]], axis=0))
+        attended = jnp.concatenate(tiles, axis=1)
+        attt_ref[...] = turned(attended)
+        hid = two_ref[...] + nn_dot(attended, exit_ref[...])
+        hid_ref[...] = hid
+        normed = hid * norm_scale(hid) * gain_ref[...]
+        norm_ref[...] = normed.astype(BF)
+        normt_ref[...] = turned(normed)
+        out_ref[...] = hid
+        acc_ref[...] = jnp.zeros_like(acc_ref)
+
+    normed = norm_ref[...]
+    gate_act = nn_dot(normed, gate_ref[...])
+    lift_act = nn_dot(normed, lift_ref[...])
+    sigma = jax.nn.sigmoid(gate_act)
+    inner = gate_act * sigma * lift_act
+    innert_ref[...] = turned(inner)
+    out_ref[...] += nn_dot(inner.astype(BF), drop_ref[...])
+    inner_grad = nt_dot(cot_ref[...], drop_ref[...])
+    gate_low, lift_low = activation_pull(gate_act, lift_act, sigma, inner_grad)
+    glow_ref[...] = gate_low
+    llow_ref[...] = lift_low
+    acc_ref[...] += nt_dot(gate_low, gate_ref[...]) + nt_dot(lift_low, lift_ref[...])
+
+    @pl.when(step == pl.num_programs(0) - 1)
+    def _():
+        back, gain_part = norm_pull(acc_ref[...], hid_ref[...], gain_ref[...])
+        again_ref[...] = gain_part
+        grad = cot_ref[...].astype(F32) + back
+        grad_ref[...] = grad
+        low = grad.astype(BF)
+        gradlow_ref[...] = low
+        sent = nt_dot(low, exit_ref[...]).astype(BF)
+        for tile in range(send_ref.shape[0] // 2):
+            for part in range(2):
+                send_ref[2 * tile + part] = sent[part * half_rows:(part + 1) * half_rows,
+                                                 tile * LANES:(tile + 1) * LANES]
+
+
+TILE = 512
+
+
+def whole_block(shape):
+    return pl.BlockSpec(shape, lambda step, rank=len(shape): (0,) * rank)
+
+
+def column_block(rows):
+    return pl.BlockSpec((rows, TILE), lambda step: (0, step))
+
+
+def row_block(columns):
+    return pl.BlockSpec((TILE, columns), lambda step: (step, 0))
+
+
+def call_tiled(kernel, tiles, ins, outs, scratch, flops, moved, name):
+    return pl.pallas_call(
+        kernel,
+        grid=(tiles,),
+        in_specs=[spec for _, spec in ins],
+        out_specs=tuple(spec for _, spec in outs),
+        out_shape=tuple(shape for shape, _ in outs),
+        scratch_shapes=scratch,
+        compiler_params=pltpu.CompilerParams(vmem_limit_bytes=VMEM_LIMIT, dimension_semantics=("arbitrary",)),
+        cost_estimate=pl.CostEstimate(flops=flops, bytes_accessed=moved, transcendentals=0),
+        name=name,
+    )(*[value for value, _ in ins])
+
+
+def feed_low(hidden, gain, gate, lift, drop):
+    rows, width = hidden.shape
+    ff = gate.shape[1]
+    S = jax.ShapeDtypeStruct
+    return call_tiled(
+        low_kernel, ff // TILE,
+        [(hidden, whole_block((rows, width))), (gain, whole_block((1, width))), (gate, column_block(width)),
+         (lift, column_block(width)), (drop, row_block(width))],
+        [(S((rows, width), F32), whole_block((rows, width))), (S((width, rows), BF), whole_block((width, rows))),
+         (S((rows, ff), BF), column_block(rows)), (S((rows, ff), BF), column_block(rows)),
+         (S((ff, rows), BF), row_block(rows))],
+        [pltpu.VMEM((rows, width), BF)], 6 * rows * width * ff, 38 << 20, "feed_low")
+
+
+def feed_low_back(grad, hidden, gain, gact, lact, gate, lift, drop):
+    rows, width = hidden.shape
+    ff = gate.shape[1]
+    S = jax.ShapeDtypeStruct
+    full = whole_block((rows, width))
+    return call_tiled(
+        low_back_kernel, ff // TILE,
+        [(grad, full), (hidden, full), (gain, whole_block((1, width))), (gact, column_block(rows)),
+         (lact, column_block(rows)), (gate, column_block(width)), (lift, column_block(width)),
+         (drop, row_block(width))],
+        [(S((rows, width), F32), full), (S((1, width), F32), whole_block((1, width))), (S((rows, width), BF), full),
+         (S((rows, width), BF), full), (S((rows, ff), BF), column_block(rows)), (S((rows, ff), BF), column_block(rows))],
+        [pltpu.VMEM((rows, width), F32)], 6 * rows * width * ff, 40 << 20, "feed_low_back")
+
+
+def feed_top(got, two, exit_weight, cotangent, gain, gate, lift, drop):
+    rows, width = two.shape
+    ff = gate.shape[1]
+    S = jax.ShapeDtypeStruct
+    full = whole_block((rows, width))
+    flat = whole_block((1, width))
+    standing = whole_block((width, rows))
+    return call_tiled(
+        top_kernel, ff // TILE,
+        [(got, whole_block(got.shape)), (two, full), (exit_weight, whole_block(exit_weight.shape)), (cotangent, full),
+         (gain, flat), (gate, column_block(width)), (lift, column_block(width)), (drop, row_block(width))],
+        [(S((rows, width), F32), full), (S((rows, width), F32), full), (S((rows, width), BF), full),
+         (S(got.shape, BF), whole_block(got.shape)), (S((width, rows), BF), standing), (S((1, width), F32), flat),
+         (S((width, rows), BF), standing), (S((ff, rows), BF), row_block(rows)), (S((rows, ff), BF), column_block(rows)),
+         (S((rows, ff), BF), column_block(rows))],
+        [pltpu.VMEM((rows, width), F32), pltpu.VMEM((rows, width), BF), pltpu.VMEM((rows, width), F32)],
+        12 * rows * width * ff, 45 << 20, "feed_top")
+
+
+PIECE = 32
+SUB = 2 * PIECE
 STRIP = 256
 RING = 8
 LAG = 2
 
 
-def sum_kernel(jobs, lines, *refs):
+def sum_kernel(jobs, sides, lines, *refs):
     count = len(jobs)
-    lefts, rights, out_ref = refs[:count], refs[count:2 * count], refs[2 * count]
-    (lbuf, rbuf, xp, xr, yp, yr, zp, us, ur, ds_, dr, fs, fr, stage,
-     lsem, rsem, xs, xv, ys, yv, uss, urv, dss, drv, fss, frv, osem) = refs[2 * count + 1:]
-    steps = sum(job[2] for job in jobs)
+    refs = list(refs)
+    take = lambda number: [refs.pop(0) for _ in range(number)]
+    lefts, rights, (small_ref,) = take(sides), take(count), take(1)
+    outs, (small_out,), lefts_b, rights_b = take(count), take(1), take(sides), take(count)
+    (lbuf, rbuf, xp, xr, yp, yr, zp, us, ur, ds_, dr, fs, fr, cs, cr, stage, sm_s, sm_r,
+     lsem, rsem, xs, xv, ys, yv, uss, urv, dss, drv, fss, frv, css, crv, osem, sms, smv, els, elv, ers, erv) = refs
+    steps = sum(job[3] for job in jobs)
     last = steps - 1 + LAG
     half = STRIP // 2
-    quarter = SUB // 2
-    tall = SUB + quarter
+    tall = SUB + PIECE
+    tokens = lbuf.shape[-1] // 2
     me = lax.axis_index("ctx")
     y = lax.axis_index("dp")
     z = me // 4
     x = (me // 2) % 2
     c = me % 2
+    top = lines - 1
+    twin = {"ctx": me + 1 - 2 * c}
     across_x = {"ctx": me + 2 - 4 * x}
     across_y = {"dp": 1 - y}
-    above = {"ctx": jnp.minimum(me + 4, 4 * lines - 4 + me % 4)}
+    above = {"ctx": jnp.minimum(me + 4, 4 * top + me % 4)}
     below = {"ctx": jnp.maximum(me - 4, me % 4)}
-    top = lines - 1
+    near = {"ctx": me + 4 - 8 * (z % 2)}
+    far = {"ctx": me + 8 - 16 * (z // 2)}
+    rounds = [twin, across_x, across_y, near, far]
 
     for buf in (xp, ur, dr, zp):
         buf[...] = jnp.zeros_like(buf)
+    sm_s[0] = small_ref[...]
 
     barrier = pltpu.get_barrier_semaphore()
-    pl.semaphore_signal(barrier, inc=1, device_id=across_x, device_id_type=MESH)
-    pl.semaphore_signal(barrier, inc=1, device_id=across_y, device_id_type=MESH)
+    for where in (twin, across_x, across_y, far):
+        pl.semaphore_signal(barrier, inc=1, device_id=where, device_id_type=MESH)
 
     @pl.when(z < top)
     def _():
@@ -816,12 +1028,27 @@
     def _():
         pl.semaphore_signal(barrier, inc=1, device_id=below, device_id_type=MESH)
 
-    pl.semaphore_wait(barrier, 2 + (z < top).astype(jnp.int32) + (z > 0).astype(jnp.int32))
+    pl.semaphore_wait(barrier, 4 + (z < top).astype(jnp.int32) + (z > 0).astype(jnp.int32))
 
     def remote(src, dst, send, recv, where):
         return pltpu.make_async_remote_copy(src_ref=src, dst_ref=dst, send_sem=send, recv_sem=recv,
                                             device_id=where, device_id_type=MESH)
 
+    def left_copy(number):
+        return remote(lefts[number], lefts_b[number], els.at[number], elv.at[number], twin)
+
+    def right_copy(number):
+        width = rights_b[number].shape[1]
+        start = pl.multiple_of((1 - c) * width, width)
+        return remote(rights[number].at[:, pl.ds(start, width)], rights_b[number], ers.at[number], erv.at[number], twin)
+
+    seen = []
+    for number, job in enumerate(jobs):
+        if job[0] not in seen:
+            seen.append(job[0])
+            left_copy(job[0]).start()
+        right_copy(number).start()
+
     def x_copy(j):
         s = j % RING
         return remote(xp.at[s, 1 - x], xr.at[s], xs.at[s], xv.at[s], across_x)
@@ -842,49 +1069,107 @@
         s = j % RING
         return remote(fs.at[s], fr.at[s], fss.at[s], frv.at[s], across_y)
 
-    def l_wait(j):
-        s = j % 2
-        pltpu.make_async_copy(lefts[0].at[:, pl.ds(0, SUB), :], lbuf.at[s], lsem.at[s]).wait()
-        pltpu.make_async_copy(rights[0].at[:, pl.ds(0, STRIP)], rbuf.at[s], rsem.at[s]).wait()
+    def c_copy(j):
+        s = j % RING
+        return remote(cs.at[s], cr.at[s], css.at[s], crv.at[s], twin)
+
+    def small_copy(k):
+        return remote(sm_s.at[k], sm_r.at[k], sms.at[k], smv.at[k], rounds[k])
+
+    def loads(number, row, column, s):
+        left = jobs[number][0]
+        width = rights_b[number].shape[1]
+        mine = pl.multiple_of(c * width + column, STRIP)
+        rows = pl.ds(row, PIECE)
+        return [
+            pltpu.make_async_copy(lefts[left].at[:, :, rows, :], lbuf.at[s, :, :, :, pl.ds(0, tokens)], lsem.at[s, 0]),
+            pltpu.make_async_copy(lefts_b[left].at[:, :, rows, :], lbuf.at[s, :, :, :, pl.ds(tokens, tokens)],
+                                  lsem.at[s, 1]),
+            pltpu.make_async_copy(rights[number].at[:, pl.ds(mine, STRIP)], rbuf.at[s, pl.ds(0, tokens)], rsem.at[s, 0]),
+            pltpu.make_async_copy(rights_b[number].at[:, pl.ds(column, STRIP)], rbuf.at[s, pl.ds(tokens, tokens)],
+                                  rsem.at[s, 1]),
+        ]
 
     def load(j):
-        s = j % 2
         begin = 0
-        for number, (subs, strips, total) in enumerate(jobs):
+        done = []
+        for number, (left, subs, strips, total) in enumerate(jobs):
+            fresh = left not in done
+            done.append(left)
+
+            @pl.when(j == begin)
+            def _(number=number, left=left, fresh=fresh):
+                if fresh:
+                    left_copy(left).wait()
+                right_copy(number).wait()
+
             @pl.when((j >= begin) & (j < begin + total))
             def _(number=number, subs=subs, begin=begin):
                 k = j - begin
-                row = pl.multiple_of((k % subs) * SUB, SUB)
+                row = pl.multiple_of((k % subs) * PIECE, PIECE)
                 column = pl.multiple_of((k // subs) * STRIP, STRIP)
-                pltpu.make_async_copy(lefts[number].at[:, pl.ds(row, SUB), :], lbuf.at[s], lsem.at[s]).start()
-                pltpu.make_async_copy(rights[number].at[:, pl.ds(column, STRIP)], rbuf.at[s], rsem.at[s]).start()
+                for copy in loads(number, row, column, j % 2):
+                    copy.start()
             begin += total
 
-    def out_copy(j):
-        s = j % 2
-        return pltpu.make_async_copy(stage.at[s], out_ref.at[j], osem.at[s])
+    def out_copies(number, j, row, column):
+        width = rights_b[number].shape[1]
+        o = j % RING
+        rows = pl.ds(row, PIECE)
+        mine = pl.multiple_of(c * width + column, STRIP)
+        other = pl.multiple_of((1 - c) * width + column, STRIP)
+        return [
+            pltpu.make_async_copy(stage.at[o, 0], outs[number].at[rows, pl.ds(mine, STRIP)], osem.at[o, 0]),
+            pltpu.make_async_copy(stage.at[o, 1], outs[number].at[rows, pl.ds(other, STRIP)], osem.at[o, 1]),
+        ]
+
+    def store(j):
+        begin = 0
+        for number, (left, subs, strips, total) in enumerate(jobs):
+            @pl.when((j >= begin) & (j < begin + total))
+            def _(number=number, subs=subs, begin=begin):
+                k = j - begin
+                row = pl.multiple_of((k % subs) * PIECE, PIECE)
+                column = pl.multiple_of((k // subs) * STRIP, STRIP)
+                for copy in out_copies(number, j, row, column):
+                    copy.start()
+            begin += total
 
     load(0)
 
     def step(t, _):
         slot = t % RING
 
+        for k in range(len(rounds) + 1):
+            @pl.when(t == LAG * k)
+            def _(k=k):
+                if k > 0:
+                    small_copy(k - 1).wait()
+                    total = sm_s[k - 1] + sm_r[k - 1]
+                    if k == len(rounds):
+                        small_out[...] = total
+                    else:
+                        sm_s[k] = total
+                if k < len(rounds):
+                    small_copy(k).start()
+
         @pl.when(t < steps)
         def _():
-            l_wait(t)
+            for copy in loads(0, 0, 0, t % 2):
+                copy.wait()
 
             @pl.when(t + 1 < steps)
             def _():
                 load(t + 1)
 
-            left = lbuf[t % 2].reshape(2 * lines * SUB, lbuf.shape[-1])
+            left = lbuf[t % 2].reshape(2 * lines * SUB, 2 * tokens)
             got = jnp.dot(left, rbuf[t % 2], preferred_element_type=F32).astype(BF)
             for line in range(lines):
                 for side in range(2):
                     row = (2 * line + side) * SUB
                     xp[slot, side, line, :SUB] = got[row:row + SUB, :half]
                     for part in range(2):
-                        yp[slot, part, side, line] = got[row + part * quarter:row + (part + 1) * quarter, half:]
+                        yp[slot, part, side, line] = got[row + part * PIECE:row + (part + 1) * PIECE, half:]
 
         @pl.when((t >= LAG) & (t <= last))
         def _():
@@ -969,21 +1254,42 @@
         def _():
             f_copy(jo).wait()
             s = jo % RING
-            o = jo % 2
-
-            @pl.when(jo >= 2)
+            fs[s, :SUB] = fs[s, :SUB] + fr[s, :SUB]
+            mine = pl.ds(pl.multiple_of(c * PIECE, PIECE), PIECE)
+            away = pl.ds(pl.multiple_of((1 - c) * PIECE, PIECE), PIECE)
+            cs[s, :, :half] = fs[s, away]
+            own, far_rows = fs[s, SUB:].astype(F32), fr[s, SUB:].astype(F32)
+            cs[s, :, half:] = jnp.where(y == c, far_rows, own).astype(BF)
+            c_copy(jo).start()
+            stage[jo % RING, 0, :, :half] = fs[s, mine].astype(F32)
+
+            @pl.when(jo >= LAG)
             def _():
-                out_copy(jo).wait()
-
-            stage[o, :SUB] = fs[s, :SUB] + fr[s, :SUB]
-            mine, other = fs[s, SUB:].astype(F32), fr[s, SUB:].astype(F32)
-            stage[o, SUB:tall] = jnp.where(y == 0, mine, other).astype(BF)
-            stage[o, tall:] = jnp.where(y == 0, other, mine).astype(BF)
-            out_copy(jo).start()
-
-    lax.fori_loop(0, last + LAG * (top + 2) + 1, step, None)
-    for j in (last - 1, last):
-        out_copy(j).wait()
+                stage[(jo - LAG) % RING, 0, :, half:] = jnp.where(y == c, own, far_rows)
+
+        jc = jo - LAG
+
+        @pl.when((jc >= 0) & (jc <= last))
+        def _():
+            c_copy(jc).wait()
+            s = jc % RING
+            stage[jc % RING, 1, :, :half] = cr[s, :, :half].astype(F32)
+
+            @pl.when(jc >= LAG)
+            def _():
+                chunk = jc - LAG
+                stage[chunk % RING, 1, :, half:] = cr[s, :, half:].astype(F32)
+                store(chunk)
+
+            @pl.when(jc >= 2 * LAG)
+            def _():
+                for copy in out_copies(0, jc - 2 * LAG, 0, 0):
+                    copy.wait()
+
+    lax.fori_loop(0, last + LAG * (top + 3) + 1, step, None)
+    for back in range(LAG):
+        for copy in out_copies(0, steps - 1 - back, 0, 0):
+            copy.wait()
     for back in range(RING):
         j = last - back
 
@@ -996,28 +1302,30 @@
             down_copy(j).wait_send()
 
 
-def sum_over_chips(pairs, lines, collective_id):
-    jobs = []
-    lefts, rights = [], []
-    for left, right in pairs:
-        rows = left.shape[0] // (2 * lines)
-        subs, strips = rows // SUB, right.shape[1] // STRIP
-        jobs.append((subs, strips, subs * strips))
-        lefts.append(left.reshape(2 * lines, rows, left.shape[1]))
-        rights.append(right)
-    steps = sum(job[2] for job in jobs)
-    tokens = pairs[0][0].shape[1]
-    half, quarter = STRIP // 2, SUB // 2
-    tall = SUB + quarter
+def sum_over_chips(lefts, works, small, lines, collective_id):
+    shaped, jobs, landing_l, landing_r, outs = [], [], [], [], []
+    for left in lefts:
+        rows, tokens = left.shape
+        shaped.append(left.reshape(2 * lines, 2, rows // (4 * lines), tokens))
+        landing_l.append(jax.ShapeDtypeStruct(shaped[-1].shape, BF))
+    for number, right in works:
+        rows = shaped[number].shape[2]
+        subs, strips = rows // PIECE, right.shape[1] // 2 // STRIP
+        jobs.append((number, subs, strips, subs * strips))
+        landing_r.append(jax.ShapeDtypeStruct((tokens, right.shape[1] // 2), BF))
+        outs.append(jax.ShapeDtypeStruct((rows, right.shape[1]), F32))
+    steps = sum(job[3] for job in jobs)
+    half = STRIP // 2
+    tall = SUB + PIECE
     top = lines - 1
     dma = pltpu.SemaphoreType.DMA
     scratch = [
-        pltpu.VMEM((2, 2 * lines, SUB, tokens), BF),
-        pltpu.VMEM((2, tokens, STRIP), BF),
+        pltpu.VMEM((2, 2 * lines, 2, PIECE, 2 * tokens), BF),
+        pltpu.VMEM((2, 2 * tokens, STRIP), BF),
         pltpu.VMEM((RING, 2, lines, tall, half), BF),
         pltpu.VMEM((RING, lines, tall, half), BF),
-        pltpu.VMEM((RING, 2, 2, lines, quarter, half), BF),
-        pltpu.VMEM((RING, 2, lines, quarter, half), BF),
+        pltpu.VMEM((RING, 2, 2, lines, PIECE, half), BF),
+        pltpu.VMEM((RING, 2, lines, PIECE, half), BF),
         pltpu.VMEM((2 * RING, lines, tall, half), BF),
         pltpu.VMEM((RING, top, tall, half), BF),
         pltpu.VMEM((RING, top, tall, half), BF),
@@ -1025,37 +1333,31 @@
         pltpu.VMEM((RING, top, tall, half), BF),
         pltpu.VMEM((RING, tall, half), BF),
         pltpu.VMEM((RING, tall, half), BF),
-        pltpu.VMEM((2, 2 * SUB, half), BF),
-        dma((2,)), dma((2,)),
-        dma((RING,)), dma((RING,)), dma((RING,)), dma((RING,)),
-        dma((RING,)), dma((RING,)), dma((RING,)), dma((RING,)),
-        dma((RING,)), dma((RING,)),
-        dma((2,)),
+        pltpu.VMEM((RING, PIECE, STRIP), BF),
+        pltpu.VMEM((RING, PIECE, STRIP), BF),
+        pltpu.VMEM((RING, 2, PIECE, STRIP), F32),
+        pltpu.VMEM((5,) + small.shape, F32),
+        pltpu.VMEM((5,) + small.shape, F32),
+        dma((2, 2)), dma((2, 2)),
+    ] + [dma((RING,))] * 12 + [
+        dma((RING, 2)), dma((5,)), dma((5,)),
+        dma((len(lefts),)), dma((len(lefts),)), dma((len(works),)), dma((len(works),)),
     ]
-    flops = 2 * steps * 2 * lines * SUB * STRIP * tokens
-    out = pl.pallas_call(
-        functools.partial(sum_kernel, jobs, lines),
-        out_shape=jax.ShapeDtypeStruct((steps + LAG, 2 * SUB, half), BF),
-        in_specs=[pl.BlockSpec(memory_space=pl.ANY)] * (2 * len(pairs)),
-        out_specs=pl.BlockSpec(memory_space=pl.ANY),
+    anywhere = pl.BlockSpec(memory_space=pl.ANY)
+    inside = pl.BlockSpec(memory_space=pltpu.VMEM)
+    flops = 2 * steps * 2 * lines * SUB * STRIP * 2 * tokens
+    got = pl.pallas_call(
+        functools.partial(sum_kernel, jobs, len(lefts), lines),
+        out_shape=tuple(outs) + (jax.ShapeDtypeStruct(small.shape, F32),) + tuple(landing_l) + tuple(landing_r),
+        in_specs=[anywhere] * (len(lefts) + len(works)) + [inside],
+        out_specs=tuple([anywhere] * len(works) + [inside] + [anywhere] * (len(lefts) + len(works))),
         scratch_shapes=scratch,
         compiler_params=pltpu.CompilerParams(collective_id=collective_id, has_side_effects=True,
                                              vmem_limit_bytes=VMEM_LIMIT),
         cost_estimate=pl.CostEstimate(flops=flops, bytes_accessed=steps * 800_000, transcendentals=0),
         name="sum_over_chips",
-    )(*lefts, *rights)
-    results = []
-    begin = 0
-    for (subs, strips, total) in jobs:
-        one = out[begin:begin + total, :SUB].reshape(strips, subs * SUB, half)
-        two = out[begin + LAG:begin + total + LAG, SUB:].reshape(strips, subs * SUB, half)
-        both = jnp.concatenate([one, two], axis=2)
-        results.append(both.transpose(1, 0, 2).reshape(subs * SUB, strips * STRIP))
-        begin += total
-    return results
-
-
-MESH = pl.DeviceIdType.MESH
+    )(*shaped, *[right for _, right in works], small)
+    return got[:len(works)], got[len(works)]
 
 
 def call_plain(kernel, outs, args, smem=0, scratch=(), flops=0, moved=0, name=None):
@@ -1082,54 +1384,12 @@
     return lax.ppermute(value, "ctx", [(i, i ^ 1) for i in range(count)])
 
 
-def halves(value, core):
-    width = value.shape[1] // 2
-    mine = lax.dynamic_slice_in_dim(value, core * width, width, 1)
-    send = lax.dynamic_slice_in_dim(value, (1 - core) * width, width, 1)
-    return mine, send
-
-
-def left_side(value):
-    return jnp.concatenate([value, sibling(value)], axis=0).T
-
-
-def right_side(values, core):
-    mine, send = zip(*[halves(value, core) for value in values])
-    mine, send = (jnp.concatenate(part, axis=1) for part in (mine, send))
-    return jnp.concatenate([mine, sibling(send)], axis=0)
-
-
-def silu_parts(gate_act, lift_act, inner_grad):
-    sigma = jax.nn.sigmoid(gate_act)
-    gate_grad = inner_grad * lift_act * sigma * (1 + gate_act * (1 - sigma))
-    return gate_grad.astype(BF), (inner_grad * gate_act * sigma).astype(BF)
-
-
 def norm_back(grad, hidden, gain):
     scale = lax.rsqrt(jnp.mean(hidden * hidden, axis=-1, keepdims=True) + EPS)
     unit = hidden * scale
     inward = grad * gain
     gain_grad = jnp.sum(grad * unit, axis=0)
     return scale * (inward - unit * jnp.mean(inward * unit, axis=-1, keepdims=True)), gain_grad
-
-
-def feed_fwd(hidden, gain, gate_weight, lift_weight, drop_weight):
-    fnormed = root_mean_square_scale(hidden, gain).astype(BF)
-    gate_act = jnp.dot(fnormed, gate_weight, preferred_element_type=F32)
-    lift_act = jnp.dot(fnormed, lift_weight, preferred_element_type=F32)
-    inner = (jax.nn.silu(gate_act) * lift_act).astype(BF)
-    result = hidden + jnp.dot(inner, drop_weight, preferred_element_type=F32)
-    return result, (fnormed, gate_act.astype(BF), lift_act.astype(BF), inner)
-
-
-def feed_bwd(grad, hidden, gain, kept, gate_weight, lift_weight, drop_weight):
-    fnormed, gate_act, lift_act, inner = kept
-    grad_low = grad.astype(BF)
-    inner_grad = outer_dot(grad_low, drop_weight)
-    gate_low, lift_low = silu_parts(gate_act.astype(F32), lift_act.astype(F32), inner_grad)
-    normed_grad = outer_dot(gate_low, gate_weight) + outer_dot(lift_low, lift_weight)
-    hidden_grad, gain_grad = norm_back(normed_grad, hidden, gain)
-    return grad + hidden_grad, gain_grad, grad_low, gate_low, lift_low
 
 
 def fast_device(tokens, lengths, cotangent, mixgain, mixentry, mixtaps, mixexit, lowgain, lowgate, lowlift,
@@ -1172,12 +1432,13 @@
     conved = conv_local(extended, taps_f, fits_one, fits_two)
     gated = (part_c * conved).astype(BF)
     hidden_one = hidden + jnp.dot(gated, mixexit, preferred_element_type=F32)
-    hidden_two, kept_low = feed_fwd(hidden_one, lowgain_f, lowgate, lowlift, lowdrop)
+    hidden_two, lownorm_t, gact_low, lact_low, lowinner_t = feed_low(
+        hidden_one, lowgain_f[None, :], lowgate, lowlift, lowdrop)
 
     heads_q, heads_k = attquery.shape[1] // head, attkeys.shape[1] // head
-    msg, normed_two, query_raw, key_raw = call_plain(
+    msg, normed_two_t, query_raw, key_raw = call_plain(
         functools.partial(project_kernel, head),
-        (shape_of((devices, half_rows, 2 * LANES), BF), shape_of((rows, width), BF),
+        (shape_of((devices, half_rows, 2 * LANES), BF), shape_of((width, rows), BF),
          shape_of((rows, attquery.shape[1]), F32), shape_of((rows, attkeys.shape[1]), F32)),
         (hidden_two, attgain_f[None, :], attquery, attkeys, attvalues, cosine, sine, querygain_2, keysgain_2),
         flops=2 * rows * width * 2 * width, moved=6 << 20, name="project")
@@ -1196,16 +1457,8 @@
         scratch=[pltpu.VMEM((group, LANES), BF), pltpu.VMEM((wide, LANES), F32)],
         flops=4 * area * LANES, moved=5 << 20, name="attend")
     got = lax.all_to_all(attended_f.astype(BF), "ctx", 0, 0)
-    attended_low = got.reshape(devices // 2, rows, LANES).transpose(1, 0, 2).reshape(rows, width)
-    hidden_three = hidden_two + jnp.dot(attended_low, attexit, preferred_element_type=F32)
-    output, kept_top = feed_fwd(hidden_three, topgain_f, topgate, toplift, topdrop)
-
-    grad = cotangent.astype(F32)
-    grad, topgain_grad, gb_top, gate_top, lift_top = feed_bwd(
-        grad, hidden_three, topgain_f, kept_top, topgate, toplift, topdrop)
-    grad_low3 = grad.astype(BF)
-    dattn = outer_dot(grad_low3, attexit).astype(BF)
-    send = dattn.reshape(2, half_rows, devices // 2, LANES).transpose(2, 0, 1, 3).reshape(devices, half_rows, LANES)
+    (output, grad, grad_low3, send, attended_t, topgain_grad, topnorm_t, topinner_t, gate_top, lift_top) = feed_top(
+        got, hidden_two, attexit, cotangent, topgain_f[None, :], topgate, toplift, topdrop)
     held_grad = lax.all_to_all(send, "ctx", 0, 0)
     dq, dkv = call_plain(
         functools.partial(attend_back_kernel, head, rows, keys, sources),
@@ -1219,18 +1472,18 @@
     send_kv = lax.dynamic_index_in_dim(dkv, 1 - core, 1, keepdims=False)
     dkv_sum = (mine_kv.astype(F32) + sibling(send_kv).astype(F32)).astype(BF)
     back = lax.all_to_all(jnp.concatenate([dq, dkv_sum], axis=2), "ctx", 0, 0)
-    raw_low, grad_two, attgain_grad, querygain_grad, keysgain_grad = call_plain(
+    rawq_low, rawk_low, rawv_low, grad_two, attgain_grad, querygain_grad, keysgain_grad = call_plain(
         functools.partial(project_back_kernel, head),
-        (shape_of((rows, 2 * width), BF), shape_of((rows, width), F32), shape_of((1, width), F32),
+        (shape_of((rows, attquery.shape[1]), BF), shape_of((rows, attkeys.shape[1]), BF),
+         shape_of((rows, attkeys.shape[1]), BF), shape_of((rows, width), F32), shape_of((1, width), F32),
          shape_of((1, LANES), F32), shape_of((1, LANES), F32)),
         (back, hidden_two, attgain_f[None, :], attquery, attkeys, attvalues, cosine, sine, querygain_2, keysgain_2,
          query_raw, key_raw, grad),
         flops=2 * rows * width * 2 * width, moved=8 << 20, name="project_back")
     fold = lambda value: value.reshape(LANES // head, head).sum(axis=0)
     querygain_grad, keysgain_grad = fold(querygain_grad), fold(keysgain_grad)
-    grad, lowgain_grad, gb_low, gate_low, lift_low = feed_bwd(
-        grad_two, hidden_one, lowgain_f, kept_low, lowgate, lowlift, lowdrop)
-    grad_low1 = grad.astype(BF)
+    grad, lowgain_grad, gb_low, grad_low1, gate_low, lift_low = feed_low_back(
+        grad_two, hidden_one, lowgain_f[None, :], gact_low, lact_low, lowgate, lowlift, lowdrop)
     gated_grad = outer_dot(grad_low1, mixexit)
     part_c_grad = gated_grad * conved
     conved_grad = gated_grad * part_c
@@ -1243,45 +1496,18 @@
     hidden_grad, mixgain_grad = norm_back(outer_dot(mixed_grad, mixentry), hidden, mixgain_f)
     tokens_grad = grad + hidden_grad
 
-    kq, kk = attquery.shape[1], attkeys.shape[1]
-    pairs = [
-        (left_side(kept_top[3]), right_side([gb_top], core)),
-        (left_side(kept_top[0]), right_side([gate_top, lift_top], core)),
-        (left_side(attended_low), right_side([grad_low3], core)),
-        (left_side(normed_two), right_side([raw_low[:, :kq], raw_low[:, kq:kq + kk], raw_low[:, kq + kk:]], core)),
-        (left_side(kept_low[3]), right_side([gb_low], core)),
-        (left_side(kept_low[0]), right_side([gate_low, lift_low], core)),
-        (left_side(gated), right_side([grad_low1], core)),
-        (left_side(normed_one), right_side([mixed_grad], core)),
-    ]
-    sums = sum_over_chips(pairs, lines, 1)
-
-    def finish(value, cuts):
-        size = value.shape[0] // 2
-        own = lax.dynamic_slice_in_dim(value, core * size, size, 0)
-        away = sibling(lax.dynamic_slice_in_dim(value, (1 - core) * size, size, 0))
-        results, start = [], 0
-        for cut in cuts:
-            a, b = own[:, start:start + cut], away[:, start:start + cut]
-            results.append(jnp.where(core == 0, jnp.concatenate([a, b], axis=1),
-                                     jnp.concatenate([b, a], axis=1)).astype(F32))
-            start += cut
-        return results
-
-    ff = lowgate.shape[1]
-    (topdrop_grad,) = finish(sums[0], [width // 2])
-    topgate_grad, toplift_grad = finish(sums[1], [ff // 2, ff // 2])
-    (attexit_grad,) = finish(sums[2], [width // 2])
-    attquery_grad, attkeys_grad, attvalues_grad = finish(sums[3], [kq // 2, kk // 2, kk // 2])
-    (lowdrop_grad,) = finish(sums[4], [width // 2])
-    lowgate_grad, lowlift_grad = finish(sums[5], [ff // 2, ff // 2])
-    (mixexit_grad,) = finish(sums[6], [width // 2])
-    (mixentry_grad,) = finish(sums[7], [mixentry.shape[1] // 2])
-    smalls = lax.psum((mixgain_grad, mixtaps_grad, lowgain_grad, attgain_grad[0], querygain_grad, keysgain_grad,
-                       topgain_grad), ("dp", "ctx"))
-    return (output, tokens_grad, smalls[0], mixentry_grad, smalls[1], mixexit_grad, smalls[2], lowgate_grad,
-            lowlift_grad, lowdrop_grad, smalls[3], attquery_grad, attkeys_grad, attvalues_grad, smalls[4],
-            smalls[5], attexit_grad, smalls[6], topgate_grad, toplift_grad, topdrop_grad)
+    lefts = [attended_t, normed_two_t, topinner_t, topnorm_t, lowinner_t, lownorm_t, gated.T, normed_one.T]
+    works = [(0, grad_low3), (1, rawq_low), (1, rawk_low), (1, rawv_low), (2, cotangent), (3, gate_top),
+             (3, lift_top), (4, gb_low), (5, gate_low), (5, lift_low), (6, grad_low1), (7, mixed_grad)]
+    heads = jnp.concatenate([querygain_grad, keysgain_grad, jnp.zeros((width - 2 * head,), F32)])
+    small = jnp.concatenate([mixgain_grad[None, :], mixtaps_grad, lowgain_grad, attgain_grad, topgain_grad,
+                             heads[None, :]], axis=0)
+    grads, small = sum_over_chips(lefts, works, small, lines, 1)
+    (attexit_grad, attquery_grad, attkeys_grad, attvalues_grad, topdrop_grad, topgate_grad, toplift_grad,
+     lowdrop_grad, lowgate_grad, lowlift_grad, mixexit_grad, mixentry_grad) = grads
+    return (output, tokens_grad, small[0], mixentry_grad, small[1:4], mixexit_grad, small[4], lowgate_grad,
+            lowlift_grad, lowdrop_grad, small[5], attquery_grad, attkeys_grad, attvalues_grad, small[7, :head],
+            small[7, head:2 * head], attexit_grad, small[6], topgate_grad, toplift_grad, topdrop_grad)
 
 
 def solution(mesh):

time: 849 us -> 663 us (0.78); the launches traced: 832 us -> 662 us
  matrix products: 110 us -> 13 us
  other arithmetic: 111 us -> 30 us
  Pallas kernels: 404 us -> 482 us
  local copies, waits for them, and re-layouts: 97.4 us -> 32.4 us
  waiting for transfers between devices: 1.57 us -> 52.1 us
  blocking collectives: 74.4 us -> 32 us
  starting transfers between devices: 30.1 us -> 18.3 us
    pallas_call x1 -> x4, Pallas kernels: 313 us -> 388 us  [the longest x1 322 us: sum_over_chips(): pl.pallas_call(functools.partial(sum_kernel, jobs, len(lefts), lines), ou...]
    dot_general x9 -> x2, matrix products: 59.1 us -> 6.47 us  [outer_dot(): lax.dot_general(left, right, (((1,), (1,)), ((), ())), preferred_element_...]
    dot_general x7 -> x0, matrix products: 45.4 us -> none  [the longest x2 17.7 us: feed_fwd(): lift_act = jnp.dot(fnormed, lift_weight, preferred_element_type=F32)]
    psum x1 -> x0, blocking collectives: 42.1 us -> none  [fast_device(): lax.psum((mixgain_grad, mixtaps_grad, lowgain_grad, attgain_grad[0], quer...]
    concatenate x15 -> x1, other arithmetic: 36.8 us -> 0.08 us  [fast_device(): jnp.concatenate([querygain_grad, keysgain_grad, jnp.zeros((width - 2 * he...]
    convert_element_type x18 -> x0, other arithmetic: 22.7 us -> none  [the longest x12 16.4 us: finish(): results.append(jnp.where(core == 0, jnp.concatenate([a, b], axis=1), jnp....]
    dynamic_slice x22 -> x0, local copies, waits for them, and re-layouts: 21.5 us -> none  [the longest x12 13.8 us: halves(): mine = lax.dynamic_slice_in_dim(value, core * width, width, 1)]
    all_to_all x1, waiting for transfers between devices: 0.01 us -> 20.7 us  [fast_device(): back = lax.all_to_all(jnp.concatenate([dq, dkv_sum], axis=2), 'ctx', 0, 0)]
  transfers between devices with their start and end apart: 31 -> 7, of which waited for: 2 -> 6; matrix products, arithmetic and copies ran while one was open for 24% -> 2% of each run, Pallas kernels for 9% -> 0%
where the time goes in v2:
time: 663 us; the launch traced here: 662 us
  Pallas kernels  482 us (73%)
  waiting for transfers between devices  52.1 us (8%)
  local copies, waits for them, and re-layouts  32.4 us (5%)
  blocking collectives  32 us (5%)
  other arithmetic  30 us (5%)
  starting transfers between devices  18.3 us (3%)
  matrix products  13 us (2%)
    pallas_call x1, Pallas kernels, sum_over_chips(): pl.pallas_call(functools.partial(sum_kernel, jobs, len(lefts), lines), ou...  322 us
    pallas_call x4, Pallas kernels, call_plain(): pl.pallas_call(kernel, out_shape=tuple(outs) if many else outs, in_specs=...  93.3 us
    pallas_call x3, Pallas kernels, call_tiled(): pl.pallas_call(kernel, grid=(tiles,), in_specs=[spec for _, spec in ins],...  66.2 us
    all_to_all x1, blocking collectives, fast_device(): held = lax.all_to_all(msg, 'ctx', 0, 0)  32 us
    all_to_all x1, waiting for transfers between devices, fast_device(): back = lax.all_to_all(jnp.concatenate([dq, dkv_sum], axis=2), 'ctx', 0, 0)  20.7 us
    unnamed x90, local copies, waits for them, and re-layouts  16.4 us
    all_to_all x1, waiting for transfers between devices, fast_device(): held_grad = lax.all_to_all(send, 'ctx', 0, 0)  14.5 us
    all_to_all x1, waiting for transfers between devices, fast_device(): got = lax.all_to_all(attended_f.astype(BF), 'ctx', 0, 0)  13.9 us
  transfers between devices with their start and end apart: 7, of which 6 were waited for; matrix products, arithmetic and copies ran while one was open for 2% of the time, Pallas kernels for 0%

profile of v2, /device:TPU:0, one launch (start us, length us, event | category | flops | bytes accessed | tf_op | source)
XLA Modules:
  0.0 661.7 jit_solution(6404403966388443353)
XLA Ops:
  0.7 1.4 fusion.10
  2.7 4.8 fusion.13
  7.6 1.6 copy-done.5
  10.2 2.4 collective-permute-start
  15.2 1.2 fusion.15
  19.5 1.2 maximum_convert_fusion
  20.7 2.7 multiply_convert_fusion.3
  23.4 1.7 convert_add_fusion.hid_ref
  25.1 17.9 %feed_low.1 = (f32[256,1024]{1,0:T(8,128)}, bf16[1024,256]{1,0:T(8,128)(2,1)}, bf16[256,4608]{1,0:T(8,128)(2,1)}, bf16[256,4608]{1,0:T(8,128)(2,1)}, bf16[4608,256]{1,0:T(8,128)(2,1)}) custom-call(f32[256,1024]{1,0:T(8,128)} %convert_add_fusion.hid_ref, f32[1,1024]{1,0:T(1,128)} %bitcast.68, bf16[1024,4608]{1,0:T(8,128)(2,1)} %gate_ref.5, ...), custom_call_target="tpu_custom_call" | custom-call | flops 7247757312 | bytes 39845888 | tf_op jit(solution)/shard_map/feed_low/pallas_call | solution.py:919
  43.0 6.4 project.1
  49.4 32.0 %all_to_all.20.q_ref = bf16[16,128,256]{2,1,0:T(8,128)(2,1)S(1)} all-to-all(bf16[16,128,256]{2,1,0:T(8,128)(2,1)} %get-tuple-element.83), channel_id=1, replica_groups=mesh['dp'=2,'ctx'=16] {'ctx'}, dimensions={0} | all-to-all | bytes 2097152 | tf_op jit(solution)/shard_map/all_to_all | solution.py:1445
  82.4 1.2 slice_bitcast_fusion.2
  84.4 1.2 pad_add_fusion.3.info_ref
  86.3 1.7 maximum_select_fusion
  88.0 1.0 copy.46
  89.0 28.8 %attend.1 = (f32[16,128,128]{2,1,0:T(8,128)}, bf16[16,2,128,128]{3,2,1,0:T(8,128)(2,1)}) custom-call(s32[4]{0:T(128)} %pad_add_fusion.3.info_ref, bf16[16,128,256]{2,1,0:T(8,128)(2,1)} %copy-done.12, bf16[4096,128]{1,0:T(8,128)(2,1)} %bitcast.54), custom_call_target="tpu_custom_call" | custom-call | flops 4294967296 | bytes 5242880 | tf_op jit(solution)/shard_map/attend/pallas_call | solution.py:1366
  117.9 2.1 convert_element_type.147
  120.0 4.7 all-to-all-start.1
  125.3 13.9 %all-to-all-done.1.got_ref = bf16[16,128,128]{2,1,0:T(8,128)(2,1)} async-done(((bf16[16,128,128]{2,1,0:T(8,128)(2,1)}), bf16[16,128,128]{2,1,0:T(8,128)(2,1)}, u32[]{:S(2)}, u32[]{:S(2)}) %all-to-all-start.1) | async-done | bytes 524320 | tf_op jit(solution)/shard_map/all_to_all | solution.py:1459
  139.2 27.7 %feed_top.1 = (f32[256,1024]{1,0:T(8,128)}, f32[256,1024]{1,0:T(8,128)}, bf16[256,1024]{1,0:T(8,128)(2,1)}, bf16[16,128,128]{2,1,0:T(8,128)(2,1)}, bf16[1024,256...) custom-call(bf16[16,128,128]{2,1,0:T(8,128)(2,1)} %all-to-all-done.1, ...), custom_call_target="tpu_custom_call" | custom-call | flops 14495514624 | bytes 47185920 | tf_op jit(solution)/shard_map/feed_top/pallas_call | solution.py:919
  166.9 4.3 all-to-all-start.2
  171.2 14.5 %all-to-all-done.2.grad_ref = bf16[16,128,128]{2,1,0:T(8,128)(2,1)} async-done(((bf16[16,128,128]{2,1,0:T(8,128)(2,1)}), bf16[16,128,128]{2,1,0:T(8,128)(2,1)}, u32[]{:S(2)}, u32[]{:S(2)}) %all-to-all-start.2) | async-done | bytes 524320 | tf_op jit(solution)/shard_map/all_to_all | solution.py:1462
  185.6 49.0 %attend_back.1 = (bf16[16,128,128]{2,1,0:T(8,128)(2,1)}, bf16[4096,128]{1,0:T(8,128)(2,1)}) custom-call(s32[4]{0:T(128)} %pad_add_fusion.3.info_ref, bf16[16,2,128,128]{3,2,1,0:T(8,128)(2,1)} %get-tuple-element.86.aug_ref, f32[16,128,128]{2,1,0:T(8,128)} %get-tuple-element.84.out_ref, bf16[16,128,128]{2,1,0:T(8,128)(2,1)} %all-to-all-done.2.grad_ref, ...), custom_call_target="tpu_custom_call" | custom-call | flops 10737418240 | bytes 8388608 | tf_op jit(solution)/shard_map/attend_back/pallas_call | solution.py:1366
  234.6 1.9 dynamic-slice_bitcast_fusion
  236.5 2.2 collective-permute-done.2
  238.7 1.3 fusion.11
  240.1 2.1 pad_maximum_fusion.1
  242.2 4.6 all-to-all-start.3
  246.8 2.1 copy.48
  248.9 20.7 %all-to-all-done.3.back_ref = bf16[16,128,256]{2,1,0:T(8,128)(2,1)} async-done(((bf16[16,128,256]{2,1,0:T(8,128)(2,1)}), bf16[16,128,256]{2,1,0:T(8,128)(2,1)}, u32[]{:S(2)}, u32[]{:S(2)}) %all-to-all-start.3) | async-done | bytes 1048608 | tf_op jit(solution)/shard_map/all_to_all | solution.py:1474
  269.5 9.0 %project_back.1 = (bf16[256,1024]{1,0:T(8,128)(2,1)}, bf16[256,512]{1,0:T(8,128)(2,1)}, bf16[256,512]{1,0:T(8,128)(2,1)}, f32[256,1024]{1,0:T(8,128)}, f32[1,102...) custom-call(bf16[16,128,256]{2,1,0:T(8,128)(2,1)} %all-to-all-done.3.back_ref, ...), custom_call_target="tpu_custom_call" | custom-call | flops 1073741824 | bytes 8388608 | tf_op jit(solution)/shard_map/project_back/pallas_call | solution.py:1366
  278.6 20.6 %feed_low_back.1 = (f32[256,1024]{1,0:T(8,128)}, f32[1,1024]{1,0:T(1,128)}, bf16[256,1024]{1,0:T(8,128)(2,1)}, bf16[256,1024]{1,0:T(8,128)(2,1)}, bf16[256,4608]{1,0:T(8,128)(2,1)}, /*index=5*/bf16[256,4608]{1,0:T(8,128)(2,1)}) custom-call(f32[256,1024]{1,0:T(8,128)} %get-tuple-element.93.grad_ref, f32[256,1024]{1,0:T(8,128)} %convert_add_fusion.hid_ref, ...), custom_call_target="tpu_custom_call" | custom-call | flops 7247757312 | bytes 41943040 | tf_op jit(solution)/shard_map/feed_low_back/pallas_call | solution.py:919
  299.2 1.9 fusion.30
  301.1 2.5 multiply_reduce_fusion.2
  304.0 1.6 pad_add_fusion
  307.7 1.7 collective-permute-start.3
  309.5 1.3 slice.126
  311.0 1.7 copy-done.6
  313.7 4.6 fusion.26
  318.4 1.3 pad_maximum_fusion.refs_19_
  321.9 322.1 %sum_over_chips.1 = (f32[64,1024]{1,0:T(8,128)}, f32[64,1024]{1,0:T(8,128)}, f32[64,512]{1,0:T(8,128)}, f32[64,512]{1,0:T(8,128)}, f32[288,1024]{1,0:T(8,128)}, ...) custom-call(bf16[8,2,64,256]{3,2,1,0:T(8,128)(2,1)} %bitcast.84, ...), custom_call_target="tpu_custom_call" | custom-call | flops 18253611008 | bytes 108800000 | tf_op jit(solution)/shard_map/sum_over_chips/pallas_call | solution.py:1349
  644.1 1.3 slice_bitcast_fusion
  645.4 1.4 slice.109
  646.8 1.6 fusion.27
  648.4 2.9 fusion.8
  652.9 1.0 copy.66
  653.9 1.0 copy.67
  654.9 1.0 copy.68
  (124 shorter events, 22.3 us)
Async XLA Ops:
  0.7 22.8 %copy-start = (bf16[1024,1024]{1,0:T(8,128)(2,1)S(1)}, bf16[1024,1024]{1,0:T(8,128)(2,1)}, u32[]{:S(2)}) copy-start(bf16[1024,1024]{1,0:T(8,128)(2,1)} %param.30) | copy-start | bytes 6291460
  7.6 1.6 copy-start.5
  9.2 3.4 copy-start.34
  9.2 4.0 copy-start.27
  9.2 7.8 %copy-start.35 = (bf16[64]{0:T(256)(128)(2,1)S(1)}, bf16[64]{0:T(256)(128)(2,1)}, u32[]{:S(2)}) copy-start(bf16[64]{0:T(256)(128)(2,1)} %param.39) | copy-start | bytes 388
  9.2 8.4 %copy-start.36 = (bf16[64]{0:T(256)(128)(2,1)S(1)}, bf16[64]{0:T(256)(128)(2,1)}, u32[]{:S(2)}) copy-start(bf16[64]{0:T(256)(128)(2,1)} %param.40) | copy-start | bytes 388
  9.2 9.1 %copy-start.31 = (bf16[1024]{0:T(1024)(128)(2,1)S(1)}, bf16[1024]{0:T(1024)(128)(2,1)}, u32[]{:S(2)}) copy-start(bf16[1024]{0:T(1024)(128)(2,1)} %param.31) | copy-start | bytes 6148
  9.2 9.6 %copy-start.32 = (bf16[1024]{0:T(1024)(128)(2,1)S(1)}, bf16[1024]{0:T(1024)(128)(2,1)}, u32[]{:S(2)}) copy-start(bf16[1024]{0:T(1024)(128)(2,1)} %param.35) | copy-start | bytes 6148
  9.4 0.8 copy-start.13
  10.2 9.3 %collective-permute-start = (bf16[2,1024]{1,0:T(2,128)(2,1)S(1)}, bf16[2,1024]{1,0:T(2,128)(2,1)S(1)}, u32[]{:S(2)}, u32[]{:S(2)}) collective-permute-start(bf16[2,1024]{1,0:T(2,128)(2,1)S(1)} %slice.119), channel_id=1, source_target_pairs={{0,1},{1,2},{2,3},{3,4},{4,5},{5,6},{6,7},{7,8},{8,9},{9,10},{10,1... | collective-permute-start | bytes 12296 | tf_op jit(solution)/shard_map/ppermute | solution.py:19
  20.7 2.7 copy-start.7
  23.4 1.7 copy-start.9
  81.5 1.0 copy-start.12
  83.6 2.6 collective-permute-start.1
  117.9 6.8 %copy-start.33 = (bf16[1024]{0:T(1024)(128)(2,1)S(1)}, bf16[1024]{0:T(1024)(128)(2,1)}, u32[]{:S(2)}) copy-start(bf16[1024]{0:T(1024)(128)(2,1)} %param.42) | copy-start | bytes 6148
  120.0 19.2 %all-to-all-start.1 = ((bf16[16,128,128]{2,1,0:T(8,128)(2,1)}), bf16[16,128,128]{2,1,0:T(8,128)(2,1)}, u32[]{:S(2)}, u32[]{:S(2)}) async-start(bf16[16,128,128]{2,1,0:T(8,128)(2,1)} %convert_element_type.147), calls=%async_computation.1 | async-start | bytes 1048576 | tf_op jit(solution)/shard_map/all_to_all | solution.py:1459
  166.9 18.7 %all-to-all-start.2 = ((bf16[16,128,128]{2,1,0:T(8,128)(2,1)}), bf16[16,128,128]{2,1,0:T(8,128)(2,1)}, u32[]{:S(2)}, u32[]{:S(2)}) async-start(bf16[16,128,128]{2,1,0:T(8,128)(2,1)} %get-tuple-element.87), calls=%async_computation.2 | async-start | bytes 1048576 | tf_op jit(solution)/shard_map/all_to_all | solution.py:1462
  236.5 2.3 collective-permute-start.2
  242.2 27.3 %all-to-all-start.3 = ((bf16[16,128,256]{2,1,0:T(8,128)(2,1)}), bf16[16,128,256]{2,1,0:T(8,128)(2,1)}, u32[]{:S(2)}, u32[]{:S(2)}) async-start(bf16[16,128,256]{2,1,0:T(8,128)(2,1)} %pad_maximum_fusion.1), calls=%async_computation.3 | async-start | bytes 2097152 | tf_op jit(solution)/shard_map/all_to_all | solution.py:1474
  299.2 1.9 copy-start.10
  303.9 1.7 copy-start.1
  303.9 1.7 copy-start.3
  303.9 2.2 copy-start.38
  304.0 2.8 copy-start.37
  307.6 3.3 copy-start.2
  307.6 3.3 copy-start.4
  307.7 3.3 collective-permute-start.3
  310.8 1.9 copy-start.6
  312.7 1.0 copy-start.14
  318.3 1.9 copy-start.11
  318.3 1.4 copy-start.8
  319.8 1.5 copy-start.28
  319.8 1.5 copy-start.29
  319.8 1.5 copy-start.30
  644.1 7.2 %copy-start.21 = (f32[64,3072]{1,0:T(8,128)S(1)}, f32[64,3072]{1,0:T(8,128)}, u32[]{:S(2)}) copy-start(f32[64,3072]{1,0:T(8,128)} %get-tuple-element.189) | copy-start | bytes 2359300
  648.3 3.8 copy-start.24
  648.3 4.5 copy-start.20
  651.3 2.6 copy-start.19
  652.9 2.0 copy-start.18
  653.9 2.0 copy-start.23
  653.9 2.8 copy-start.26
  654.9 2.4 copy-start.25
  654.9 3.0 copy-start.22
  654.9 3.8 copy-start.17
  655.9 3.7 copy-start.16
  658.7 2.0 copy-start.15

commit v3 on v2

--- a/solution.py
+++ b/solution.py
@@ -585,17 +585,15 @@
         put(2 * tile + 1, LANES, jnp.where(lane < head, swap_heads(keys, head), values))
 
 
-def project_back_kernel(head, back_ref, hid_ref, gain_ref, wq_ref, wk_ref, wv_ref, cos_ref, sin_ref, qg_ref,
+def project_back_kernel(head, backq_ref, backk_ref, hid_ref, gain_ref, wq_ref, wk_ref, wv_ref, cos_ref, sin_ref, qg_ref,
                         kg_ref, qraw_ref, kraw_ref, grad_ref,
                         rawq_ref, rawk_ref, rawv_ref, two_ref, again_ref, qgain_ref, kgain_ref):
     blocks = same_head(head)
     cosine, sine = cos_ref[...], sin_ref[...]
-    half_rows = back_ref.shape[1]
     lane = lane_of(cosine.shape)
 
-    def fetch(dest, start):
-        return jnp.concatenate(
-            [back_ref[2 * dest + part, :, start:start + LANES] for part in range(2)], axis=0).astype(F32)
+    def fetch(source, dest):
+        return jnp.concatenate([source[2 * dest], source[2 * dest + 1]], axis=0).astype(F32)
 
     def through(grad, raw, gain):
         scale = lax.rsqrt(head_mean(raw * raw, blocks) + EPS)
@@ -609,13 +607,13 @@
     width_k = wk_ref.shape[1]
     gain_total = jnp.zeros((1, LANES), F32)
     for tile in range(width_q // LANES):
-        got, part = through(fetch(tile, 0), qraw_ref[:, tile * LANES:(tile + 1) * LANES], qg_ref[...])
+        got, part = through(fetch(backq_ref, tile), qraw_ref[:, tile * LANES:(tile + 1) * LANES], qg_ref[...])
         gain_total = gain_total + part
         rawq_ref[:, tile * LANES:(tile + 1) * LANES] = got.astype(BF)
     qgain_ref[...] = gain_total
     gain_total = jnp.zeros((1, LANES), F32)
     for tile in range(width_k // LANES):
-        even, odd = fetch(2 * tile, LANES), fetch(2 * tile + 1, LANES)
+        even, odd = fetch(backk_ref, 2 * tile), fetch(backk_ref, 2 * tile + 1)
         keys = jnp.where(lane < head, even, swap_heads(odd, head))
         values = jnp.where(lane < head, swap_heads(even, head), odd)
         got, part = through(keys, kraw_ref[:, tile * LANES:(tile + 1) * LANES], kg_ref[...])
@@ -641,137 +639,6 @@
     return (key >= begin) & (key <= token)
 
 
-def need_mask(first, second, part, base, start, rows, half_rows, keys, sources):
-    lowest = base * rows + part * half_rows
-    highest = (base + sources - 1) * rows + (part + 1) * half_rows - 1
-    begin = jnp.where(highest >= second, second, jnp.where(highest >= first, first, 0))
-    return (start + keys - 1 > lowest) | (start < begin)
-
-
-def attend_kernel(head, rows, keys, sources, info_ref, q_ref, kv_ref, out_ref, aug_ref, ones_ref, acc_ref):
-    first, second, part = info_ref[0], info_ref[1], info_ref[2]
-    half_rows = q_ref.shape[1]
-    wide = sources * 2 * half_rows
-    factor = math.log2(math.e) / math.sqrt(head)
-    ones_ref[...] = jnp.where(lane_of(kv_ref.shape) < head, jnp.ones_like(kv_ref), kv_ref[...])
-    lane = lane_of((half_rows, LANES))
-
-    def block(index, _):
-        base = index * sources
-        stack = []
-        for source in range(sources):
-            tile = q_ref[base + source][:, :LANES].astype(F32)
-            stack.append(jnp.where(lane < head, tile, 0.0))
-            stack.append(jnp.where(lane < head, swap_heads(tile, head), 0.0))
-        queries = jnp.concatenate(stack, axis=0).astype(BF)
-        acc_ref[...] = jnp.zeros_like(acc_ref)
-        last = (base + sources - 1) * rows + (part + 1) * half_rows
-        count = (last + keys - 1) // keys
-
-        def visit(step, _):
-            start = pl.multiple_of(step * keys, keys)
-            raw = lax.dot_general(queries, kv_ref[pl.ds(start, keys)], ONES_NT, preferred_element_type=F32)
-            raised = jnp.exp2(raw * factor)
-            masked = need_mask(first, second, part, base, start, rows, half_rows, keys, sources)
-
-            @pl.when(masked)
-            def _():
-                ok = allowed_block(0, 1, (wide, keys), first, second, part, base, start, rows, half_rows)
-                acc_ref[...] += jnp.dot(jnp.where(ok, raised, 0.0).astype(BF), ones_ref[pl.ds(start, keys)],
-                                        preferred_element_type=F32)
-
-            @pl.when(jnp.logical_not(masked))
-            def _():
-                acc_ref[...] += jnp.dot(raised.astype(BF), ones_ref[pl.ds(start, keys)],
-                                        preferred_element_type=F32)
-
-        lax.fori_loop(0, count, visit, None)
-        for source in range(sources):
-            tile = q_ref[base + source][:, :LANES].astype(F32)
-            outs = []
-            for which in range(2):
-                place = (2 * source + which) * half_rows
-                acc = acc_ref[place:place + half_rows]
-                turned = swap_heads(acc, head)
-                outs.append(turned / acc if which == 0 else acc / turned)
-                high, middle, low = three_parts(-math.sqrt(head) * jnp.log(turned))
-                query = tile if which == 0 else swap_heads(tile, head)
-                extra = jnp.where(lane == head, high, jnp.where(lane == head + 1, middle,
-                                                                jnp.where(lane == head + 2, low, 0.0)))
-                aug_ref[base + source, which] = jnp.where(lane < head, query, extra).astype(BF)
-            out_ref[base + source] = jnp.where(lane < head, outs[0], outs[1])
-
-    lax.fori_loop(0, q_ref.shape[0] // sources, block, None)
-
-
-def attend_back_kernel(head, rows, keys, sources, info_ref, aug_ref, out_ref, grad_ref, kv_ref,
-                       dq_ref, dkv_ref, kone_ref, vone_ref, dk_ref, dv_ref, acc_ref):
-    first, second, part = info_ref[0], info_ref[1], info_ref[2]
-    half_rows = grad_ref.shape[1]
-    wide = sources * 2 * half_rows
-    factor = math.log2(math.e) / math.sqrt(head)
-    whole = lane_of(kv_ref.shape)
-    vone_ref[...] = jnp.where(whole < head, jnp.ones_like(kv_ref), kv_ref[...])
-    kone_ref[...] = jnp.where(whole < head, kv_ref[...], jnp.ones_like(kv_ref))
-    dk_ref[...] = jnp.zeros_like(dk_ref)
-    dv_ref[...] = jnp.zeros_like(dv_ref)
-    lane = lane_of((half_rows, LANES))
-
-    def block(index, _):
-        base = index * sources
-        stack_q, stack_d = [], []
-        for source in range(sources):
-            grad = grad_ref[base + source].astype(F32)
-            spread = grad * out_ref[base + source]
-            for which in range(2):
-                stack_q.append(aug_ref[base + source, which])
-                mine = (lane < head) if which == 0 else (lane >= head)
-                delta = jnp.sum(jnp.where(mine, spread, 0.0), axis=1, keepdims=True)
-                high, middle, low = three_parts(-delta)
-                extra = jnp.where(lane == 0, high, jnp.where(lane == 1, middle, jnp.where(lane == 2, low, 0.0)))
-                moved = swap_heads(grad, head) if which == 0 else grad
-                stack_d.append(jnp.where(lane < head, extra, moved).astype(BF))
-        queries = jnp.concatenate(stack_q, axis=0)
-        grads = jnp.concatenate(stack_d, axis=0)
-        acc_ref[...] = jnp.zeros_like(acc_ref)
-        last = (base + sources - 1) * rows + (part + 1) * half_rows
-        count = (last + keys - 1) // keys
-
-        def visit(step, _):
-            start = pl.multiple_of(step * keys, keys)
-            here = pl.ds(start, keys)
-
-            def finish(prob):
-                along = lax.dot_general(vone_ref[here], grads, ONES_NT, preferred_element_type=F32)
-                score = (prob * along).astype(BF)
-                dv_ref[here] += jnp.dot(prob.astype(BF), grads, preferred_element_type=F32)
-                dk_ref[here] += jnp.dot(score, queries, preferred_element_type=F32)
-                acc_ref[...] += lax.dot_general(score, kone_ref[here], ONES_TN, preferred_element_type=F32)
-
-            raw = lax.dot_general(kone_ref[here], queries, ONES_NT, preferred_element_type=F32)
-            masked = need_mask(first, second, part, base, start, rows, half_rows, keys, sources)
-
-            @pl.when(masked)
-            def _():
-                ok = allowed_block(1, 0, (keys, wide), first, second, part, base, start, rows, half_rows)
-                finish(jnp.where(ok, jnp.exp2(jnp.where(ok, raw, 0.0) * factor), 0.0))
-
-            @pl.when(jnp.logical_not(masked))
-            def _():
-                finish(jnp.exp2(raw * factor))
-
-        lax.fori_loop(0, count, visit, None)
-        for source in range(sources):
-            place = 2 * source * half_rows
-            one = acc_ref[place:place + half_rows]
-            two = acc_ref[place + half_rows:place + 2 * half_rows]
-            both = jnp.where(lane < head, one, swap_heads(two, head)) * (1.0 / math.sqrt(head))
-            dq_ref[base + source] = both.astype(BF)
-
-    lax.fori_loop(0, grad_ref.shape[0] // sources, block, None)
-    dkv_ref[...] = jnp.where(whole < head, dk_ref[...] * (1.0 / math.sqrt(head)), dv_ref[...]).astype(BF)
-
-
 MESH = pl.DeviceIdType.MESH
 
 
@@ -901,18 +768,19 @@
 
 
 TILE = 512
+WIDE_TILE = 1152
 
 
 def whole_block(shape):
     return pl.BlockSpec(shape, lambda step, rank=len(shape): (0,) * rank)
 
 
-def column_block(rows):
-    return pl.BlockSpec((rows, TILE), lambda step: (0, step))
-
-
-def row_block(columns):
-    return pl.BlockSpec((TILE, columns), lambda step: (step, 0))
+def column_block(rows, tile=TILE):
+    return pl.BlockSpec((rows, tile), lambda step: (0, step))
+
+
+def row_block(columns, tile=TILE):
+    return pl.BlockSpec((tile, columns), lambda step: (step, 0))
 
 
 def call_tiled(kernel, tiles, ins, outs, scratch, flops, moved, name):
@@ -934,12 +802,12 @@
     ff = gate.shape[1]
     S = jax.ShapeDtypeStruct
     return call_tiled(
-        low_kernel, ff // TILE,
-        [(hidden, whole_block((rows, width))), (gain, whole_block((1, width))), (gate, column_block(width)),
-         (lift, column_block(width)), (drop, row_block(width))],
+        low_kernel, ff // WIDE_TILE,
+        [(hidden, whole_block((rows, width))), (gain, whole_block((1, width))), (gate, column_block(width, WIDE_TILE)),
+         (lift, column_block(width, WIDE_TILE)), (drop, row_block(width, WIDE_TILE))],
         [(S((rows, width), F32), whole_block((rows, width))), (S((width, rows), BF), whole_block((width, rows))),
-         (S((rows, ff), BF), column_block(rows)), (S((rows, ff), BF), column_block(rows)),
-         (S((ff, rows), BF), row_block(rows))],
+         (S((rows, ff), BF), column_block(rows, WIDE_TILE)), (S((rows, ff), BF), column_block(rows, WIDE_TILE)),
+         (S((ff, rows), BF), row_block(rows, WIDE_TILE))],
         [pltpu.VMEM((rows, width), BF)], 6 * rows * width * ff, 38 << 20, "feed_low")
 
 
@@ -949,12 +817,12 @@
     S = jax.ShapeDtypeStruct
     full = whole_block((rows, width))
     return call_tiled(
-        low_back_kernel, ff // TILE,
-        [(grad, full), (hidden, full), (gain, whole_block((1, width))), (gact, column_block(rows)),
-         (lact, column_block(rows)), (gate, column_block(width)), (lift, column_block(width)),
-         (drop, row_block(width))],
+        low_back_kernel, ff // WIDE_TILE,
+        [(grad, full), (hidden, full), (gain, whole_block((1, width))), (gact, column_block(rows, WIDE_TILE)),
+         (lact, column_block(rows, WIDE_TILE)), (gate, column_block(width, WIDE_TILE)), (lift, column_block(width, WIDE_TILE)),
+         (drop, row_block(width, WIDE_TILE))],
         [(S((rows, width), F32), full), (S((1, width), F32), whole_block((1, width))), (S((rows, width), BF), full),
-         (S((rows, width), BF), full), (S((rows, ff), BF), column_block(rows)), (S((rows, ff), BF), column_block(rows))],
+         (S((rows, width), BF), full), (S((rows, ff), BF), column_block(rows, WIDE_TILE)), (S((rows, ff), BF), column_block(rows, WIDE_TILE))],
         [pltpu.VMEM((rows, width), F32)], 6 * rows * width * ff, 40 << 20, "feed_low_back")
 
 
@@ -975,6 +843,325 @@
          (S((rows, ff), BF), column_block(rows))],
         [pltpu.VMEM((rows, width), F32), pltpu.VMEM((rows, width), BF), pltpu.VMEM((rows, width), F32)],
         12 * rows * width * ff, 45 << 20, "feed_top")
+
+
+def sweep_keys(visit, index, tail, part, base, rows, half_rows, keys, sources):
+    lowest = base * rows + part * half_rows
+    end = (base + sources - 1) * rows + (part + 1) * half_rows
+    count = (end + keys - 1) // keys
+    free = jnp.where(end > tail, 0, jnp.maximum((lowest + 1) // keys - 1, 0))
+    lax.fori_loop(0, free, lambda step, _: visit(step + 1, False), None)
+    lax.fori_loop(0, count - free, lambda step, _: visit(jnp.where(step == 0, 0, free + step), True), None)
+
+
+def greet(me, count):
+    barrier = pltpu.get_barrier_semaphore()
+
+    def hello(step, _):
+        pl.semaphore_signal(barrier, inc=1, device_id={"ctx": lax.rem(me + step, count)}, device_id_type=MESH)
+
+    lax.fori_loop(1, count, hello, None)
+    pl.semaphore_wait(barrier, count - 1)
+
+
+def attend_kernel(head, rows, keys, sources, count, info_ref, msg_ref, got_ref, out_ref, aug_ref, all_ref,
+                  land, kv, tiles, arrive, ones_ref, acc_ref, msend, mrecv, fsend, frecv, gsend, grecv):
+    first, second = info_ref[0], info_ref[1]
+    me = lax.axis_index("ctx")
+    part = me % 2
+    twin = {"ctx": me + 1 - 2 * part}
+    half_rows = msg_ref.shape[1]
+    wide = sources * 2 * half_rows
+    span = sources * rows
+    factor = math.log2(math.e) / math.sqrt(head)
+    lane = lane_of((half_rows, LANES))
+    greet(me, count)
+
+    def remote(src, dst, send, recv, where):
+        return pltpu.make_async_remote_copy(src_ref=src, dst_ref=dst, send_sem=send, recv_sem=recv,
+                                            device_id=where, device_id_type=MESH)
+
+    def msg_copy(owner, dest):
+        return remote(msg_ref.at[dest], land.at[owner], msend.at[dest], mrecv.at[owner], {"ctx": dest})
+
+    def share_copy(source):
+        return remote(kv.at[source, part], kv.at[source, part], fsend.at[source], frecv.at[source], twin)
+
+    def tile_copy(owner, dest):
+        return remote(tiles.at[dest], arrive.at[owner], gsend.at[dest], grecv.at[owner], {"ctx": dest})
+
+    def start_msg(step, _):
+        msg_copy(me, lax.rem(me + step, count)).start()
+
+    lax.fori_loop(1, count, start_msg, None)
+    land[me] = msg_ref[me]
+
+    def share(source):
+        @pl.when(source != me)
+        def _():
+            msg_copy(source, me).wait_recv()
+
+        kv[source, part] = land[source, :, LANES:]
+        share_copy(source).start()
+
+    def compute(index):
+        base = index * sources
+        stack = []
+        for source in range(sources):
+            share_copy(base + source).wait_recv()
+            both = kv[base + source].reshape(rows, LANES)
+            place = pl.ds(pl.multiple_of((base + source) * rows, rows), rows)
+            all_ref[place] = both
+            ones_ref[place] = jnp.where(lane_of(both.shape) < head, jnp.ones_like(both), both)
+            tile = land[base + source, :, :LANES].astype(F32)
+            stack.append(jnp.where(lane < head, tile, 0.0))
+            stack.append(jnp.where(lane < head, swap_heads(tile, head), 0.0))
+        queries = jnp.concatenate(stack, axis=0).astype(BF)
+        acc_ref[...] = jnp.zeros_like(acc_ref)
+
+        def visit(step, masked):
+            start = pl.multiple_of(step * keys, keys)
+            here = pl.ds(start, keys)
+            raised = jnp.exp2(lax.dot_general(queries, all_ref[here], ONES_NT, preferred_element_type=F32) * factor)
+            if masked:
+                ok = allowed_block(0, 1, (wide, keys), first, second, part, base, start, rows, half_rows)
+                raised = jnp.where(ok, raised, 0.0)
+            acc_ref[...] += jnp.dot(raised.astype(BF), ones_ref[here], preferred_element_type=F32)
+
+        sweep_keys(visit, index, count * rows - rows, part, base, rows, half_rows, keys, sources)
+        for source in range(sources):
+            tile = land[base + source, :, :LANES].astype(F32)
+            outs = []
+            for which in range(2):
+                place = (2 * source + which) * half_rows
+                acc = acc_ref[place:place + half_rows]
+                turn = swap_heads(acc, head)
+                outs.append(turn / acc if which == 0 else acc / turn)
+                high, middle, low = three_parts(-math.sqrt(head) * jnp.log(turn))
+                query = tile if which == 0 else swap_heads(tile, head)
+                extra = jnp.where(lane == head, high, jnp.where(lane == head + 1, middle,
+                                                                jnp.where(lane == head + 2, low, 0.0)))
+                aug_ref[base + source, which] = jnp.where(lane < head, query, extra).astype(BF)
+            out = jnp.where(lane < head, outs[0], outs[1])
+            out_ref[base + source] = out
+            tiles[base + source] = out.astype(BF)
+
+            @pl.when(base + source != me)
+            def _(source=source):
+                tile_copy(me, base + source).start()
+
+    def block(index, _):
+        @pl.when(index < count // sources)
+        def _():
+            for source in range(sources):
+                share(index * sources + source)
+
+        @pl.when(index > 0)
+        def _():
+            compute(index - 1)
+
+    lax.fori_loop(0, count // sources + 1, block, None)
+    arrive[me] = tiles[me]
+
+    def drain(other, _):
+        share_copy(other).wait_send()
+
+        @pl.when(other != me)
+        def _():
+            msg_copy(me, other).wait_send()
+            tile_copy(me, other).wait_send()
+            tile_copy(other, me).wait_recv()
+
+    lax.fori_loop(0, count, drain, None)
+    got_ref[...] = arrive[...]
+
+
+def attend_back_kernel(head, rows, keys, sources, count, info_ref, aug_ref, out_ref, kv_ref, msg_ref,
+                       gotq_ref, gotk_ref,
+                       land, tiles, away, near, sums, arrive_q, arrive_k, kone_ref, vone_ref, kturn_ref, dk_ref,
+                       dv_ref, acc_ref, msend, mrecv, fsend, frecv, gsend, grecv, ksend, krecv):
+    first, second = info_ref[0], info_ref[1]
+    me = lax.axis_index("ctx")
+    part = me % 2
+    twin = {"ctx": me + 1 - 2 * part}
+    half_rows = msg_ref.shape[1]
+    wide = sources * 2 * half_rows
+    factor = math.log2(math.e) / math.sqrt(head)
+    shrink = 1.0 / math.sqrt(head)
+    lane = lane_of((half_rows, LANES))
+    greet(me, count)
+
+    def remote(src, dst, send, recv, where):
+        return pltpu.make_async_remote_copy(src_ref=src, dst_ref=dst, send_sem=send, recv_sem=recv,
+                                            device_id=where, device_id_type=MESH)
+
+    def msg_copy(owner, dest):
+        return remote(msg_ref.at[dest], land.at[owner], msend.at[dest], mrecv.at[owner], {"ctx": dest})
+
+    def share_copy(source):
+        return remote(away.at[source], near.at[source], fsend.at[source], frecv.at[source], twin)
+
+    def q_copy(owner, dest):
+        return remote(tiles.at[dest], arrive_q.at[owner], gsend.at[dest], grecv.at[owner], {"ctx": dest})
+
+    def k_copy(owner, dest):
+        return remote(sums.at[dest], arrive_k.at[owner], ksend.at[dest], krecv.at[owner], {"ctx": dest})
+
+    def start_msg(step, _):
+        msg_copy(me, lax.rem(me + count - step, count)).start()
+
+    lax.fori_loop(1, count, start_msg, None)
+    land[me] = msg_ref[me]
+    whole = lane_of(kv_ref.shape)
+    vone_ref[...] = jnp.where(whole < head, jnp.ones_like(kv_ref), kv_ref[...])
+    kone_ref[...] = jnp.where(whole < head, kv_ref[...], jnp.ones_like(kv_ref))
+    kturn_ref[...] = turned(kv_ref[...])
+    dk_ref[...] = jnp.zeros_like(dk_ref)
+    dv_ref[...] = jnp.zeros_like(dv_ref)
+
+    def rows_of(source, which):
+        return pl.ds(pl.multiple_of(source * rows + which * half_rows, half_rows), half_rows)
+
+    def key_tile(source, which):
+        here = rows_of(source, which)
+        return jnp.where(lane < head, dk_ref[here] * shrink, dv_ref[here])
+
+    def compute(index):
+        base = index * sources
+        stack_q, stack_d = [], []
+        for source in range(sources):
+            @pl.when(base + source != me)
+            def _(source=source):
+                msg_copy(base + source, me).wait_recv()
+
+            grad = land[base + source].astype(F32)
+            spread = grad * out_ref[base + source]
+            for which in range(2):
+                stack_q.append(aug_ref[base + source, which])
+                mine = (lane < head) if which == 0 else (lane >= head)
+                delta = jnp.sum(jnp.where(mine, spread, 0.0), axis=1, keepdims=True)
+                high, middle, low = three_parts(-delta)
+                extra = jnp.where(lane == 0, high, jnp.where(lane == 1, middle, jnp.where(lane == 2, low, 0.0)))
+                moved = swap_heads(grad, head) if which == 0 else grad
+                stack_d.append(jnp.where(lane < head, extra, moved).astype(BF))
+        queries = jnp.concatenate(stack_q, axis=0)
+        grads = jnp.concatenate(stack_d, axis=0)
+        acc_ref[...] = jnp.zeros_like(acc_ref)
+
+        def visit(step, masked):
+            start = pl.multiple_of(step * keys, keys)
+            here = pl.ds(start, keys)
+            raw = lax.dot_general(kone_ref[here], queries, ONES_NT, preferred_element_type=F32)
+            if masked:
+                ok = allowed_block(1, 0, (keys, wide), first, second, part, base, start, rows, half_rows)
+                prob = jnp.where(ok, jnp.exp2(jnp.where(ok, raw, 0.0) * factor), 0.0)
+            else:
+                prob = jnp.exp2(raw * factor)
+            along = lax.dot_general(vone_ref[here], grads, ONES_NT, preferred_element_type=F32)
+            score = (prob * along).astype(BF)
+            dv_ref[here] += jnp.dot(prob.astype(BF), grads, preferred_element_type=F32)
+            dk_ref[here] += jnp.dot(score, queries, preferred_element_type=F32)
+            acc_ref[...] += jnp.dot(kturn_ref[:, here], score, preferred_element_type=F32)
+
+        sweep_keys(visit, index, count * rows - rows, part, base, rows, half_rows, keys, sources)
+        acc = acc_ref[...].T
+        for source in range(sources):
+            place = 2 * source * half_rows
+            one = acc[place:place + half_rows]
+            two = acc[place + half_rows:place + 2 * half_rows]
+            tiles[base + source] = (jnp.where(lane < head, one, swap_heads(two, head)) * shrink).astype(BF)
+
+            @pl.when(base + source != me)
+            def _(source=source):
+                q_copy(me, base + source).start()
+
+            away[base + source] = key_tile(base + source, 1 - part).astype(BF)
+            share_copy(base + source).start()
+
+    def finish(index):
+        for source in range(sources):
+            block = index * sources + source
+            share_copy(block).wait_recv()
+            sums[block] = (key_tile(block, part) + near[block].astype(F32)).astype(BF)
+
+            @pl.when(block != me)
+            def _(block=block):
+                k_copy(me, block).start()
+
+    def sweep(step, _):
+        index = count // sources - 1 - step
+
+        @pl.when(index >= 0)
+        def _():
+            compute(jnp.maximum(index, 0))
+
+        @pl.when(step > 0)
+        def _():
+            finish(index + 1)
+
+    lax.fori_loop(0, count // sources + 1, sweep, None)
+    arrive_q[me] = tiles[me]
+    arrive_k[me] = sums[me]
+
+    def drain(other, _):
+        share_copy(other).wait_send()
+
+        @pl.when(other != me)
+        def _():
+            msg_copy(me, other).wait_send()
+            q_copy(me, other).wait_send()
+            k_copy(me, other).wait_send()
+            q_copy(other, me).wait_recv()
+            k_copy(other, me).wait_recv()
+
+    lax.fori_loop(0, count, drain, None)
+    gotq_ref[...] = arrive_q[...]
+    gotk_ref[...] = arrive_k[...]
+
+
+def exchange_attend(msg, info, head, rows, collective_id):
+    count, half_rows = msg.shape[0], msg.shape[1]
+    keys, sources = 512, 2
+    group = count * rows
+    dma = pltpu.SemaphoreType.DMA((count,))
+    S = jax.ShapeDtypeStruct
+    tile = (count, half_rows, LANES)
+    return pl.pallas_call(
+        functools.partial(attend_kernel, head, rows, keys, sources, count),
+        out_shape=(S(tile, BF), S(tile, F32), S((count, 2, half_rows, LANES), BF), S((group, LANES), BF)),
+        in_specs=[pl.BlockSpec(memory_space=pltpu.SMEM)] + vmem_specs(1),
+        out_specs=tuple(vmem_specs(4)),
+        scratch_shapes=[pltpu.VMEM((count, half_rows, 2 * LANES), BF), pltpu.VMEM((count, 2, half_rows, LANES), BF),
+                        pltpu.VMEM(tile, BF), pltpu.VMEM(tile, BF), pltpu.VMEM((group, LANES), BF),
+                        pltpu.VMEM((sources * rows, LANES), F32)] + [dma] * 6,
+        compiler_params=pltpu.CompilerParams(collective_id=collective_id, has_side_effects=True,
+                                             vmem_limit_bytes=VMEM_LIMIT),
+        cost_estimate=pl.CostEstimate(flops=2 * group * group * LANES, bytes_accessed=6 << 20, transcendentals=0),
+        name="attend",
+    )(info, msg)
+
+
+def exchange_attend_back(msg, info, augmented, attended, all_kv, head, rows, collective_id):
+    count, half_rows = msg.shape[0], msg.shape[1]
+    keys, sources = 512, 2
+    group = count * rows
+    dma = pltpu.SemaphoreType.DMA((count,))
+    S = jax.ShapeDtypeStruct
+    tile = (count, half_rows, LANES)
+    long = (group, LANES)
+    return pl.pallas_call(
+        functools.partial(attend_back_kernel, head, rows, keys, sources, count),
+        out_shape=(S(tile, BF), S(tile, BF)),
+        in_specs=[pl.BlockSpec(memory_space=pltpu.SMEM)] + vmem_specs(4),
+        out_specs=tuple(vmem_specs(2)),
+        scratch_shapes=[pltpu.VMEM(tile, BF)] * 7 + [
+            pltpu.VMEM(long, BF), pltpu.VMEM(long, BF), pltpu.VMEM((LANES, group), BF), pltpu.VMEM(long, F32),
+            pltpu.VMEM(long, F32), pltpu.VMEM((LANES, sources * rows), F32)] + [dma] * 8,
+        compiler_params=pltpu.CompilerParams(collective_id=collective_id, has_side_effects=True,
+                                             vmem_limit_bytes=VMEM_LIMIT),
+        cost_estimate=pl.CostEstimate(flops=5 * group * group * LANES, bytes_accessed=8 << 20, transcendentals=0),
+        name="attend_back",
+    )(info, augmented, attended, all_kv, msg)
 
 
 PIECE = 32
@@ -1400,7 +1587,6 @@
     devices = lax.axis_size("ctx")
     lines = devices // 4
     half_rows = rows // 2
-    group = devices * rows
     place = lax.axis_index("ctx")
     core = place % 2
     first = lengths[0, 0]
@@ -1418,7 +1604,7 @@
     angle = position[:, None] * (THETA ** (-spot.astype(F32) * 2.0 / head))[None, :]
     cosine = jnp.cos(angle)
     sine = jnp.sin(angle) * jnp.where(jnp.arange(LANES) % head < head // 2, -1.0, 1.0)[None, :]
-    info = jnp.stack([first, second, core, core]).astype(jnp.int32)
+    info = jnp.stack([first, second]).astype(jnp.int32)
 
     hidden = tokens.astype(F32)
     normed_one = root_mean_square_scale(hidden, mixgain_f).astype(BF)
@@ -1442,42 +1628,16 @@
          shape_of((rows, attquery.shape[1]), F32), shape_of((rows, attkeys.shape[1]), F32)),
         (hidden_two, attgain_f[None, :], attquery, attkeys, attvalues, cosine, sine, querygain_2, keysgain_2),
         flops=2 * rows * width * 2 * width, moved=6 << 20, name="project")
-    held = lax.all_to_all(msg, "ctx", 0, 0)
-    held_kv = held[:, :, LANES:]
-    other_kv = sibling(held_kv)
-    pair = jnp.where(core == 0, jnp.stack([held_kv, other_kv], axis=1), jnp.stack([other_kv, held_kv], axis=1))
-    all_kv = pair.reshape(group, LANES)
-    keys, sources = 512, 2
-    wide = sources * rows
-    area = group * group // 2 // 2 * 2
-    attended_f, augmented = call_plain(
-        functools.partial(attend_kernel, head, rows, keys, sources),
-        (shape_of((devices, half_rows, LANES), F32), shape_of((devices, 2, half_rows, LANES), BF)),
-        (info, held, all_kv), smem=1,
-        scratch=[pltpu.VMEM((group, LANES), BF), pltpu.VMEM((wide, LANES), F32)],
-        flops=4 * area * LANES, moved=5 << 20, name="attend")
-    got = lax.all_to_all(attended_f.astype(BF), "ctx", 0, 0)
+    got, attended_f, augmented, all_kv = exchange_attend(msg, info, head, rows, 2)
     (output, grad, grad_low3, send, attended_t, topgain_grad, topnorm_t, topinner_t, gate_top, lift_top) = feed_top(
         got, hidden_two, attexit, cotangent, topgain_f[None, :], topgate, toplift, topdrop)
-    held_grad = lax.all_to_all(send, "ctx", 0, 0)
-    dq, dkv = call_plain(
-        functools.partial(attend_back_kernel, head, rows, keys, sources),
-        (shape_of((devices, half_rows, LANES), BF), shape_of((group, LANES), BF)),
-        (info, augmented, attended_f, held_grad, all_kv), smem=1,
-        scratch=[pltpu.VMEM((group, LANES), BF), pltpu.VMEM((group, LANES), BF),
-                 pltpu.VMEM((group, LANES), F32), pltpu.VMEM((group, LANES), F32), pltpu.VMEM((wide, LANES), F32)],
-        flops=10 * area * LANES, moved=8 << 20, name="attend_back")
-    dkv = dkv.reshape(devices, 2, half_rows, LANES)
-    mine_kv = lax.dynamic_index_in_dim(dkv, core, 1, keepdims=False)
-    send_kv = lax.dynamic_index_in_dim(dkv, 1 - core, 1, keepdims=False)
-    dkv_sum = (mine_kv.astype(F32) + sibling(send_kv).astype(F32)).astype(BF)
-    back = lax.all_to_all(jnp.concatenate([dq, dkv_sum], axis=2), "ctx", 0, 0)
+    back_q, back_k = exchange_attend_back(send, info, augmented, attended_f, all_kv, head, rows, 3)
     rawq_low, rawk_low, rawv_low, grad_two, attgain_grad, querygain_grad, keysgain_grad = call_plain(
         functools.partial(project_back_kernel, head),
         (shape_of((rows, attquery.shape[1]), BF), shape_of((rows, attkeys.shape[1]), BF),
          shape_of((rows, attkeys.shape[1]), BF), shape_of((rows, width), F32), shape_of((1, width), F32),
          shape_of((1, LANES), F32), shape_of((1, LANES), F32)),
-        (back, hidden_two, attgain_f[None, :], attquery, attkeys, attvalues, cosine, sine, querygain_2, keysgain_2,
+        (back_q, back_k, hidden_two, attgain_f[None, :], attquery, attkeys, attvalues, cosine, sine, querygain_2, keysgain_2,
          query_raw, key_raw, grad),
         flops=2 * rows * width * 2 * width, moved=8 << 20, name="project_back")
     fold = lambda value: value.reshape(LANES // head, head).sum(axis=0)

time: 663 us -> 588 us (0.89)
  waiting for transfers between devices: 52.1 us -> 0.01 us
  Pallas kernels: 482 us -> 519 us
  blocking collectives: 32 us -> 0 us
  starting transfers between devices: 18.3 us -> 3.9 us
  other arithmetic: 30 us -> 21.6 us
    pallas_call x0 -> x2, Pallas kernels: none -> 122 us  [the longest x1 77.3 us: exchange_attend_back(): pl.pallas_call(functools.partial(attend_back_kernel, head, rows, keys, so...]
    pallas_call x4 -> x2, Pallas kernels: 93.3 us -> 15.5 us  [call_plain(): pl.pallas_call(kernel, out_shape=tuple(outs) if many else outs, in_specs=...]
    all_to_all x3 -> x0, waiting for transfers between devices: 49 us -> none  [the longest x1 20.7 us: fast_device(): back = lax.all_to_all(jnp.concatenate([dq, dkv_sum], axis=2), 'ctx', 0, 0)]
    all_to_all x1 -> x0, blocking collectives: 32 us -> none  [fast_device(): held = lax.all_to_all(msg, 'ctx', 0, 0)]
    all_to_all x3 -> x0, starting transfers between devices: 13.5 us -> none  [the longest x1 4.65 us: fast_device(): got = lax.all_to_all(attended_f.astype(BF), 'ctx', 0, 0)]
    unnamed x90 -> x86, local copies, waits for them, and re-layouts: 16.4 us -> 14.9 us
  transfers between devices with their start and end apart: 7 -> 2, of which waited for: 6 -> 0; matrix products, arithmetic and copies ran while one was open for 2% -> 2% of each run, Pallas kernels for 0% -> 0%
where the time goes in v3:
time: 588 us; the launch traced here: 587 us
  Pallas kernels  519 us (88%)
  local copies, waits for them, and re-layouts  26.8 us (5%)
  other arithmetic  21.6 us (4%)
  matrix products  13 us (2%)
    pallas_call x1, Pallas kernels, sum_over_chips(): pl.pallas_call(functools.partial(sum_kernel, jobs, len(lefts), lines), ou...  319 us
    pallas_call x1, Pallas kernels, exchange_attend_back(): pl.pallas_call(functools.partial(attend_back_kernel, head, rows, keys, so...  77.3 us
    pallas_call x3, Pallas kernels, call_tiled(): pl.pallas_call(kernel, grid=(tiles,), in_specs=[spec for _, spec in ins],...  62.9 us
    pallas_call x1, Pallas kernels, exchange_attend(): pl.pallas_call(functools.partial(attend_kernel, head, rows, keys, sources...  44.3 us
    pallas_call x2, Pallas kernels, call_plain(): pl.pallas_call(kernel, out_shape=tuple(outs) if many else outs, in_specs=...  15.5 us
    unnamed x86, local copies, waits for them, and re-layouts  14.9 us
  transfers between devices with their start and end apart: 2, of which 0 were waited for; matrix products, arithmetic and copies ran while one was open for 2% of the time, Pallas kernels for 0%

profile of v3, /device:TPU:0, one launch (start us, length us, event | category | flops | bytes accessed | tf_op | source)
XLA Modules:
  0.0 586.9 jit_solution(16052864956613371191)
XLA Ops:
  0.7 1.4 fusion.10
  2.1 0.7 convert_element_type.114
  2.7 4.8 fusion.12
  7.6 1.6 copy-done.5
  9.4 2.4 collective-permute-start
  13.7 0.7 fusion.20
  14.4 0.7 and_convert_fusion
  15.1 1.2 fusion.14
  16.3 1.2 pad_add_fusion.3.info_ref
  20.7 2.7 multiply_convert_fusion.3
  23.4 1.7 convert_add_fusion.hid_ref
  25.1 16.2 %feed_low.1 = (f32[256,1024]{1,0:T(8,128)}, bf16[1024,256]{1,0:T(8,128)(2,1)}, bf16[256,4608]{1,0:T(8,128)(2,1)}, bf16[256,4608]{1,0:T(8,128)(2,1)}, bf16[4608,256]{1,0:T(8,128)(2,1)}) custom-call(f32[256,1024]{1,0:T(8,128)} %convert_add_fusion.hid_ref, f32[1,1024]{1,0:T(1,128)} %bitcast.51, bf16[1024,4608]{1,0:T(8,128)(2,1)} %gate_ref.5, ...), custom_call_target="tpu_custom_call" | custom-call | flops 7247757312 | bytes 39845888 | tf_op jit(solution)/shard_map/feed_low/pallas_call | solution.py:787
  41.3 6.4 %project.1 = (bf16[16,128,256]{2,1,0:T(8,128)(2,1)}, bf16[1024,256]{1,0:T(8,128)(2,1)}, f32[256,1024]{1,0:T(8,128)}, f32[256,512]{1,0:T(8,128)}) custom-call(f32[256,1024]{1,0:T(8,128)} %get-tuple-element.84.hid_ref.two_ref, f32[1,1024]{1,0:T(1,128)} %bitcast.49, bf16[1024,1024]{1,0:T(8,128)(2,1)} %wq_ref.3, bf16[1024,512]{1,0:T(8,128)(2,1)} %wk_ref.3, ...), custom_call_target="tpu_custom_call" | custom-call | flops 1073741824 | bytes 6291456 | tf_op jit(solution)/shard_map/project/pallas_call | solution.py:1553
  47.7 44.3 %attend.1 = (bf16[16,128,128]{2,1,0:T(8,128)(2,1)}, f32[16,128,128]{2,1,0:T(8,128)}, bf16[16,2,128,128]{3,2,1,0:T(8,128)(2,1)}, bf16[4096,128]{1,0:T(8,128)(2,1)}) custom-call(s32[2]{0:T(128)} %pad_add_fusion.3.info_ref, bf16[16,128,256]{2,1,0:T(8,128)(2,1)} %get-tuple-element.85.msg_ref), custom_call_target="tpu_custom_call" | custom-call | flops 4294967296 | bytes 6291456 | tf_op jit(solution)/shard_map/attend/pallas_call | solution.py:1129
  92.0 27.7 %feed_top.1 = (f32[256,1024]{1,0:T(8,128)}, f32[256,1024]{1,0:T(8,128)}, bf16[256,1024]{1,0:T(8,128)(2,1)}, bf16[16,128,128]{2,1,0:T(8,128)(2,1)}, bf16[1024,256...) custom-call(bf16[16,128,128]{2,1,0:T(8,128)(2,1)} %get-tuple-element, ...), custom_call_target="tpu_custom_call" | custom-call | flops 14495514624 | bytes 47185920 | tf_op jit(solution)/shard_map/feed_top/pallas_call | solution.py:787
  119.7 77.3 %attend_back.1 = (bf16[16,128,128]{2,1,0:T(8,128)(2,1)}, bf16[16,128,128]{2,1,0:T(8,128)(2,1)}) custom-call(s32[2]{0:T(128)} %pad_add_fusion.3.info_ref, bf16[16,2,128,128]{3,2,1,0:T(8,128)(2,1)} %get-tuple-element.88.aug_ref, f32[16,128,128]{2,1,0:T(8,128)} %get-tuple-element.89.out_ref, bf16[4096,128]{1,0:T(8,128)(2,1)} %get-tuple-element.90.kv_ref, ...), custom_call_target="tpu_custom_call" | custom-call | flops 10737418240 | bytes 8388608 | tf_op jit(solution)/shard_map/attend_back/pallas_call | solution.py:1152
  197.0 9.1 %project_back.1 = (bf16[256,1024]{1,0:T(8,128)(2,1)}, bf16[256,512]{1,0:T(8,128)(2,1)}, bf16[256,512]{1,0:T(8,128)(2,1)}, f32[256,1024]{1,0:T(8,128)}, f32[1,102...) custom-call(bf16[16,128,128]{2,1,0:T(8,128)(2,1)} %get-tuple-element.92.backq_ref, ...), custom_call_target="tpu_custom_call" | custom-call | flops 1073741824 | bytes 8388608 | tf_op jit(solution)/shard_map/project_back/pallas_call | solution.py:1553
  206.1 19.1 %feed_low_back.1 = (f32[256,1024]{1,0:T(8,128)}, f32[1,1024]{1,0:T(1,128)}, bf16[256,1024]{1,0:T(8,128)(2,1)}, bf16[256,1024]{1,0:T(8,128)(2,1)}, bf16[256,4608]{1,0:T(8,128)(2,1)}, /*index=5*/bf16[256,4608]{1,0:T(8,128)(2,1)}) custom-call(f32[256,1024]{1,0:T(8,128)} %get-tuple-element.97.grad_ref, f32[256,1024]{1,0:T(8,128)} %convert_add_fusion.hid_ref, ...), custom_call_target="tpu_custom_call" | custom-call | flops 7247757312 | bytes 41943040 | tf_op jit(solution)/shard_map/feed_low_back/pallas_call | solution.py:787
  225.2 1.9 fusion.29
  227.1 2.5 multiply_reduce_fusion.2
  229.9 1.6 pad_add_fusion
  232.0 0.7 reduce.9
  232.7 0.7 reduce.8
  233.6 1.5 collective-permute-start.1
  235.3 2.1 copy.45
  237.3 1.5 slice.121
  239.2 1.6 copy-done.6
  241.8 4.6 fusion.25
  246.5 1.3 pad_maximum_fusion.refs_19_
  248.4 1.0 copy.46
  249.4 0.7 concatenate.18.refs_20_
  250.1 319.3 %sum_over_chips.1 = (f32[64,1024]{1,0:T(8,128)}, f32[64,1024]{1,0:T(8,128)}, f32[64,512]{1,0:T(8,128)}, f32[64,512]{1,0:T(8,128)}, f32[288,1024]{1,0:T(8,128)}, ...) custom-call(bf16[8,2,64,256]{3,2,1,0:T(8,128)(2,1)} %bitcast.67, ...), custom_call_target="tpu_custom_call" | custom-call | flops 18253611008 | bytes 108800000 | tf_op jit(solution)/shard_map/sum_over_chips/pallas_call | solution.py:1536
  569.4 1.3 slice_bitcast_fusion
  570.7 1.4 slice.105
  572.1 1.5 fusion.26
  573.6 2.9 fusion.8
  576.5 0.9 copy.60
  577.4 0.7 copy.61
  578.1 1.0 copy.62
  579.1 1.0 copy.63
  580.1 1.0 copy.64
  581.2 0.7 copy.65
  581.9 0.7 copy.66
  582.5 0.7 copy.67
  583.2 0.7 copy.68
  583.9 1.0 copy.69
  584.9 1.0 copy.70
  585.9 1.0 copy.71
  (102 shorter events, 7.2 us)
Async XLA Ops:
  0.7 22.8 %copy-start = (bf16[1024,1024]{1,0:T(8,128)(2,1)S(1)}, bf16[1024,1024]{1,0:T(8,128)(2,1)}, u32[]{:S(2)}) copy-start(bf16[1024,1024]{1,0:T(8,128)(2,1)} %param.30) | copy-start | bytes 6291460
  7.6 1.6 copy-start.5
  9.2 2.6 copy-start.32
  9.2 5.8 copy-start.25
  9.2 8.3 %copy-start.33 = (bf16[64]{0:T(256)(128)(2,1)S(1)}, bf16[64]{0:T(256)(128)(2,1)}, u32[]{:S(2)}) copy-start(bf16[64]{0:T(256)(128)(2,1)} %param.39) | copy-start | bytes 388
  9.2 8.9 %copy-start.34 = (bf16[64]{0:T(256)(128)(2,1)S(1)}, bf16[64]{0:T(256)(128)(2,1)}, u32[]{:S(2)}) copy-start(bf16[64]{0:T(256)(128)(2,1)} %param.40) | copy-start | bytes 388
  9.2 9.5 %copy-start.29 = (bf16[1024]{0:T(1024)(128)(2,1)S(1)}, bf16[1024]{0:T(1024)(128)(2,1)}, u32[]{:S(2)}) copy-start(bf16[1024]{0:T(1024)(128)(2,1)} %param.31) | copy-start | bytes 6148
  9.2 10.1 %copy-start.30 = (bf16[1024]{0:T(1024)(128)(2,1)S(1)}, bf16[1024]{0:T(1024)(128)(2,1)}, u32[]{:S(2)}) copy-start(bf16[1024]{0:T(1024)(128)(2,1)} %param.35) | copy-start | bytes 6148
  9.3 10.7 %copy-start.31 = (bf16[1024]{0:T(1024)(128)(2,1)S(1)}, bf16[1024]{0:T(1024)(128)(2,1)}, u32[]{:S(2)}) copy-start(bf16[1024]{0:T(1024)(128)(2,1)} %param.42) | copy-start | bytes 6148
  9.4 11.1 %collective-permute-start = (bf16[2,1024]{1,0:T(2,128)(2,1)S(1)}, bf16[2,1024]{1,0:T(2,128)(2,1)S(1)}, u32[]{:S(2)}, u32[]{:S(2)}) collective-permute-start(bf16[2,1024]{1,0:T(2,128)(2,1)S(1)} %slice.115), channel_id=1, source_target_pairs={{0,1},{1,2},{2,3},{3,4},{4,5},{5,6},{6,7},{7,8},{8,9},{9,10},{10,1... | collective-permute-start | bytes 12296 | tf_op jit(solution)/shard_map/ppermute | solution.py:19
  20.7 2.7 copy-start.7
  23.4 1.7 copy-start.9
  225.2 1.9 copy-start.10
  229.9 1.7 copy-start.1
  229.9 1.7 copy-start.3
  229.9 2.2 copy-start.36
  229.9 2.8 copy-start.35
  233.6 5.2 collective-permute-start.1
  237.3 1.5 copy-start.2
  237.3 1.9 copy-start.4
  238.8 2.0 copy-start.6
  240.8 1.0 copy-start.12
  246.5 1.9 copy-start.11
  246.5 1.4 copy-start.8
  247.9 1.5 copy-start.26
  247.9 1.5 copy-start.27
  247.9 1.5 copy-start.28
  569.3 7.2 %copy-start.19 = (f32[64,3072]{1,0:T(8,128)S(1)}, f32[64,3072]{1,0:T(8,128)}, u32[]{:S(2)}) copy-start(f32[64,3072]{1,0:T(8,128)} %get-tuple-element.191) | copy-start | bytes 2359300
  573.6 3.8 copy-start.22
  573.6 4.5 copy-start.18
  576.5 2.6 copy-start.17
  578.1 2.0 copy-start.16
  579.1 2.0 copy-start.21
  579.1 2.8 copy-start.24
  580.1 2.4 copy-start.23
  580.1 3.0 copy-start.20
  580.1 3.8 copy-start.15
  581.2 3.7 copy-start.14
  583.9 2.0 copy-start.13

commit v4 on v3

--- a/solution.py
+++ b/solution.py
@@ -511,6 +511,12 @@
 ONES_NT = (((1,), (1,)), ((), ()))
 ONES_TN = (((0,), (0,)), ((), ()))
 VMEM_LIMIT = 60 * 1024 * 1024
+PIECE = 16
+SUB = 2 * PIECE
+STRIP = 256
+RING = 16
+LAG = 3
+AHEAD = 8
 
 
 def vmem_specs(count):
@@ -587,7 +593,7 @@
 
 def project_back_kernel(head, backq_ref, backk_ref, hid_ref, gain_ref, wq_ref, wk_ref, wv_ref, cos_ref, sin_ref, qg_ref,
                         kg_ref, qraw_ref, kraw_ref, grad_ref,
-                        rawq_ref, rawk_ref, rawv_ref, two_ref, again_ref, qgain_ref, kgain_ref):
+                        rawq_ref, keep_ref, send_ref, two_ref, again_ref, qgain_ref, kgain_ref):
     blocks = same_head(head)
     cosine, sine = cos_ref[...], sin_ref[...]
     lane = lane_of(cosine.shape)
@@ -612,17 +618,19 @@
         rawq_ref[:, tile * LANES:(tile + 1) * LANES] = got.astype(BF)
     qgain_ref[...] = gain_total
     gain_total = jnp.zeros((1, LANES), F32)
+    key_tiles, value_tiles = [], []
     for tile in range(width_k // LANES):
         even, odd = fetch(backk_ref, 2 * tile), fetch(backk_ref, 2 * tile + 1)
         keys = jnp.where(lane < head, even, swap_heads(odd, head))
         values = jnp.where(lane < head, swap_heads(even, head), odd)
         got, part = through(keys, kraw_ref[:, tile * LANES:(tile + 1) * LANES], kg_ref[...])
         gain_total = gain_total + part
-        rawk_ref[:, tile * LANES:(tile + 1) * LANES] = got.astype(BF)
-        rawv_ref[:, tile * LANES:(tile + 1) * LANES] = values.astype(BF)
+        key_tiles.append(got.astype(BF))
+        value_tiles.append(values.astype(BF))
     kgain_ref[...] = gain_total
-    normed_grad = nt_dot(rawq_ref[...], wq_ref[...]) + nt_dot(rawk_ref[...], wk_ref[...])
-    normed_grad += nt_dot(rawv_ref[...], wv_ref[...])
+    keys, values = jnp.concatenate(key_tiles, axis=1), jnp.concatenate(value_tiles, axis=1)
+    keep_ref[...], send_ref[...] = kept_first(keys, values)
+    normed_grad = nt_dot(rawq_ref[...], wq_ref[...]) + nt_dot(keys, wk_ref[...]) + nt_dot(values, wv_ref[...])
     hid = hid_ref[...]
     scale = lax.rsqrt(jnp.mean(hid * hid, axis=-1, keepdims=True) + EPS)
     unit = hid * scale
@@ -656,6 +664,11 @@
     inward = normed_grad * gain
     back = scale * (inward - unit * jnp.mean(inward * unit, axis=-1, keepdims=True))
     return back, jnp.sum(normed_grad * unit, axis=0, keepdims=True)
+
+
+def kept_first(one, two):
+    first = lax.axis_index("dp") == 0
+    return jnp.where(first, one, two), jnp.where(first, two, one)
 
 
 def nt_dot(left, right):
@@ -705,8 +718,7 @@
     gate_act, lift_act = gact_ref[...].astype(F32), lact_ref[...].astype(F32)
     inner_grad = nt_dot(low_ref[...], drop_ref[...])
     gate_low, lift_low = activation_pull(gate_act, lift_act, jax.nn.sigmoid(gate_act), inner_grad)
-    glow_ref[...] = gate_low
-    llow_ref[...] = lift_low
+    glow_ref[...], llow_ref[...] = kept_first(gate_low, lift_low)
     acc_ref[...] += nt_dot(gate_low, gate_ref[...]) + nt_dot(lift_low, lift_ref[...])
 
     @pl.when(step == pl.num_programs(0) - 1)
@@ -748,8 +760,7 @@
     out_ref[...] += nn_dot(inner.astype(BF), drop_ref[...])
     inner_grad = nt_dot(cot_ref[...], drop_ref[...])
     gate_low, lift_low = activation_pull(gate_act, lift_act, sigma, inner_grad)
-    glow_ref[...] = gate_low
-    llow_ref[...] = lift_low
+    glow_ref[...], llow_ref[...] = kept_first(gate_low, lift_low)
     acc_ref[...] += nt_dot(gate_low, gate_ref[...]) + nt_dot(lift_low, lift_ref[...])
 
     @pl.when(step == pl.num_programs(0) - 1)
@@ -823,7 +834,7 @@
          (drop, row_block(width, WIDE_TILE))],
         [(S((rows, width), F32), full), (S((1, width), F32), whole_block((1, width))), (S((rows, width), BF), full),
          (S((rows, width), BF), full), (S((rows, ff), BF), column_block(rows, WIDE_TILE)), (S((rows, ff), BF), column_block(rows, WIDE_TILE))],
-        [pltpu.VMEM((rows, width), F32)], 6 * rows * width * ff, 40 << 20, "feed_low_back")
+        [pltpu.VMEM((rows, width), F32)], 1 << 20, 1 << 10, "feed_low_back")
 
 
 def feed_top(got, two, exit_weight, cotangent, gain, gate, lift, drop):
@@ -861,11 +872,43 @@
         pl.semaphore_signal(barrier, inc=1, device_id={"ctx": lax.rem(me + step, count)}, device_id_type=MESH)
 
     lax.fori_loop(1, count, hello, None)
-    pl.semaphore_wait(barrier, count - 1)
-
-
-def attend_kernel(head, rows, keys, sources, count, info_ref, msg_ref, got_ref, out_ref, aug_ref, all_ref,
-                  land, kv, tiles, arrive, ones_ref, acc_ref, msend, mrecv, fsend, frecv, gsend, grecv):
+    pl.semaphore_signal(barrier, inc=1, device_id={"dp": 1 - lax.axis_index("dp")}, device_id_type=MESH)
+    pl.semaphore_wait(barrier, count)
+
+
+def hosted_copies(kinds, sources, landings, sends, recvs):
+    y = lax.axis_index("dp")
+    copies = []
+    for number, (kind, source, landing) in enumerate(zip(kinds, sources, landings)):
+        if kind == "rows":
+            height = landing.shape[2]
+            source = source.at[:, :, pl.ds(pl.multiple_of((1 - y) * height, PIECE), height), :]
+        if kind == "columns":
+            width = landing.shape[1]
+            source = source.at[:, pl.ds(pl.multiple_of((1 - y) * width, STRIP), width)]
+        copies.append(pltpu.make_async_remote_copy(
+            src_ref=source, dst_ref=landing, send_sem=sends.at[number], recv_sem=recvs.at[number],
+            device_id={"dp": 1 - y}, device_id_type=MESH))
+    return copies
+
+
+def hosted_shapes(hosted):
+    shapes = []
+    for kind, value in hosted:
+        shape = list(value.shape)
+        if kind == "rows":
+            shape[2] //= 2
+        if kind == "columns":
+            shape[1] //= 2
+        shapes.append(jax.ShapeDtypeStruct(tuple(shape), value.dtype))
+    return shapes
+
+
+def attend_kernel(head, rows, keys, sources, count, kinds, *refs):
+    extra = len(kinds)
+    (info_ref, msg_ref), guests, refs = refs[:2], refs[2:2 + extra], refs[2 + extra:]
+    (got_ref, out_ref, aug_ref, all_ref), landings, refs = refs[:4], refs[4:4 + extra], refs[4 + extra:]
+    (land, kv, tiles, arrive, ones_ref, acc_ref, msend, mrecv, fsend, frecv, gsend, grecv, hsend, hrecv) = refs
     first, second = info_ref[0], info_ref[1]
     me = lax.axis_index("ctx")
     part = me % 2
@@ -894,6 +937,9 @@
         msg_copy(me, lax.rem(me + step, count)).start()
 
     lax.fori_loop(1, count, start_msg, None)
+    hosted = hosted_copies(kinds, guests, landings, hsend, hrecv)
+    for copy in hosted:
+        copy.start()
     land[me] = msg_ref[me]
 
     def share(source):
@@ -974,12 +1020,16 @@
 
     lax.fori_loop(0, count, drain, None)
     got_ref[...] = arrive[...]
-
-
-def attend_back_kernel(head, rows, keys, sources, count, info_ref, aug_ref, out_ref, kv_ref, msg_ref,
-                       gotq_ref, gotk_ref,
-                       land, tiles, away, near, sums, arrive_q, arrive_k, kone_ref, vone_ref, kturn_ref, dk_ref,
-                       dv_ref, acc_ref, msend, mrecv, fsend, frecv, gsend, grecv, ksend, krecv):
+    for copy in hosted:
+        copy.wait()
+
+
+def attend_back_kernel(head, rows, keys, sources, count, kinds, *refs):
+    extra = len(kinds)
+    (info_ref, aug_ref, out_ref, kv_ref, msg_ref), guests, refs = refs[:5], refs[5:5 + extra], refs[5 + extra:]
+    (gotq_ref, gotk_ref), landings, refs = refs[:2], refs[2:2 + extra], refs[2 + extra:]
+    (land, tiles, away, near, sums, arrive_q, arrive_k, kone_ref, vone_ref, kturn_ref, dk_ref, dv_ref, acc_ref,
+     msend, mrecv, fsend, frecv, gsend, grecv, ksend, krecv, hsend, hrecv) = refs
     first, second = info_ref[0], info_ref[1]
     me = lax.axis_index("ctx")
     part = me % 2
@@ -1011,6 +1061,9 @@
         msg_copy(me, lax.rem(me + count - step, count)).start()
 
     lax.fori_loop(1, count, start_msg, None)
+    hosted = hosted_copies(kinds, guests, landings, hsend, hrecv)
+    for copy in hosted:
+        copy.start()
     land[me] = msg_ref[me]
     whole = lane_of(kv_ref.shape)
     vone_ref[...] = jnp.where(whole < head, jnp.ones_like(kv_ref), kv_ref[...])
@@ -1117,73 +1170,80 @@
     lax.fori_loop(0, count, drain, None)
     gotq_ref[...] = arrive_q[...]
     gotk_ref[...] = arrive_k[...]
-
-
-def exchange_attend(msg, info, head, rows, collective_id):
+    for copy in hosted:
+        copy.wait()
+
+
+def exchange_attend(msg, info, head, rows, hosted, collective_id):
     count, half_rows = msg.shape[0], msg.shape[1]
     keys, sources = 512, 2
     group = count * rows
     dma = pltpu.SemaphoreType.DMA((count,))
     S = jax.ShapeDtypeStruct
     tile = (count, half_rows, LANES)
+    kinds = [kind for kind, _ in hosted]
+    guests = [value for _, value in hosted]
+    hdma = pltpu.SemaphoreType.DMA((len(hosted),))
+    anywhere = [pl.BlockSpec(memory_space=pl.ANY)] * len(hosted)
     return pl.pallas_call(
-        functools.partial(attend_kernel, head, rows, keys, sources, count),
-        out_shape=(S(tile, BF), S(tile, F32), S((count, 2, half_rows, LANES), BF), S((group, LANES), BF)),
-        in_specs=[pl.BlockSpec(memory_space=pltpu.SMEM)] + vmem_specs(1),
-        out_specs=tuple(vmem_specs(4)),
+        functools.partial(attend_kernel, head, rows, keys, sources, count, kinds),
+        out_shape=(S(tile, BF), S(tile, F32), S((count, 2, half_rows, LANES), BF), S((group, LANES), BF),
+                   *hosted_shapes(hosted)),
+        in_specs=[pl.BlockSpec(memory_space=pltpu.SMEM)] + vmem_specs(1) + anywhere,
+        out_specs=tuple(vmem_specs(4) + anywhere),
         scratch_shapes=[pltpu.VMEM((count, half_rows, 2 * LANES), BF), pltpu.VMEM((count, 2, half_rows, LANES), BF),
                         pltpu.VMEM(tile, BF), pltpu.VMEM(tile, BF), pltpu.VMEM((group, LANES), BF),
-                        pltpu.VMEM((sources * rows, LANES), F32)] + [dma] * 6,
+                        pltpu.VMEM((sources * rows, LANES), F32)] + [dma] * 6 + [hdma] * 2,
         compiler_params=pltpu.CompilerParams(collective_id=collective_id, has_side_effects=True,
                                              vmem_limit_bytes=VMEM_LIMIT),
         cost_estimate=pl.CostEstimate(flops=2 * group * group * LANES, bytes_accessed=6 << 20, transcendentals=0),
         name="attend",
-    )(info, msg)
-
-
-def exchange_attend_back(msg, info, augmented, attended, all_kv, head, rows, collective_id):
+    )(info, msg, *guests)
+
+
+def exchange_attend_back(msg, info, augmented, attended, all_kv, head, rows, hosted, collective_id):
     count, half_rows = msg.shape[0], msg.shape[1]
     keys, sources = 512, 2
     group = count * rows
     dma = pltpu.SemaphoreType.DMA((count,))
     S = jax.ShapeDtypeStruct
     tile = (count, half_rows, LANES)
+    kinds = [kind for kind, _ in hosted]
+    guests = [value for _, value in hosted]
+    hdma = pltpu.SemaphoreType.DMA((len(hosted),))
+    anywhere = [pl.BlockSpec(memory_space=pl.ANY)] * len(hosted)
     long = (group, LANES)
     return pl.pallas_call(
-        functools.partial(attend_back_kernel, head, rows, keys, sources, count),
-        out_shape=(S(tile, BF), S(tile, BF)),
-        in_specs=[pl.BlockSpec(memory_space=pltpu.SMEM)] + vmem_specs(4),
-        out_specs=tuple(vmem_specs(2)),
+        functools.partial(attend_back_kernel, head, rows, keys, sources, count, kinds),
+        out_shape=(S(tile, BF), S(tile, BF), *hosted_shapes(hosted)),
+        in_specs=[pl.BlockSpec(memory_space=pltpu.SMEM)] + vmem_specs(4) + anywhere,
+        out_specs=tuple(vmem_specs(2) + anywhere),
         scratch_shapes=[pltpu.VMEM(tile, BF)] * 7 + [
             pltpu.VMEM(long, BF), pltpu.VMEM(long, BF), pltpu.VMEM((LANES, group), BF), pltpu.VMEM(long, F32),
-            pltpu.VMEM(long, F32), pltpu.VMEM((LANES, sources * rows), F32)] + [dma] * 8,
+            pltpu.VMEM(long, F32), pltpu.VMEM((LANES, sources * rows), F32)] + [dma] * 8 + [hdma] * 2,
         compiler_params=pltpu.CompilerParams(collective_id=collective_id, has_side_effects=True,
                                              vmem_limit_bytes=VMEM_LIMIT),
         cost_estimate=pl.CostEstimate(flops=5 * group * group * LANES, bytes_accessed=8 << 20, transcendentals=0),
         name="attend_back",
-    )(info, augmented, attended, all_kv, msg)
-
-
-PIECE = 32
-SUB = 2 * PIECE
-STRIP = 256
-RING = 8
-LAG = 2
-
-
-def sum_kernel(jobs, sides, lines, *refs):
+    )(info, augmented, attended, all_kv, msg, *guests)
+
+
+def sum_kernel(jobs, sides, weights, lines, *refs):
     count = len(jobs)
     refs = list(refs)
     take = lambda number: [refs.pop(0) for _ in range(number)]
-    lefts, rights, (small_ref,) = take(sides), take(count), take(1)
-    outs, (small_out,), lefts_b, rights_b = take(count), take(1), take(sides), take(count)
-    (lbuf, rbuf, xp, xr, yp, yr, zp, us, ur, ds_, dr, fs, fr, cs, cr, stage, sm_s, sm_r,
-     lsem, rsem, xs, xv, ys, yv, uss, urv, dss, drv, fss, frv, css, crv, osem, sms, smv, els, elv, ers, erv) = refs
-    steps = sum(job[3] for job in jobs)
-    last = steps - 1 + LAG
-    half = STRIP // 2
-    tall = SUB + PIECE
-    tokens = lbuf.shape[-1] // 2
+    lefts, lefts_y, rights = take(sides), take(sides), take(count)
+    sent = [refs.pop(0) if job["late"] and job["kind"] == "pair" else None for job in jobs]
+    early_y = [None if job["late"] else refs.pop(0) for job in jobs]
+    (small_ref,) = take(1)
+    outs, (small_out,) = take(weights), take(1)
+    lefts_s, lefts_ys, rights_s, rights_ys = take(sides), take(sides), take(count), take(count)
+    rights_y = [refs.pop(0) if job["late"] else early for job, early in zip(jobs, early_y)]
+    (lbuf, rbuf, xp, xr, zp, us, ur, ds_, dr, fs, fr, cs, cr, stage, sm_s, sm_r,
+     lsem, rsem, xs, xv, uss, urv, dss, drv, fss, frv, css, crv, osem, sms, smv, els, elv, ers, erv, yrs, yrv) = refs
+    steps = sum(job["total"] for job in jobs)
+    last = steps - 1
+    tokens = lbuf.shape[-1] // 4
     me = lax.axis_index("ctx")
     y = lax.axis_index("dp")
     z = me // 4
@@ -1199,7 +1259,7 @@
     far = {"ctx": me + 8 - 16 * (z // 2)}
     rounds = [twin, across_x, across_y, near, far]
 
-    for buf in (xp, ur, dr, zp):
+    for buf in (ur, dr, zp):
         buf[...] = jnp.zeros_like(buf)
     sm_s[0] = small_ref[...]
 
@@ -1221,111 +1281,182 @@
         return pltpu.make_async_remote_copy(src_ref=src, dst_ref=dst, send_sem=send, recv_sem=recv,
                                             device_id=where, device_id_type=MESH)
 
-    def left_copy(number):
-        return remote(lefts[number], lefts_b[number], els.at[number], elv.at[number], twin)
-
-    def right_copy(number):
-        width = rights_b[number].shape[1]
-        start = pl.multiple_of((1 - c) * width, width)
-        return remote(rights[number].at[:, pl.ds(start, width)], rights_b[number], ers.at[number], erv.at[number], twin)
-
-    seen = []
-    for number, job in enumerate(jobs):
-        if job[0] not in seen:
-            seen.append(job[0])
-            left_copy(job[0]).start()
-        right_copy(number).start()
+    def row_base(number):
+        height = lefts_s[number].shape[2]
+        return y * height if height < lefts[number].shape[2] else 0
+
+    def column_base(number):
+        width = 2 * rights_s[number].shape[1]
+        return y * width if jobs[number]["kind"] == "quarter" else 0
+
+    def left_copies(number):
+        height = lefts_s[number].shape[2]
+        rows = pl.ds(pl.multiple_of(row_base(number), PIECE), height)
+        return [
+            remote(lefts[number].at[:, :, rows, :], lefts_s[number], els.at[number, 0], elv.at[number, 0], twin),
+            remote(lefts_y[number], lefts_ys[number], els.at[number, 1], elv.at[number, 1], twin),
+        ]
+
+    def right_own(number):
+        width = rights_s[number].shape[1]
+        start = pl.multiple_of(column_base(number) + (1 - c) * width, STRIP)
+        return remote(rights[number].at[:, pl.ds(start, width)], rights_s[number], ers.at[number, 0],
+                      erv.at[number, 0], twin)
+
+    def right_forward(number):
+        width = rights_s[number].shape[1]
+        start = pl.multiple_of((1 - c) * width, STRIP)
+        return remote(rights_y[number].at[:, pl.ds(start, width)], rights_ys[number], ers.at[number, 1],
+                      erv.at[number, 1], twin)
+
+    def right_cross(number, piece=None):
+        width = 2 * rights_s[number].shape[1]
+        kind = jobs[number]["kind"]
+        source = sent[number] if kind == "pair" else rights[number]
+        start = (1 - y) * width if kind == "quarter" else 0
+        rows, inside = slice(None), 0
+        size = width
+        if piece is not None:
+            rows = pl.ds(pl.multiple_of((piece & 1) * (tokens // 2), PIECE), tokens // 2)
+            inside, size = (piece >> 1) * STRIP, STRIP
+        place = pl.ds(pl.multiple_of(inside, STRIP), size)
+        if piece is None:
+            landing = rights_y[number]
+        else:
+            landing = rights_y[number].at[rows, place]
+        return remote(source.at[rows, pl.ds(pl.multiple_of(start + inside, STRIP), size)], landing,
+                      yrs.at[number], yrv.at[number], across_y)
 
     def x_copy(j):
-        s = j % RING
+        s = j & (RING - 1)
         return remote(xp.at[s, 1 - x], xr.at[s], xs.at[s], xv.at[s], across_x)
 
-    def y_copy(j):
-        s = j % RING
-        return remote(yp.at[s, 1 - y], yr.at[s], ys.at[s], yv.at[s], across_y)
-
     def up_copy(j):
-        s = j % RING
+        s = j & (RING - 1)
         return remote(us.at[s], ur.at[s], uss.at[s], urv.at[s], above)
 
     def down_copy(j):
-        s = j % RING
+        s = j & (RING - 1)
         return remote(ds_.at[s], dr.at[s], dss.at[s], drv.at[s], below)
 
     def f_copy(j):
-        s = j % RING
+        s = j & (RING - 1)
         return remote(fs.at[s], fr.at[s], fss.at[s], frv.at[s], across_y)
 
     def c_copy(j):
-        s = j % RING
+        s = j & (RING - 1)
         return remote(cs.at[s], cr.at[s], css.at[s], crv.at[s], twin)
 
     def small_copy(k):
         return remote(sm_s.at[k], sm_r.at[k], sms.at[k], smv.at[k], rounds[k])
 
-    def loads(number, row, column, s):
-        left = jobs[number][0]
-        width = rights_b[number].shape[1]
-        mine = pl.multiple_of(c * width + column, STRIP)
-        rows = pl.ds(row, PIECE)
-        return [
-            pltpu.make_async_copy(lefts[left].at[:, :, rows, :], lbuf.at[s, :, :, :, pl.ds(0, tokens)], lsem.at[s, 0]),
-            pltpu.make_async_copy(lefts_b[left].at[:, :, rows, :], lbuf.at[s, :, :, :, pl.ds(tokens, tokens)],
-                                  lsem.at[s, 1]),
-            pltpu.make_async_copy(rights[number].at[:, pl.ds(mine, STRIP)], rbuf.at[s, pl.ds(0, tokens)], rsem.at[s, 0]),
-            pltpu.make_async_copy(rights_b[number].at[:, pl.ds(column, STRIP)], rbuf.at[s, pl.ds(tokens, tokens)],
-                                  rsem.at[s, 1]),
-        ]
-
-    def load(j):
+    def loads(number):
+        job = jobs[number]
+        left, s = job["left"], number % 2
+        height, width = lefts_s[left].shape[2], rights_s[number].shape[1]
+        own_rows = pl.ds(pl.multiple_of(row_base(left), PIECE), height)
+        own_columns = pl.ds(pl.multiple_of(column_base(number) + c * width, STRIP), width)
+        mine = pl.ds(pl.multiple_of(c * width, STRIP), width)
+        copies = []
+        for place, source in enumerate([lefts[left].at[:, :, own_rows, :], lefts_s[left], lefts_y[left],
+                                        lefts_ys[left]]):
+            copies.append(pltpu.make_async_copy(
+                source, lbuf.at[s, :, :, pl.ds(0, height), pl.ds(place * tokens, tokens)], lsem.at[s, place]))
+        for place, source in enumerate([rights[number].at[:, own_columns], rights_s[number],
+                                        rights_y[number].at[:, mine], rights_ys[number]]):
+            copies.append(pltpu.make_async_copy(
+                source, rbuf.at[s, pl.ds(place * tokens, tokens), pl.ds(0, width)], rsem.at[s, place]))
+        return copies
+
+    def each_job(j, visit):
         begin = 0
-        done = []
-        for number, (left, subs, strips, total) in enumerate(jobs):
-            fresh = left not in done
-            done.append(left)
-
-            @pl.when(j == begin)
-            def _(number=number, left=left, fresh=fresh):
+        for number, job in enumerate(jobs):
+            @pl.when((j >= begin) & (j < begin + job["total"]))
+            def _(number=number, begin=begin):
+                visit(number, j - begin)
+            begin += job["total"]
+
+    def begins():
+        begin = 0
+        for number, job in enumerate(jobs):
+            yield number, job, begin
+            begin += job["total"]
+
+    def out_copies(number, k, j):
+        job = jobs[number]
+        o = j & (RING - 1)
+        row = pl.multiple_of(lax.rem(k, job["subs"]) * PIECE, PIECE)
+        column = pl.multiple_of(lax.div(k, job["subs"]) * STRIP, STRIP)
+        width = rights_s[number].shape[1]
+        copies = []
+        for line in range(2):
+            for core in range(2):
+                out = outs[job["outs"][line if job["kind"] == "pair" else 0]]
+                rows, columns = row, core * width + column
+                if job["kind"] == "quarter":
+                    columns = line * 2 * width + columns
+                if job["kind"] == "drop":
+                    rows = line * lefts_s[job["left"]].shape[2] + row
+                copies.append(pltpu.make_async_copy(
+                    stage.at[o, line, core],
+                    out.at[pl.ds(pl.multiple_of(rows, PIECE), PIECE), pl.ds(pl.multiple_of(columns, STRIP), STRIP)],
+                    osem.at[o, line, core]))
+        return copies
+
+    def out_wait(j):
+        for copy in out_copies(0, 0, j):
+            copy.wait()
+
+    started = []
+    for number, job, begin in begins():
+        if job["left"] not in started:
+            started.append(job["left"])
+            for copy in left_copies(job["left"]):
+                copy.start()
+        right_own(number).start()
+        if not job["late"]:
+            right_forward(number).start()
+
+    def step(t, _):
+        slot = t & (RING - 1)
+
+        for number, job, begin in begins():
+            if job["late"]:
+                ago = t - job["issue"]
+                piece = ago - (ago >> 2)
+                pieces = 4 * rights_s[number].shape[1] // STRIP
+
+                @pl.when((ago >= 0) & (ago & 3 != 3) & (piece < pieces))
+                def _(number=number, piece=piece):
+                    right_cross(number, piece).start()
+
+                @pl.when(t == begin - job["ahead"])
+                def _(number=number):
+                    right_cross(number).wait()
+                    right_forward(number).start()
+
+        done, before = [], 0
+        for number, job, begin in begins():
+            fresh = job["left"] not in done
+            done.append(job["left"])
+
+            @pl.when(t == max(before, begin - AHEAD))
+            def _(number=number, job=job, fresh=fresh):
                 if fresh:
-                    left_copy(left).wait()
-                right_copy(number).wait()
-
-            @pl.when((j >= begin) & (j < begin + total))
-            def _(number=number, subs=subs, begin=begin):
-                k = j - begin
-                row = pl.multiple_of((k % subs) * PIECE, PIECE)
-                column = pl.multiple_of((k // subs) * STRIP, STRIP)
-                for copy in loads(number, row, column, j % 2):
+                    for copy in left_copies(job["left"]):
+                        copy.wait()
+                right_own(number).wait()
+                right_forward(number).wait()
+                for copy in loads(number):
                     copy.start()
-            begin += total
-
-    def out_copies(number, j, row, column):
-        width = rights_b[number].shape[1]
-        o = j % RING
-        rows = pl.ds(row, PIECE)
-        mine = pl.multiple_of(c * width + column, STRIP)
-        other = pl.multiple_of((1 - c) * width + column, STRIP)
-        return [
-            pltpu.make_async_copy(stage.at[o, 0], outs[number].at[rows, pl.ds(mine, STRIP)], osem.at[o, 0]),
-            pltpu.make_async_copy(stage.at[o, 1], outs[number].at[rows, pl.ds(other, STRIP)], osem.at[o, 1]),
-        ]
-
-    def store(j):
-        begin = 0
-        for number, (left, subs, strips, total) in enumerate(jobs):
-            @pl.when((j >= begin) & (j < begin + total))
-            def _(number=number, subs=subs, begin=begin):
-                k = j - begin
-                row = pl.multiple_of((k % subs) * PIECE, PIECE)
-                column = pl.multiple_of((k // subs) * STRIP, STRIP)
-                for copy in out_copies(number, j, row, column):
-                    copy.start()
-            begin += total
-
-    load(0)
-
-    def step(t, _):
-        slot = t % RING
+
+            before = begin
+
+        for number, job, begin in begins():
+            @pl.when(t == begin)
+            def _(number=number):
+                for copy in loads(number):
+                    copy.wait()
 
         for k in range(len(rounds) + 1):
             @pl.when(t == LAG * k)
@@ -1342,48 +1473,36 @@
 
         @pl.when(t < steps)
         def _():
-            for copy in loads(0, 0, 0, t % 2):
-                copy.wait()
-
-            @pl.when(t + 1 < steps)
-            def _():
-                load(t + 1)
-
-            left = lbuf[t % 2].reshape(2 * lines * SUB, 2 * tokens)
-            got = jnp.dot(left, rbuf[t % 2], preferred_element_type=F32).astype(BF)
+            which, begin_now, subs_now = 0, 0, jobs[0]["subs"]
+            for number, job, begin in begins():
+                here = t >= begin
+                begin_now = jnp.where(here, begin, begin_now)
+                subs_now = jnp.where(here, job["subs"], subs_now)
+                which = jnp.where(here, number % 2, which)
+            row = lax.rem(t - begin_now, subs_now) * PIECE
+            column = lax.div(t - begin_now, subs_now) * STRIP
+            rows = pl.ds(pl.multiple_of(row, PIECE), PIECE)
+            left = lbuf[which, :, :, rows, :].reshape(2 * lines * SUB, 4 * tokens)
+            right = rbuf[which, :, pl.ds(pl.multiple_of(column, STRIP), STRIP)]
+            got = jnp.dot(left, right, preferred_element_type=F32).astype(BF)
             for line in range(lines):
                 for side in range(2):
                     row = (2 * line + side) * SUB
-                    xp[slot, side, line, :SUB] = got[row:row + SUB, :half]
-                    for part in range(2):
-                        yp[slot, part, side, line] = got[row + part * PIECE:row + (part + 1) * PIECE, half:]
-
-        @pl.when((t >= LAG) & (t <= last))
-        def _():
-            y_copy(t - LAG).wait()
-            s = (t - LAG) % RING
-            xp[slot, :, :, SUB:] = yp[s, y] + yr[s]
-
-        @pl.when(t < steps)
-        def _():
-            y_copy(t).start()
-
-        @pl.when(t <= last)
-        def _():
+                    xp[slot, side, line] = got[row:row + SUB]
             x_copy(t).start()
 
         @pl.when((t >= LAG) & (t - LAG <= last))
         def _():
             x_copy(t - LAG).wait()
-            s = (t - LAG) % RING
-            zp[(t - LAG) % (2 * RING)] = xp[s, x] + xr[s]
+            s = (t - LAG) & (RING - 1)
+            zp[(t - LAG) & (2 * RING - 1)] = xp[s, x] + xr[s]
 
         ju = t - LAG * (1 + z)
 
         @pl.when((ju >= 0) & (ju <= last))
         def _():
-            s = ju % RING
-            held = ju % (2 * RING)
+            s = ju & (RING - 1)
+            held = ju & (2 * RING - 1)
 
             @pl.when(z > 0)
             def _():
@@ -1407,8 +1526,8 @@
 
         @pl.when((jd >= 0) & (jd <= last))
         def _():
-            s = jd % RING
-            held = jd % (2 * RING)
+            s = jd & (RING - 1)
+            held = jd & (2 * RING - 1)
 
             @pl.when(z < top)
             def _():
@@ -1432,7 +1551,7 @@
 
         @pl.when((jf >= 0) & (jf <= last))
         def _():
-            fs[jf % RING] = zp[jf % (2 * RING), z]
+            fs[jf & (RING - 1)] = zp[jf & (2 * RING - 1), z]
             f_copy(jf).start()
 
         jo = jf - LAG
@@ -1440,43 +1559,37 @@
         @pl.when((jo >= 0) & (jo <= last))
         def _():
             f_copy(jo).wait()
-            s = jo % RING
-            fs[s, :SUB] = fs[s, :SUB] + fr[s, :SUB]
+            s = jo & (RING - 1)
             mine = pl.ds(pl.multiple_of(c * PIECE, PIECE), PIECE)
             away = pl.ds(pl.multiple_of((1 - c) * PIECE, PIECE), PIECE)
-            cs[s, :, :half] = fs[s, away]
-            own, far_rows = fs[s, SUB:].astype(F32), fr[s, SUB:].astype(F32)
-            cs[s, :, half:] = jnp.where(y == c, far_rows, own).astype(BF)
+            cs[s, y] = fs[s, away]
+            cs[s, 1 - y] = fr[s, away]
             c_copy(jo).start()
-            stage[jo % RING, 0, :, :half] = fs[s, mine].astype(F32)
-
-            @pl.when(jo >= LAG)
-            def _():
-                stage[(jo - LAG) % RING, 0, :, half:] = jnp.where(y == c, own, far_rows)
+            stage[s, y, c] = fs[s, mine].astype(F32)
+            stage[s, 1 - y, c] = fr[s, mine].astype(F32)
 
         jc = jo - LAG
 
         @pl.when((jc >= 0) & (jc <= last))
         def _():
             c_copy(jc).wait()
-            s = jc % RING
-            stage[jc % RING, 1, :, :half] = cr[s, :, :half].astype(F32)
+            s = jc & (RING - 1)
+            stage[s, 0, 1 - c] = cr[s, 0].astype(F32)
+            stage[s, 1, 1 - c] = cr[s, 1].astype(F32)
+
+            def start(number, k):
+                for copy in out_copies(number, k, jc):
+                    copy.start()
+
+            each_job(jc, start)
 
             @pl.when(jc >= LAG)
             def _():
-                chunk = jc - LAG
-                stage[chunk % RING, 1, :, half:] = cr[s, :, half:].astype(F32)
-                store(chunk)
-
-            @pl.when(jc >= 2 * LAG)
-            def _():
-                for copy in out_copies(0, jc - 2 * LAG, 0, 0):
-                    copy.wait()
+                out_wait(jc - LAG)
 
     lax.fori_loop(0, last + LAG * (top + 3) + 1, step, None)
     for back in range(LAG):
-        for copy in out_copies(0, steps - 1 - back, 0, 0):
-            copy.wait()
+        out_wait(last - back)
     for back in range(RING):
         j = last - back
 
@@ -1490,61 +1603,67 @@
 
 
 def sum_over_chips(lefts, works, small, lines, collective_id):
-    shaped, jobs, landing_l, landing_r, outs = [], [], [], [], []
-    for left in lefts:
-        rows, tokens = left.shape
-        shaped.append(left.reshape(2 * lines, 2, rows // (4 * lines), tokens))
-        landing_l.append(jax.ShapeDtypeStruct(shaped[-1].shape, BF))
-    for number, right in works:
-        rows = shaped[number].shape[2]
-        subs, strips = rows // PIECE, right.shape[1] // 2 // STRIP
-        jobs.append((number, subs, strips, subs * strips))
-        landing_r.append(jax.ShapeDtypeStruct((tokens, right.shape[1] // 2), BF))
-        outs.append(jax.ShapeDtypeStruct((rows, right.shape[1]), F32))
-    steps = sum(job[3] for job in jobs)
-    half = STRIP // 2
-    tall = SUB + PIECE
+    S = jax.ShapeDtypeStruct
+    jobs, landing_r, landing_y, outs, sent, early = [], [], [], [], [], []
+    shaped = [own.reshape(2 * lines, 2, own.shape[0] // (4 * lines), own.shape[1]) for own, _ in lefts]
+    crossed = [cross for _, cross in lefts]
+    tokens = shaped[0].shape[-1]
+    for work in works:
+        job = {name: work[name] for name in ("left", "kind", "late", "issue", "ahead")}
+        columns = work["own"].shape[1]
+        width = columns // 4 if job["kind"] == "quarter" else columns // 2
+        height = crossed[job["left"]].shape[2]
+        job["subs"], job["strips"] = height // PIECE, width // STRIP
+        job["total"] = job["subs"] * job["strips"]
+        job["outs"] = []
+        for _ in range(2 if job["kind"] == "pair" else 1):
+            job["outs"].append(len(outs))
+            outs.append(S((shaped[job["left"]].shape[2], columns), F32))
+        landing_r.append(S((tokens, width), BF))
+        if job["late"]:
+            landing_y.append(S((tokens, 2 * width), BF))
+            if job["kind"] == "pair":
+                sent.append(work["cross"])
+        else:
+            early.append(work["cross"])
+        jobs.append(job)
+    steps = sum(job["total"] for job in jobs)
     top = lines - 1
     dma = pltpu.SemaphoreType.DMA
+    ring = lambda *shape: pltpu.VMEM((RING,) + shape, BF)
     scratch = [
-        pltpu.VMEM((2, 2 * lines, 2, PIECE, 2 * tokens), BF),
-        pltpu.VMEM((2, 2 * tokens, STRIP), BF),
-        pltpu.VMEM((RING, 2, lines, tall, half), BF),
-        pltpu.VMEM((RING, lines, tall, half), BF),
-        pltpu.VMEM((RING, 2, 2, lines, PIECE, half), BF),
-        pltpu.VMEM((RING, 2, lines, PIECE, half), BF),
-        pltpu.VMEM((2 * RING, lines, tall, half), BF),
-        pltpu.VMEM((RING, top, tall, half), BF),
-        pltpu.VMEM((RING, top, tall, half), BF),
-        pltpu.VMEM((RING, top, tall, half), BF),
-        pltpu.VMEM((RING, top, tall, half), BF),
-        pltpu.VMEM((RING, tall, half), BF),
-        pltpu.VMEM((RING, tall, half), BF),
-        pltpu.VMEM((RING, PIECE, STRIP), BF),
-        pltpu.VMEM((RING, PIECE, STRIP), BF),
-        pltpu.VMEM((RING, 2, PIECE, STRIP), F32),
+        pltpu.VMEM((2, 2 * lines, 2, max(value.shape[2] for value in crossed), 4 * tokens), BF),
+        pltpu.VMEM((2, 4 * tokens, max(value.shape[1] for value in landing_r)), BF),
+        ring(2, lines, SUB, STRIP), ring(lines, SUB, STRIP),
+        pltpu.VMEM((2 * RING, lines, SUB, STRIP), BF),
+        ring(top, SUB, STRIP), ring(top, SUB, STRIP), ring(top, SUB, STRIP), ring(top, SUB, STRIP),
+        ring(SUB, STRIP), ring(SUB, STRIP), ring(2, PIECE, STRIP), ring(2, PIECE, STRIP),
+        pltpu.VMEM((RING, 2, 2, PIECE, STRIP), F32),
         pltpu.VMEM((5,) + small.shape, F32),
         pltpu.VMEM((5,) + small.shape, F32),
-        dma((2, 2)), dma((2, 2)),
-    ] + [dma((RING,))] * 12 + [
-        dma((RING, 2)), dma((5,)), dma((5,)),
-        dma((len(lefts),)), dma((len(lefts),)), dma((len(works),)), dma((len(works),)),
+        dma((2, 4)), dma((2, 4)),
+    ] + [dma((RING,))] * 10 + [
+        dma((RING, 2, 2)), dma((5,)), dma((5,)),
+        dma((len(lefts), 2)), dma((len(lefts), 2)), dma((len(works), 2)), dma((len(works), 2)),
+        dma((len(works),)), dma((len(works),)),
     ]
     anywhere = pl.BlockSpec(memory_space=pl.ANY)
     inside = pl.BlockSpec(memory_space=pltpu.VMEM)
-    flops = 2 * steps * 2 * lines * SUB * STRIP * 2 * tokens
+    landings = [S(value.shape, BF) for value in crossed] * 2 + landing_r * 2 + landing_y
+    operands = shaped + crossed + [work["own"] for work in works] + sent + early
+    flops = 2 * steps * 2 * lines * SUB * STRIP * 4 * tokens
     got = pl.pallas_call(
-        functools.partial(sum_kernel, jobs, len(lefts), lines),
-        out_shape=tuple(outs) + (jax.ShapeDtypeStruct(small.shape, F32),) + tuple(landing_l) + tuple(landing_r),
-        in_specs=[anywhere] * (len(lefts) + len(works)) + [inside],
-        out_specs=tuple([anywhere] * len(works) + [inside] + [anywhere] * (len(lefts) + len(works))),
+        functools.partial(sum_kernel, jobs, len(lefts), len(outs), lines),
+        out_shape=tuple(outs) + (S(small.shape, F32),) + tuple(landings),
+        in_specs=[anywhere] * len(operands) + [inside],
+        out_specs=tuple([anywhere] * len(outs) + [inside] + [anywhere] * len(landings)),
         scratch_shapes=scratch,
         compiler_params=pltpu.CompilerParams(collective_id=collective_id, has_side_effects=True,
                                              vmem_limit_bytes=VMEM_LIMIT),
-        cost_estimate=pl.CostEstimate(flops=flops, bytes_accessed=steps * 800_000, transcendentals=0),
+        cost_estimate=pl.CostEstimate(flops=flops, bytes_accessed=steps * 1_100_000, transcendentals=0),
         name="sum_over_chips",
-    )(*shaped, *[right for _, right in works], small)
-    return got[:len(works)], got[len(works)]
+    )(*operands, small)
+    return got[:len(outs)], got[len(outs)]
 
 
 def call_plain(kernel, outs, args, smem=0, scratch=(), flops=0, moved=0, name=None):
@@ -1628,22 +1747,37 @@
          shape_of((rows, attquery.shape[1]), F32), shape_of((rows, attkeys.shape[1]), F32)),
         (hidden_two, attgain_f[None, :], attquery, attkeys, attvalues, cosine, sine, querygain_2, keysgain_2),
         flops=2 * rows * width * 2 * width, moved=6 << 20, name="project")
-    got, attended_f, augmented, all_kv = exchange_attend(msg, info, head, rows, 2)
-    (output, grad, grad_low3, send, attended_t, topgain_grad, topnorm_t, topinner_t, gate_top, lift_top) = feed_top(
+    upright = lambda value: value.reshape(devices // 2, 2, value.shape[0] // devices, rows)
+    over_dp = lambda value: lax.ppermute(value, "dp", [(0, 1), (1, 0)])
+    gated_t, normed_one_t = gated.T, normed_one.T
+    msg, gated_y, normed_one_y, cotangent_y = lax.optimization_barrier(
+        (msg, over_dp(gated_t), over_dp(normed_one_t), over_dp(cotangent)))
+    gated_y, normed_one_y = upright(gated_y), upright(normed_one_y)
+    got, attended_f, augmented, all_kv, lowinner_y, lownorm_y = exchange_attend(
+        msg, info, head, rows, [("rows", upright(lowinner_t)), ("whole", upright(lownorm_t))], 2)
+    (output, grad, grad_low3, send, attended_t, topgain_grad, topnorm_t, topinner_t, keep_top, send_top) = feed_top(
         got, hidden_two, attexit, cotangent, topgain_f[None, :], topgate, toplift, topdrop)
-    back_q, back_k = exchange_attend_back(send, info, augmented, attended_f, all_kv, head, rows, 3)
-    rawq_low, rawk_low, rawv_low, grad_two, attgain_grad, querygain_grad, keysgain_grad = call_plain(
+    send, normed_two_y = lax.optimization_barrier((send, over_dp(normed_two_t)))
+    normed_two_y = upright(normed_two_y)
+    back_q, back_k, topinner_y, topnorm_y, attended_y, grad_low3_y = exchange_attend_back(
+        send, info, augmented, attended_f, all_kv, head, rows,
+        [("rows", upright(topinner_t)), ("whole", upright(topnorm_t)), ("whole", upright(attended_t)),
+         ("columns", grad_low3)], 3)
+    back_q, send_top = lax.optimization_barrier((back_q, send_top))
+    top_y_one = over_dp(send_top[:half_rows])
+    rawq_low, keep_kv, send_kv, grad_two, attgain_grad, querygain_grad, keysgain_grad = call_plain(
         functools.partial(project_back_kernel, head),
         (shape_of((rows, attquery.shape[1]), BF), shape_of((rows, attkeys.shape[1]), BF),
          shape_of((rows, attkeys.shape[1]), BF), shape_of((rows, width), F32), shape_of((1, width), F32),
          shape_of((1, LANES), F32), shape_of((1, LANES), F32)),
         (back_q, back_k, hidden_two, attgain_f[None, :], attquery, attkeys, attvalues, cosine, sine, querygain_2, keysgain_2,
          query_raw, key_raw, grad),
-        flops=2 * rows * width * 2 * width, moved=8 << 20, name="project_back")
+        flops=1 << 20, moved=1 << 10, name="project_back")
     fold = lambda value: value.reshape(LANES // head, head).sum(axis=0)
     querygain_grad, keysgain_grad = fold(querygain_grad), fold(keysgain_grad)
-    grad, lowgain_grad, gb_low, grad_low1, gate_low, lift_low = feed_low_back(
+    grad, lowgain_grad, gb_low, grad_low1, keep_low, send_low = feed_low_back(
         grad_two, hidden_one, lowgain_f[None, :], gact_low, lact_low, lowgate, lowlift, lowdrop)
+    grad, grad_low1, top_y_one = lax.optimization_barrier((grad, grad_low1, top_y_one))
     gated_grad = outer_dot(grad_low1, mixexit)
     part_c_grad = gated_grad * conved
     conved_grad = gated_grad * part_c
@@ -1655,16 +1789,27 @@
         [product_grad * part_x, part_c_grad, product_grad * part_b], axis=1).astype(BF)
     hidden_grad, mixgain_grad = norm_back(outer_dot(mixed_grad, mixentry), hidden, mixgain_f)
     tokens_grad = grad + hidden_grad
-
-    lefts = [attended_t, normed_two_t, topinner_t, topnorm_t, lowinner_t, lownorm_t, gated.T, normed_one.T]
-    works = [(0, grad_low3), (1, rawq_low), (1, rawk_low), (1, rawv_low), (2, cotangent), (3, gate_top),
-             (3, lift_top), (4, gb_low), (5, gate_low), (5, lift_low), (6, grad_low1), (7, mixed_grad)]
+    mixgain_grad, tokens_grad, top_y_two = lax.optimization_barrier(
+        (mixgain_grad, tokens_grad, over_dp(send_top[half_rows:])))
+    top_y = jnp.concatenate([top_y_one, top_y_two], axis=0)
+
+    lefts = [(attended_t, attended_y), (topinner_t, topinner_y), (topnorm_t, topnorm_y), (normed_two_t, normed_two_y),
+             (lowinner_t, lowinner_y), (lownorm_t, lownorm_y), (gated_t, gated_y), (normed_one_t, normed_one_y)]
+
+    def work(left, kind, own, cross=None, issue=-1, ahead=12):
+        return dict(left=left, kind=kind, own=own, cross=cross, late=issue >= 0, issue=issue, ahead=ahead)
+
+    works = [work(0, "quarter", grad_low3, grad_low3_y), work(1, "drop", cotangent, cotangent_y),
+             work(2, "pair", keep_top, top_y), work(3, "quarter", rawq_low, issue=0),
+             work(3, "pair", keep_kv, send_kv, issue=5), work(4, "drop", gb_low, issue=10),
+             work(5, "pair", keep_low, send_low, issue=20), work(6, "quarter", grad_low1, issue=68),
+             work(7, "quarter", mixed_grad, issue=73)]
     heads = jnp.concatenate([querygain_grad, keysgain_grad, jnp.zeros((width - 2 * head,), F32)])
     small = jnp.concatenate([mixgain_grad[None, :], mixtaps_grad, lowgain_grad, attgain_grad, topgain_grad,
                              heads[None, :]], axis=0)
     grads, small = sum_over_chips(lefts, works, small, lines, 1)
-    (attexit_grad, attquery_grad, attkeys_grad, attvalues_grad, topdrop_grad, topgate_grad, toplift_grad,
-     lowdrop_grad, lowgate_grad, lowlift_grad, mixexit_grad, mixentry_grad) = grads
+    (attexit_grad, topdrop_grad, topgate_grad, toplift_grad, attquery_grad, attkeys_grad, attvalues_grad, lowdrop_grad,
+     lowgate_grad, lowlift_grad, mixexit_grad, mixentry_grad) = grads
     return (output, tokens_grad, small[0], mixentry_grad, small[1:4], mixexit_grad, small[4], lowgate_grad,
             lowlift_grad, lowdrop_grad, small[5], attquery_grad, attkeys_grad, attvalues_grad, small[7, :head],
             small[7, head:2 * head], attexit_grad, small[6], topgate_grad, toplift_grad, topdrop_grad)

time: 588 us -> 510 us (0.87)
  Pallas kernels: 519 us -> 425 us
  local copies, waits for them, and re-layouts: 26.8 us -> 35 us
  starting transfers between devices: 3.9 us -> 9.99 us
    pallas_call x1, Pallas kernels: 319 us -> 224 us  [sum_over_chips(): pl.pallas_call(functools.partial(sum_kernel, jobs, len(lefts), len(outs),...]
    pallas_call x1, Pallas kernels: 44.3 us -> 53.1 us  [exchange_attend(): pl.pallas_call(functools.partial(attend_kernel, head, rows, keys, sources...]
    pallas_call x1, Pallas kernels: 77.3 us -> 69.9 us  [exchange_attend_back(): pl.pallas_call(functools.partial(attend_back_kernel, head, rows, keys, so...]
    ppermute x0 -> x6, starting transfers between devices: none -> 7.11 us  [fast_device(): over_dp = lambda value: lax.ppermute(value, 'dp', [(0, 1), (1, 0)])]
    unnamed x86 -> x72, local copies, waits for them, and re-layouts: 14.9 us -> 16.1 us
  transfers between devices with their start and end apart: 2 -> 8, of which waited for: 0 -> 1; matrix products, arithmetic and copies ran while one was open for 2% -> 8% of each run, Pallas kernels for 0% -> 26%
where the time goes in v4:
time: 510 us; the launch traced here: 509 us
  Pallas kernels  425 us (83%)
  local copies, waits for them, and re-layouts  35 us (7%)
  other arithmetic  23.4 us (5%)
  matrix products  11.6 us (2%)
  starting transfers between devices  9.99 us (2%)
    pallas_call x1, Pallas kernels, sum_over_chips(): pl.pallas_call(functools.partial(sum_kernel, jobs, len(lefts), len(outs),...  224 us
    pallas_call x1, Pallas kernels, exchange_attend_back(): pl.pallas_call(functools.partial(attend_back_kernel, head, rows, keys, so...  69.9 us
    pallas_call x3, Pallas kernels, call_tiled(): pl.pallas_call(kernel, grid=(tiles,), in_specs=[spec for _, spec in ins],...  63.2 us
    pallas_call x1, Pallas kernels, exchange_attend(): pl.pallas_call(functools.partial(attend_kernel, head, rows, keys, sources...  53.1 us
    unnamed x72, local copies, waits for them, and re-layouts  16.1 us
    pallas_call x2, Pallas kernels, call_plain(): pl.pallas_call(kernel, out_shape=tuple(outs) if many else outs, in_specs=...  15.6 us
  transfers between devices with their start and end apart: 8, of which 1 were waited for; matrix products, arithmetic and copies ran while one was open for 8% of the time, Pallas kernels for 26%

profile of v4, /device:TPU:0, one launch (start us, length us, event | category | flops | bytes accessed | tf_op | source)
XLA Modules:
  0.0 509.3 jit_solution(4654985062752194766)
XLA Ops:
  0.7 1.4 fusion.10
  2.7 2.1 fusion.11
  4.8 3.0 collective-permute-start.2
  7.8 4.8 fusion.12
  12.7 1.6 copy-done.1
  14.5 0.8 copy-done.6
  15.3 1.5 collective-permute-start
  20.0 1.2 fusion.14
  21.3 1.2 pad_add_fusion.3.refs_0_
  25.5 1.2 maximum_convert_fusion
  26.7 2.7 multiply_convert_fusion.3
  29.4 1.8 collective-permute-start.1
  31.3 1.7 convert_add_fusion.hid_ref
  33.0 16.2 %feed_low.1 = (f32[256,1024]{1,0:T(8,128)}, bf16[1024,256]{1,0:T(8,128)(2,1)}, bf16[256,4608]{1,0:T(8,128)(2,1)}, bf16[256,4608]{1,0:T(8,128)(2,1)}, bf16[4608,256]{1,0:T(8,128)(2,1)}) custom-call(f32[256,1024]{1,0:T(8,128)} %convert_add_fusion.hid_ref, f32[1,1024]{1,0:T(1,128)} %bitcast.57, bf16[1024,4608]{1,0:T(8,128)(2,1)} %gate_ref.5, ...), custom_call_target="tpu_custom_call" | custom-call | flops 7247757312 | bytes 39845888 | tf_op jit(solution)/shard_map/feed_low/pallas_call | solution.py:798
  49.1 6.4 %project.1 = (bf16[16,128,256]{2,1,0:T(8,128)(2,1)}, bf16[1024,256]{1,0:T(8,128)(2,1)}, f32[256,1024]{1,0:T(8,128)}, f32[256,512]{1,0:T(8,128)}) custom-call(f32[256,1024]{1,0:T(8,128)} %get-tuple-element.104.hid_ref.two_ref, f32[1,1024]{1,0:T(1,128)} %bitcast.55, bf16[1024,1024]{1,0:T(8,128)(2,1)} %wq_ref.3, bf16[1024,512]{1,0:T(8,128)(2,1)} %wk_ref.3, ...), custom_call_target="tpu_custom_call" | custom-call | flops 1073741824 | bytes 6291456 | tf_op jit(solution)/shard_map/project/pallas_call | solution.py:1672
  55.8 53.1 %attend.1 = (bf16[16,128,128]{2,1,0:T(8,128)(2,1)}, f32[16,128,128]{2,1,0:T(8,128)}, bf16[16,2,128,128]{3,2,1,0:T(8,128)(2,1)}, bf16[4096,128]{1,0:T(8,128)(2,1)...) custom-call(s32[2]{0:T(128)} %pad_add_fusion.3.refs_0_, ...), custom_call_target="tpu_custom_call" | custom-call | flops 4294967296 | bytes 6291456 | tf_op jit(solution)/shard_map/attend/pallas_call | solution.py:1188
  108.9 27.7 %feed_top.1 = (f32[256,1024]{1,0:T(8,128)}, f32[256,1024]{1,0:T(8,128)}, bf16[256,1024]{1,0:T(8,128)(2,1)}, bf16[16,128,128]{2,1,0:T(8,128)(2,1)}, bf16[1024,256...) custom-call(bf16[16,128,128]{2,1,0:T(8,128)(2,1)} %get-tuple-element, ...), custom_call_target="tpu_custom_call" | custom-call | flops 14495514624 | bytes 47185920 | tf_op jit(solution)/shard_map/feed_top/pallas_call | solution.py:798
  136.6 69.9 %attend_back.1 = (bf16[16,128,128]{2,1,0:T(8,128)(2,1)}, bf16[16,128,128]{2,1,0:T(8,128)(2,1)}, bf16[8,2,144,256]{3,2,1,0:T(8,128)(2,1)}, bf16[8,2,64,256]{3,2,1...) custom-call(s32[2]{0:T(128)} %pad_add_fusion.3.refs_0_, ...), custom_call_target="tpu_custom_call" | custom-call | flops 10737418240 | bytes 8388608 | tf_op jit(solution)/shard_map/attend_back/pallas_call | solution.py:1216
  206.6 3.2 fusion.26
  210.3 2.1 copy.48
  212.3 2.0 copy.47
  214.4 2.0 copy.49
  216.4 2.1 copy.50
  218.5 9.2 %project_back.1 = (bf16[256,1024]{1,0:T(8,128)(2,1)}, bf16[256,512]{1,0:T(8,128)(2,1)}, bf16[256,512]{1,0:T(8,128)(2,1)}, f32[256,1024]{1,0:T(8,128)}, f32[1,102...) custom-call(bf16[16,128,128]{2,1,0:T(8,128)(2,1)} %get-tuple-element.123.backq_ref, ...), custom_call_target="tpu_custom_call" | custom-call | flops 1048576 | bytes 1024 | tf_op jit(solution)/shard_map/project_back/pallas_call | solution.py:1672
  228.2 1.3 reduce.9
  229.5 1.3 reduce.8
  231.0 1.6 collective-permute-start.7
  232.6 19.3 %feed_low_back.1 = (f32[256,1024]{1,0:T(8,128)}, f32[1,1024]{1,0:T(1,128)}, bf16[256,1024]{1,0:T(8,128)(2,1)}, bf16[256,1024]{1,0:T(8,128)(2,1)}, bf16[256,4608]{1,0:T(8,128)(2,1)}, /*index=5*/bf16[256,4608]{1,0:T(8,128)(2,1)}) custom-call(f32[256,1024]{1,0:T(8,128)} %get-tuple-element.128.grad_ref, f32[256,1024]{1,0:T(8,128)} %convert_add_fusion.hid_ref, ...), custom_call_target="tpu_custom_call" | custom-call | flops 1048576 | bytes 1024 | tf_op jit(solution)/shard_map/feed_low_back/pallas_call | solution.py:798
  252.0 3.0 multiply_reduce_fusion.2
  255.7 1.4 collective-permute-start.6
  257.3 1.6 collective-permute-done.6
  260.2 2.0 fusion.6
  262.3 1.3 fusion.9
  263.5 1.3 pad_maximum_fusion.1.refs_24_
  264.8 3.2 pad_maximum_fusion.refs_29_
  268.7 223.6 %sum_over_chips.1 = (f32[64,1024]{1,0:T(8,128)}, f32[288,1024]{1,0:T(8,128)}, f32[64,4608]{1,0:T(8,128)}, f32[64,4608]{1,0:T(8,128)}, f32[64,1024]{1,0:T(8,128)}...) custom-call(bf16[8,2,64,256]{3,2,1,0:T(8,128)(2,1)} %bitcast.79, ...), custom_call_target="tpu_custom_call" | custom-call | flops 18253611008 | bytes 149600000 | tf_op jit(solution)/shard_map/sum_over_chips/pallas_call | solution.py:1655
  492.4 1.4 slice_bitcast_fusion
  493.7 1.4 slice.113
  495.1 1.5 fusion.27
  496.6 2.2 copy.64
  498.8 1.7 copy.65
  500.5 1.0 copy.66
  501.5 1.0 copy.67
  502.5 1.0 copy.68
  503.5 0.7 copy.69
  506.3 1.0 copy.73
  507.3 1.0 copy.74
  508.3 1.0 copy.75
  (104 shorter events, 12.2 us)
Async XLA Ops:
  0.7 30.6 %copy-start = (bf16[1024,1024]{1,0:T(8,128)(2,1)S(1)}, bf16[1024,1024]{1,0:T(8,128)(2,1)}, u32[]{:S(2)}) copy-start(bf16[1024,1024]{1,0:T(8,128)(2,1)} %param.30) | copy-start | bytes 6291460
  4.8 50.9 %collective-permute-start.2 = (bf16[1024,256]{0,1:T(8,128)(2,1)}, bf16[1024,256]{0,1:T(8,128)(2,1)}, u32[]{:S(2)}, u32[]{:S(2)}) collective-permute-start(bf16[1024,256]{0,1:T(8,128)(2,1)} %fusion.11), channel_id=1, source_target_pairs={{0,16},{16,0},{1,17},{17,1},{2,18},{18,2},{3,19},{19,3},{4,20},{20... | collective-permute-start | bytes 1572872 | tf_op jit(solution)/shard_map/ppermute | solution.py:1751
  7.8 48.0 %collective-permute-start.3 = (bf16[256,1024]{1,0:T(8,128)(2,1)}, bf16[256,1024]{1,0:T(8,128)(2,1)}, u32[]{:S(2)}, u32[]{:S(2)}) collective-permute-start(bf16[256,1024]{1,0:T(8,128)(2,1)} %refs_17_.1), channel_id=1, source_target_pairs={{0,16},{16,0},{1,17},{17,1},{2,18},{18,2},{3,19},{19,3},{4,20},{20... | collective-permute-start | bytes 1572872 | tf_op jit(solution)/shard_map/ppermute | solution.py:1751
  12.7 1.6 copy-start.1
  14.3 2.5 copy-start.25
  14.3 5.7 %copy-start.18 = (bf16[3,1024]{1,0:T(4,128)(2,1)S(1)}, bf16[3,1024]{1,0:T(4,128)(2,1)}, u32[]{:S(2)}) copy-start(bf16[3,1024]{1,0:T(4,128)(2,1)} %param.29) | copy-start | bytes 18436
  14.3 8.2 %copy-start.26 = (bf16[64]{0:T(256)(128)(2,1)S(1)}, bf16[64]{0:T(256)(128)(2,1)}, u32[]{:S(2)}) copy-start(bf16[64]{0:T(256)(128)(2,1)} %param.39) | copy-start | bytes 388
  14.3 8.8 %copy-start.27 = (bf16[64]{0:T(256)(128)(2,1)S(1)}, bf16[64]{0:T(256)(128)(2,1)}, u32[]{:S(2)}) copy-start(bf16[64]{0:T(256)(128)(2,1)} %param.40) | copy-start | bytes 388
  14.3 9.4 %copy-start.22 = (bf16[1024]{0:T(1024)(128)(2,1)S(1)}, bf16[1024]{0:T(1024)(128)(2,1)}, u32[]{:S(2)}) copy-start(bf16[1024]{0:T(1024)(128)(2,1)} %param.31) | copy-start | bytes 6148
  14.3 10.0 %copy-start.23 = (bf16[1024]{0:T(1024)(128)(2,1)S(1)}, bf16[1024]{0:T(1024)(128)(2,1)}, u32[]{:S(2)}) copy-start(bf16[1024]{0:T(1024)(128)(2,1)} %param.35) | copy-start | bytes 6148
  14.3 10.6 %copy-start.24 = (bf16[1024]{0:T(1024)(128)(2,1)S(1)}, bf16[1024]{0:T(1024)(128)(2,1)}, u32[]{:S(2)}) copy-start(bf16[1024]{0:T(1024)(128)(2,1)} %param.42) | copy-start | bytes 6148
  14.5 0.8 copy-start.6
  15.3 10.2 %collective-permute-start = (bf16[2,1024]{1,0:T(2,128)(2,1)S(1)}, bf16[2,1024]{1,0:T(2,128)(2,1)S(1)}, u32[]{:S(2)}, u32[]{:S(2)}) collective-permute-start(bf16[2,1024]{1,0:T(2,128)(2,1)S(1)} %slice.123), channel_id=1, source_target_pairs={{0,1},{1,2},{2,3},{3,4},{4,5},{5,6},{6,7},{7,8},{8,9},{9,10},{10,1... | collective-permute-start | bytes 12296 | tf_op jit(solution)/shard_map/ppermute | solution.py:19
  26.7 4.6 copy-start.3
  29.4 3.5 copy-start.5
  29.4 26.3 %collective-permute-start.1 = (bf16[1024,256]{0,1:T(8,128)(2,1)S(1)}, bf16[1024,256]{0,1:T(8,128)(2,1)}, u32[]{:S(2)}, u32[]{:S(2)}) collective-permute-start(bf16[1024,256]{0,1:T(8,128)(2,1)S(1)} %bitcast.43), channel_id=1, source_target_pairs={{0,16},{16,0},{1,17},{17,1},{2,18},{18,2},{3,19},{19,3},{4,20},{20... | collective-permute-start | bytes 1572872 | tf_op jit(solution)/shard_map/ppermute | solution.py:1751
  55.5 81.1 %collective-permute-start.4 = (bf16[1024,256]{1,0:T(8,128)(2,1)}, bf16[1024,256]{1,0:T(8,128)(2,1)}, u32[]{:S(2)}, u32[]{:S(2)}) collective-permute-start(bf16[1024,256]{1,0:T(8,128)(2,1)} %get-tuple-element.115), channel_id=1, source_target_pairs={{0,16},{16,0},{1,17},{17,1},{2,18},{18,2},{3,19},{19,3},{4,20},{20... | collective-permute-start | bytes 1572872 | tf_op jit(solution)/shard_map/ppermute | solution.py:1751
  209.8 42.2 %collective-permute-start.5 = (bf16[128,4608]{1,0:T(8,128)(2,1)}, bf16[128,4608]{1,0:T(8,128)(2,1)}, u32[]{:S(2)}, u32[]{:S(2)}) collective-permute-start(bf16[128,4608]{1,0:T(8,128)(2,1)} %get-tuple-element.186), channel_id=1, source_target_pairs={{0,16},{16,0},{1,17},{17,1},{2,18},{18,2},{3,19},{19,3},{4,20},{20... | collective-permute-start | bytes 3538952 | tf_op jit(solution)/shard_map/ppermute | solution.py:1751
  231.0 33.8 %collective-permute-start.7 = (bf16[128,4608]{1,0:T(8,128)(2,1)}, bf16[128,4608]{1,0:T(8,128)(2,1)}, u32[]{:S(2)}, u32[]{:S(2)}) collective-permute-start(bf16[128,4608]{1,0:T(8,128)(2,1)} %get-tuple-element.185), channel_id=1, source_target_pairs={{0,16},{16,0},{1,17},{17,1},{2,18},{18,2},{3,19},{19,3},{4,20},{20... | collective-permute-start | bytes 3538952 | tf_op jit(solution)/shard_map/ppermute | solution.py:1751
  251.9 7.6 %slice-start = ((s8[6291456]{0:T(1024)(128)(4,1)}), s8[4194304]{0:T(1024)(128)(4,1)S(1)}, s32[]{:S(2)}) async-start(s8[6291456]{0:T(1024)(128)(4,1)} %bitcast.69), calls=%async_computation | async-start | bytes 8388608
  255.2 4.4 slice-start.1
  255.7 3.2 collective-permute-start.6
  257.3 1.9 copy-start.2
  259.2 1.0 copy-start.4
  260.2 2.0 copy-start.13
  264.8 3.2 copy-start.19
  264.8 3.2 copy-start.20
  264.8 3.2 copy-start.21
  492.4 8.1 %copy-start.12 = (f32[64,4608]{1,0:T(8,128)S(1)}, f32[64,4608]{1,0:T(8,128)}, u32[]{:S(2)}) copy-start(f32[64,4608]{1,0:T(8,128)} %get-tuple-element.237) | copy-start | bytes 3538948
  496.6 4.9 copy-start.11
  500.5 2.0 copy-start.10
  501.5 2.0 copy-start.15
  501.5 2.8 copy-start.17
  502.5 2.4 copy-start.16
  502.5 3.0 copy-start.14
  502.5 3.8 copy-start.9
  503.5 3.7 copy-start.8
  506.2 2.0 copy-start.7

commit v5 on v4

--- a/solution.py
+++ b/solution.py
@@ -527,6 +527,10 @@
     return lax.broadcasted_iota(jnp.int32, shape, len(shape) - 1)
 
 
+def row_of(ref):
+    return ref[...].astype(F32).reshape(1, ref.shape[0])
+
+
 def same_head(head):
     row = lax.broadcasted_iota(jnp.int32, (LANES, LANES), 0) // head
     column = lax.broadcasted_iota(jnp.int32, (LANES, LANES), 1) // head
@@ -560,7 +564,7 @@
                    msg_ref, normt_ref, qraw_ref, kraw_ref):
     hid = hid_ref[...]
     scale = lax.rsqrt(jnp.mean(hid * hid, axis=-1, keepdims=True) + EPS)
-    normed = hid * scale * gain_ref[...]
+    normed = hid * scale * row_of(gain_ref)
     normt_ref[...] = turned(normed)
     normed = normed.astype(BF)
     blocks = same_head(head)
@@ -635,7 +639,7 @@
     scale = lax.rsqrt(jnp.mean(hid * hid, axis=-1, keepdims=True) + EPS)
     unit = hid * scale
     again_ref[...] = jnp.sum(normed_grad * unit, axis=0, keepdims=True)
-    inward = normed_grad * gain_ref[...]
+    inward = normed_grad * row_of(gain_ref)
     two_ref[...] = grad_ref[...] + scale * (inward - unit * jnp.mean(inward * unit, axis=-1, keepdims=True))
 
 
@@ -691,7 +695,7 @@
     @pl.when(step == 0)
     def _():
         hid = hid_ref[...]
-        normed = hid * norm_scale(hid) * gain_ref[...]
+        normed = hid * norm_scale(hid) * row_of(gain_ref)
         norm_ref[...] = normed.astype(BF)
         normt_ref[...] = turned(normed)
         out_ref[...] = hid
@@ -723,7 +727,7 @@
 
     @pl.when(step == pl.num_programs(0) - 1)
     def _():
-        back, gain_part = norm_pull(acc_ref[...], hid_ref[...], gain_ref[...])
+        back, gain_part = norm_pull(acc_ref[...], hid_ref[...], row_of(gain_ref))
         again_ref[...] = gain_part
         out = grad_ref[...] + back
         out_ref[...] = out
@@ -731,8 +735,8 @@
 
 
 def top_kernel(got_ref, two_ref, exit_ref, cot_ref, gain_ref, gate_ref, lift_ref, drop_ref,
-               out_ref, grad_ref, gradlow_ref, send_ref, attt_ref, again_ref, normt_ref, innert_ref, glow_ref,
-               llow_ref, hid_ref, norm_ref, acc_ref):
+               out_ref, grad_ref, gradlow_ref, send_ref, attt_ref, again_ref, normt_ref, innert_ref, keep_ref,
+               senda_ref, sendb_ref, hid_ref, norm_ref, acc_ref):
     step = pl.program_id(0)
     half_rows = got_ref.shape[1]
 
@@ -745,7 +749,7 @@
         attt_ref[...] = turned(attended)
         hid = two_ref[...] + nn_dot(attended, exit_ref[...])
         hid_ref[...] = hid
-        normed = hid * norm_scale(hid) * gain_ref[...]
+        normed = hid * norm_scale(hid) * row_of(gain_ref)
         norm_ref[...] = normed.astype(BF)
         normt_ref[...] = turned(normed)
         out_ref[...] = hid
@@ -760,12 +764,13 @@
     out_ref[...] += nn_dot(inner.astype(BF), drop_ref[...])
     inner_grad = nt_dot(cot_ref[...], drop_ref[...])
     gate_low, lift_low = activation_pull(gate_act, lift_act, sigma, inner_grad)
-    glow_ref[...], llow_ref[...] = kept_first(gate_low, lift_low)
+    keep_ref[...], sent_part = kept_first(gate_low, lift_low)
+    senda_ref[...], sendb_ref[...] = sent_part[:half_rows], sent_part[half_rows:]
     acc_ref[...] += nt_dot(gate_low, gate_ref[...]) + nt_dot(lift_low, lift_ref[...])
 
     @pl.when(step == pl.num_programs(0) - 1)
     def _():
-        back, gain_part = norm_pull(acc_ref[...], hid_ref[...], gain_ref[...])
+        back, gain_part = norm_pull(acc_ref[...], hid_ref[...], row_of(gain_ref))
         again_ref[...] = gain_part
         grad = cot_ref[...].astype(F32) + back
         grad_ref[...] = grad
@@ -814,7 +819,7 @@
     S = jax.ShapeDtypeStruct
     return call_tiled(
         low_kernel, ff // WIDE_TILE,
-        [(hidden, whole_block((rows, width))), (gain, whole_block((1, width))), (gate, column_block(width, WIDE_TILE)),
+        [(hidden, whole_block((rows, width))), (gain, whole_block((width,))), (gate, column_block(width, WIDE_TILE)),
          (lift, column_block(width, WIDE_TILE)), (drop, row_block(width, WIDE_TILE))],
         [(S((rows, width), F32), whole_block((rows, width))), (S((width, rows), BF), whole_block((width, rows))),
          (S((rows, ff), BF), column_block(rows, WIDE_TILE)), (S((rows, ff), BF), column_block(rows, WIDE_TILE)),
@@ -829,7 +834,7 @@
     full = whole_block((rows, width))
     return call_tiled(
         low_back_kernel, ff // WIDE_TILE,
-        [(grad, full), (hidden, full), (gain, whole_block((1, width))), (gact, column_block(rows, WIDE_TILE)),
+        [(grad, full), (hidden, full), (gain, whole_block((width,))), (gact, column_block(rows, WIDE_TILE)),
          (lact, column_block(rows, WIDE_TILE)), (gate, column_block(width, WIDE_TILE)), (lift, column_block(width, WIDE_TILE)),
          (drop, row_block(width, WIDE_TILE))],
         [(S((rows, width), F32), full), (S((1, width), F32), whole_block((1, width))), (S((rows, width), BF), full),
@@ -847,13 +852,138 @@
     return call_tiled(
         top_kernel, ff // TILE,
         [(got, whole_block(got.shape)), (two, full), (exit_weight, whole_block(exit_weight.shape)), (cotangent, full),
-         (gain, flat), (gate, column_block(width)), (lift, column_block(width)), (drop, row_block(width))],
+         (gain, whole_block((width,))), (gate, column_block(width)), (lift, column_block(width)), (drop, row_block(width))],
         [(S((rows, width), F32), full), (S((rows, width), F32), full), (S((rows, width), BF), full),
          (S(got.shape, BF), whole_block(got.shape)), (S((width, rows), BF), standing), (S((1, width), F32), flat),
          (S((width, rows), BF), standing), (S((ff, rows), BF), row_block(rows)), (S((rows, ff), BF), column_block(rows)),
-         (S((rows, ff), BF), column_block(rows))],
+         (S((rows // 2, ff), BF), column_block(rows // 2)), (S((rows // 2, ff), BF), column_block(rows // 2))],
         [pltpu.VMEM((rows, width), F32), pltpu.VMEM((rows, width), BF), pltpu.VMEM((rows, width), F32)],
         12 * rows * width * ff, 45 << 20, "feed_top")
+
+
+MIX_TILE = 256
+HALO = 16
+
+
+def shifted(value, steps):
+    return pltpu.roll(value, steps, 0)
+
+
+def mix_kernel(tok_ref, prev_ref, pos_ref, gain_ref, taps_ref, entb_ref, entc_ref, entx_ref, exit_ref,
+               out_ref, normt_ref, gatedt_ref, b_ref, c_ref, x_ref, conv_ref, prod_ref, norm_ref):
+    step = pl.program_id(0)
+
+    @pl.when(step == 0)
+    def _():
+        hid = tok_ref[...].astype(F32)
+        normed = hid * norm_scale(hid) * row_of(gain_ref)
+        norm_ref[HALO:] = normed.astype(BF)
+        normt_ref[...] = turned(normed)
+        before = prev_ref[...].astype(F32)
+        norm_ref[:HALO] = (before * norm_scale(before) * row_of(gain_ref)).astype(BF)
+        out_ref[...] = hid
+
+    taps = taps_ref[...].astype(F32)
+    part_b = nn_dot(norm_ref[...], entb_ref[...])
+    part_x = nn_dot(norm_ref[...], entx_ref[...])
+    part_c = nn_dot(norm_ref[HALO:], entc_ref[...])
+    product = (part_b * part_x).astype(BF)
+    prod_ref[...] = product
+    product = product.astype(F32)
+    one = jnp.where(pos_ref[...] >= 1.0, shifted(product, 1)[HALO:], 0.0)
+    two = jnp.where(pos_ref[...] >= 2.0, shifted(product, 2)[HALO:], 0.0)
+    conved = taps[2:3] * product[HALO:] + taps[1:2] * one + taps[0:1] * two
+    gated = part_c * conved
+    b_ref[...] = part_b[HALO:].astype(BF)
+    c_ref[...] = part_c.astype(BF)
+    x_ref[...] = part_x[HALO:].astype(BF)
+    conv_ref[...] = conved.astype(BF)
+    gatedt_ref[...] = turned(gated)
+    out_ref[...] += nn_dot(gated.astype(BF), exit_ref[...])
+
+
+def mix_back_kernel(grad_ref, low_ref, next_ref, cnext_ref, pos_ref, tok_ref, gain_ref, taps_ref, b_ref, c_ref, x_ref,
+                    conv_ref, prod_ref, entb_ref, entc_ref, entx_ref, exit_ref,
+                    out_ref, again_ref, taps_out_ref, mixed_ref, acc_ref):
+    step = pl.program_id(0)
+    rows, width = grad_ref.shape
+    tile = b_ref.shape[1]
+
+    @pl.when(step == 0)
+    def _():
+        acc_ref[...] = jnp.zeros_like(acc_ref)
+
+    taps = taps_ref[...].astype(F32)
+    lows = jnp.concatenate([low_ref[...], next_ref[...]], axis=0)
+    gated_grad = nt_dot(lows, exit_ref[...])
+    gate = jnp.concatenate([c_ref[...], cnext_ref[...]], axis=0).astype(F32)
+    conved_grad = gated_grad * gate
+    first = jnp.where(pos_ref[...] >= 1.0, conved_grad, 0.0)
+    second = jnp.where(pos_ref[...] >= 2.0, conved_grad, 0.0)
+    ahead_one = shifted(first, rows + HALO - 1)[:rows]
+    ahead_two = shifted(second, rows + HALO - 2)[:rows]
+    own = conved_grad[:rows]
+    product_grad = taps[2:3] * own + taps[1:2] * ahead_one + taps[0:1] * ahead_two
+    product = prod_ref[...].astype(F32)
+    total = lambda value: jnp.sum(value, axis=0, keepdims=True)
+    taps_out_ref[0:1] = total(shifted(product, 2)[HALO:] * second[:rows])
+    taps_out_ref[1:2] = total(shifted(product, 1)[HALO:] * first[:rows])
+    taps_out_ref[2:3] = total(product[HALO:] * own)
+    b_low = (product_grad * x_ref[...].astype(F32)).astype(BF)
+    c_low = (gated_grad[:rows] * conv_ref[...].astype(F32)).astype(BF)
+    x_low = (product_grad * b_ref[...].astype(F32)).astype(BF)
+    for place, value in enumerate((b_low, c_low, x_low)):
+        mixed_ref[:, pl.ds(pl.multiple_of(place * width + step * tile, tile), tile)] = value
+    acc_ref[...] += nt_dot(b_low, entb_ref[...]) + nt_dot(c_low, entc_ref[...]) + nt_dot(x_low, entx_ref[...])
+
+    @pl.when(step == pl.num_programs(0) - 1)
+    def _():
+        back, gain_part = norm_pull(acc_ref[...], tok_ref[...].astype(F32), row_of(gain_ref))
+        again_ref[...] = gain_part
+        out_ref[...] = grad_ref[...] + back
+
+
+def mix_specs(width):
+    tiles = width // MIX_TILE
+    entry = [pl.BlockSpec((width, MIX_TILE), lambda step, part=part: (0, part * tiles + step)) for part in range(3)]
+    return tiles, entry, row_block(width, MIX_TILE)
+
+
+def mix_forward(tokens, before, position, gain, taps, entry, exit_weight):
+    rows, width = tokens.shape
+    tiles, entry_specs, exit_spec = mix_specs(width)
+    S = jax.ShapeDtypeStruct
+    full = whole_block((rows, width))
+    columns = column_block(rows, MIX_TILE)
+    return call_tiled(
+        mix_kernel, tiles,
+        [(tokens, full), (before, whole_block(before.shape)), (position, whole_block(position.shape)),
+         (gain, whole_block((width,))), (taps, column_block(3, MIX_TILE)), *[(entry, spec) for spec in entry_specs],
+         (exit_weight, exit_spec)],
+        [(S((rows, width), F32), full), (S((width, rows), BF), whole_block((width, rows))),
+         (S((width, rows), BF), row_block(rows, MIX_TILE))] + [(S((rows, width), BF), columns)] * 4
+        + [(S((rows + HALO, width), BF), column_block(rows + HALO, MIX_TILE))],
+        [pltpu.VMEM((rows + HALO, width), BF)], 8 * rows * width * width, 12 << 20, "mix")
+
+
+def mix_backward(grad, low, after, gate_after, position, tokens, gain, taps, kept, entry, exit_weight):
+    rows, width = grad.shape
+    tiles, entry_specs, exit_spec = mix_specs(width)
+    S = jax.ShapeDtypeStruct
+    full = whole_block((rows, width))
+    flat = whole_block((1, width))
+    columns = column_block(rows, MIX_TILE)
+    part_b, part_c, part_x, conved, product = kept
+    return call_tiled(
+        mix_back_kernel, tiles,
+        [(grad, full), (low, full), (after, whole_block(after.shape)), (gate_after, column_block(HALO, MIX_TILE)),
+         (position, whole_block(position.shape)), (tokens, full), (gain, whole_block((width,))), (taps, column_block(3, MIX_TILE)),
+         (part_b, columns), (part_c, columns), (part_x, columns), (conved, columns),
+         (product, column_block(rows + HALO, MIX_TILE)), *[(entry, spec) for spec in entry_specs],
+         (exit_weight, exit_spec)],
+        [(S((rows, width), F32), full), (S((1, width), F32), flat), (S((3, width), F32), column_block(3, MIX_TILE)),
+         (S((rows, 3 * width), BF), whole_block((rows, 3 * width)))],
+        [pltpu.VMEM((rows, width), F32)], 8 * rows * width * width, 16 << 20, "mix_back")
 
 
 def sweep_keys(visit, index, tail, part, base, rows, half_rows, keys, sources):
@@ -1234,11 +1364,11 @@
     take = lambda number: [refs.pop(0) for _ in range(number)]
     lefts, lefts_y, rights = take(sides), take(sides), take(count)
     sent = [refs.pop(0) if job["late"] and job["kind"] == "pair" else None for job in jobs]
-    early_y = [None if job["late"] else refs.pop(0) for job in jobs]
+    early_y = [None if job["late"] else take(job["parts"]) for job in jobs]
     (small_ref,) = take(1)
     outs, (small_out,) = take(weights), take(1)
     lefts_s, lefts_ys, rights_s, rights_ys = take(sides), take(sides), take(count), take(count)
-    rights_y = [refs.pop(0) if job["late"] else early for job, early in zip(jobs, early_y)]
+    rights_y = [take(1) if job["late"] else early for job, early in zip(jobs, early_y)]
     (lbuf, rbuf, xp, xr, zp, us, ur, ds_, dr, fs, fr, cs, cr, stage, sm_s, sm_r,
      lsem, rsem, xs, xv, uss, urv, dss, drv, fss, frv, css, crv, osem, sms, smv, els, elv, ers, erv, yrs, yrv) = refs
     steps = sum(job["total"] for job in jobs)
@@ -1305,9 +1435,11 @@
 
     def right_forward(number):
         width = rights_s[number].shape[1]
-        start = pl.multiple_of((1 - c) * width, STRIP)
-        return remote(rights_y[number].at[:, pl.ds(start, width)], rights_ys[number], ers.at[number, 1],
-                      erv.at[number, 1], twin)
+        columns = pl.ds(pl.multiple_of((1 - c) * width, STRIP), width)
+        tall = tokens // len(rights_y[number])
+        return [remote(source.at[:, columns], rights_ys[number].at[pl.ds(part * tall, tall)],
+                       ers.at[number, 1 + part], erv.at[number, 1 + part], twin)
+                for part, source in enumerate(rights_y[number])]
 
     def right_cross(number, piece=None):
         width = 2 * rights_s[number].shape[1]
@@ -1321,9 +1453,9 @@
             inside, size = (piece >> 1) * STRIP, STRIP
         place = pl.ds(pl.multiple_of(inside, STRIP), size)
         if piece is None:
-            landing = rights_y[number]
+            landing = rights_y[number][0]
         else:
-            landing = rights_y[number].at[rows, place]
+            landing = rights_y[number][0].at[rows, place]
         return remote(source.at[rows, pl.ds(pl.multiple_of(start + inside, STRIP), size)], landing,
                       yrs.at[number], yrv.at[number], across_y)
 
@@ -1362,10 +1494,12 @@
                                         lefts_ys[left]]):
             copies.append(pltpu.make_async_copy(
                 source, lbuf.at[s, :, :, pl.ds(0, height), pl.ds(place * tokens, tokens)], lsem.at[s, place]))
-        for place, source in enumerate([rights[number].at[:, own_columns], rights_s[number],
-                                        rights_y[number].at[:, mine], rights_ys[number]]):
+        tall = tokens // len(rights_y[number])
+        pieces = [(0, rights[number].at[:, own_columns]), (tokens, rights_s[number]), (3 * tokens, rights_ys[number])]
+        pieces += [(2 * tokens + part * tall, source.at[:, mine]) for part, source in enumerate(rights_y[number])]
+        for place, (start, source) in enumerate(pieces):
             copies.append(pltpu.make_async_copy(
-                source, rbuf.at[s, pl.ds(place * tokens, tokens), pl.ds(0, width)], rsem.at[s, place]))
+                source, rbuf.at[s, pl.ds(start, source.shape[0]), pl.ds(0, width)], rsem.at[s, place]))
         return copies
 
     def each_job(j, visit):
@@ -1415,7 +1549,8 @@
                 copy.start()
         right_own(number).start()
         if not job["late"]:
-            right_forward(number).start()
+            for copy in right_forward(number):
+                copy.start()
 
     def step(t, _):
         slot = t & (RING - 1)
@@ -1433,7 +1568,8 @@
                 @pl.when(t == begin - job["ahead"])
                 def _(number=number):
                     right_cross(number).wait()
-                    right_forward(number).start()
+                    for copy in right_forward(number):
+                        copy.start()
 
         done, before = [], 0
         for number, job, begin in begins():
@@ -1446,7 +1582,8 @@
                     for copy in left_copies(job["left"]):
                         copy.wait()
                 right_own(number).wait()
-                right_forward(number).wait()
+                for copy in right_forward(number):
+                    copy.wait()
                 for copy in loads(number):
                     copy.start()
 
@@ -1625,7 +1762,8 @@
             if job["kind"] == "pair":
                 sent.append(work["cross"])
         else:
-            early.append(work["cross"])
+            job["parts"] = len(work["cross"])
+            early.extend(work["cross"])
         jobs.append(job)
     steps = sum(job["total"] for job in jobs)
     top = lines - 1
@@ -1641,10 +1779,10 @@
         pltpu.VMEM((RING, 2, 2, PIECE, STRIP), F32),
         pltpu.VMEM((5,) + small.shape, F32),
         pltpu.VMEM((5,) + small.shape, F32),
-        dma((2, 4)), dma((2, 4)),
+        dma((2, 4)), dma((2, 5)),
     ] + [dma((RING,))] * 10 + [
         dma((RING, 2, 2)), dma((5,)), dma((5,)),
-        dma((len(lefts), 2)), dma((len(lefts), 2)), dma((len(works), 2)), dma((len(works), 2)),
+        dma((len(lefts), 2)), dma((len(lefts), 2)), dma((len(works), 3)), dma((len(works), 3)),
         dma((len(works),)), dma((len(works),)),
     ]
     anywhere = pl.BlockSpec(memory_space=pl.ANY)
@@ -1666,6 +1804,48 @@
     return got[:len(outs)], got[len(outs)]
 
 
+def hand_over_kernel(count, head, *refs):
+    sources, small_ref, results = refs[:count], refs[count], refs[count + 1:2 * count + 1]
+    mix_ref, taps_ref, low_ref, att_ref, top_ref, query_ref, keys_ref = refs[2 * count + 1:2 * count + 8]
+    holds, (ins, outs) = refs[2 * count + 8:3 * count + 8], refs[3 * count + 8:]
+    arrive = [pltpu.make_async_copy(source, hold, ins.at[number])
+              for number, (source, hold) in enumerate(zip(sources, holds))]
+    leave = [pltpu.make_async_copy(hold, result, outs.at[number])
+             for number, (hold, result) in enumerate(zip(holds, results))]
+    for copy in arrive:
+        copy.start()
+    mix_ref[...] = small_ref[0]
+    taps_ref[...] = small_ref[1:4]
+    low_ref[...] = small_ref[4]
+    att_ref[...] = small_ref[5]
+    top_ref[...] = small_ref[6]
+    query_ref[...] = small_ref[7, :head]
+    keys_ref[...] = small_ref[7, LANES:LANES + head]
+    for first, then in zip(arrive, leave):
+        first.wait()
+        then.start()
+    for copy in leave:
+        copy.wait()
+
+
+def hand_over(grads, small, head):
+    count, width = len(grads), small.shape[1]
+    S = jax.ShapeDtypeStruct
+    anywhere = [pl.BlockSpec(memory_space=pl.ANY)] * count
+    smalls = (S((width,), F32), S((3, width), F32), S((width,), F32), S((width,), F32), S((width,), F32),
+              S((head,), F32), S((head,), F32))
+    got = pl.pallas_call(
+        functools.partial(hand_over_kernel, count, head),
+        out_shape=tuple(S(value.shape, F32) for value in grads) + smalls,
+        in_specs=anywhere + vmem_specs(1),
+        out_specs=tuple(anywhere + vmem_specs(len(smalls))),
+        scratch_shapes=[pltpu.VMEM(value.shape, F32) for value in grads] + [pltpu.SemaphoreType.DMA((count,))] * 2,
+        compiler_params=pltpu.CompilerParams(vmem_limit_bytes=VMEM_LIMIT),
+        name="hand_over",
+    )(*grads, small)
+    return got[:count], got[count:]
+
+
 def call_plain(kernel, outs, args, smem=0, scratch=(), flops=0, moved=0, name=None):
     specs = [pl.BlockSpec(memory_space=pltpu.SMEM)] * smem + vmem_specs(len(args) - smem)
     many = isinstance(outs, (tuple, list))
@@ -1688,14 +1868,6 @@
 def sibling(value):
     count = lax.axis_size("ctx")
     return lax.ppermute(value, "ctx", [(i, i ^ 1) for i in range(count)])
-
-
-def norm_back(grad, hidden, gain):
-    scale = lax.rsqrt(jnp.mean(hidden * hidden, axis=-1, keepdims=True) + EPS)
-    unit = hidden * scale
-    inward = grad * gain
-    gain_grad = jnp.sum(grad * unit, axis=0)
-    return scale * (inward - unit * jnp.mean(inward * unit, axis=-1, keepdims=True)), gain_grad
 
 
 def fast_device(tokens, lengths, cotangent, mixgain, mixentry, mixtaps, mixexit, lowgain, lowgate, lowlift,
@@ -1714,9 +1886,6 @@
     my_seg = segment_of(mine, first, second)
     begin = jnp.where(my_seg == 0, 0, jnp.where(my_seg == 1, first, second))
     position = (mine - begin).astype(F32)
-    gains = [value.astype(F32) for value in (mixgain, lowgain, attgain, topgain)]
-    mixgain_f, lowgain_f, attgain_f, topgain_f = gains
-    taps_f = mixtaps.astype(F32)
     twice = lambda gain: jnp.tile(gain.astype(F32), LANES // head)[None, :]
     querygain_2, keysgain_2 = twice(querygain), twice(keysgain)
     spot = jnp.arange(LANES, dtype=jnp.int32) % (head // 2)
@@ -1725,73 +1894,59 @@
     sine = jnp.sin(angle) * jnp.where(jnp.arange(LANES) % head < head // 2, -1.0, 1.0)[None, :]
     info = jnp.stack([first, second]).astype(jnp.int32)
 
-    hidden = tokens.astype(F32)
-    normed_one = root_mean_square_scale(hidden, mixgain_f).astype(BF)
-    mixed = jnp.dot(normed_one, mixentry, preferred_element_type=F32)
-    part_b, part_c, part_x = (mixed[:, i * width:(i + 1) * width] for i in range(3))
-    product = (part_b * part_x).astype(BF)
-    borrowed = passed_along(product[rows - 2:], "ctx", 1)
-    extended = jnp.concatenate([borrowed, product], axis=0).astype(F32)
-    fits_one = ((mine >= 1) & (segment_of(mine - 1, first, second) == my_seg)).astype(F32)[:, None]
-    fits_two = ((mine >= 2) & (segment_of(mine - 2, first, second) == my_seg)).astype(F32)[:, None]
-    conved = conv_local(extended, taps_f, fits_one, fits_two)
-    gated = (part_c * conved).astype(BF)
-    hidden_one = hidden + jnp.dot(gated, mixexit, preferred_element_type=F32)
+    before = passed_along(tokens[rows - HALO:], "ctx", 1)
+    spot_of = lambda where: (where - jnp.where(where >= second, second, jnp.where(where >= first, first, 0))).astype(F32)
+    (hidden_one, normed_one_t, gated_t, part_b, part_c, part_x, conved, product) = mix_forward(
+        tokens, before, position[:, None], mixgain, mixtaps, mixentry, mixexit)
+    gate_after = passed_along(part_c[:HALO], "ctx", -1)
     hidden_two, lownorm_t, gact_low, lact_low, lowinner_t = feed_low(
-        hidden_one, lowgain_f[None, :], lowgate, lowlift, lowdrop)
+        hidden_one, lowgain, lowgate, lowlift, lowdrop)
 
     heads_q, heads_k = attquery.shape[1] // head, attkeys.shape[1] // head
     msg, normed_two_t, query_raw, key_raw = call_plain(
         functools.partial(project_kernel, head),
         (shape_of((devices, half_rows, 2 * LANES), BF), shape_of((width, rows), BF),
          shape_of((rows, attquery.shape[1]), F32), shape_of((rows, attkeys.shape[1]), F32)),
-        (hidden_two, attgain_f[None, :], attquery, attkeys, attvalues, cosine, sine, querygain_2, keysgain_2),
+        (hidden_two, attgain, attquery, attkeys, attvalues, cosine, sine, querygain_2, keysgain_2),
         flops=2 * rows * width * 2 * width, moved=6 << 20, name="project")
     upright = lambda value: value.reshape(devices // 2, 2, value.shape[0] // devices, rows)
     over_dp = lambda value: lax.ppermute(value, "dp", [(0, 1), (1, 0)])
-    gated_t, normed_one_t = gated.T, normed_one.T
-    msg, gated_y, normed_one_y, cotangent_y = lax.optimization_barrier(
-        (msg, over_dp(gated_t), over_dp(normed_one_t), over_dp(cotangent)))
+    msg, gated_y, normed_one_y, cotangent_y, gate_after = lax.optimization_barrier(
+        (msg, over_dp(gated_t), over_dp(normed_one_t), over_dp(cotangent), gate_after))
     gated_y, normed_one_y = upright(gated_y), upright(normed_one_y)
     got, attended_f, augmented, all_kv, lowinner_y, lownorm_y = exchange_attend(
         msg, info, head, rows, [("rows", upright(lowinner_t)), ("whole", upright(lownorm_t))], 2)
-    (output, grad, grad_low3, send, attended_t, topgain_grad, topnorm_t, topinner_t, keep_top, send_top) = feed_top(
-        got, hidden_two, attexit, cotangent, topgain_f[None, :], topgate, toplift, topdrop)
+    (output, grad, grad_low3, send, attended_t, topgain_grad, topnorm_t, topinner_t, keep_top, send_top_a,
+     send_top_b) = feed_top(
+        got, hidden_two, attexit, cotangent, topgain, topgate, toplift, topdrop)
     send, normed_two_y = lax.optimization_barrier((send, over_dp(normed_two_t)))
     normed_two_y = upright(normed_two_y)
     back_q, back_k, topinner_y, topnorm_y, attended_y, grad_low3_y = exchange_attend_back(
         send, info, augmented, attended_f, all_kv, head, rows,
         [("rows", upright(topinner_t)), ("whole", upright(topnorm_t)), ("whole", upright(attended_t)),
          ("columns", grad_low3)], 3)
-    back_q, send_top = lax.optimization_barrier((back_q, send_top))
-    top_y_one = over_dp(send_top[:half_rows])
+    back_q, send_top_a, send_top_b = lax.optimization_barrier((back_q, send_top_a, send_top_b))
+    top_y_one = over_dp(send_top_a)
     rawq_low, keep_kv, send_kv, grad_two, attgain_grad, querygain_grad, keysgain_grad = call_plain(
         functools.partial(project_back_kernel, head),
         (shape_of((rows, attquery.shape[1]), BF), shape_of((rows, attkeys.shape[1]), BF),
          shape_of((rows, attkeys.shape[1]), BF), shape_of((rows, width), F32), shape_of((1, width), F32),
          shape_of((1, LANES), F32), shape_of((1, LANES), F32)),
-        (back_q, back_k, hidden_two, attgain_f[None, :], attquery, attkeys, attvalues, cosine, sine, querygain_2, keysgain_2,
+        (back_q, back_k, hidden_two, attgain, attquery, attkeys, attvalues, cosine, sine, querygain_2, keysgain_2,
          query_raw, key_raw, grad),
         flops=1 << 20, moved=1 << 10, name="project_back")
     fold = lambda value: value.reshape(LANES // head, head).sum(axis=0)
     querygain_grad, keysgain_grad = fold(querygain_grad), fold(keysgain_grad)
     grad, lowgain_grad, gb_low, grad_low1, keep_low, send_low = feed_low_back(
-        grad_two, hidden_one, lowgain_f[None, :], gact_low, lact_low, lowgate, lowlift, lowdrop)
+        grad_two, hidden_one, lowgain, gact_low, lact_low, lowgate, lowlift, lowdrop)
     grad, grad_low1, top_y_one = lax.optimization_barrier((grad, grad_low1, top_y_one))
-    gated_grad = outer_dot(grad_low1, mixexit)
-    part_c_grad = gated_grad * conved
-    conved_grad = gated_grad * part_c
-    _, pull_conv = jax.vjp(lambda ext, taps: conv_local(ext, taps, fits_one, fits_two), extended, taps_f)
-    extended_grad, mixtaps_grad = pull_conv(conved_grad)
-    returned_rim = passed_along(extended_grad[:2], "ctx", -1)
-    product_grad = extended_grad[2:].at[rows - 2:].add(returned_rim)
-    mixed_grad = jnp.concatenate(
-        [product_grad * part_x, part_c_grad, product_grad * part_b], axis=1).astype(BF)
-    hidden_grad, mixgain_grad = norm_back(outer_dot(mixed_grad, mixentry), hidden, mixgain_f)
-    tokens_grad = grad + hidden_grad
+    ext = place * rows + jnp.arange(rows + HALO, dtype=jnp.int32)
+    after = passed_along(grad_low1[:HALO], "ctx", -1)
+    tokens_grad, mixgain_grad, mixtaps_grad, mixed_grad = mix_backward(
+        grad, grad_low1, after, gate_after, spot_of(ext)[:, None], tokens, mixgain, mixtaps,
+        (part_b, part_c, part_x, conved, product), mixentry, mixexit)
     mixgain_grad, tokens_grad, top_y_two = lax.optimization_barrier(
-        (mixgain_grad, tokens_grad, over_dp(send_top[half_rows:])))
-    top_y = jnp.concatenate([top_y_one, top_y_two], axis=0)
+        (mixgain_grad, tokens_grad, over_dp(send_top_b)))
 
     lefts = [(attended_t, attended_y), (topinner_t, topinner_y), (topnorm_t, topnorm_y), (normed_two_t, normed_two_y),
              (lowinner_t, lowinner_y), (lownorm_t, lownorm_y), (gated_t, gated_y), (normed_one_t, normed_one_y)]
@@ -1799,20 +1954,22 @@
     def work(left, kind, own, cross=None, issue=-1, ahead=12):
         return dict(left=left, kind=kind, own=own, cross=cross, late=issue >= 0, issue=issue, ahead=ahead)
 
-    works = [work(0, "quarter", grad_low3, grad_low3_y), work(1, "drop", cotangent, cotangent_y),
-             work(2, "pair", keep_top, top_y), work(3, "quarter", rawq_low, issue=0),
+    works = [work(0, "quarter", grad_low3, (grad_low3_y,)), work(1, "drop", cotangent, (cotangent_y,)),
+             work(2, "pair", keep_top, (top_y_one, top_y_two)), work(3, "quarter", rawq_low, issue=0),
              work(3, "pair", keep_kv, send_kv, issue=5), work(4, "drop", gb_low, issue=10),
              work(5, "pair", keep_low, send_low, issue=20), work(6, "quarter", grad_low1, issue=68),
              work(7, "quarter", mixed_grad, issue=73)]
-    heads = jnp.concatenate([querygain_grad, keysgain_grad, jnp.zeros((width - 2 * head,), F32)])
-    small = jnp.concatenate([mixgain_grad[None, :], mixtaps_grad, lowgain_grad, attgain_grad, topgain_grad,
+    heads = jnp.concatenate([querygain_grad, jnp.zeros((LANES - head,), F32), keysgain_grad, jnp.zeros((width - LANES - head,), F32)])
+    small = jnp.concatenate([mixgain_grad, mixtaps_grad, lowgain_grad, attgain_grad, topgain_grad,
                              heads[None, :]], axis=0)
     grads, small = sum_over_chips(lefts, works, small, lines, 1)
+    grads, smalls = hand_over(grads, small, head)
     (attexit_grad, topdrop_grad, topgate_grad, toplift_grad, attquery_grad, attkeys_grad, attvalues_grad, lowdrop_grad,
      lowgate_grad, lowlift_grad, mixexit_grad, mixentry_grad) = grads
-    return (output, tokens_grad, small[0], mixentry_grad, small[1:4], mixexit_grad, small[4], lowgate_grad,
-            lowlift_grad, lowdrop_grad, small[5], attquery_grad, attkeys_grad, attvalues_grad, small[7, :head],
-            small[7, head:2 * head], attexit_grad, small[6], topgate_grad, toplift_grad, topdrop_grad)
+    (mixgain_grad, mixtaps_grad, lowgain_grad, attgain_grad, topgain_grad, querygain_grad, keysgain_grad) = smalls
+    return (output, tokens_grad, mixgain_grad, mixentry_grad, mixtaps_grad, mixexit_grad, lowgain_grad, lowgate_grad,
+            lowlift_grad, lowdrop_grad, attgain_grad, attquery_grad, attkeys_grad, attvalues_grad, querygain_grad,
+            keysgain_grad, attexit_grad, topgain_grad, topgate_grad, toplift_grad, topdrop_grad)
 
 
 def solution(mesh):

time: 510 us -> 492 us (0.965)
  Pallas kernels: 425 us -> 454 us
  local copies, waits for them, and re-layouts: 35 us -> 9.54 us
  other arithmetic: 23.4 us -> 8.59 us
  matrix products: 11.6 us -> 0 us
    pallas_call x3 -> x5, Pallas kernels: 63.2 us -> 82.2 us  [call_tiled(): pl.pallas_call(kernel, grid=(tiles,), in_specs=[spec for _, spec in ins],...]
    unnamed x72 -> x26, local copies, waits for them, and re-layouts: 16.1 us -> 1.28 us
    dot_general x4 -> x0, matrix products: 11.6 us -> none  [the longest x2 5.02 us: outer_dot(): lax.dot_general(left, right, (((1,), (1,)), ((), ())), preferred_element_...]
    pallas_call x0 -> x1, Pallas kernels: none -> 8.27 us  [hand_over(): pl.pallas_call(functools.partial(hand_over_kernel, count, head), out_shap...]
  transfers between devices with their start and end apart: 8 -> 9, of which waited for: 1 -> 3; matrix products, arithmetic and copies ran while one was open for 8% -> 3% of each run, Pallas kernels for 26% -> 31%
where the time goes in v5:
time: 492 us; the launch traced here: 491 us
  Pallas kernels  454 us (92%)
  starting transfers between devices  11.8 us (2%)
  local copies, waits for them, and re-layouts  9.54 us (2%)
  other arithmetic  8.59 us (2%)
  waiting for transfers between devices  5.29 us (1%)
    pallas_call x1, Pallas kernels, sum_over_chips(): pl.pallas_call(functools.partial(sum_kernel, jobs, len(lefts), len(outs),...  222 us
    pallas_call x5, Pallas kernels, call_tiled(): pl.pallas_call(kernel, grid=(tiles,), in_specs=[spec for _, spec in ins],...  82.2 us
    pallas_call x1, Pallas kernels, exchange_attend_back(): pl.pallas_call(functools.partial(attend_back_kernel, head, rows, keys, so...  71.9 us
    pallas_call x1, Pallas kernels, exchange_attend(): pl.pallas_call(functools.partial(attend_kernel, head, rows, keys, sources...  53.2 us
    pallas_call x2, Pallas kernels, call_plain(): pl.pallas_call(kernel, out_shape=tuple(outs) if many else outs, in_specs=...  15.5 us
  transfers between devices with their start and end apart: 9, of which 3 were waited for; matrix products, arithmetic and copies ran while one was open for 3% of the time, Pallas kernels for 31%

profile of v5, /device:TPU:0, one launch (start us, length us, event | category | flops | bytes accessed | tf_op | source)
XLA Modules:
  0.0 491.1 jit_solution(11647838100627038108)
XLA Ops:
  0.7 0.8 slice.17
  1.4 2.3 collective-permute-start
  3.8 2.4 collective-permute-start.3
  6.2 1.3 fusion.14
  8.8 0.7 fusion.9
  9.5 1.4 subtract_convert_fusion.1.pos_ref
  10.8 1.2 fusion.2
  12.1 1.2 pad_add_fusion.refs_0_
  13.3 0.7 tile.4
  14.0 0.6 broadcast_in_dim_tile.6.qg_ref
  14.6 0.7 tile.5
  15.2 0.6 broadcast_in_dim_tile.7.kg_ref
  15.8 0.6 copy-done.1
  16.4 8.5 %mix.1 = (f32[256,1024]{1,0:T(8,128)}, bf16[1024,256]{1,0:T(8,128)(2,1)}, bf16[1024,256]{1,0:T(8,128)(2,1)}, bf16[256,1024]{1,0:T(8,128)(2,1)}, bf16[256,1024]{1...) custom-call(bf16[256,1024]{1,0:T(8,128)(2,1)} %tok_ref.3, ...), custom_call_target="tpu_custom_call" | custom-call | flops 2147483648 | bytes 12582912 | tf_op jit(solution)/shard_map/mix/pallas_call | solution.py:803
  24.9 0.8 slice.18
  25.7 1.5 collective-permute-start.4
  27.1 0.1 collective-permute-start.1
  27.2 2.0 collective-permute-start.2
  29.2 16.0 %feed_low.1 = (f32[256,1024]{1,0:T(8,128)}, bf16[1024,256]{1,0:T(8,128)(2,1)}, bf16[256,4608]{1,0:T(8,128)(2,1)}, bf16[256,4608]{1,0:T(8,128)(2,1)}, bf16[4608,256]{1,0:T(8,128)(2,1)}) custom-call(f32[256,1024]{1,0:T(8,128)} %get-tuple-element.126.hid_ref, bf16[1024]{0:T(1024)(128)(2,1)} %gain_ref.12, bf16[1024,4608]{1,0:T(8,128)(2,1)} %gate_ref.5, ...), custom_call_target="tpu_custom_call" | custom-call | flops 7247757312 | bytes 39845888 | tf_op jit(solution)/shard_map/feed_low/pallas_call | solution.py:803
  45.2 6.4 %project.1 = (bf16[16,128,256]{2,1,0:T(8,128)(2,1)}, bf16[1024,256]{1,0:T(8,128)(2,1)}, f32[256,1024]{1,0:T(8,128)}, f32[256,512]{1,0:T(8,128)}) custom-call(f32[256,1024]{1,0:T(8,128)} %get-tuple-element.127.hid_ref.two_ref, bf16[1024]{0:T(1024)(128)(2,1)} %gain_ref.11, bf16[1024,1024]{1,0:T(8,128)(2,1)} %wq_ref.3, bf16[1024,512]{1,0:T(8,128)(2,1)} %wk_ref.3, ...), custom_call_target="tpu_custom_call" | custom-call | flops 1073741824 | bytes 6291456 | tf_op jit(solution)/shard_map/project/pallas_call | solution.py:1852
  51.6 0.1 collective-permute-start.5
  51.7 0.0 collective-permute-done.4.cnext_ref
  51.7 0.5 collective-permute-done.2
  52.3 53.2 %attend.1 = (bf16[16,128,128]{2,1,0:T(8,128)(2,1)}, f32[16,128,128]{2,1,0:T(8,128)}, bf16[16,2,128,128]{3,2,1,0:T(8,128)(2,1)}, bf16[4096,128]{1,0:T(8,128)(2,1)...) custom-call(s32[2]{0:T(128)} %pad_add_fusion.refs_0_, ...), custom_call_target="tpu_custom_call" | custom-call | flops 4294967296 | bytes 6291456 | tf_op jit(solution)/shard_map/attend/pallas_call | solution.py:1318
  105.5 27.4 %feed_top.1 = (f32[256,1024]{1,0:T(8,128)}, f32[256,1024]{1,0:T(8,128)}, bf16[256,1024]{1,0:T(8,128)(2,1)}, bf16[16,128,128]{2,1,0:T(8,128)(2,1)}, bf16[1024,256...) custom-call(bf16[16,128,128]{2,1,0:T(8,128)(2,1)} %get-tuple-element, ...), custom_call_target="tpu_custom_call" | custom-call | flops 14495514624 | bytes 47185920 | tf_op jit(solution)/shard_map/feed_top/pallas_call | solution.py:803
  132.9 0.0 copy-start.8
  132.9 71.9 %attend_back.1 = (bf16[16,128,128]{2,1,0:T(8,128)(2,1)}, bf16[16,128,128]{2,1,0:T(8,128)(2,1)}, bf16[8,2,144,256]{3,2,1,0:T(8,128)(2,1)}, bf16[8,2,64,256]{3,2,1...) custom-call(s32[2]{0:T(128)} %pad_add_fusion.refs_0_, ...), custom_call_target="tpu_custom_call" | custom-call | flops 10737418240 | bytes 8388608 | tf_op jit(solution)/shard_map/attend_back/pallas_call | solution.py:1346
  204.8 0.6 collective-permute-start.6
  205.4 1.5 collective-permute-start.8
  206.9 1.3 subtract_convert_fusion.pos_ref
  208.2 9.1 %project_back.1 = (bf16[256,1024]{1,0:T(8,128)(2,1)}, bf16[256,512]{1,0:T(8,128)(2,1)}, bf16[256,512]{1,0:T(8,128)(2,1)}, f32[256,1024]{1,0:T(8,128)}, f32[1,102...) custom-call(bf16[16,128,128]{2,1,0:T(8,128)(2,1)} %get-tuple-element.150.backq_ref, ...), custom_call_target="tpu_custom_call" | custom-call | flops 1048576 | bytes 1024 | tf_op jit(solution)/shard_map/project_back/pallas_call | solution.py:1852
  217.4 0.5 broadcast.178
  217.9 1.3 reduce.7
  219.2 1.3 reduce.6
  220.5 0.1 reshape.190
  220.6 0.1 reshape.189
  220.7 19.2 %feed_low_back.1 = (f32[256,1024]{1,0:T(8,128)}, f32[1,1024]{1,0:T(1,128)}, bf16[256,1024]{1,0:T(8,128)(2,1)}, bf16[256,1024]{1,0:T(8,128)(2,1)}, bf16[256,4608]{1,0:T(8,128)(2,1)}, /*index=5*/bf16[256,4608]{1,0:T(8,128)(2,1)}) custom-call(f32[256,1024]{1,0:T(8,128)} %get-tuple-element.155.grad_ref, f32[256,1024]{1,0:T(8,128)} %get-tuple-element.126.hid_ref, ...), custom_call_target="tpu_custom_call" | custom-call | flops 1048576 | bytes 1024 | tf_op jit(solution)/shard_map/feed_low_back/pallas_call | solution.py:803
  240.0 0.0 copy-start.6
  240.0 0.8 slice.19
  240.8 1.3 collective-permute-start.7
  242.1 0.1 pad_maximum_fusion
  242.1 1.7 collective-permute-done.7.next_ref
  243.8 0.6 copy-done.2
  244.5 11.2 %mix_back.1 = (f32[256,1024]{1,0:T(8,128)}, f32[1,1024]{1,0:T(1,128)}, f32[3,1024]{1,0:T(4,128)}, bf16[256,3072]{1,0:T(8,128)(2,1)}) custom-call(f32[256,1024]{1,0:T(8,128)} %get-tuple-element.161.grad_ref, bf16[256,1024]{1,0:T(8,128)(2,1)} %get-tuple-element.162.low_ref.refs_23_, bf16[16,1024]{1,0:T(8,128)(2,1)} %copy-done.2, bf16[16,1024]{1,0:T(8,128)(2,1)} %copy-done, ...), custom_call_target="tpu_custom_call" | custom-call | flops 2147483648 | bytes 16777216 | tf_op jit(solution)/shard_map/mix_back/pallas_call | solution.py:803
  255.6 3.0 collective-permute-done.8.refs_30_
  258.7 1.5 concatenate.7.refs_31_
  260.1 222.5 %sum_over_chips.1 = (f32[64,1024]{1,0:T(8,128)}, f32[288,1024]{1,0:T(8,128)}, f32[64,4608]{1,0:T(8,128)}, f32[64,4608]{1,0:T(8,128)}, f32[64,1024]{1,0:T(8,128)}...) custom-call(bf16[8,2,64,256]{3,2,1,0:T(8,128)(2,1)} %bitcast.30, ...), custom_call_target="tpu_custom_call" | custom-call | flops 18253611008 | bytes 149600000 | tf_op jit(solution)/shard_map/sum_over_chips/pallas_call | solution.py:1793
  482.6 8.3 %hand_over.1 = (f32[64,1024]{1,0:T(8,128)}, f32[288,1024]{1,0:T(8,128)}, f32[64,4608]{1,0:T(8,128)}, f32[64,4608]{1,0:T(8,128)}, f32[64,1024]{1,0:T(8,128)}, /*i...) custom-call(f32[64,1024]{1,0:T(8,128)} %get-tuple-element.199.refs_0, ...), custom_call_target="tpu_custom_call" | custom-call | tf_op jit(solution)/shard_map/hand_over/pallas_call | solution.py:1837
  (32 shorter events, 0.1 us)
Async XLA Ops:
  1.4 14.4 %collective-permute-start = (bf16[16,1024]{1,0:T(8,128)(2,1)S(1)}, bf16[16,1024]{1,0:T(8,128)(2,1)S(1)}, u32[]{:S(2)}, u32[]{:S(2)}) collective-permute-start(bf16[16,1024]{1,0:T(8,128)(2,1)S(1)} %slice.17), channel_id=1, source_target_pairs={{0,1},{1,2},{2,3},{3,4},{4,5},{5,6},{6,7},{7,8},{8,9},{9,10},{10,1... | collective-permute-start | bytes 98312 | tf_op jit(solution)/shard_map/ppermute | solution.py:19
  3.8 47.9 %collective-permute-start.3 = (bf16[256,1024]{1,0:T(8,128)(2,1)}, bf16[256,1024]{1,0:T(8,128)(2,1)S(1)}, u32[]{:S(2)}, u32[]{:S(2)}) collective-permute-start(bf16[256,1024]{1,0:T(8,128)(2,1)} %refs_17_.1), channel_id=1, source_target_pairs={{0,16},{16,0},{1,17},{17,1},{2,18},{18,2},{3,19},{19,3},{4,20},{20... | collective-permute-start | bytes 1572872 | tf_op jit(solution)/shard_map/ppermute | solution.py:1913
  15.8 0.6 copy-start.1
  25.7 26.0 %collective-permute-start.4 = (bf16[16,1024]{1,0:T(8,128)(2,1)S(1)}, bf16[16,1024]{1,0:T(8,128)(2,1)S(1)}, u32[]{:S(2)}, u32[]{:S(2)}) collective-permute-start(bf16[16,1024]{1,0:T(8,128)(2,1)S(1)} %slice.18), channel_id=1, source_target_pairs={{1,0},{2,1},{3,2},{4,3},{5,4},{6,5},{7,6},{8,7},{9,8},{10,9},{11,1... | collective-permute-start | bytes 98312 | tf_op jit(solution)/shard_map/ppermute | solution.py:19
  27.1 24.6 %collective-permute-start.1 = (bf16[1024,256]{1,0:T(8,128)(2,1)}, bf16[1024,256]{1,0:T(8,128)(2,1)S(1)}, u32[]{:S(2)}, u32[]{:S(2)}) collective-permute-start(bf16[1024,256]{1,0:T(8,128)(2,1)} %get-tuple-element.129), channel_id=1, source_target_pairs={{0,16},{16,0},{1,17},{17,1},{2,18},{18,2},{3,19},{19,3},{4,20},{20... | collective-permute-start | bytes 1572872 | tf_op jit(solution)/shard_map/ppermute | solution.py:1913
  27.2 25.0 %collective-permute-start.2 = (bf16[1024,256]{1,0:T(8,128)(2,1)}, bf16[1024,256]{1,0:T(8,128)(2,1)S(1)}, u32[]{:S(2)}, u32[]{:S(2)}) collective-permute-start(bf16[1024,256]{1,0:T(8,128)(2,1)} %get-tuple-element.130), channel_id=1, source_target_pairs={{0,16},{16,0},{1,17},{17,1},{2,18},{18,2},{3,19},{19,3},{4,20},{20... | collective-permute-start | bytes 1572872 | tf_op jit(solution)/shard_map/ppermute | solution.py:1913
  51.6 81.3 %collective-permute-start.5 = (bf16[1024,256]{1,0:T(8,128)(2,1)}, bf16[1024,256]{1,0:T(8,128)(2,1)S(1)}, u32[]{:S(2)}, u32[]{:S(2)}) collective-permute-start(bf16[1024,256]{1,0:T(8,128)(2,1)} %get-tuple-element.141), channel_id=1, source_target_pairs={{0,16},{16,0},{1,17},{17,1},{2,18},{18,2},{3,19},{19,3},{4,20},{20... | collective-permute-start | bytes 1572872 | tf_op jit(solution)/shard_map/ppermute | solution.py:1913
  51.7 53.8 %copy-start = (bf16[16,1024]{1,0:T(8,128)(2,1)}, bf16[16,1024]{1,0:T(8,128)(2,1)S(1)}, u32[]{:S(2)}) copy-start(bf16[16,1024]{1,0:T(8,128)(2,1)S(1)} %collective-permute-done.4.cnext_ref) | copy-start | bytes 98308
  51.7 53.8 %copy-start.9 = (bf16[256,1024]{1,0:T(8,128)(2,1)}, bf16[256,1024]{1,0:T(8,128)(2,1)S(1)}, u32[]{:S(2)}) copy-start(bf16[256,1024]{1,0:T(8,128)(2,1)S(1)} %collective-permute-done.3.refs_28_) | copy-start | bytes 1572868
  51.7 53.7 %copy-start.10 = (bf16[1024,256]{1,0:T(8,128)(2,1)}, bf16[1024,256]{1,0:T(8,128)(2,1)S(1)}, u32[]{:S(2)}) copy-start(bf16[1024,256]{1,0:T(8,128)(2,1)S(1)} %collective-permute-done.1) | copy-start | bytes 1572868
  52.3 53.2 %copy-start.11 = (bf16[1024,256]{1,0:T(8,128)(2,1)}, bf16[1024,256]{1,0:T(8,128)(2,1)S(1)}, u32[]{:S(2)}) copy-start(bf16[1024,256]{1,0:T(8,128)(2,1)S(1)} %collective-permute-done.2) | copy-start | bytes 1572868
  132.9 71.9 %copy-start.12 = (bf16[1024,256]{1,0:T(8,128)(2,1)}, bf16[1024,256]{1,0:T(8,128)(2,1)S(1)}, u32[]{:S(2)}) copy-start(bf16[1024,256]{1,0:T(8,128)(2,1)S(1)} %collective-permute-done.5) | copy-start | bytes 1572868
  132.9 72.5 %copy-start.8 = (bf16[128,4608]{1,0:T(8,128)(2,1)S(1)}, bf16[128,4608]{1,0:T(8,128)(2,1)}, u32[]{:S(2)}) copy-start(bf16[128,4608]{1,0:T(8,128)(2,1)} %get-tuple-element.170) | copy-start | bytes 3538948
  204.8 35.2 %collective-permute-start.6 = (bf16[128,4608]{1,0:T(8,128)(2,1)}, bf16[128,4608]{1,0:T(8,128)(2,1)S(1)}, u32[]{:S(2)}, u32[]{:S(2)}) collective-permute-start(bf16[128,4608]{1,0:T(8,128)(2,1)} %get-tuple-element.160), channel_id=1, source_target_pairs={{0,16},{16,0},{1,17},{17,1},{2,18},{18,2},{3,19},{19,3},{4,20},{20... | collective-permute-start | bytes 3538952 | tf_op jit(solution)/shard_map/ppermute | solution.py:1913
  205.4 53.3 %collective-permute-start.8 = (bf16[128,4608]{1,0:T(8,128)(2,1)S(1)}, bf16[128,4608]{1,0:T(8,128)(2,1)S(1)}, u32[]{:S(2)}, u32[]{:S(2)}) collective-permute-start(bf16[128,4608]{1,0:T(8,128)(2,1)S(1)} %copy-done.8), channel_id=1, source_target_pairs={{0,16},{16,0},{1,17},{17,1},{2,18},{18,2},{3,19},{19,3},{4,20},{20... | collective-permute-start | bytes 3538952 | tf_op jit(solution)/shard_map/ppermute | solution.py:1913
  240.0 15.7 %copy-start.6 = (bf16[128,4608]{1,0:T(8,128)(2,1)}, bf16[128,4608]{1,0:T(8,128)(2,1)S(1)}, u32[]{:S(2)}) copy-start(bf16[128,4608]{1,0:T(8,128)(2,1)S(1)} %collective-permute-done.6.refs_29_) | copy-start | bytes 3538948
  240.8 3.1 collective-permute-start.7
  243.8 0.6 copy-start.2
  244.5 14.2 %copy-start.3 = (f32[1,1024]{1,0:T(1,128)S(1)}, f32[1,1024]{1,0:T(1,128)}, u32[]{:S(2)}) copy-start(f32[1,1024]{1,0:T(1,128)} %get-tuple-element.196) | copy-start | bytes 12292
  244.5 14.2 %copy-start.4 = (f32[1,1024]{1,0:T(1,128)S(1)}, f32[1,1024]{1,0:T(1,128)}, u32[]{:S(2)}) copy-start(f32[1,1024]{1,0:T(1,128)} %get-tuple-element.195) | copy-start | bytes 12292
  244.5 14.2 %copy-start.5 = (f32[1,1024]{1,0:T(1,128)S(1)}, f32[1,1024]{1,0:T(1,128)}, u32[]{:S(2)}) copy-start(f32[1,1024]{1,0:T(1,128)} %get-tuple-element.194) | copy-start | bytes 12292
  258.7 1.5 copy-start.7

commit v6 on v5

--- a/solution.py
+++ b/solution.py
@@ -517,6 +517,7 @@
 RING = 16
 LAG = 3
 AHEAD = 8
+SMALL_ROWS = ((0, 0), (1, 0), (4, 0), (5, 0), (6, 0), (7, 0), (7, LANES))
 
 
 def vmem_specs(count):
@@ -534,11 +535,18 @@
 def same_head(head):
     row = lax.broadcasted_iota(jnp.int32, (LANES, LANES), 0) // head
     column = lax.broadcasted_iota(jnp.int32, (LANES, LANES), 1) // head
-    return jnp.where(row == column, 1.0 / head, 0.0).astype(F32)
+    return jnp.where(row == column, 1.0 / head, 0.0).astype(BF)
 
 
 def head_mean(value, blocks):
-    return jnp.dot(value, blocks, precision=lax.Precision.HIGHEST, preferred_element_type=F32)
+    high = value.astype(BF)
+    low = (value - high.astype(F32)).astype(BF)
+    return (jnp.dot(high, blocks, preferred_element_type=F32) + jnp.dot(low, blocks, preferred_element_type=F32))
+
+
+def twice(ref):
+    row = row_of(ref)
+    return jnp.concatenate([row, row], axis=1)
 
 
 def other_half(value, head):
@@ -568,6 +576,7 @@
     normt_ref[...] = turned(normed)
     normed = normed.astype(BF)
     blocks = same_head(head)
+    query_gain, keys_gain = twice(qg_ref), twice(kg_ref)
     cosine, sine = cos_ref[...], sin_ref[...]
     half_rows = msg_ref.shape[1]
     lane = lane_of(cosine.shape)
@@ -584,12 +593,12 @@
     qraw = jnp.dot(normed, wq_ref[...], preferred_element_type=F32)
     qraw_ref[...] = qraw
     for tile in range(qraw.shape[1] // LANES):
-        put(tile, 0, prepared(qraw[:, tile * LANES:(tile + 1) * LANES], qg_ref[...]))
+        put(tile, 0, prepared(qraw[:, tile * LANES:(tile + 1) * LANES], query_gain))
     kraw = jnp.dot(normed, wk_ref[...], preferred_element_type=F32)
     kraw_ref[...] = kraw
     vraw = jnp.dot(normed, wv_ref[...], preferred_element_type=F32)
     for tile in range(kraw.shape[1] // LANES):
-        keys = prepared(kraw[:, tile * LANES:(tile + 1) * LANES], kg_ref[...])
+        keys = prepared(kraw[:, tile * LANES:(tile + 1) * LANES], keys_gain)
         values = vraw[:, tile * LANES:(tile + 1) * LANES]
         put(2 * tile, LANES, jnp.where(lane < head, keys, swap_heads(values, head)))
         put(2 * tile + 1, LANES, jnp.where(lane < head, swap_heads(keys, head), values))
@@ -598,6 +607,7 @@
 def project_back_kernel(head, backq_ref, backk_ref, hid_ref, gain_ref, wq_ref, wk_ref, wv_ref, cos_ref, sin_ref, qg_ref,
                         kg_ref, qraw_ref, kraw_ref, grad_ref,
                         rawq_ref, keep_ref, send_ref, two_ref, again_ref, qgain_ref, kgain_ref):
+    query_gain, keys_gain = twice(qg_ref), twice(kg_ref)
     blocks = same_head(head)
     cosine, sine = cos_ref[...], sin_ref[...]
     lane = lane_of(cosine.shape)
@@ -617,7 +627,7 @@
     width_k = wk_ref.shape[1]
     gain_total = jnp.zeros((1, LANES), F32)
     for tile in range(width_q // LANES):
-        got, part = through(fetch(backq_ref, tile), qraw_ref[:, tile * LANES:(tile + 1) * LANES], qg_ref[...])
+        got, part = through(fetch(backq_ref, tile), qraw_ref[:, tile * LANES:(tile + 1) * LANES], query_gain)
         gain_total = gain_total + part
         rawq_ref[:, tile * LANES:(tile + 1) * LANES] = got.astype(BF)
     qgain_ref[...] = gain_total
@@ -627,7 +637,7 @@
         even, odd = fetch(backk_ref, 2 * tile), fetch(backk_ref, 2 * tile + 1)
         keys = jnp.where(lane < head, even, swap_heads(odd, head))
         values = jnp.where(lane < head, swap_heads(even, head), odd)
-        got, part = through(keys, kraw_ref[:, tile * LANES:(tile + 1) * LANES], kg_ref[...])
+        got, part = through(keys, kraw_ref[:, tile * LANES:(tile + 1) * LANES], keys_gain)
         gain_total = gain_total + part
         key_tiles.append(got.astype(BF))
         value_tiles.append(values.astype(BF))
@@ -890,8 +900,8 @@
     product = (part_b * part_x).astype(BF)
     prod_ref[...] = product
     product = product.astype(F32)
-    one = jnp.where(pos_ref[...] >= 1.0, shifted(product, 1)[HALO:], 0.0)
-    two = jnp.where(pos_ref[...] >= 2.0, shifted(product, 2)[HALO:], 0.0)
+    one = jnp.where(pos_ref[:-HALO] >= 1.0, shifted(product, 1)[HALO:], 0.0)
+    two = jnp.where(pos_ref[:-HALO] >= 2.0, shifted(product, 2)[HALO:], 0.0)
     conved = taps[2:3] * product[HALO:] + taps[1:2] * one + taps[0:1] * two
     gated = part_c * conved
     b_ref[...] = part_b[HALO:].astype(BF)
@@ -1039,7 +1049,8 @@
     (info_ref, msg_ref), guests, refs = refs[:2], refs[2:2 + extra], refs[2 + extra:]
     (got_ref, out_ref, aug_ref, all_ref), landings, refs = refs[:4], refs[4:4 + extra], refs[4 + extra:]
     (land, kv, tiles, arrive, ones_ref, acc_ref, msend, mrecv, fsend, frecv, gsend, grecv, hsend, hrecv) = refs
-    first, second = info_ref[0], info_ref[1]
+    first = info_ref[0, 0]
+    second = first + info_ref[0, 1]
     me = lax.axis_index("ctx")
     part = me % 2
     twin = {"ctx": me + 1 - 2 * part}
@@ -1160,7 +1171,8 @@
     (gotq_ref, gotk_ref), landings, refs = refs[:2], refs[2:2 + extra], refs[2 + extra:]
     (land, tiles, away, near, sums, arrive_q, arrive_k, kone_ref, vone_ref, kturn_ref, dk_ref, dv_ref, acc_ref,
      msend, mrecv, fsend, frecv, gsend, grecv, ksend, krecv, hsend, hrecv) = refs
-    first, second = info_ref[0], info_ref[1]
+    first = info_ref[0, 0]
+    second = first + info_ref[0, 1]
     me = lax.axis_index("ctx")
     part = me % 2
     twin = {"ctx": me + 1 - 2 * part}
@@ -1365,7 +1377,7 @@
     lefts, lefts_y, rights = take(sides), take(sides), take(count)
     sent = [refs.pop(0) if job["late"] and job["kind"] == "pair" else None for job in jobs]
     early_y = [None if job["late"] else take(job["parts"]) for job in jobs]
-    (small_ref,) = take(1)
+    small_refs = take(len(SMALL_ROWS))
     outs, (small_out,) = take(weights), take(1)
     lefts_s, lefts_ys, rights_s, rights_ys = take(sides), take(sides), take(count), take(count)
     rights_y = [take(1) if job["late"] else early for job, early in zip(jobs, early_y)]
@@ -1391,7 +1403,9 @@
 
     for buf in (ur, dr, zp):
         buf[...] = jnp.zeros_like(buf)
-    sm_s[0] = small_ref[...]
+    sm_s[0] = jnp.zeros(sm_s.shape[1:], F32)
+    for (row, column), ref in zip(SMALL_ROWS, small_refs):
+        sm_s[0, row:row + ref.shape[0], column:column + ref.shape[1]] = ref[...]
 
     barrier = pltpu.get_barrier_semaphore()
     for where in (twin, across_x, across_y, far):
@@ -1766,6 +1780,7 @@
             early.extend(work["cross"])
         jobs.append(job)
     steps = sum(job["total"] for job in jobs)
+    flat = (8, small[0].shape[1])
     top = lines - 1
     dma = pltpu.SemaphoreType.DMA
     ring = lambda *shape: pltpu.VMEM((RING,) + shape, BF)
@@ -1777,8 +1792,8 @@
         ring(top, SUB, STRIP), ring(top, SUB, STRIP), ring(top, SUB, STRIP), ring(top, SUB, STRIP),
         ring(SUB, STRIP), ring(SUB, STRIP), ring(2, PIECE, STRIP), ring(2, PIECE, STRIP),
         pltpu.VMEM((RING, 2, 2, PIECE, STRIP), F32),
-        pltpu.VMEM((5,) + small.shape, F32),
-        pltpu.VMEM((5,) + small.shape, F32),
+        pltpu.VMEM((5,) + flat, F32),
+        pltpu.VMEM((5,) + flat, F32),
         dma((2, 4)), dma((2, 5)),
     ] + [dma((RING,))] * 10 + [
         dma((RING, 2, 2)), dma((5,)), dma((5,)),
@@ -1792,15 +1807,15 @@
     flops = 2 * steps * 2 * lines * SUB * STRIP * 4 * tokens
     got = pl.pallas_call(
         functools.partial(sum_kernel, jobs, len(lefts), len(outs), lines),
-        out_shape=tuple(outs) + (S(small.shape, F32),) + tuple(landings),
-        in_specs=[anywhere] * len(operands) + [inside],
+        out_shape=tuple(outs) + (S(flat, F32),) + tuple(landings),
+        in_specs=[anywhere] * len(operands) + [inside] * len(small),
         out_specs=tuple([anywhere] * len(outs) + [inside] + [anywhere] * len(landings)),
         scratch_shapes=scratch,
         compiler_params=pltpu.CompilerParams(collective_id=collective_id, has_side_effects=True,
                                              vmem_limit_bytes=VMEM_LIMIT),
         cost_estimate=pl.CostEstimate(flops=flops, bytes_accessed=steps * 1_100_000, transcendentals=0),
         name="sum_over_chips",
-    )(*operands, small)
+    )(*operands, *small)
     return got[:len(outs)], got[len(outs)]
 
 
@@ -1819,8 +1834,8 @@
     low_ref[...] = small_ref[4]
     att_ref[...] = small_ref[5]
     top_ref[...] = small_ref[6]
-    query_ref[...] = small_ref[7, :head]
-    keys_ref[...] = small_ref[7, LANES:LANES + head]
+    query_ref[...] = small_ref[7, :head] + small_ref[7, head:LANES]
+    keys_ref[...] = small_ref[7, LANES:LANES + head] + small_ref[7, LANES + head:2 * LANES]
     for first, then in zip(arrive, leave):
         first.wait()
         then.start()
@@ -1882,22 +1897,17 @@
     core = place % 2
     first = lengths[0, 0]
     second = first + lengths[0, 1]
-    mine = place * rows + jnp.arange(rows, dtype=jnp.int32)
-    my_seg = segment_of(mine, first, second)
-    begin = jnp.where(my_seg == 0, 0, jnp.where(my_seg == 1, first, second))
-    position = (mine - begin).astype(F32)
-    twice = lambda gain: jnp.tile(gain.astype(F32), LANES // head)[None, :]
-    querygain_2, keysgain_2 = twice(querygain), twice(keysgain)
+    where = place * rows + jnp.arange(rows + HALO, dtype=jnp.int32)
+    begin = jnp.where(where >= second, second, jnp.where(where >= first, first, 0))
+    spots = (where - begin).astype(F32)[:, None]
     spot = jnp.arange(LANES, dtype=jnp.int32) % (head // 2)
-    angle = position[:, None] * (THETA ** (-spot.astype(F32) * 2.0 / head))[None, :]
+    angle = spots[:rows] * (THETA ** (-spot.astype(F32) * 2.0 / head))[None, :]
     cosine = jnp.cos(angle)
     sine = jnp.sin(angle) * jnp.where(jnp.arange(LANES) % head < head // 2, -1.0, 1.0)[None, :]
-    info = jnp.stack([first, second]).astype(jnp.int32)
 
     before = passed_along(tokens[rows - HALO:], "ctx", 1)
-    spot_of = lambda where: (where - jnp.where(where >= second, second, jnp.where(where >= first, first, 0))).astype(F32)
     (hidden_one, normed_one_t, gated_t, part_b, part_c, part_x, conved, product) = mix_forward(
-        tokens, before, position[:, None], mixgain, mixtaps, mixentry, mixexit)
+        tokens, before, spots, mixgain, mixtaps, mixentry, mixexit)
     gate_after = passed_along(part_c[:HALO], "ctx", -1)
     hidden_two, lownorm_t, gact_low, lact_low, lowinner_t = feed_low(
         hidden_one, lowgain, lowgate, lowlift, lowdrop)
@@ -1907,7 +1917,7 @@
         functools.partial(project_kernel, head),
         (shape_of((devices, half_rows, 2 * LANES), BF), shape_of((width, rows), BF),
          shape_of((rows, attquery.shape[1]), F32), shape_of((rows, attkeys.shape[1]), F32)),
-        (hidden_two, attgain, attquery, attkeys, attvalues, cosine, sine, querygain_2, keysgain_2),
+        (hidden_two, attgain, attquery, attkeys, attvalues, cosine, sine, querygain, keysgain),
         flops=2 * rows * width * 2 * width, moved=6 << 20, name="project")
     upright = lambda value: value.reshape(devices // 2, 2, value.shape[0] // devices, rows)
     over_dp = lambda value: lax.ppermute(value, "dp", [(0, 1), (1, 0)])
@@ -1915,14 +1925,14 @@
         (msg, over_dp(gated_t), over_dp(normed_one_t), over_dp(cotangent), gate_after))
     gated_y, normed_one_y = upright(gated_y), upright(normed_one_y)
     got, attended_f, augmented, all_kv, lowinner_y, lownorm_y = exchange_attend(
-        msg, info, head, rows, [("rows", upright(lowinner_t)), ("whole", upright(lownorm_t))], 2)
+        msg, lengths, head, rows, [("rows", upright(lowinner_t)), ("whole", upright(lownorm_t))], 2)
     (output, grad, grad_low3, send, attended_t, topgain_grad, topnorm_t, topinner_t, keep_top, send_top_a,
      send_top_b) = feed_top(
         got, hidden_two, attexit, cotangent, topgain, topgate, toplift, topdrop)
     send, normed_two_y = lax.optimization_barrier((send, over_dp(normed_two_t)))
     normed_two_y = upright(normed_two_y)
     back_q, back_k, topinner_y, topnorm_y, attended_y, grad_low3_y = exchange_attend_back(
-        send, info, augmented, attended_f, all_kv, head, rows,
+        send, lengths, augmented, attended_f, all_kv, head, rows,
         [("rows", upright(topinner_t)), ("whole", upright(topnorm_t)), ("whole", upright(attended_t)),
          ("columns", grad_low3)], 3)
     back_q, send_top_a, send_top_b = lax.optimization_barrier((back_q, send_top_a, send_top_b))
@@ -1932,18 +1942,15 @@
         (shape_of((rows, attquery.shape[1]), BF), shape_of((rows, attkeys.shape[1]), BF),
          shape_of((rows, attkeys.shape[1]), BF), shape_of((rows, width), F32), shape_of((1, width), F32),
          shape_of((1, LANES), F32), shape_of((1, LANES), F32)),
-        (back_q, back_k, hidden_two, attgain, attquery, attkeys, attvalues, cosine, sine, querygain_2, keysgain_2,
+        (back_q, back_k, hidden_two, attgain, attquery, attkeys, attvalues, cosine, sine, querygain, keysgain,
          query_raw, key_raw, grad),
         flops=1 << 20, moved=1 << 10, name="project_back")
-    fold = lambda value: value.reshape(LANES // head, head).sum(axis=0)
-    querygain_grad, keysgain_grad = fold(querygain_grad), fold(keysgain_grad)
     grad, lowgain_grad, gb_low, grad_low1, keep_low, send_low = feed_low_back(
         grad_two, hidden_one, lowgain, gact_low, lact_low, lowgate, lowlift, lowdrop)
     grad, grad_low1, top_y_one = lax.optimization_barrier((grad, grad_low1, top_y_one))
-    ext = place * rows + jnp.arange(rows + HALO, dtype=jnp.int32)
     after = passed_along(grad_low1[:HALO], "ctx", -1)
     tokens_grad, mixgain_grad, mixtaps_grad, mixed_grad = mix_backward(
-        grad, grad_low1, after, gate_after, spot_of(ext)[:, None], tokens, mixgain, mixtaps,
+        grad, grad_low1, after, gate_after, spots, tokens, mixgain, mixtaps,
         (part_b, part_c, part_x, conved, product), mixentry, mixexit)
     mixgain_grad, tokens_grad, top_y_two = lax.optimization_barrier(
         (mixgain_grad, tokens_grad, over_dp(send_top_b)))
@@ -1959,9 +1966,7 @@
              work(3, "pair", keep_kv, send_kv, issue=5), work(4, "drop", gb_low, issue=10),
              work(5, "pair", keep_low, send_low, issue=20), work(6, "quarter", grad_low1, issue=68),
              work(7, "quarter", mixed_grad, issue=73)]
-    heads = jnp.concatenate([querygain_grad, jnp.zeros((LANES - head,), F32), keysgain_grad, jnp.zeros((width - LANES - head,), F32)])
-    small = jnp.concatenate([mixgain_grad, mixtaps_grad, lowgain_grad, attgain_grad, topgain_grad,
-                             heads[None, :]], axis=0)
+    small = (mixgain_grad, mixtaps_grad, lowgain_grad, attgain_grad, topgain_grad, querygain_grad, keysgain_grad)
     grads, small = sum_over_chips(lefts, works, small, lines, 1)
     grads, smalls = hand_over(grads, small, head)
     (attexit_grad, topdrop_grad, topgate_grad, toplift_grad, attquery_grad, attkeys_grad, attvalues_grad, lowdrop_grad,

time: 492 us -> 487 us (0.990)
  waiting for transfers between devices: 5.29 us -> 12.4 us
  other arithmetic: 8.59 us -> 3.24 us
    ppermute x6, waiting for transfers between devices: 3.58 us -> 10.6 us  [fast_device(): over_dp = lambda value: lax.ppermute(value, 'dp', [(0, 1), (1, 0)])]
  transfers between devices with their start and end apart: 9 -> 9, of which waited for: 3 -> 3; matrix products, arithmetic and copies ran while one was open for 3% -> 1% of each run, Pallas kernels for 31% -> 30%
where the time goes in v6:
time: 487 us; the launch traced here: 486 us
  Pallas kernels  451 us (93%)
  waiting for transfers between devices  12.4 us (3%)
  starting transfers between devices  11.6 us (2%)
  local copies, waits for them, and re-layouts  5.91 us (1%)
    pallas_call x1, Pallas kernels, sum_over_chips(): pl.pallas_call(functools.partial(sum_kernel, jobs, len(lefts), len(outs),...  223 us
    pallas_call x5, Pallas kernels, call_tiled(): pl.pallas_call(kernel, grid=(tiles,), in_specs=[spec for _, spec in ins],...  82 us
    pallas_call x1, Pallas kernels, exchange_attend_back(): pl.pallas_call(functools.partial(attend_back_kernel, head, rows, keys, so...  71.9 us
    pallas_call x1, Pallas kernels, exchange_attend(): pl.pallas_call(functools.partial(attend_kernel, head, rows, keys, sources...  52.5 us
    pallas_call x2, Pallas kernels, call_plain(): pl.pallas_call(kernel, out_shape=tuple(outs) if many else outs, in_specs=...  13.5 us
    ppermute x6, waiting for transfers between devices, fast_device(): over_dp = lambda value: lax.ppermute(value, 'dp', [(0, 1), (1, 0)])  10.6 us
  transfers between devices with their start and end apart: 9, of which 3 were waited for; matrix products, arithmetic and copies ran while one was open for 1% of the time, Pallas kernels for 30%

profile of v6, /device:TPU:0, one launch (start us, length us, event | category | flops | bytes accessed | tf_op | source)
XLA Modules:
  0.0 486.1 jit_solution(822618962681067286)
XLA Ops:
  0.7 0.8 slice.19
  1.4 2.3 collective-permute-start
  3.8 2.4 collective-permute-start.3
  6.2 1.3 fusion.9
  8.8 0.7 subtract_convert_fusion.1
  9.5 1.2 fusion.2
  10.7 1.3 subtract_convert_fusion.pos_ref
  12.1 0.0 collective-permute-done.prev_ref
  12.1 0.6 copy-done.1
  12.7 8.5 %mix.1 = (f32[256,1024]{1,0:T(8,128)}, bf16[1024,256]{1,0:T(8,128)(2,1)}, bf16[1024,256]{1,0:T(8,128)(2,1)}, bf16[256,1024]{1,0:T(8,128)(2,1)}, bf16[256,1024]{1...) custom-call(bf16[256,1024]{1,0:T(8,128)(2,1)} %tok_ref.3, ...), custom_call_target="tpu_custom_call" | custom-call | flops 2147483648 | bytes 12582912 | tf_op jit(solution)/shard_map/mix/pallas_call | solution.py:813
  21.2 0.8 slice.23
  21.9 1.3 collective-permute-start.4
  23.2 0.1 collective-permute-start.1
  23.3 2.0 collective-permute-start.2
  25.3 16.0 %feed_low.1 = (f32[256,1024]{1,0:T(8,128)}, bf16[1024,256]{1,0:T(8,128)(2,1)}, bf16[256,4608]{1,0:T(8,128)(2,1)}, bf16[256,4608]{1,0:T(8,128)(2,1)}, bf16[4608,256]{1,0:T(8,128)(2,1)}) custom-call(f32[256,1024]{1,0:T(8,128)} %get-tuple-element.126.hid_ref, bf16[1024]{0:T(1024)(128)(2,1)} %gain_ref.12, bf16[1024,4608]{1,0:T(8,128)(2,1)} %gate_ref.5, ...), custom_call_target="tpu_custom_call" | custom-call | flops 7247757312 | bytes 39845888 | tf_op jit(solution)/shard_map/feed_low/pallas_call | solution.py:813
  41.3 5.7 %project.1 = (bf16[16,128,256]{2,1,0:T(8,128)(2,1)}, bf16[1024,256]{1,0:T(8,128)(2,1)}, f32[256,1024]{1,0:T(8,128)}, f32[256,512]{1,0:T(8,128)}) custom-call(f32[256,1024]{1,0:T(8,128)} %get-tuple-element.127.hid_ref.two_ref, bf16[1024]{0:T(1024)(128)(2,1)} %gain_ref.11, bf16[1024,1024]{1,0:T(8,128)(2,1)} %wq_ref.3, bf16[1024,512]{1,0:T(8,128)(2,1)} %wk_ref.3, ...), custom_call_target="tpu_custom_call" | custom-call | flops 1073741824 | bytes 6291456 | tf_op jit(solution)/shard_map/project/pallas_call | solution.py:1867
  47.0 0.1 collective-permute-start.5
  47.1 0.0 collective-permute-done.4.cnext_ref
  47.1 0.0 collective-permute-done.3.refs_28_
  47.1 0.0 copy-start.6
  47.1 0.0 collective-permute-done.1
  47.1 0.0 copy-start.7
  47.1 1.2 collective-permute-done.2
  48.4 52.5 %attend.1 = (bf16[16,128,128]{2,1,0:T(8,128)(2,1)}, f32[16,128,128]{2,1,0:T(8,128)}, bf16[16,2,128,128]{3,2,1,0:T(8,128)(2,1)}, bf16[4096,128]{1,0:T(8,128)(2,1)...) custom-call(s32[1,3]{1,0:T(1,128)} %refs_0_.3, bf16[16,128,256]{2,1,0:T(8,128)(2,1)} %get-tuple-element.132.refs_1_, ...), custom_call_target="tpu_custom_call" | custom-call | flops 4294967296 | bytes 6291456 | tf_op jit(solution)/shard_map/attend/pallas_call | solution.py:1330
  100.8 0.0 copy-done
  100.9 0.0 copy-done.6
  100.9 0.0 copy-done.7
  100.9 0.0 copy-done.8
  100.9 27.4 %feed_top.1 = (f32[256,1024]{1,0:T(8,128)}, f32[256,1024]{1,0:T(8,128)}, bf16[256,1024]{1,0:T(8,128)(2,1)}, bf16[16,128,128]{2,1,0:T(8,128)(2,1)}, bf16[1024,256...) custom-call(bf16[16,128,128]{2,1,0:T(8,128)(2,1)} %get-tuple-element, ...), custom_call_target="tpu_custom_call" | custom-call | flops 14495514624 | bytes 47185920 | tf_op jit(solution)/shard_map/feed_top/pallas_call | solution.py:813
  128.3 0.0 collective-permute-done.5
  128.3 0.0 copy-start.9
  128.3 0.0 copy-start.5
  128.3 71.9 %attend_back.1 = (bf16[16,128,128]{2,1,0:T(8,128)(2,1)}, bf16[16,128,128]{2,1,0:T(8,128)(2,1)}, bf16[8,2,144,256]{3,2,1,0:T(8,128)(2,1)}, bf16[8,2,64,256]{3,2,1...) custom-call(s32[1,3]{1,0:T(1,128)} %refs_0_.3, ...), custom_call_target="tpu_custom_call" | custom-call | flops 10737418240 | bytes 8388608 | tf_op jit(solution)/shard_map/attend_back/pallas_call | solution.py:1358
  200.2 0.6 collective-permute-start.6
  200.8 1.5 collective-permute-start.8
  202.3 7.8 %project_back.1 = (bf16[256,1024]{1,0:T(8,128)(2,1)}, bf16[256,512]{1,0:T(8,128)(2,1)}, bf16[256,512]{1,0:T(8,128)(2,1)}, f32[256,1024]{1,0:T(8,128)}, f32[1,102...) custom-call(bf16[16,128,128]{2,1,0:T(8,128)(2,1)} %get-tuple-element.150.backq_ref, ...), custom_call_target="tpu_custom_call" | custom-call | flops 1048576 | bytes 1024 | tf_op jit(solution)/shard_map/project_back/pallas_call | solution.py:1867
  210.1 19.2 %feed_low_back.1 = (f32[256,1024]{1,0:T(8,128)}, f32[1,1024]{1,0:T(1,128)}, bf16[256,1024]{1,0:T(8,128)(2,1)}, bf16[256,1024]{1,0:T(8,128)(2,1)}, bf16[256,4608]{1,0:T(8,128)(2,1)}, /*index=5*/bf16[256,4608]{1,0:T(8,128)(2,1)}) custom-call(f32[256,1024]{1,0:T(8,128)} %get-tuple-element.155.grad_ref, f32[256,1024]{1,0:T(8,128)} %get-tuple-element.126.hid_ref, ...), custom_call_target="tpu_custom_call" | custom-call | flops 1048576 | bytes 1024 | tf_op jit(solution)/shard_map/feed_low_back/pallas_call | solution.py:813
  229.3 0.0 collective-permute-done.6.refs_29_
  229.3 0.0 copy-start.3
  229.3 0.8 slice.24
  230.1 1.3 collective-permute-start.7
  231.4 1.8 collective-permute-done.7.next_ref
  233.2 0.6 copy-done.2
  233.8 10.9 %mix_back.1 = (f32[256,1024]{1,0:T(8,128)}, f32[1,1024]{1,0:T(1,128)}, f32[3,1024]{1,0:T(4,128)}, bf16[256,3072]{1,0:T(8,128)(2,1)}) custom-call(f32[256,1024]{1,0:T(8,128)} %get-tuple-element.161.grad_ref, bf16[256,1024]{1,0:T(8,128)(2,1)} %get-tuple-element.162.low_ref.refs_23_, bf16[16,1024]{1,0:T(8,128)(2,1)} %copy-done.2, bf16[16,1024]{1,0:T(8,128)(2,1)} %copy-done, ...), custom_call_target="tpu_custom_call" | custom-call | flops 2147483648 | bytes 16777216 | tf_op jit(solution)/shard_map/mix_back/pallas_call | solution.py:813
  244.8 9.3 %collective-permute-done.8.refs_30_ = bf16[128,4608]{1,0:T(8,128)(2,1)S(1)} collective-permute-done((bf16[128,4608]{1,0:T(8,128)(2,1)S(1)}, bf16[128,4608]{1,0:T(8,128)(2,1)S(1)}, u32[]{:S(2)}, u32[]{:S(2)}) %collective-permute-start.8) | collective-permute-done | bytes 1179680 | tf_op jit(solution)/shard_map/ppermute | solution.py:1923
  254.1 1.0 copy-done.4
  255.1 222.5 %sum_over_chips.1 = (f32[64,1024]{1,0:T(8,128)}, f32[288,1024]{1,0:T(8,128)}, f32[64,4608]{1,0:T(8,128)}, f32[64,4608]{1,0:T(8,128)}, f32[64,1024]{1,0:T(8,128)}...) custom-call(bf16[8,2,64,256]{3,2,1,0:T(8,128)(2,1)} %bitcast.26, ...), custom_call_target="tpu_custom_call" | custom-call | flops 18253611008 | bytes 149600000 | tf_op jit(solution)/shard_map/sum_over_chips/pallas_call | solution.py:1808
  477.6 8.3 %hand_over.1 = (f32[64,1024]{1,0:T(8,128)}, f32[288,1024]{1,0:T(8,128)}, f32[64,4608]{1,0:T(8,128)}, f32[64,4608]{1,0:T(8,128)}, f32[64,1024]{1,0:T(8,128)}, /*i...) custom-call(f32[64,1024]{1,0:T(8,128)} %get-tuple-element.199.refs_0, ...), custom_call_target="tpu_custom_call" | custom-call | tf_op jit(solution)/shard_map/hand_over/pallas_call | solution.py:1852
  (10 shorter events, 0.0 us)
Async XLA Ops:
  1.4 10.7 %collective-permute-start = (bf16[16,1024]{1,0:T(8,128)(2,1)S(1)}, bf16[16,1024]{1,0:T(8,128)(2,1)S(1)}, u32[]{:S(2)}, u32[]{:S(2)}) collective-permute-start(bf16[16,1024]{1,0:T(8,128)(2,1)S(1)} %slice.19), channel_id=1, source_target_pairs={{0,1},{1,2},{2,3},{3,4},{4,5},{5,6},{6,7},{7,8},{8,9},{9,10},{10,1... | collective-permute-start | bytes 98312 | tf_op jit(solution)/shard_map/ppermute | solution.py:19
  3.8 43.3 %collective-permute-start.3 = (bf16[256,1024]{1,0:T(8,128)(2,1)}, bf16[256,1024]{1,0:T(8,128)(2,1)S(1)}, u32[]{:S(2)}, u32[]{:S(2)}) collective-permute-start(bf16[256,1024]{1,0:T(8,128)(2,1)} %refs_17_.1), channel_id=1, source_target_pairs={{0,16},{16,0},{1,17},{17,1},{2,18},{18,2},{3,19},{19,3},{4,20},{20... | collective-permute-start | bytes 1572872 | tf_op jit(solution)/shard_map/ppermute | solution.py:1923
  12.1 0.6 copy-start.1
  21.9 25.2 %collective-permute-start.4 = (bf16[16,1024]{1,0:T(8,128)(2,1)S(1)}, bf16[16,1024]{1,0:T(8,128)(2,1)S(1)}, u32[]{:S(2)}, u32[]{:S(2)}) collective-permute-start(bf16[16,1024]{1,0:T(8,128)(2,1)S(1)} %slice.23), channel_id=1, source_target_pairs={{1,0},{2,1},{3,2},{4,3},{5,4},{6,5},{7,6},{8,7},{9,8},{10,9},{11,1... | collective-permute-start | bytes 98312 | tf_op jit(solution)/shard_map/ppermute | solution.py:19
  23.2 23.9 %collective-permute-start.1 = (bf16[1024,256]{1,0:T(8,128)(2,1)}, bf16[1024,256]{1,0:T(8,128)(2,1)S(1)}, u32[]{:S(2)}, u32[]{:S(2)}) collective-permute-start(bf16[1024,256]{1,0:T(8,128)(2,1)} %get-tuple-element.129), channel_id=1, source_target_pairs={{0,16},{16,0},{1,17},{17,1},{2,18},{18,2},{3,19},{19,3},{4,20},{20... | collective-permute-start | bytes 1572872 | tf_op jit(solution)/shard_map/ppermute | solution.py:1923
  23.3 25.1 %collective-permute-start.2 = (bf16[1024,256]{1,0:T(8,128)(2,1)}, bf16[1024,256]{1,0:T(8,128)(2,1)S(1)}, u32[]{:S(2)}, u32[]{:S(2)}) collective-permute-start(bf16[1024,256]{1,0:T(8,128)(2,1)} %get-tuple-element.130), channel_id=1, source_target_pairs={{0,16},{16,0},{1,17},{17,1},{2,18},{18,2},{3,19},{19,3},{4,20},{20... | collective-permute-start | bytes 1572872 | tf_op jit(solution)/shard_map/ppermute | solution.py:1923
  47.0 81.3 %collective-permute-start.5 = (bf16[1024,256]{1,0:T(8,128)(2,1)}, bf16[1024,256]{1,0:T(8,128)(2,1)S(1)}, u32[]{:S(2)}, u32[]{:S(2)}) collective-permute-start(bf16[1024,256]{1,0:T(8,128)(2,1)} %get-tuple-element.141), channel_id=1, source_target_pairs={{0,16},{16,0},{1,17},{17,1},{2,18},{18,2},{3,19},{19,3},{4,20},{20... | collective-permute-start | bytes 1572872 | tf_op jit(solution)/shard_map/ppermute | solution.py:1923
  47.1 53.8 %copy-start = (bf16[16,1024]{1,0:T(8,128)(2,1)}, bf16[16,1024]{1,0:T(8,128)(2,1)S(1)}, u32[]{:S(2)}) copy-start(bf16[16,1024]{1,0:T(8,128)(2,1)S(1)} %collective-permute-done.4.cnext_ref) | copy-start | bytes 98308
  47.1 53.8 %copy-start.6 = (bf16[256,1024]{1,0:T(8,128)(2,1)}, bf16[256,1024]{1,0:T(8,128)(2,1)S(1)}, u32[]{:S(2)}) copy-start(bf16[256,1024]{1,0:T(8,128)(2,1)S(1)} %collective-permute-done.3.refs_28_) | copy-start | bytes 1572868
  47.1 53.8 %copy-start.7 = (bf16[1024,256]{1,0:T(8,128)(2,1)}, bf16[1024,256]{1,0:T(8,128)(2,1)S(1)}, u32[]{:S(2)}) copy-start(bf16[1024,256]{1,0:T(8,128)(2,1)S(1)} %collective-permute-done.1) | copy-start | bytes 1572868
  48.4 52.5 %copy-start.8 = (bf16[1024,256]{1,0:T(8,128)(2,1)}, bf16[1024,256]{1,0:T(8,128)(2,1)S(1)}, u32[]{:S(2)}) copy-start(bf16[1024,256]{1,0:T(8,128)(2,1)S(1)} %collective-permute-done.2) | copy-start | bytes 1572868
  128.3 71.9 %copy-start.9 = (bf16[1024,256]{1,0:T(8,128)(2,1)}, bf16[1024,256]{1,0:T(8,128)(2,1)S(1)}, u32[]{:S(2)}) copy-start(bf16[1024,256]{1,0:T(8,128)(2,1)S(1)} %collective-permute-done.5) | copy-start | bytes 1572868
  128.3 72.5 %copy-start.5 = (bf16[128,4608]{1,0:T(8,128)(2,1)S(1)}, bf16[128,4608]{1,0:T(8,128)(2,1)}, u32[]{:S(2)}) copy-start(bf16[128,4608]{1,0:T(8,128)(2,1)} %get-tuple-element.170) | copy-start | bytes 3538948
  200.2 29.1 %collective-permute-start.6 = (bf16[128,4608]{1,0:T(8,128)(2,1)}, bf16[128,4608]{1,0:T(8,128)(2,1)S(1)}, u32[]{:S(2)}, u32[]{:S(2)}) collective-permute-start(bf16[128,4608]{1,0:T(8,128)(2,1)} %get-tuple-element.160), channel_id=1, source_target_pairs={{0,16},{16,0},{1,17},{17,1},{2,18},{18,2},{3,19},{19,3},{4,20},{20... | collective-permute-start | bytes 3538952 | tf_op jit(solution)/shard_map/ppermute | solution.py:1923
  200.8 53.3 %collective-permute-start.8 = (bf16[128,4608]{1,0:T(8,128)(2,1)S(1)}, bf16[128,4608]{1,0:T(8,128)(2,1)S(1)}, u32[]{:S(2)}, u32[]{:S(2)}) collective-permute-start(bf16[128,4608]{1,0:T(8,128)(2,1)S(1)} %copy-done.5), channel_id=1, source_target_pairs={{0,16},{16,0},{1,17},{17,1},{2,18},{18,2},{3,19},{19,3},{4,20},{20... | collective-permute-start | bytes 3538952 | tf_op jit(solution)/shard_map/ppermute | solution.py:1923
  229.3 15.4 %copy-start.3 = (bf16[128,4608]{1,0:T(8,128)(2,1)}, bf16[128,4608]{1,0:T(8,128)(2,1)S(1)}, u32[]{:S(2)}) copy-start(bf16[128,4608]{1,0:T(8,128)(2,1)S(1)} %collective-permute-done.6.refs_29_) | copy-start | bytes 3538948
  230.1 3.1 collective-permute-start.7
  233.2 0.6 copy-start.2
  254.1 1.0 copy-start.4

commit v7 on v6

--- a/solution.py
+++ b/solution.py
@@ -515,8 +515,11 @@
 SUB = 2 * PIECE
 STRIP = 256
 RING = 16
-LAG = 3
+LAG = 4
+LINE_LAG = 4
+CORE_LAG = 1
 AHEAD = 8
+LINE_FIRST = 6
 SMALL_ROWS = ((0, 0), (1, 0), (4, 0), (5, 0), (6, 0), (7, 0), (7, LANES))
 
 
@@ -1381,8 +1384,8 @@
     outs, (small_out,) = take(weights), take(1)
     lefts_s, lefts_ys, rights_s, rights_ys = take(sides), take(sides), take(count), take(count)
     rights_y = [take(1) if job["late"] else early for job, early in zip(jobs, early_y)]
-    (lbuf, rbuf, xp, xr, zp, us, ur, ds_, dr, fs, fr, cs, cr, stage, sm_s, sm_r,
-     lsem, rsem, xs, xv, uss, urv, dss, drv, fss, frv, css, crv, osem, sms, smv, els, elv, ers, erv, yrs, yrv) = refs
+    (lbuf, rbuf, xp, xr, x2r, zp, us, ur, ds_, dr, fs, fr, cs, cr, stage, sm_s, sm_r,
+     lsem, rsem, xs, xv, x2s, x2v, uss, urv, dss, drv, fss, frv, css, crv, osem, sms, smv, els, elv, ers, erv, yrs, yrv) = refs
     steps = sum(job["total"] for job in jobs)
     last = steps - 1
     tokens = lbuf.shape[-1] // 4
@@ -1477,13 +1480,27 @@
         s = j & (RING - 1)
         return remote(xp.at[s, 1 - x], xr.at[s], xs.at[s], xv.at[s], across_x)
 
-    def up_copy(j):
+    def x2_copy(j):
         s = j & (RING - 1)
-        return remote(us.at[s], ur.at[s], uss.at[s], urv.at[s], above)
-
-    def down_copy(j):
+        return remote(zp.at[j & (2 * RING - 1), z, 1 - x], x2r.at[s], x2s.at[s], x2v.at[s], across_x)
+
+    def line_first(j):
+        return lax.rem(j, LINE_FIRST) == LINE_FIRST - 1
+
+    def either(j, act):
+        both = line_first(j)
+        pl.when(both)(lambda: act(True))
+        pl.when(jnp.logical_not(both))(lambda: act(False))
+
+    def up_copy(j, both):
         s = j & (RING - 1)
-        return remote(ds_.at[s], dr.at[s], dss.at[s], drv.at[s], below)
+        src, dst = (us.at[s], ur.at[s]) if both else (us.at[s, :, 0], ur.at[s, :, 0])
+        return remote(src, dst, uss.at[s], urv.at[s], above)
+
+    def down_copy(j, both):
+        s = j & (RING - 1)
+        src, dst = (ds_.at[s], dr.at[s]) if both else (ds_.at[s, :, 0], dr.at[s, :, 0])
+        return remote(src, dst, dss.at[s], drv.at[s], below)
 
     def f_copy(j):
         s = j & (RING - 1)
@@ -1636,19 +1653,28 @@
             left = lbuf[which, :, :, rows, :].reshape(2 * lines * SUB, 4 * tokens)
             right = rbuf[which, :, pl.ds(pl.multiple_of(column, STRIP), STRIP)]
             got = jnp.dot(left, right, preferred_element_type=F32).astype(BF)
-            for line in range(lines):
-                for side in range(2):
-                    row = (2 * line + side) * SUB
-                    xp[slot, side, line] = got[row:row + SUB]
-            x_copy(t).start()
-
-        @pl.when((t >= LAG) & (t - LAG <= last))
+            @pl.when(line_first(t))
+            def _():
+                for line in range(lines):
+                    for side in range(2):
+                        row = (2 * line + side) * SUB
+                        zp[t & (2 * RING - 1), line, side] = got[row:row + SUB]
+
+            @pl.when(jnp.logical_not(line_first(t)))
+            def _():
+                for line in range(lines):
+                    for side in range(2):
+                        row = (2 * line + side) * SUB
+                        xp[slot, side, line] = got[row:row + SUB]
+                x_copy(t).start()
+
+        @pl.when((t >= LAG) & (t - LAG <= last) & jnp.logical_not(line_first(jnp.maximum(t - LAG, 0))))
         def _():
             x_copy(t - LAG).wait()
             s = (t - LAG) & (RING - 1)
-            zp[(t - LAG) & (2 * RING - 1)] = xp[s, x] + xr[s]
-
-        ju = t - LAG * (1 + z)
+            zp[(t - LAG) & (2 * RING - 1), :, 0] = xp[s, x] + xr[s]
+
+        ju = t - LAG - LINE_LAG * z
 
         @pl.when((ju >= 0) & (ju <= last))
         def _():
@@ -1657,23 +1683,23 @@
 
             @pl.when(z > 0)
             def _():
-                up_copy(ju).wait_recv()
+                either(ju, lambda both: up_copy(ju, both).wait_recv())
                 zp[held, z] = zp[held, z] + ur[s, 0]
 
             @pl.when(z < top)
             def _():
                 @pl.when(ju >= RING)
                 def _():
-                    up_copy(ju).wait_send()
+                    either(ju - RING, lambda both: up_copy(ju - RING, both).wait_send())
 
                 for m in range(top):
                     own = zp[held, jnp.minimum(z + 1 + m, top)]
                     if m + 1 < top:
                         own = own + ur[s, m + 1]
                     us[s, m] = own
-                up_copy(ju).start()
-
-        jd = t - LAG * (1 + top - z)
+                either(ju, lambda both: up_copy(ju, both).start())
+
+        jd = t - LAG - LINE_LAG * (top - z)
 
         @pl.when((jd >= 0) & (jd <= last))
         def _():
@@ -1682,27 +1708,43 @@
 
             @pl.when(z < top)
             def _():
-                down_copy(jd).wait_recv()
+                either(jd, lambda both: down_copy(jd, both).wait_recv())
                 zp[held, z] = zp[held, z] + dr[s, 0]
 
             @pl.when(z > 0)
             def _():
                 @pl.when(jd >= RING)
                 def _():
-                    down_copy(jd).wait_send()
+                    either(jd - RING, lambda both: down_copy(jd - RING, both).wait_send())
 
                 for m in range(top):
                     own = zp[held, jnp.maximum(z - 1 - m, 0)]
                     if m + 1 < top:
                         own = own + dr[s, m + 1]
                     ds_[s, m] = own
-                down_copy(jd).start()
-
-        jf = t - LAG * (1 + top)
+                either(jd, lambda both: down_copy(jd, both).start())
+
+        jx = t - LAG - LINE_LAG * top
+
+        @pl.when((jx >= 0) & (jx <= last) & line_first(jnp.maximum(jx, 0)))
+        def _():
+            x2_copy(jx).start()
+
+        jf = jx - LAG
 
         @pl.when((jf >= 0) & (jf <= last))
         def _():
-            fs[jf & (RING - 1)] = zp[jf & (2 * RING - 1), z]
+            s = jf & (RING - 1)
+            held = jf & (2 * RING - 1)
+
+            def gather(both):
+                if both:
+                    x2_copy(jf).wait()
+                    fs[s] = zp[held, z, x] + x2r[s]
+                else:
+                    fs[s] = zp[held, z, 0]
+
+            either(jf, gather)
             f_copy(jf).start()
 
         jo = jf - LAG
@@ -1719,7 +1761,7 @@
             stage[s, y, c] = fs[s, mine].astype(F32)
             stage[s, 1 - y, c] = fr[s, mine].astype(F32)
 
-        jc = jo - LAG
+        jc = jo - CORE_LAG
 
         @pl.when((jc >= 0) & (jc <= last))
         def _():
@@ -1738,7 +1780,7 @@
             def _():
                 out_wait(jc - LAG)
 
-    lax.fori_loop(0, last + LAG * (top + 3) + 1, step, None)
+    lax.fori_loop(0, last + 3 * LAG + LINE_LAG * top + CORE_LAG + 1, step, None)
     for back in range(LAG):
         out_wait(last - back)
     for back in range(RING):
@@ -1746,11 +1788,11 @@
 
         @pl.when(z < top)
         def _(j=j):
-            up_copy(j).wait_send()
+            up_copy(j, j % LINE_FIRST == LINE_FIRST - 1).wait_send()
 
         @pl.when(z > 0)
         def _(j=j):
-            down_copy(j).wait_send()
+            down_copy(j, j % LINE_FIRST == LINE_FIRST - 1).wait_send()
 
 
 def sum_over_chips(lefts, works, small, lines, collective_id):
@@ -1787,15 +1829,15 @@
     scratch = [
         pltpu.VMEM((2, 2 * lines, 2, max(value.shape[2] for value in crossed), 4 * tokens), BF),
         pltpu.VMEM((2, 4 * tokens, max(value.shape[1] for value in landing_r)), BF),
-        ring(2, lines, SUB, STRIP), ring(lines, SUB, STRIP),
-        pltpu.VMEM((2 * RING, lines, SUB, STRIP), BF),
-        ring(top, SUB, STRIP), ring(top, SUB, STRIP), ring(top, SUB, STRIP), ring(top, SUB, STRIP),
+        ring(2, lines, SUB, STRIP), ring(lines, SUB, STRIP), ring(SUB, STRIP),
+        pltpu.VMEM((2 * RING, lines, 2, SUB, STRIP), BF),
+        ring(top, 2, SUB, STRIP), ring(top, 2, SUB, STRIP), ring(top, 2, SUB, STRIP), ring(top, 2, SUB, STRIP),
         ring(SUB, STRIP), ring(SUB, STRIP), ring(2, PIECE, STRIP), ring(2, PIECE, STRIP),
         pltpu.VMEM((RING, 2, 2, PIECE, STRIP), F32),
         pltpu.VMEM((5,) + flat, F32),
         pltpu.VMEM((5,) + flat, F32),
         dma((2, 4)), dma((2, 5)),
-    ] + [dma((RING,))] * 10 + [
+    ] + [dma((RING,))] * 12 + [
         dma((RING, 2, 2)), dma((5,)), dma((5,)),
         dma((len(lefts), 2)), dma((len(lefts), 2)), dma((len(works), 3)), dma((len(works), 3)),
         dma((len(works),)), dma((len(works),)),

time: 487 us -> 482 us (0.990)
  Pallas kernels: 451 us -> 445 us
    pallas_call x1, Pallas kernels: 223 us -> 217 us  [sum_over_chips(): pl.pallas_call(functools.partial(sum_kernel, jobs, len(lefts), len(outs),...]
  transfers between devices with their start and end apart: 9 -> 9, of which waited for: 3 -> 3; matrix products, arithmetic and copies ran while one was open for 1% -> 1% of each run, Pallas kernels for 30% -> 31%
where the time goes in v7:
time: 482 us; the launch traced here: 481 us
  Pallas kernels  445 us (92%)
  waiting for transfers between devices  12.4 us (3%)
  starting transfers between devices  11.6 us (2%)
  local copies, waits for them, and re-layouts  5.91 us (1%)
    pallas_call x1, Pallas kernels, sum_over_chips(): pl.pallas_call(functools.partial(sum_kernel, jobs, len(lefts), len(outs),...  217 us
    pallas_call x5, Pallas kernels, call_tiled(): pl.pallas_call(kernel, grid=(tiles,), in_specs=[spec for _, spec in ins],...  82 us
    pallas_call x1, Pallas kernels, exchange_attend_back(): pl.pallas_call(functools.partial(attend_back_kernel, head, rows, keys, so...  71.9 us
    pallas_call x1, Pallas kernels, exchange_attend(): pl.pallas_call(functools.partial(attend_kernel, head, rows, keys, sources...  52.5 us
    pallas_call x2, Pallas kernels, call_plain(): pl.pallas_call(kernel, out_shape=tuple(outs) if many else outs, in_specs=...  13.5 us
    ppermute x6, waiting for transfers between devices, fast_device(): over_dp = lambda value: lax.ppermute(value, 'dp', [(0, 1), (1, 0)])  10.6 us
  transfers between devices with their start and end apart: 9, of which 3 were waited for; matrix products, arithmetic and copies ran while one was open for 1% of the time, Pallas kernels for 31%

profile of v7, /device:TPU:0, one launch (start us, length us, event | category | flops | bytes accessed | tf_op | source)
XLA Modules:
  0.0 480.8 jit_solution(9032148937586763201)
XLA Ops:
  0.7 0.8 slice.19
  1.4 2.3 collective-permute-start
  3.8 2.4 collective-permute-start.3
  6.2 1.3 fusion.9
  8.8 0.7 subtract_convert_fusion.1
  9.5 1.2 fusion.2
  10.7 1.3 subtract_convert_fusion.pos_ref
  12.1 0.0 collective-permute-done.prev_ref
  12.1 0.6 copy-done.1
  12.7 8.5 %mix.1 = (f32[256,1024]{1,0:T(8,128)}, bf16[1024,256]{1,0:T(8,128)(2,1)}, bf16[1024,256]{1,0:T(8,128)(2,1)}, bf16[256,1024]{1,0:T(8,128)(2,1)}, bf16[256,1024]{1...) custom-call(bf16[256,1024]{1,0:T(8,128)(2,1)} %tok_ref.3, ...), custom_call_target="tpu_custom_call" | custom-call | flops 2147483648 | bytes 12582912 | tf_op jit(solution)/shard_map/mix/pallas_call | solution.py:816
  21.2 0.8 slice.23
  21.9 1.3 collective-permute-start.4
  23.2 0.1 collective-permute-start.1
  23.3 2.0 collective-permute-start.2
  25.3 16.0 %feed_low.1 = (f32[256,1024]{1,0:T(8,128)}, bf16[1024,256]{1,0:T(8,128)(2,1)}, bf16[256,4608]{1,0:T(8,128)(2,1)}, bf16[256,4608]{1,0:T(8,128)(2,1)}, bf16[4608,256]{1,0:T(8,128)(2,1)}) custom-call(f32[256,1024]{1,0:T(8,128)} %get-tuple-element.126.hid_ref, bf16[1024]{0:T(1024)(128)(2,1)} %gain_ref.12, bf16[1024,4608]{1,0:T(8,128)(2,1)} %gate_ref.5, ...), custom_call_target="tpu_custom_call" | custom-call | flops 7247757312 | bytes 39845888 | tf_op jit(solution)/shard_map/feed_low/pallas_call | solution.py:816
  41.3 5.7 %project.1 = (bf16[16,128,256]{2,1,0:T(8,128)(2,1)}, bf16[1024,256]{1,0:T(8,128)(2,1)}, f32[256,1024]{1,0:T(8,128)}, f32[256,512]{1,0:T(8,128)}) custom-call(f32[256,1024]{1,0:T(8,128)} %get-tuple-element.127.hid_ref.two_ref, bf16[1024]{0:T(1024)(128)(2,1)} %gain_ref.11, bf16[1024,1024]{1,0:T(8,128)(2,1)} %wq_ref.3, bf16[1024,512]{1,0:T(8,128)(2,1)} %wk_ref.3, ...), custom_call_target="tpu_custom_call" | custom-call | flops 1073741824 | bytes 6291456 | tf_op jit(solution)/shard_map/project/pallas_call | solution.py:1909
  47.0 0.1 collective-permute-start.5
  47.1 0.0 collective-permute-done.4.cnext_ref
  47.1 0.0 collective-permute-done.3.refs_28_
  47.1 0.0 copy-start.6
  47.1 0.0 collective-permute-done.1
  47.1 1.2 collective-permute-done.2
  48.4 52.5 %attend.1 = (bf16[16,128,128]{2,1,0:T(8,128)(2,1)}, f32[16,128,128]{2,1,0:T(8,128)}, bf16[16,2,128,128]{3,2,1,0:T(8,128)(2,1)}, bf16[4096,128]{1,0:T(8,128)(2,1)...) custom-call(s32[1,3]{1,0:T(1,128)} %refs_0_.3, bf16[16,128,256]{2,1,0:T(8,128)(2,1)} %get-tuple-element.132.refs_1_, ...), custom_call_target="tpu_custom_call" | custom-call | flops 4294967296 | bytes 6291456 | tf_op jit(solution)/shard_map/attend/pallas_call | solution.py:1333
  100.8 0.0 copy-done
  100.9 0.0 copy-done.6
  100.9 0.0 copy-done.7
  100.9 0.0 copy-done.8
  100.9 27.4 %feed_top.1 = (f32[256,1024]{1,0:T(8,128)}, f32[256,1024]{1,0:T(8,128)}, bf16[256,1024]{1,0:T(8,128)(2,1)}, bf16[16,128,128]{2,1,0:T(8,128)(2,1)}, bf16[1024,256...) custom-call(bf16[16,128,128]{2,1,0:T(8,128)(2,1)} %get-tuple-element, ...), custom_call_target="tpu_custom_call" | custom-call | flops 14495514624 | bytes 47185920 | tf_op jit(solution)/shard_map/feed_top/pallas_call | solution.py:816
  128.3 0.0 collective-permute-done.5
  128.3 0.0 copy-start.5
  128.3 71.9 %attend_back.1 = (bf16[16,128,128]{2,1,0:T(8,128)(2,1)}, bf16[16,128,128]{2,1,0:T(8,128)(2,1)}, bf16[8,2,144,256]{3,2,1,0:T(8,128)(2,1)}, bf16[8,2,64,256]{3,2,1...) custom-call(s32[1,3]{1,0:T(1,128)} %refs_0_.3, ...), custom_call_target="tpu_custom_call" | custom-call | flops 10737418240 | bytes 8388608 | tf_op jit(solution)/shard_map/attend_back/pallas_call | solution.py:1361
  200.2 0.0 copy-done.9
  200.2 0.6 collective-permute-start.6
  200.8 1.5 collective-permute-start.8
  202.3 7.8 %project_back.1 = (bf16[256,1024]{1,0:T(8,128)(2,1)}, bf16[256,512]{1,0:T(8,128)(2,1)}, bf16[256,512]{1,0:T(8,128)(2,1)}, f32[256,1024]{1,0:T(8,128)}, f32[1,102...) custom-call(bf16[16,128,128]{2,1,0:T(8,128)(2,1)} %get-tuple-element.150.backq_ref, ...), custom_call_target="tpu_custom_call" | custom-call | flops 1048576 | bytes 1024 | tf_op jit(solution)/shard_map/project_back/pallas_call | solution.py:1909
  210.1 19.2 %feed_low_back.1 = (f32[256,1024]{1,0:T(8,128)}, f32[1,1024]{1,0:T(1,128)}, bf16[256,1024]{1,0:T(8,128)(2,1)}, bf16[256,1024]{1,0:T(8,128)(2,1)}, bf16[256,4608]{1,0:T(8,128)(2,1)}, /*index=5*/bf16[256,4608]{1,0:T(8,128)(2,1)}) custom-call(f32[256,1024]{1,0:T(8,128)} %get-tuple-element.155.grad_ref, f32[256,1024]{1,0:T(8,128)} %get-tuple-element.126.hid_ref, ...), custom_call_target="tpu_custom_call" | custom-call | flops 1048576 | bytes 1024 | tf_op jit(solution)/shard_map/feed_low_back/pallas_call | solution.py:816
  229.3 0.0 collective-permute-done.6.refs_29_
  229.3 0.0 copy-start.3
  229.3 0.8 slice.24
  230.1 1.3 collective-permute-start.7
  231.4 1.8 collective-permute-done.7.next_ref
  233.2 0.6 copy-done.2
  233.8 10.9 %mix_back.1 = (f32[256,1024]{1,0:T(8,128)}, f32[1,1024]{1,0:T(1,128)}, f32[3,1024]{1,0:T(4,128)}, bf16[256,3072]{1,0:T(8,128)(2,1)}) custom-call(f32[256,1024]{1,0:T(8,128)} %get-tuple-element.161.grad_ref, bf16[256,1024]{1,0:T(8,128)(2,1)} %get-tuple-element.162.low_ref.refs_23_, bf16[16,1024]{1,0:T(8,128)(2,1)} %copy-done.2, bf16[16,1024]{1,0:T(8,128)(2,1)} %copy-done, ...), custom_call_target="tpu_custom_call" | custom-call | flops 2147483648 | bytes 16777216 | tf_op jit(solution)/shard_map/mix_back/pallas_call | solution.py:816
  244.8 0.0 copy-done.3
  244.8 9.3 %collective-permute-done.8.refs_30_ = bf16[128,4608]{1,0:T(8,128)(2,1)S(1)} collective-permute-done((bf16[128,4608]{1,0:T(8,128)(2,1)S(1)}, bf16[128,4608]{1,0:T(8,128)(2,1)S(1)}, u32[]{:S(2)}, u32[]{:S(2)}) %collective-permute-start.8) | collective-permute-done | bytes 1179680 | tf_op jit(solution)/shard_map/ppermute | solution.py:1965
  254.1 1.0 copy-done.4
  255.1 217.2 %sum_over_chips.1 = (f32[64,1024]{1,0:T(8,128)}, f32[288,1024]{1,0:T(8,128)}, f32[64,4608]{1,0:T(8,128)}, f32[64,4608]{1,0:T(8,128)}, f32[64,1024]{1,0:T(8,128)}...) custom-call(bf16[8,2,64,256]{3,2,1,0:T(8,128)(2,1)} %bitcast.26, ...), custom_call_target="tpu_custom_call" | custom-call | flops 18253611008 | bytes 149600000 | tf_op jit(solution)/shard_map/sum_over_chips/pallas_call | solution.py:1850
  472.4 8.3 %hand_over.1 = (f32[64,1024]{1,0:T(8,128)}, f32[288,1024]{1,0:T(8,128)}, f32[64,4608]{1,0:T(8,128)}, f32[64,4608]{1,0:T(8,128)}, f32[64,1024]{1,0:T(8,128)}, /*i...) custom-call(f32[64,1024]{1,0:T(8,128)} %get-tuple-element.199.refs_0, ...), custom_call_target="tpu_custom_call" | custom-call | tf_op jit(solution)/shard_map/hand_over/pallas_call | solution.py:1894
  (10 shorter events, 0.0 us)
Async XLA Ops:
  1.4 10.7 %collective-permute-start = (bf16[16,1024]{1,0:T(8,128)(2,1)S(1)}, bf16[16,1024]{1,0:T(8,128)(2,1)S(1)}, u32[]{:S(2)}, u32[]{:S(2)}) collective-permute-start(bf16[16,1024]{1,0:T(8,128)(2,1)S(1)} %slice.19), channel_id=1, source_target_pairs={{0,1},{1,2},{2,3},{3,4},{4,5},{5,6},{6,7},{7,8},{8,9},{9,10},{10,1... | collective-permute-start | bytes 98312 | tf_op jit(solution)/shard_map/ppermute | solution.py:19
  3.8 43.3 %collective-permute-start.3 = (bf16[256,1024]{1,0:T(8,128)(2,1)}, bf16[256,1024]{1,0:T(8,128)(2,1)S(1)}, u32[]{:S(2)}, u32[]{:S(2)}) collective-permute-start(bf16[256,1024]{1,0:T(8,128)(2,1)} %refs_17_.1), channel_id=1, source_target_pairs={{0,16},{16,0},{1,17},{17,1},{2,18},{18,2},{3,19},{19,3},{4,20},{20... | collective-permute-start | bytes 1572872 | tf_op jit(solution)/shard_map/ppermute | solution.py:1965
  12.1 0.6 copy-start.1
  21.9 25.2 %collective-permute-start.4 = (bf16[16,1024]{1,0:T(8,128)(2,1)S(1)}, bf16[16,1024]{1,0:T(8,128)(2,1)S(1)}, u32[]{:S(2)}, u32[]{:S(2)}) collective-permute-start(bf16[16,1024]{1,0:T(8,128)(2,1)S(1)} %slice.23), channel_id=1, source_target_pairs={{1,0},{2,1},{3,2},{4,3},{5,4},{6,5},{7,6},{8,7},{9,8},{10,9},{11,1... | collective-permute-start | bytes 98312 | tf_op jit(solution)/shard_map/ppermute | solution.py:19
  23.2 23.9 %collective-permute-start.1 = (bf16[1024,256]{1,0:T(8,128)(2,1)}, bf16[1024,256]{1,0:T(8,128)(2,1)S(1)}, u32[]{:S(2)}, u32[]{:S(2)}) collective-permute-start(bf16[1024,256]{1,0:T(8,128)(2,1)} %get-tuple-element.129), channel_id=1, source_target_pairs={{0,16},{16,0},{1,17},{17,1},{2,18},{18,2},{3,19},{19,3},{4,20},{20... | collective-permute-start | bytes 1572872 | tf_op jit(solution)/shard_map/ppermute | solution.py:1965
  23.3 25.1 %collective-permute-start.2 = (bf16[1024,256]{1,0:T(8,128)(2,1)}, bf16[1024,256]{1,0:T(8,128)(2,1)S(1)}, u32[]{:S(2)}, u32[]{:S(2)}) collective-permute-start(bf16[1024,256]{1,0:T(8,128)(2,1)} %get-tuple-element.130), channel_id=1, source_target_pairs={{0,16},{16,0},{1,17},{17,1},{2,18},{18,2},{3,19},{19,3},{4,20},{20... | collective-permute-start | bytes 1572872 | tf_op jit(solution)/shard_map/ppermute | solution.py:1965
  47.0 81.3 %collective-permute-start.5 = (bf16[1024,256]{1,0:T(8,128)(2,1)}, bf16[1024,256]{1,0:T(8,128)(2,1)S(1)}, u32[]{:S(2)}, u32[]{:S(2)}) collective-permute-start(bf16[1024,256]{1,0:T(8,128)(2,1)} %get-tuple-element.141), channel_id=1, source_target_pairs={{0,16},{16,0},{1,17},{17,1},{2,18},{18,2},{3,19},{19,3},{4,20},{20... | collective-permute-start | bytes 1572872 | tf_op jit(solution)/shard_map/ppermute | solution.py:1965
  47.1 53.8 %copy-start = (bf16[16,1024]{1,0:T(8,128)(2,1)}, bf16[16,1024]{1,0:T(8,128)(2,1)S(1)}, u32[]{:S(2)}) copy-start(bf16[16,1024]{1,0:T(8,128)(2,1)S(1)} %collective-permute-done.4.cnext_ref) | copy-start | bytes 98308
  47.1 53.8 %copy-start.6 = (bf16[256,1024]{1,0:T(8,128)(2,1)}, bf16[256,1024]{1,0:T(8,128)(2,1)S(1)}, u32[]{:S(2)}) copy-start(bf16[256,1024]{1,0:T(8,128)(2,1)S(1)} %collective-permute-done.3.refs_28_) | copy-start | bytes 1572868
  47.1 53.8 %copy-start.7 = (bf16[1024,256]{1,0:T(8,128)(2,1)}, bf16[1024,256]{1,0:T(8,128)(2,1)S(1)}, u32[]{:S(2)}) copy-start(bf16[1024,256]{1,0:T(8,128)(2,1)S(1)} %collective-permute-done.1) | copy-start | bytes 1572868
  48.4 52.5 %copy-start.8 = (bf16[1024,256]{1,0:T(8,128)(2,1)}, bf16[1024,256]{1,0:T(8,128)(2,1)S(1)}, u32[]{:S(2)}) copy-start(bf16[1024,256]{1,0:T(8,128)(2,1)S(1)} %collective-permute-done.2) | copy-start | bytes 1572868
  128.3 71.9 %copy-start.9 = (bf16[1024,256]{1,0:T(8,128)(2,1)}, bf16[1024,256]{1,0:T(8,128)(2,1)S(1)}, u32[]{:S(2)}) copy-start(bf16[1024,256]{1,0:T(8,128)(2,1)S(1)} %collective-permute-done.5) | copy-start | bytes 1572868
  128.3 72.5 %copy-start.5 = (bf16[128,4608]{1,0:T(8,128)(2,1)S(1)}, bf16[128,4608]{1,0:T(8,128)(2,1)}, u32[]{:S(2)}) copy-start(bf16[128,4608]{1,0:T(8,128)(2,1)} %get-tuple-element.170) | copy-start | bytes 3538948
  200.2 29.1 %collective-permute-start.6 = (bf16[128,4608]{1,0:T(8,128)(2,1)}, bf16[128,4608]{1,0:T(8,128)(2,1)S(1)}, u32[]{:S(2)}, u32[]{:S(2)}) collective-permute-start(bf16[128,4608]{1,0:T(8,128)(2,1)} %get-tuple-element.160), channel_id=1, source_target_pairs={{0,16},{16,0},{1,17},{17,1},{2,18},{18,2},{3,19},{19,3},{4,20},{20... | collective-permute-start | bytes 3538952 | tf_op jit(solution)/shard_map/ppermute | solution.py:1965
  200.8 53.3 %collective-permute-start.8 = (bf16[128,4608]{1,0:T(8,128)(2,1)S(1)}, bf16[128,4608]{1,0:T(8,128)(2,1)S(1)}, u32[]{:S(2)}, u32[]{:S(2)}) collective-permute-start(bf16[128,4608]{1,0:T(8,128)(2,1)S(1)} %copy-done.5), channel_id=1, source_target_pairs={{0,16},{16,0},{1,17},{17,1},{2,18},{18,2},{3,19},{19,3},{4,20},{20... | collective-permute-start | bytes 3538952 | tf_op jit(solution)/shard_map/ppermute | solution.py:1965
  229.3 15.4 %copy-start.3 = (bf16[128,4608]{1,0:T(8,128)(2,1)}, bf16[128,4608]{1,0:T(8,128)(2,1)S(1)}, u32[]{:S(2)}) copy-start(bf16[128,4608]{1,0:T(8,128)(2,1)S(1)} %collective-permute-done.6.refs_29_) | copy-start | bytes 3538948
  230.1 3.1 collective-permute-start.7
  233.2 0.6 copy-start.2
  254.1 1.0 copy-start.4

commit v8 on v7

--- a/solution.py
+++ b/solution.py
@@ -1103,7 +1103,7 @@
             place = pl.ds(pl.multiple_of((base + source) * rows, rows), rows)
             all_ref[place] = both
             ones_ref[place] = jnp.where(lane_of(both.shape) < head, jnp.ones_like(both), both)
-            tile = land[base + source, :, :LANES].astype(F32)
+            tile = land[base + source, :, :LANES].astype(F32) * factor
             stack.append(jnp.where(lane < head, tile, 0.0))
             stack.append(jnp.where(lane < head, swap_heads(tile, head), 0.0))
         queries = jnp.concatenate(stack, axis=0).astype(BF)
@@ -1112,7 +1112,7 @@
         def visit(step, masked):
             start = pl.multiple_of(step * keys, keys)
             here = pl.ds(start, keys)
-            raised = jnp.exp2(lax.dot_general(queries, all_ref[here], ONES_NT, preferred_element_type=F32) * factor)
+            raised = jnp.exp2(lax.dot_general(queries, all_ref[here], ONES_NT, preferred_element_type=F32))
             if masked:
                 ok = allowed_block(0, 1, (wide, keys), first, second, part, base, start, rows, half_rows)
                 raised = jnp.where(ok, raised, 0.0)
@@ -1120,14 +1120,14 @@
 
         sweep_keys(visit, index, count * rows - rows, part, base, rows, half_rows, keys, sources)
         for source in range(sources):
-            tile = land[base + source, :, :LANES].astype(F32)
+            tile = land[base + source, :, :LANES].astype(F32) * factor
             outs = []
             for which in range(2):
                 place = (2 * source + which) * half_rows
                 acc = acc_ref[place:place + half_rows]
                 turn = swap_heads(acc, head)
                 outs.append(turn / acc if which == 0 else acc / turn)
-                high, middle, low = three_parts(-math.sqrt(head) * jnp.log(turn))
+                high, middle, low = three_parts(-math.log2(math.e) * jnp.log(turn))
                 query = tile if which == 0 else swap_heads(tile, head)
                 extra = jnp.where(lane == head, high, jnp.where(lane == head + 1, middle,
                                                                 jnp.where(lane == head + 2, low, 0.0)))
@@ -1181,7 +1181,6 @@
     twin = {"ctx": me + 1 - 2 * part}
     half_rows = msg_ref.shape[1]
     wide = sources * 2 * half_rows
-    factor = math.log2(math.e) / math.sqrt(head)
     shrink = 1.0 / math.sqrt(head)
     lane = lane_of((half_rows, LANES))
     greet(me, count)
@@ -1222,7 +1221,7 @@
 
     def key_tile(source, which):
         here = rows_of(source, which)
-        return jnp.where(lane < head, dk_ref[here] * shrink, dv_ref[here])
+        return jnp.where(lane < head, dk_ref[here] * math.log(2.0), dv_ref[here])
 
     def compute(index):
         base = index * sources
@@ -1252,9 +1251,9 @@
             raw = lax.dot_general(kone_ref[here], queries, ONES_NT, preferred_element_type=F32)
             if masked:
                 ok = allowed_block(1, 0, (keys, wide), first, second, part, base, start, rows, half_rows)
-                prob = jnp.where(ok, jnp.exp2(jnp.where(ok, raw, 0.0) * factor), 0.0)
+                prob = jnp.where(ok, jnp.exp2(jnp.where(ok, raw, 0.0)), 0.0)
             else:
-                prob = jnp.exp2(raw * factor)
+                prob = jnp.exp2(raw)
             along = lax.dot_general(vone_ref[here], grads, ONES_NT, preferred_element_type=F32)
             score = (prob * along).astype(BF)
             dv_ref[here] += jnp.dot(prob.astype(BF), grads, preferred_element_type=F32)

time: 482 us -> 481 us (level)
  no operation moved by 1% of the time
where the time goes in v8:
time: 481 us; the launch traced here: 480 us
  Pallas kernels  445 us (93%)
  waiting for transfers between devices  12.4 us (3%)
  starting transfers between devices  11.6 us (2%)
  local copies, waits for them, and re-layouts  5.91 us (1%)
    pallas_call x1, Pallas kernels, sum_over_chips(): pl.pallas_call(functools.partial(sum_kernel, jobs, len(lefts), len(outs),...  217 us
    pallas_call x5, Pallas kernels, call_tiled(): pl.pallas_call(kernel, grid=(tiles,), in_specs=[spec for _, spec in ins],...  81.9 us
    pallas_call x1, Pallas kernels, exchange_attend_back(): pl.pallas_call(functools.partial(attend_back_kernel, head, rows, keys, so...  71.6 us
    pallas_call x1, Pallas kernels, exchange_attend(): pl.pallas_call(functools.partial(attend_kernel, head, rows, keys, sources...  52.5 us
    pallas_call x2, Pallas kernels, call_plain(): pl.pallas_call(kernel, out_shape=tuple(outs) if many else outs, in_specs=...  13.5 us
    ppermute x6, waiting for transfers between devices, fast_device(): over_dp = lambda value: lax.ppermute(value, 'dp', [(0, 1), (1, 0)])  10.6 us
  transfers between devices with their start and end apart: 9, of which 3 were waited for; matrix products, arithmetic and copies ran while one was open for 1% of the time, Pallas kernels for 31%

profile of v8, /device:TPU:0, one launch (start us, length us, event | category | flops | bytes accessed | tf_op | source)
XLA Modules:
  0.0 480.5 jit_solution(12223460762621506110)
XLA Ops:
  0.7 0.8 slice.19
  1.4 2.3 collective-permute-start
  3.8 2.4 collective-permute-start.3
  6.2 1.3 fusion.9
  8.8 0.7 subtract_convert_fusion.1
  9.5 1.2 fusion.2
  10.7 1.3 subtract_convert_fusion.pos_ref
  12.1 0.0 collective-permute-done.prev_ref
  12.1 0.6 copy-done.1
  12.7 8.5 %mix.1 = (f32[256,1024]{1,0:T(8,128)}, bf16[1024,256]{1,0:T(8,128)(2,1)}, bf16[1024,256]{1,0:T(8,128)(2,1)}, bf16[256,1024]{1,0:T(8,128)(2,1)}, bf16[256,1024]{1...) custom-call(bf16[256,1024]{1,0:T(8,128)(2,1)} %tok_ref.3, ...), custom_call_target="tpu_custom_call" | custom-call | flops 2147483648 | bytes 12582912 | tf_op jit(solution)/shard_map/mix/pallas_call | solution.py:816
  21.2 0.8 slice.23
  21.9 1.3 collective-permute-start.4
  23.2 0.1 collective-permute-start.1
  23.3 2.0 collective-permute-start.2
  25.3 16.0 %feed_low.1 = (f32[256,1024]{1,0:T(8,128)}, bf16[1024,256]{1,0:T(8,128)(2,1)}, bf16[256,4608]{1,0:T(8,128)(2,1)}, bf16[256,4608]{1,0:T(8,128)(2,1)}, bf16[4608,256]{1,0:T(8,128)(2,1)}) custom-call(f32[256,1024]{1,0:T(8,128)} %get-tuple-element.126.hid_ref, bf16[1024]{0:T(1024)(128)(2,1)} %gain_ref.12, bf16[1024,4608]{1,0:T(8,128)(2,1)} %gate_ref.5, ...), custom_call_target="tpu_custom_call" | custom-call | flops 7247757312 | bytes 39845888 | tf_op jit(solution)/shard_map/feed_low/pallas_call | solution.py:816
  41.3 5.7 %project.1 = (bf16[16,128,256]{2,1,0:T(8,128)(2,1)}, bf16[1024,256]{1,0:T(8,128)(2,1)}, f32[256,1024]{1,0:T(8,128)}, f32[256,512]{1,0:T(8,128)}) custom-call(f32[256,1024]{1,0:T(8,128)} %get-tuple-element.127.hid_ref.two_ref, bf16[1024]{0:T(1024)(128)(2,1)} %gain_ref.11, bf16[1024,1024]{1,0:T(8,128)(2,1)} %wq_ref.3, bf16[1024,512]{1,0:T(8,128)(2,1)} %wk_ref.3, ...), custom_call_target="tpu_custom_call" | custom-call | flops 1073741824 | bytes 6291456 | tf_op jit(solution)/shard_map/project/pallas_call | solution.py:1908
  47.0 0.1 collective-permute-start.5
  47.1 0.0 collective-permute-done.4.cnext_ref
  47.1 0.0 collective-permute-done.3.refs_28_
  47.1 0.0 copy-start.6
  47.1 0.0 collective-permute-done.1
  47.1 0.0 copy-start.7
  47.1 1.2 collective-permute-done.2
  48.4 52.5 %attend.1 = (bf16[16,128,128]{2,1,0:T(8,128)(2,1)}, f32[16,128,128]{2,1,0:T(8,128)}, bf16[16,2,128,128]{3,2,1,0:T(8,128)(2,1)}, bf16[4096,128]{1,0:T(8,128)(2,1)...) custom-call(s32[1,3]{1,0:T(1,128)} %refs_0_.3, bf16[16,128,256]{2,1,0:T(8,128)(2,1)} %get-tuple-element.132.refs_1_, ...), custom_call_target="tpu_custom_call" | custom-call | flops 4294967296 | bytes 6291456 | tf_op jit(solution)/shard_map/attend/pallas_call | solution.py:1332
  100.8 0.0 copy-done
  100.9 0.0 copy-done.6
  100.9 0.0 copy-done.7
  100.9 0.0 copy-done.8
  100.9 27.4 %feed_top.1 = (f32[256,1024]{1,0:T(8,128)}, f32[256,1024]{1,0:T(8,128)}, bf16[256,1024]{1,0:T(8,128)(2,1)}, bf16[16,128,128]{2,1,0:T(8,128)(2,1)}, bf16[1024,256...) custom-call(bf16[16,128,128]{2,1,0:T(8,128)(2,1)} %get-tuple-element, ...), custom_call_target="tpu_custom_call" | custom-call | flops 14495514624 | bytes 47185920 | tf_op jit(solution)/shard_map/feed_top/pallas_call | solution.py:816
  128.3 0.0 collective-permute-done.5
  128.3 0.0 copy-start.9
  128.3 0.0 copy-start.5
  128.3 71.6 %attend_back.1 = (bf16[16,128,128]{2,1,0:T(8,128)(2,1)}, bf16[16,128,128]{2,1,0:T(8,128)(2,1)}, bf16[8,2,144,256]{3,2,1,0:T(8,128)(2,1)}, bf16[8,2,64,256]{3,2,1...) custom-call(s32[1,3]{1,0:T(1,128)} %refs_0_.3, ...), custom_call_target="tpu_custom_call" | custom-call | flops 10737418240 | bytes 8388608 | tf_op jit(solution)/shard_map/attend_back/pallas_call | solution.py:1360
  199.9 0.6 collective-permute-start.6
  200.5 1.5 collective-permute-start.8
  202.0 7.8 %project_back.1 = (bf16[256,1024]{1,0:T(8,128)(2,1)}, bf16[256,512]{1,0:T(8,128)(2,1)}, bf16[256,512]{1,0:T(8,128)(2,1)}, f32[256,1024]{1,0:T(8,128)}, f32[1,102...) custom-call(bf16[16,128,128]{2,1,0:T(8,128)(2,1)} %get-tuple-element.150.backq_ref, ...), custom_call_target="tpu_custom_call" | custom-call | flops 1048576 | bytes 1024 | tf_op jit(solution)/shard_map/project_back/pallas_call | solution.py:1908
  209.8 19.2 %feed_low_back.1 = (f32[256,1024]{1,0:T(8,128)}, f32[1,1024]{1,0:T(1,128)}, bf16[256,1024]{1,0:T(8,128)(2,1)}, bf16[256,1024]{1,0:T(8,128)(2,1)}, bf16[256,4608]{1,0:T(8,128)(2,1)}, /*index=5*/bf16[256,4608]{1,0:T(8,128)(2,1)}) custom-call(f32[256,1024]{1,0:T(8,128)} %get-tuple-element.155.grad_ref, f32[256,1024]{1,0:T(8,128)} %get-tuple-element.126.hid_ref, ...), custom_call_target="tpu_custom_call" | custom-call | flops 1048576 | bytes 1024 | tf_op jit(solution)/shard_map/feed_low_back/pallas_call | solution.py:816
  229.0 0.0 collective-permute-done.6.refs_29_
  229.0 0.0 copy-start.3
  229.0 0.8 slice.24
  229.8 1.3 collective-permute-start.7
  231.1 1.8 collective-permute-done.7.next_ref
  232.9 0.6 copy-done.2
  233.5 10.9 %mix_back.1 = (f32[256,1024]{1,0:T(8,128)}, f32[1,1024]{1,0:T(1,128)}, f32[3,1024]{1,0:T(4,128)}, bf16[256,3072]{1,0:T(8,128)(2,1)}) custom-call(f32[256,1024]{1,0:T(8,128)} %get-tuple-element.161.grad_ref, bf16[256,1024]{1,0:T(8,128)(2,1)} %get-tuple-element.162.low_ref.refs_23_, bf16[16,1024]{1,0:T(8,128)(2,1)} %copy-done.2, bf16[16,1024]{1,0:T(8,128)(2,1)} %copy-done, ...), custom_call_target="tpu_custom_call" | custom-call | flops 2147483648 | bytes 16777216 | tf_op jit(solution)/shard_map/mix_back/pallas_call | solution.py:816
  244.4 9.4 %collective-permute-done.8.refs_30_ = bf16[128,4608]{1,0:T(8,128)(2,1)S(1)} collective-permute-done((bf16[128,4608]{1,0:T(8,128)(2,1)S(1)}, bf16[128,4608]{1,0:T(8,128)(2,1)S(1)}, u32[]{:S(2)}, u32[]{:S(2)}) %collective-permute-start.8) | collective-permute-done | bytes 1179680 | tf_op jit(solution)/shard_map/ppermute | solution.py:1964
  253.8 1.0 copy-done.4
  254.8 217.2 %sum_over_chips.1 = (f32[64,1024]{1,0:T(8,128)}, f32[288,1024]{1,0:T(8,128)}, f32[64,4608]{1,0:T(8,128)}, f32[64,4608]{1,0:T(8,128)}, f32[64,1024]{1,0:T(8,128)}...) custom-call(bf16[8,2,64,256]{3,2,1,0:T(8,128)(2,1)} %bitcast.26, ...), custom_call_target="tpu_custom_call" | custom-call | flops 18253611008 | bytes 149600000 | tf_op jit(solution)/shard_map/sum_over_chips/pallas_call | solution.py:1849
  472.0 8.3 %hand_over.1 = (f32[64,1024]{1,0:T(8,128)}, f32[288,1024]{1,0:T(8,128)}, f32[64,4608]{1,0:T(8,128)}, f32[64,4608]{1,0:T(8,128)}, f32[64,1024]{1,0:T(8,128)}, /*i...) custom-call(f32[64,1024]{1,0:T(8,128)} %get-tuple-element.199.refs_0, ...), custom_call_target="tpu_custom_call" | custom-call | tf_op jit(solution)/shard_map/hand_over/pallas_call | solution.py:1893
  (10 shorter events, 0.0 us)
Async XLA Ops:
  1.4 10.7 %collective-permute-start = (bf16[16,1024]{1,0:T(8,128)(2,1)S(1)}, bf16[16,1024]{1,0:T(8,128)(2,1)S(1)}, u32[]{:S(2)}, u32[]{:S(2)}) collective-permute-start(bf16[16,1024]{1,0:T(8,128)(2,1)S(1)} %slice.19), channel_id=1, source_target_pairs={{0,1},{1,2},{2,3},{3,4},{4,5},{5,6},{6,7},{7,8},{8,9},{9,10},{10,1... | collective-permute-start | bytes 98312 | tf_op jit(solution)/shard_map/ppermute | solution.py:19
  3.8 43.3 %collective-permute-start.3 = (bf16[256,1024]{1,0:T(8,128)(2,1)}, bf16[256,1024]{1,0:T(8,128)(2,1)S(1)}, u32[]{:S(2)}, u32[]{:S(2)}) collective-permute-start(bf16[256,1024]{1,0:T(8,128)(2,1)} %refs_17_.1), channel_id=1, source_target_pairs={{0,16},{16,0},{1,17},{17,1},{2,18},{18,2},{3,19},{19,3},{4,20},{20... | collective-permute-start | bytes 1572872 | tf_op jit(solution)/shard_map/ppermute | solution.py:1964
  12.1 0.6 copy-start.1
  21.9 25.2 %collective-permute-start.4 = (bf16[16,1024]{1,0:T(8,128)(2,1)S(1)}, bf16[16,1024]{1,0:T(8,128)(2,1)S(1)}, u32[]{:S(2)}, u32[]{:S(2)}) collective-permute-start(bf16[16,1024]{1,0:T(8,128)(2,1)S(1)} %slice.23), channel_id=1, source_target_pairs={{1,0},{2,1},{3,2},{4,3},{5,4},{6,5},{7,6},{8,7},{9,8},{10,9},{11,1... | collective-permute-start | bytes 98312 | tf_op jit(solution)/shard_map/ppermute | solution.py:19
  23.2 23.9 %collective-permute-start.1 = (bf16[1024,256]{1,0:T(8,128)(2,1)}, bf16[1024,256]{1,0:T(8,128)(2,1)S(1)}, u32[]{:S(2)}, u32[]{:S(2)}) collective-permute-start(bf16[1024,256]{1,0:T(8,128)(2,1)} %get-tuple-element.129), channel_id=1, source_target_pairs={{0,16},{16,0},{1,17},{17,1},{2,18},{18,2},{3,19},{19,3},{4,20},{20... | collective-permute-start | bytes 1572872 | tf_op jit(solution)/shard_map/ppermute | solution.py:1964
  23.3 25.1 %collective-permute-start.2 = (bf16[1024,256]{1,0:T(8,128)(2,1)}, bf16[1024,256]{1,0:T(8,128)(2,1)S(1)}, u32[]{:S(2)}, u32[]{:S(2)}) collective-permute-start(bf16[1024,256]{1,0:T(8,128)(2,1)} %get-tuple-element.130), channel_id=1, source_target_pairs={{0,16},{16,0},{1,17},{17,1},{2,18},{18,2},{3,19},{19,3},{4,20},{20... | collective-permute-start | bytes 1572872 | tf_op jit(solution)/shard_map/ppermute | solution.py:1964
  47.0 81.3 %collective-permute-start.5 = (bf16[1024,256]{1,0:T(8,128)(2,1)}, bf16[1024,256]{1,0:T(8,128)(2,1)S(1)}, u32[]{:S(2)}, u32[]{:S(2)}) collective-permute-start(bf16[1024,256]{1,0:T(8,128)(2,1)} %get-tuple-element.141), channel_id=1, source_target_pairs={{0,16},{16,0},{1,17},{17,1},{2,18},{18,2},{3,19},{19,3},{4,20},{20... | collective-permute-start | bytes 1572872 | tf_op jit(solution)/shard_map/ppermute | solution.py:1964
  47.1 53.8 %copy-start = (bf16[16,1024]{1,0:T(8,128)(2,1)}, bf16[16,1024]{1,0:T(8,128)(2,1)S(1)}, u32[]{:S(2)}) copy-start(bf16[16,1024]{1,0:T(8,128)(2,1)S(1)} %collective-permute-done.4.cnext_ref) | copy-start | bytes 98308
  47.1 53.8 %copy-start.6 = (bf16[256,1024]{1,0:T(8,128)(2,1)}, bf16[256,1024]{1,0:T(8,128)(2,1)S(1)}, u32[]{:S(2)}) copy-start(bf16[256,1024]{1,0:T(8,128)(2,1)S(1)} %collective-permute-done.3.refs_28_) | copy-start | bytes 1572868
  47.1 53.8 %copy-start.7 = (bf16[1024,256]{1,0:T(8,128)(2,1)}, bf16[1024,256]{1,0:T(8,128)(2,1)S(1)}, u32[]{:S(2)}) copy-start(bf16[1024,256]{1,0:T(8,128)(2,1)S(1)} %collective-permute-done.1) | copy-start | bytes 1572868
  48.4 52.5 %copy-start.8 = (bf16[1024,256]{1,0:T(8,128)(2,1)}, bf16[1024,256]{1,0:T(8,128)(2,1)S(1)}, u32[]{:S(2)}) copy-start(bf16[1024,256]{1,0:T(8,128)(2,1)S(1)} %collective-permute-done.2) | copy-start | bytes 1572868
  128.3 71.6 %copy-start.9 = (bf16[1024,256]{1,0:T(8,128)(2,1)}, bf16[1024,256]{1,0:T(8,128)(2,1)S(1)}, u32[]{:S(2)}) copy-start(bf16[1024,256]{1,0:T(8,128)(2,1)S(1)} %collective-permute-done.5) | copy-start | bytes 1572868
  128.3 72.2 %copy-start.5 = (bf16[128,4608]{1,0:T(8,128)(2,1)S(1)}, bf16[128,4608]{1,0:T(8,128)(2,1)}, u32[]{:S(2)}) copy-start(bf16[128,4608]{1,0:T(8,128)(2,1)} %get-tuple-element.170) | copy-start | bytes 3538948
  199.9 29.1 %collective-permute-start.6 = (bf16[128,4608]{1,0:T(8,128)(2,1)}, bf16[128,4608]{1,0:T(8,128)(2,1)S(1)}, u32[]{:S(2)}, u32[]{:S(2)}) collective-permute-start(bf16[128,4608]{1,0:T(8,128)(2,1)} %get-tuple-element.160), channel_id=1, source_target_pairs={{0,16},{16,0},{1,17},{17,1},{2,18},{18,2},{3,19},{19,3},{4,20},{20... | collective-permute-start | bytes 3538952 | tf_op jit(solution)/shard_map/ppermute | solution.py:1964
  200.5 53.3 %collective-permute-start.8 = (bf16[128,4608]{1,0:T(8,128)(2,1)S(1)}, bf16[128,4608]{1,0:T(8,128)(2,1)S(1)}, u32[]{:S(2)}, u32[]{:S(2)}) collective-permute-start(bf16[128,4608]{1,0:T(8,128)(2,1)S(1)} %copy-done.5), channel_id=1, source_target_pairs={{0,16},{16,0},{1,17},{17,1},{2,18},{18,2},{3,19},{19,3},{4,20},{20... | collective-permute-start | bytes 3538952 | tf_op jit(solution)/shard_map/ppermute | solution.py:1964
  229.0 15.4 %copy-start.3 = (bf16[128,4608]{1,0:T(8,128)(2,1)}, bf16[128,4608]{1,0:T(8,128)(2,1)S(1)}, u32[]{:S(2)}) copy-start(bf16[128,4608]{1,0:T(8,128)(2,1)S(1)} %collective-permute-done.6.refs_29_) | copy-start | bytes 3538948
  229.8 3.1 collective-permute-start.7
  232.9 0.6 copy-start.2
  253.8 1.0 copy-start.4
